TPU v7x, 32 devices: a whole 2x2x4 slice. The times are simulated.
32 devices in a mesh: frames: 2 (over y), row: 4 (over x, core), col: 4 (over z).
Axes of the slice: x: 2, y: 2, z: 4, core: 2. Of those that a mesh axis runs over, the one named last changes fastest.
Arguments:
- mask_pixels: int32 [2048, 2048], P(('frames', 'row'), 'col'), parts along dimension 0, may hold values 0 or 1
- across_taps: bfloat16 [12, 2, 33], replicated, may hold values from -1 to 1
- down_taps: bfloat16 [12, 2, 33], replicated, may hold values from -1 to 1
- kernel_weights: float32 [12], replicated, may hold values from 0.05 to 0.5
- library: bfloat16 [32, 64, 128], P('col'), may hold values from 0 to 4
- cell_ids: int32 [8, 4, 8], P(('frames', 'row'), 'col'), parts along dimension 0, may hold values from 0 to 31, as said below
- cell_slots: int32 [8, 4, 8], P(('frames', 'row'), 'col'), parts along dimension 0, may hold values from 0 to 15, as said below
- cell_count: int32 [8, 4], P(('frames', 'row'), 'col'), parts along dimension 0, may hold values from 2 to 8
Outputs:
- resist: float32 [2048, 2048], P(('frames', 'row'), 'col'), parts along dimension 0
There are 2 independent parts, one for each index of `frames`. A program takes and returns all parts, laid end to end along the dimension named above; an argument that names none is the same for every part. Nothing has to cross between parts.
Inputs may be any that keep to these rules, and one draw needn't show every extreme that they name: `cell_ids`: among the 8 entries of a tile's list, at most 2 name cells of one block of 8 consecutive ids (k * 8 to k * 8 + 7), and the first two entries name cells of one such block. `cell_slots`: the slots of a tile's list are distinct.
All inputs are finite; a program needn't handle non-finite values. No bound on the sum of `mask_pixels` on one device may be relied on, other than what follows from the above.
Results may differ from a plain program's by a relative error of at most 0.00045.
Values may be sent and summed in bfloat16 or wider, within the bound.
No kernel may reach another device: no remote copies, remote signals or barrier semaphores. Data moves between devices by JAX's collectives and lax.ppermute only.
A program may use at most 64 MiB of HBM per device.

v0:
```python
import jax
import jax.numpy as jnp
from jax import lax
from jax.sharding import PartitionSpec as P

BLUR_HALF = 8


BLUR_SIGMA = 4.0


def extended_2(x, sides, width):
    for axis, dim in sides:
        count, length = (lax.axis_size(axis), x.shape[dim])
        up = [(i, (i + 1) % count) for i in range(count - 1)]
        down = [(j, i) for i, j in up]
        last = lax.slice_in_dim(x, length - width, length, axis=dim)
        initial = lax.slice_in_dim(x, 0, width, axis=dim)
        before = lax.ppermute(last, axis, up)
        after = lax.ppermute(initial, axis, down)
        x = jnp.concatenate([before, x, after], axis=dim)
    return x


def band_matrix(tap_values, half_width):
    window = 128 + 2 * half_width
    grid_shape = (window, 128, 2 * half_width + 1)
    in_index = lax.broadcasted_iota(jnp.int32, grid_shape, 0)
    out_index = lax.broadcasted_iota(jnp.int32, grid_shape, 1)
    lag_index = lax.broadcasted_iota(jnp.int32, grid_shape, 2)
    picker = (in_index - out_index == lag_index).astype(tap_values.dtype)
    return jnp.einsum(
        "...t,ijt->...ij",
        tap_values,
        picker,
        preferred_element_type=jnp.float32,
        precision=lax.Precision.HIGHEST,
    )


def blur_taps(half_width):
    offsets = (
        lax.broadcasted_iota(jnp.int32, (2 * half_width + 1,), 0).astype(jnp.float32) - half_width
    )
    weights = jnp.exp(-offsets * offsets / (2.0 * BLUR_SIGMA * BLUR_SIGMA))
    return weights / jnp.sum(weights)


def windows_last(padded, half_width):
    length = padded.shape[-1] - 2 * half_width
    blocks = length // 128
    pad_spec = [(0, 0)] * (padded.ndim - 1) + [(0, 128 - 2 * half_width)]
    spread = jnp.pad(padded, pad_spec).reshape(padded.shape[:-1] + (blocks + 1, 128))
    return jnp.concatenate([spread[..., :blocks, :], spread[..., 1:, : 2 * half_width]], axis=-1)


def windows_rows(padded, half_width):
    length = padded.shape[-2] - 2 * half_width
    blocks = length // 128
    pad_spec = [(0, 0)] * (padded.ndim - 2) + [(0, 128 - 2 * half_width), (0, 0)]
    spread = jnp.pad(padded, pad_spec).reshape(
        padded.shape[:-2] + (blocks + 1, 128, padded.shape[-1])
    )
    return jnp.concatenate(
        [spread[..., :blocks, :, :], spread[..., 1:, : 2 * half_width, :]], axis=-2
    )


def blur_straight(extended, blur_mat, half_width):
    sideways = jnp.einsum(
        "rbi,ij->rbj", windows_last(extended, half_width), blur_mat, precision=lax.Precision.HIGHEST
    )
    sideways = sideways.reshape(extended.shape[0], -1)
    downward = jnp.einsum(
        "biw,ij->bjw", windows_rows(sideways, half_width), blur_mat, precision=lax.Precision.HIGHEST
    )
    return downward.reshape(-1, sideways.shape[1])


def place_cells(library, cell_ids, cell_slots, cell_count, tile_rows, tile_cols, out_spec):
    cell_rows, cell_cols = (library.shape[1], library.shape[2])
    slot_rows = tile_rows // cell_rows
    slot_cols = tile_cols // cell_cols
    entries = cell_ids.shape[-1]
    ids_flat = cell_ids.reshape(entries)
    entry_iota = lax.broadcasted_iota(jnp.int32, (entries,), 0)
    is_live = entry_iota < cell_count.reshape(())
    slot_hit = (
        cell_slots.reshape(entries, 1)
        == lax.broadcasted_iota(jnp.int32, (1, slot_rows * slot_cols), 1)
    ) & is_live[:, None]
    slot_hit = slot_hit.astype(jnp.float32)
    sizes_by_letter = {"a": slot_rows, "p": cell_rows, "b": slot_cols, "q": cell_cols}
    empty_sum = jnp.zeros(tuple((sizes_by_letter[letter] for letter in out_spec)), jnp.float32)
    shard_cells = lax.all_gather(library, "col", axis=0, tiled=True)
    count_here = shard_cells.shape[0]
    id_match = (ids_flat[:, None] == lax.broadcasted_iota(jnp.int32, (1, count_here), 1)).astype(
        jnp.float32
    )
    place_table = (
        jnp.dot(slot_hit.T, id_match).reshape(slot_rows, slot_cols, count_here).astype(jnp.bfloat16)
    )
    return empty_sum + jnp.einsum(
        "abk,kpq->" + out_spec, place_table, shard_cells, preferred_element_type=jnp.float32
    )


def on_device(
    mask_pixels, across_taps, down_taps, kernel_weights, library, cell_ids, cell_slots, cell_count
):
    tile_rows, tile_cols = mask_pixels.shape
    half_width = (across_taps.shape[-1] - 1) // 2
    pixels = mask_pixels.astype(jnp.bfloat16)
    padded_mask = extended_2(pixels, (("col", 1),), half_width)
    first_mats = band_matrix(across_taps, half_width).astype(jnp.bfloat16)
    second_mats = band_matrix(down_taps, half_width).astype(jnp.bfloat16)
    blur_mat = band_matrix(blur_taps(BLUR_HALF), BLUR_HALF)
    tall_mask = extended_2(padded_mask, (("row", 0),), half_width)
    tall_windows = windows_last(tall_mask, half_width)
    tall_rows = tile_rows + 2 * half_width

    def kernel_step(running, inputs):
        first_mat, second_mat, weight = inputs
        pass_one = jnp.einsum(
            "rbi,pij->prbj", tall_windows, first_mat, preferred_element_type=jnp.float32
        )
        pass_one = pass_one.reshape(2, tall_rows, tile_cols).astype(jnp.bfloat16)
        pass_two = jnp.einsum(
            "pbiw,pij->pbjw",
            windows_rows(pass_one, half_width),
            second_mat,
            preferred_element_type=jnp.float32,
        )
        pass_two = pass_two.reshape(2, tile_rows, tile_cols)
        return (running + weight * jnp.sum(pass_two * pass_two, axis=0), None)

    start_total = jnp.zeros((tile_rows, tile_cols), jnp.float32)
    flat_image = lax.scan(kernel_step, start_total, (first_mats, second_mats, kernel_weights))[0]
    placed = place_cells(library, cell_ids, cell_slots, cell_count, tile_rows, tile_cols, "apbq")
    intensity = flat_image + placed.reshape(tile_rows, tile_cols)
    extended = extended_2(
        intensity.astype(jnp.bfloat16), (("row", 0), ("col", 1)), BLUR_HALF
    ).astype(intensity.dtype)
    return blur_straight(extended, blur_mat, BLUR_HALF)


def solution(mesh):
    placed = (
        P(("frames", "row"), "col"),
        P(),
        P(),
        P(),
        P("col", None, None),
        P(("frames", "row"), "col", None),
        P(("frames", "row"), "col", None),
        P(("frames", "row"), "col"),
    )
    return jax.shard_map(
        on_device,
        mesh=mesh,
        in_specs=placed,
        out_specs=P(("frames", "row"), "col"),
        check_vma=False,
    )
```

profile of v0, /device:TPU:0, one launch (start us, length us, event | category | flops | bytes accessed | tf_op | source)
XLA Modules:
  0.0 97.8 jit_solution(8133458689836300485)
XLA Ops:
  1.2 4.9 %collective-permute-start = (bf16[256,16]{1,0:T(8,128)(2,1)S(1)}, bf16[256,16]{1,0:T(8,128)(2,1)S(1)}, u32[]{:S(2)}, u32[]{:S(2)}) collective-permute-start(bf16[256,16]{1,0:T(8,128)(2,1)S(1)} %get-tuple-element.140), channel_id=1, source_target_pairs={{0,1},{1,2},{2,3},{4,5},{5,6},{6,7},{8,9},{9,10},{10,11},{12,13},{... | collective-permute-start | bytes 24584 | tf_op jit(solution)/shard_map/ppermute | solution.py:19
  6.1 1.3 %collective-permute-start.1 = (bf16[256,16]{1,0:T(8,128)(2,1)S(1)}, bf16[256,16]{1,0:T(8,128)(2,1)S(1)}, u32[]{:S(2)}, u32[]{:S(2)}) collective-permute-start(bf16[256,16]{1,0:T(8,128)(2,1)S(1)} %get-tuple-element.141), channel_id=1, source_target_pairs={{1,0},{2,1},{3,2},{5,4},{6,5},{7,6},{9,8},{10,9},{11,10},{13,12},{... | collective-permute-start | bytes 24584 | tf_op jit(solution)/shard_map/ppermute | solution.py:20
  7.4 1.4 %fusion.29 = bf16[12,2,160,128]{3,0,1,2:T(8,128)(2,1)S(1)} fusion(bf16[12,2,33]{2,1,0:T(2,128)(2,1)} %param.12), kind=kOutput, calls=%fused_computation.27 | convolution fusion | flops 34283520 | bytes 984624 | tf_op jit(solution)/shard_map/...t,ijt->...ij/dot_general | solution.py:32
  8.9 1.8 %fusion.26 = bf16[12,2,160,128]{3,0,1,2:T(8,128)(2,1)} fusion(bf16[12,2,33]{2,1,0:T(2,128)(2,1)S(1)} %copy-done.2), kind=kOutput, calls=%fused_computation.26 | convolution fusion | flops 34283520 | bytes 984624 | tf_op jit(solution)/shard_map/...t,ijt->...ij/dot_general | solution.py:32
  11.8 16.1 %all_gather.3 = bf16[32,64,128]{2,0,1:T(8,128)(2,1)S(1)} all-gather(bf16[8,64,128]{2,0,1:T(8,128)(2,1)S(1)} %copy.32), channel_id=1, replica_groups=mesh['frames'=2,'row'=4,'col'=4] {'col'}, dimensions={0}, use_global_device_ids=true | all-gather | bytes 655360 | tf_op jit(solution)/shard_map/all_gather | solution.py:95
  28.0 1.3 %collective-permute-start.2 = (bf16[16,544]{1,0:T(8,128)(2,1)S(1)}, bf16[16,544]{1,0:T(8,128)(2,1)S(1)}, u32[]{:S(2)}, u32[]{:S(2)}) collective-permute-start(bf16[16,544]{1,0:T(8,128)(2,1)S(1)} %get-tuple-element.134), channel_id=1, source_target_pairs={{0,4},{4,8},{8,12},{1,5},{5,9},{9,13},{2,6},{6,10},{10,14},{3,7},{... | collective-permute-start | bytes 52232 | tf_op jit(solution)/shard_map/ppermute | solution.py:19
  29.3 1.3 %collective-permute-start.3 = (bf16[16,544]{1,0:T(8,128)(2,1)S(1)}, bf16[16,544]{1,0:T(8,128)(2,1)S(1)}, u32[]{:S(2)}, u32[]{:S(2)}) collective-permute-start(bf16[16,544]{1,0:T(8,128)(2,1)S(1)} %get-tuple-element.135), channel_id=1, source_target_pairs={{4,0},{8,4},{12,8},{5,1},{9,5},{13,9},{6,2},{10,6},{14,10},{7,3},{... | collective-permute-start | bytes 52232 | tf_op jit(solution)/shard_map/ppermute | solution.py:20
  30.8 1.3 %copy.30 = bf16[12,2,160,128]{3,2,1,0:T(8,128)(2,1)} copy(bf16[12,2,160,128]{3,0,1,2:T(8,128)(2,1)S(1)} %fusion.29) | data formatting | bytes 1966080
  32.5 1.6 %collective-permute-done.3 = bf16[16,544]{1,0:T(8,128)(2,1)S(1)} collective-permute-done((bf16[16,544]{1,0:T(8,128)(2,1)S(1)}, bf16[16,544]{1,0:T(8,128)(2,1)S(1)}, u32[]{:S(2)}, u32[]{:S(2)}) %collective-permute-start.3) | collective-permute-done | bytes 17440 | tf_op jit(solution)/shard_map/ppermute | solution.py:20
  35.2 39.7 %while.13 = (s32[]{:T(128)}, f32[256,512]{1,0:T(8,128)S(1)}, f32[12]{0:T(128)S(1)}, bf16[12,2,160,128]{3,2,1,0:T(8,128)(2,1)}, bf16[12,2,160,128]{3,2,1,0:T(8,12...) while((s32[]{:T(128)}, f32[256,512]{1,0:T(8,128)S(1)}, ...), condition=%wide.region_3.4_spmd.clone, body=%wide.region_1.3_spmd.clone.sunk | while | flops 180649984 | bytes 8913533 | solution.py:138
  39.2 1.3 %fusion.88 = f32[128,2,512]{2,0,1:T(8,128)S(1)} fusion(bf16[2,2,32,512]{3,2,1,0:T(8,128)(2,1)S(1)} %slice.94, bf16[2,2,128,512]{3,2,1,0:T(8,128)(2,1)S(1)} %slice.95, bf16[12,2,160,128]{3,2,1,0:T(8,128)(2,1)} %get-tuple-element.200, s32[]{:T(128)} %get-tuple-element.188), kind=kOutput, calls=%fused_computation.2.clone.1 | convolution fusion | flops 85590016 | bytes 1262080 | tf_op jit(solution)/shard_map/while/body/eval_jaxpr/pbiw,pij->pbjw/dot_general | solution.py:128
  42.5 1.3 %fusion.88 = f32[128,2,512]{2,0,1:T(8,128)S(1)} fusion(bf16[2,2,32,512]{3,2,1,0:T(8,128)(2,1)S(1)} %slice.94, bf16[2,2,128,512]{3,2,1,0:T(8,128)(2,1)S(1)} %slice.95, bf16[12,2,160,128]{3,2,1,0:T(8,128)(2,1)} %get-tuple-element.200, s32[]{:T(128)} %get-tuple-element.188), kind=kOutput, calls=%fused_computation.2.clone.1 | convolution fusion | flops 85590016 | bytes 1262080 | tf_op jit(solution)/shard_map/while/body/eval_jaxpr/pbiw,pij->pbjw/dot_general | solution.py:128
  49.1 1.3 %fusion.88 = f32[128,2,512]{2,0,1:T(8,128)S(1)} fusion(bf16[2,2,32,512]{3,2,1,0:T(8,128)(2,1)S(1)} %slice.94, bf16[2,2,128,512]{3,2,1,0:T(8,128)(2,1)S(1)} %slice.95, bf16[12,2,160,128]{3,2,1,0:T(8,128)(2,1)} %get-tuple-element.200, s32[]{:T(128)} %get-tuple-element.188), kind=kOutput, calls=%fused_computation.2.clone.1 | convolution fusion | flops 85590016 | bytes 1262080 | tf_op jit(solution)/shard_map/while/body/eval_jaxpr/pbiw,pij->pbjw/dot_general | solution.py:128
  52.4 1.3 %fusion.88 = f32[128,2,512]{2,0,1:T(8,128)S(1)} fusion(bf16[2,2,32,512]{3,2,1,0:T(8,128)(2,1)S(1)} %slice.94, bf16[2,2,128,512]{3,2,1,0:T(8,128)(2,1)S(1)} %slice.95, bf16[12,2,160,128]{3,2,1,0:T(8,128)(2,1)} %get-tuple-element.200, s32[]{:T(128)} %get-tuple-element.188), kind=kOutput, calls=%fused_computation.2.clone.1 | convolution fusion | flops 85590016 | bytes 1262080 | tf_op jit(solution)/shard_map/while/body/eval_jaxpr/pbiw,pij->pbjw/dot_general | solution.py:128
  59.0 1.3 %fusion.88 = f32[128,2,512]{2,0,1:T(8,128)S(1)} fusion(bf16[2,2,32,512]{3,2,1,0:T(8,128)(2,1)S(1)} %slice.94, bf16[2,2,128,512]{3,2,1,0:T(8,128)(2,1)S(1)} %slice.95, bf16[12,2,160,128]{3,2,1,0:T(8,128)(2,1)} %get-tuple-element.200, s32[]{:T(128)} %get-tuple-element.188), kind=kOutput, calls=%fused_computation.2.clone.1 | convolution fusion | flops 85590016 | bytes 1262080 | tf_op jit(solution)/shard_map/while/body/eval_jaxpr/pbiw,pij->pbjw/dot_general | solution.py:128
  62.3 1.3 %fusion.88 = f32[128,2,512]{2,0,1:T(8,128)S(1)} fusion(bf16[2,2,32,512]{3,2,1,0:T(8,128)(2,1)S(1)} %slice.94, bf16[2,2,128,512]{3,2,1,0:T(8,128)(2,1)S(1)} %slice.95, bf16[12,2,160,128]{3,2,1,0:T(8,128)(2,1)} %get-tuple-element.200, s32[]{:T(128)} %get-tuple-element.188), kind=kOutput, calls=%fused_computation.2.clone.1 | convolution fusion | flops 85590016 | bytes 1262080 | tf_op jit(solution)/shard_map/while/body/eval_jaxpr/pbiw,pij->pbjw/dot_general | solution.py:128
  68.9 1.3 %fusion.88 = f32[128,2,512]{2,0,1:T(8,128)S(1)} fusion(bf16[2,2,32,512]{3,2,1,0:T(8,128)(2,1)S(1)} %slice.94, bf16[2,2,128,512]{3,2,1,0:T(8,128)(2,1)S(1)} %slice.95, bf16[12,2,160,128]{3,2,1,0:T(8,128)(2,1)} %get-tuple-element.200, s32[]{:T(128)} %get-tuple-element.188), kind=kOutput, calls=%fused_computation.2.clone.1 | convolution fusion | flops 85590016 | bytes 1262080 | tf_op jit(solution)/shard_map/while/body/eval_jaxpr/pbiw,pij->pbjw/dot_general | solution.py:128
  75.0 4.4 %collective-permute-start.4 = (bf16[8,512]{1,0:T(8,128)(2,1)S(1)}, bf16[8,512]{1,0:T(8,128)(2,1)S(1)}, u32[]{:S(2)}, u32[]{:S(2)}) collective-permute-start(bf16[8,512]{1,0:T(8,128)(2,1)S(1)} %get-tuple-element.138), channel_id=1, source_target_pairs={{0,4},{4,8},{8,12},{1,5},{5,9},{9,13},{2,6},{6,10},{10,14},{3,7},{... | collective-permute-start | bytes 24584 | tf_op jit(solution)/shard_map/ppermute | solution.py:19
  79.5 1.3 %collective-permute-start.5 = (bf16[8,512]{1,0:T(8,128)(2,1)S(1)}, bf16[8,512]{1,0:T(8,128)(2,1)S(1)}, u32[]{:S(2)}, u32[]{:S(2)}) collective-permute-start(bf16[8,512]{1,0:T(8,128)(2,1)S(1)} %get-tuple-element.139), channel_id=1, source_target_pairs={{4,0},{8,4},{12,8},{5,1},{9,5},{13,9},{6,2},{10,6},{14,10},{7,3},{... | collective-permute-start | bytes 24584 | tf_op jit(solution)/shard_map/ppermute | solution.py:20
  82.6 3.9 %collective-permute-start.6 = (bf16[272,8]{1,0:T(8,128)(2,1)S(1)}, bf16[272,8]{1,0:T(8,128)(2,1)S(1)}, u32[]{:S(2)}, u32[]{:S(2)}) collective-permute-start(bf16[272,8]{1,0:T(8,128)(2,1)S(1)} %get-tuple-element.136), channel_id=1, source_target_pairs={{0,1},{1,2},{2,3},{4,5},{5,6},{6,7},{8,9},{9,10},{10,11},{12,13},{... | collective-permute-start | bytes 13064 | tf_op jit(solution)/shard_map/ppermute | solution.py:19
  86.5 1.3 %collective-permute-start.7 = (bf16[272,8]{1,0:T(8,128)(2,1)S(1)}, bf16[272,8]{1,0:T(8,128)(2,1)S(1)}, u32[]{:S(2)}, u32[]{:S(2)}) collective-permute-start(bf16[272,8]{1,0:T(8,128)(2,1)S(1)} %get-tuple-element.137), channel_id=1, source_target_pairs={{1,0},{2,1},{3,2},{5,4},{6,5},{7,6},{9,8},{10,9},{11,10},{13,12},{... | collective-permute-start | bytes 13064 | tf_op jit(solution)/shard_map/ppermute | solution.py:20
  89.0 3.7 %collective-permute-done.7 = bf16[272,8]{1,0:T(8,128)(2,1)S(1)} collective-permute-done((bf16[272,8]{1,0:T(8,128)(2,1)S(1)}, bf16[272,8]{1,0:T(8,128)(2,1)S(1)}, u32[]{:S(2)}, u32[]{:S(2)}) %collective-permute-start.7) | collective-permute-done | bytes 4384 | tf_op jit(solution)/shard_map/ppermute | solution.py:20
  93.3 2.3 %fusion.32 = f32[272,4,128]{2,0,1:T(8,128)S(1)} fusion(f32[144,128,1]{1,0,2:T(8,128)S(1)} %bitcast.115, f32[272,4,16]{0,2,1:T(8,128)S(1)} %slice.85, f32[272,4,128]{0,2,1:T(8,128)S(1)} %slice.84), kind=kOutput, calls=%fused_computation.30 | convolution fusion | flops 240804864 | bytes 1257472 | tf_op jit(solution)/shard_map/rbi,ij->rbj/dot_general | solution.py:70
  96.4 1.4 %fusion.41 = f32[128,2,512]{2,0,1:T(8,128)} fusion(f32[144,128,1]{1,0,2:T(8,128)S(1)} %bitcast.116, f32[2,16,512]{2,1,0:T(8,128)S(1)} %slice.87, f32[2,128,512]{2,1,0:T(8,128)S(1)} %slice.72), kind=kOutput, calls=%fused_computation.40 | convolution fusion | flops 226639872 | bytes 1187840 | tf_op jit(solution)/shard_map/biw,ij->bjw/dot_general | solution.py:74
  (150 shorter events, 37.6 us)
Async XLA Ops:
  0.0 8.9 %copy-start.2 = (bf16[12,2,33]{2,1,0:T(2,128)(2,1)S(1)}, bf16[12,2,33]{2,1,0:T(2,128)(2,1)}, u32[]{:S(2)}) copy-start(bf16[12,2,33]{2,1,0:T(2,128)(2,1)} %param.11) | copy-start | bytes 4756
  1.2 26.7 %collective-permute-start = (bf16[256,16]{1,0:T(8,128)(2,1)S(1)}, bf16[256,16]{1,0:T(8,128)(2,1)S(1)}, u32[]{:S(2)}, u32[]{:S(2)}) collective-permute-start(bf16[256,16]{1,0:T(8,128)(2,1)S(1)} %get-tuple-element.140), channel_id=1, source_target_pairs={{0,1},{1,2},{2,3},{4,5},{5,6},{6,7},{8,9},{9,10},{10,11},{12,13},{... | collective-permute-start | bytes 24584 | tf_op jit(solution)/shard_map/ppermute | solution.py:19
  6.1 21.8 %collective-permute-start.1 = (bf16[256,16]{1,0:T(8,128)(2,1)S(1)}, bf16[256,16]{1,0:T(8,128)(2,1)S(1)}, u32[]{:S(2)}, u32[]{:S(2)}) collective-permute-start(bf16[256,16]{1,0:T(8,128)(2,1)S(1)} %get-tuple-element.141), channel_id=1, source_target_pairs={{1,0},{2,1},{3,2},{5,4},{6,5},{7,6},{9,8},{10,9},{11,10},{13,12},{... | collective-permute-start | bytes 24584 | tf_op jit(solution)/shard_map/ppermute | solution.py:20
  8.9 1.9 %copy-start.1 = (bf16[8,64,128]{2,1,0:T(8,128)(2,1)S(1)}, bf16[8,64,128]{2,1,0:T(8,128)(2,1)}, u32[]{:S(2)}) copy-start(bf16[8,64,128]{2,1,0:T(8,128)(2,1)} %param.14) | copy-start | bytes 393220
  8.9 2.6 %copy-start.3 = (s32[1,1,8]{2,1,0:T(1,128)S(1)}, s32[1,1,8]{2,1,0:T(1,128)}, u32[]{:S(2)}) copy-start(s32[1,1,8]{2,1,0:T(1,128)} %param.15) | copy-start | bytes 100
  8.9 2.6 %copy-start.4 = (s32[1,1,8]{2,1,0:T(1,128)S(1)}, s32[1,1,8]{2,1,0:T(1,128)}, u32[]{:S(2)}) copy-start(s32[1,1,8]{2,1,0:T(1,128)} %param.16) | copy-start | bytes 100
  28.0 4.5 %collective-permute-start.2 = (bf16[16,544]{1,0:T(8,128)(2,1)S(1)}, bf16[16,544]{1,0:T(8,128)(2,1)S(1)}, u32[]{:S(2)}, u32[]{:S(2)}) collective-permute-start(bf16[16,544]{1,0:T(8,128)(2,1)S(1)} %get-tuple-element.134), channel_id=1, source_target_pairs={{0,4},{4,8},{8,12},{1,5},{5,9},{9,13},{2,6},{6,10},{10,14},{3,7},{... | collective-permute-start | bytes 52232 | tf_op jit(solution)/shard_map/ppermute | solution.py:19
  29.3 4.8 %collective-permute-start.3 = (bf16[16,544]{1,0:T(8,128)(2,1)S(1)}, bf16[16,544]{1,0:T(8,128)(2,1)S(1)}, u32[]{:S(2)}, u32[]{:S(2)}) collective-permute-start(bf16[16,544]{1,0:T(8,128)(2,1)S(1)} %get-tuple-element.135), channel_id=1, source_target_pairs={{4,0},{8,4},{12,8},{5,1},{9,5},{13,9},{6,2},{10,6},{14,10},{7,3},{... | collective-permute-start | bytes 52232 | tf_op jit(solution)/shard_map/ppermute | solution.py:20
  30.8 1.3 %copy-start = (bf16[12,2,160,128]{3,0,1,2:T(8,128)(2,1)S(1)}, bf16[12,2,160,128]{3,0,1,2:T(8,128)(2,1)}, u32[]{:S(2)}) copy-start(bf16[12,2,160,128]{3,0,1,2:T(8,128)(2,1)} %fusion.26) | copy-start | bytes 2949124
  34.5 0.7 copy-start.5
  75.0 6.5 %collective-permute-start.4 = (bf16[8,512]{1,0:T(8,128)(2,1)S(1)}, bf16[8,512]{1,0:T(8,128)(2,1)S(1)}, u32[]{:S(2)}, u32[]{:S(2)}) collective-permute-start(bf16[8,512]{1,0:T(8,128)(2,1)S(1)} %get-tuple-element.138), channel_id=1, source_target_pairs={{0,4},{4,8},{8,12},{1,5},{5,9},{9,13},{2,6},{6,10},{10,14},{3,7},{... | collective-permute-start | bytes 24584 | tf_op jit(solution)/shard_map/ppermute | solution.py:19
  79.5 3.1 %collective-permute-start.5 = (bf16[8,512]{1,0:T(8,128)(2,1)S(1)}, bf16[8,512]{1,0:T(8,128)(2,1)S(1)}, u32[]{:S(2)}, u32[]{:S(2)}) collective-permute-start(bf16[8,512]{1,0:T(8,128)(2,1)S(1)} %get-tuple-element.139), channel_id=1, source_target_pairs={{4,0},{8,4},{12,8},{5,1},{9,5},{13,9},{6,2},{10,6},{14,10},{7,3},{... | collective-permute-start | bytes 24584 | tf_op jit(solution)/shard_map/ppermute | solution.py:20
  82.6 6.4 %collective-permute-start.6 = (bf16[272,8]{1,0:T(8,128)(2,1)S(1)}, bf16[272,8]{1,0:T(8,128)(2,1)S(1)}, u32[]{:S(2)}, u32[]{:S(2)}) collective-permute-start(bf16[272,8]{1,0:T(8,128)(2,1)S(1)} %get-tuple-element.136), channel_id=1, source_target_pairs={{0,1},{1,2},{2,3},{4,5},{5,6},{6,7},{8,9},{9,10},{10,11},{12,13},{... | collective-permute-start | bytes 13064 | tf_op jit(solution)/shard_map/ppermute | solution.py:19
  86.5 6.2 %collective-permute-start.7 = (bf16[272,8]{1,0:T(8,128)(2,1)S(1)}, bf16[272,8]{1,0:T(8,128)(2,1)S(1)}, u32[]{:S(2)}, u32[]{:S(2)}) collective-permute-start(bf16[272,8]{1,0:T(8,128)(2,1)S(1)} %get-tuple-element.137), channel_id=1, source_target_pairs={{1,0},{2,1},{3,2},{5,4},{6,5},{7,6},{9,8},{10,9},{11,10},{13,12},{... | collective-permute-start | bytes 13064 | tf_op jit(solution)/shard_map/ppermute | solution.py:20
where the time goes:
time: 99.3 us; the launch traced here: 97.8 us
  matrix products  28.8 us (29%)
  starting transfers between devices  19.7 us (20%)
  blocking collectives  16.1 us (16%)
  local copies, waits for them, and re-layouts  13.4 us (13%)
  other arithmetic  11.7 us (12%)
  waiting for transfers between devices  6.27 us (6%)
    all_gather x1, blocking collectives, place_cells(): shard_cells = lax.all_gather(library, 'col', axis=0, tiled=True)  16.1 us
    dot_general x12, matrix products, kernel_step(): jnp.einsum('pbiw,pij->pbjw', windows_rows(pass_one, half_width), second_m...  15.3 us
    ppermute x4, starting transfers between devices, extended_2(): before = lax.ppermute(last, axis, up)  14.5 us
    mul x12, other arithmetic, kernel_step(): return (running + weight * jnp.sum(pass_two * pass_two, axis=0), None)  7.17 us
    dynamic_slice x12, local copies, waits for them, and re-layouts, on_device(): lax.scan(kernel_step, start_total, (first_mats, second_mats, kernel_weigh...  7.1 us
    ppermute x4, waiting for transfers between devices, extended_2(): after = lax.ppermute(initial, axis, down)  6.26 us
    ppermute x4, starting transfers between devices, extended_2(): after = lax.ppermute(initial, axis, down)  5.17 us
    dot_general x12, matrix products, kernel_step(): jnp.einsum('rbi,pij->prbj', tall_windows, first_mat, preferred_element_ty...  4.83 us
  transfers between devices with their start and end apart: 8, of which 3 were waited for; matrix products, arithmetic and copies ran while one was open for 8% of the time, Pallas kernels for 0%

commit v1 on v0

v1 whole, which is shorter than its diff:
```python
import functools
import math

import jax
import jax.numpy as jnp
from jax import lax
from jax.experimental import pallas as pl
from jax.experimental.pallas import tpu as pltpu
from jax.sharding import PartitionSpec as P

BLUR_HALF = 8
BLUR_SIGMA = 4.0
HALF = 16
RIM = HALF + BLUR_HALF
STRIP = 32
CB = 176
NB = 3
MAIN = 224
EDGE_IN = 80
EDGE_OUT = 48
EDGE_AT = (0, 48, 128)
WIDE = 640
F32 = jnp.float32
BF16 = jnp.bfloat16
VMEM = pl.BlockSpec(memory_space=pltpu.VMEM)
SMEM = pl.BlockSpec(memory_space=pltpu.SMEM)
PARAMS = pltpu.CompilerParams(vmem_limit_bytes=40 * 1024 * 1024)


def dot_nt(a, b):
    return lax.dot_general(a, b, (((1,), (1,)), ((), ())), preferred_element_type=F32)


def dot_nn(a, b):
    return lax.dot_general(a, b, (((1,), (0,)), ((), ())), preferred_element_type=F32)


def prep_kernel(mask, table, first, last, pixels):
    full = mask[...].astype(F32)
    pixels[...] = full
    cols = full.shape[1]
    first[0:STRIP, :] = full[:, 0:128].T[0:STRIP].astype(BF16)
    last[0:STRIP, :] = full[:, cols - 128 : cols].T[128 - STRIP :].astype(BF16)
    first[STRIP:, :] = table[...]
    last[STRIP:, :] = table[...]


def mid_kernel(pixels, left, right, table, top, bottom, wide):
    rows = pixels.shape[0]
    lhs = left[0:STRIP, :].astype(F32)
    rhs = right[0:STRIP, :].astype(F32)
    fill = jnp.zeros((128 - STRIP, rows), F32)
    lhs = jnp.concatenate([lhs, fill], axis=0).T
    rhs = jnp.concatenate([rhs, fill], axis=0).T
    full = jnp.concatenate(
        [lhs[:, STRIP - RIM : STRIP], pixels[...], rhs[:, 0 : WIDE - RIM - pixels.shape[1]]], axis=1
    )
    wide[...] = full
    top[0:STRIP, :] = full[0:STRIP].astype(BF16)
    bottom[0:STRIP, :] = full[rows - STRIP :].astype(BF16)
    tables = jnp.concatenate(
        [left[STRIP:, 0:128], table[:, 0:128], right[STRIP:, 0:128], jnp.zeros((16, 256), BF16)], axis=1
    )
    top[STRIP:, :] = tables
    bottom[STRIP:, :] = tables


def bands_kernel(across, down, b1, d_main, d_edge, g_hi, g_lo, g2_hi, g2_lo):
    row = lax.broadcasted_iota(jnp.int32, (128, 128), 0)
    lane = lax.broadcasted_iota(jnp.int32, (128, 128), 1)
    zero = jnp.zeros((128, 128), F32)

    def blur_matrix(width, shift):
        at = lax.broadcasted_iota(jnp.int32, (128, width), 1)
        lag = at - lax.broadcasted_iota(jnp.int32, (128, width), 0) - shift
        total = sum(math.exp(-(t * t) / (2 * BLUR_SIGMA**2)) for t in range(-BLUR_HALF, BLUR_HALF + 1))
        off = (lag - BLUR_HALF).astype(F32)
        g = jnp.exp(-off * off / (2.0 * BLUR_SIGMA * BLUR_SIGMA)) * (1.0 / total)
        g = jnp.where((lag >= 0) & (lag <= 2 * BLUR_HALF), g, 0.0)
        hi = g.astype(BF16)
        return hi, (g - hi.astype(F32)).astype(BF16)

    g_hi[...], g_lo[...] = blur_matrix(256, 0)
    g2_hi[...], g2_lo[...] = blur_matrix(384, 128 - BLUR_HALF)

    def step(kp, carry):
        taps = jnp.broadcast_to(across[pl.ds(kp, 1), :], (128, 128))
        cyc = pltpu.roll(taps, 0, 1, stride=1, stride_axis=0)
        upper = jnp.where(lane >= row, cyc, 0.0).astype(BF16)
        over = jnp.where(lane < row, cyc, 0.0).astype(BF16)
        b1[kp, 0:128, 0:128] = upper
        b1[kp, 0:128, 128:256] = over
        b1[kp, 128:CB, 0:128] = jnp.zeros((CB - 128, 128), BF16)
        b1[kp, 128:CB, 128:256] = upper[0 : CB - 128]
        taps = jnp.broadcast_to(down[pl.ds(kp, 1), :], (128, 128))
        cyc = pltpu.roll(taps, 0, 1, stride=1, stride_axis=0).T
        same = jnp.where(row >= lane, cyc, 0.0)
        over = jnp.where(row < lane, cyc, 0.0)
        d_main[kp, 0:128, 0:128] = same.astype(BF16)
        d_main[kp, 0:128, 128:256] = zero.astype(BF16)
        d_main[kp, 128:256, 0:128] = over.astype(BF16)
        d_main[kp, 128:256, 128:256] = same.astype(BF16)
        edge = jnp.where(lane < EDGE_OUT, same, 0.0)
        moved = pltpu.roll(edge, EDGE_AT[1], 1)[0:EDGE_IN].astype(BF16)
        edge = edge[0:EDGE_IN].astype(BF16)
        none = jnp.zeros((EDGE_IN, 128), BF16)
        d_edge[kp, 0:EDGE_IN, 0:128] = edge
        d_edge[kp, 0:EDGE_IN, 128:256] = none
        d_edge[kp, EDGE_IN : 2 * EDGE_IN, 0:128] = moved
        d_edge[kp, EDGE_IN : 2 * EDGE_IN, 128:256] = none
        d_edge[kp, 2 * EDGE_IN : 3 * EDGE_IN, 0:128] = none
        d_edge[kp, 2 * EDGE_IN : 3 * EDGE_IN, 128:256] = edge
        d_edge[kp, 3 * EDGE_IN :, :] = jnp.zeros((256 - 3 * EDGE_IN, 256), BF16)
        return carry

    lax.fori_loop(0, across.shape[0], step, 0)


def socs_kernel(weights, wide, above, below, b1, d_main, d_edge, acc, x_win, first):
    rows = wide.shape[0]
    full = jnp.concatenate(
        [
            above[0:STRIP, :].astype(F32)[STRIP - RIM :],
            wide[...],
            below[0:STRIP, :].astype(F32)[0:RIM],
        ],
        axis=0,
    )
    edge_rows = []
    for b in range(NB):
        part = full[:, CB * b : CB * b + 256]
        x_win[b] = part[0:256].astype(BF16)
        edge_rows.append(part[MAIN : MAIN + EDGE_IN])
    edge_rows.append(jnp.zeros((256 - NB * EDGE_IN, 256), F32))
    x_win[NB] = jnp.concatenate(edge_rows, axis=0).astype(BF16)
    acc[...] = jnp.zeros(acc.shape, F32)

    def step(k, carry):
        taps = b1[pl.ds(2 * k, 2)].reshape(2 * CB, 256)
        for j in range(NB + 1):
            part = dot_nt(taps, x_win[j]).astype(BF16)
            first[0, j] = part[0:CB]
            first[1, j] = part[CB:]
        weight = weights[k]
        total = None
        for p in range(2):
            second = dot_nn(first[p, 0:NB].reshape(NB * CB, 256), d_main[2 * k + p])
            total = second * second if total is None else total + second * second
        acc[0:NB] += (weight * total).reshape(NB, CB, 256)
        total = None
        for p in range(2):
            second = dot_nn(first[p, NB], d_edge[2 * k + p])
            total = second * second if total is None else total + second * second
        acc[NB] += weight * total
        return carry

    lax.fori_loop(0, b1.shape[0] // 2, step, 0)


def final_kernel(entries, per, tables, place, acc, g_hi, g_lo, g2_hi, g2_lo, *rest):
    shards = rest[:-6]
    out, cells, slots, placed, flat, blurred = rest[-6:]
    count = len(shards)
    rows, cols = out.shape
    for i, shard in enumerate(shards):
        cells[pl.ds(i * per, per)] = shard[...]
    empty = count * per
    cells[empty] = jnp.zeros(cells.shape[1:], BF16)
    col = place[4]

    for t in range(9):
        for s in range(16):
            slots[t * 17 + s] = empty
        live = tables[t, 2 * entries]
        for n in range(entries):
            cell = tables[t, n]
            owner = cell // per
            behind = jnp.where(owner <= col, col - owner, col - owner + count)
            at = jnp.where(n < live, tables[t, entries + n], 16)
            slots[t * 17 + at] = behind * per + cell - owner * per

    slot_rows, slot_cols = rows // 64, cols // 128
    for i in range(-1, slot_rows + 1):
        for j in range(-1, slot_cols + 1):
            ti = 0 if i < 0 else (2 if i == slot_rows else 1)
            tj = 0 if j < 0 else (2 if j == slot_cols else 1)
            image = slots[(3 * ti + tj) * 17 + (i % slot_rows) * slot_cols + j % slot_cols]
            lanes = slice(128 + 128 * j, 256 + 128 * j)
            if i < 0:
                placed[0:8, lanes] = cells[image, 48:64, :].astype(F32)[8:16]
            elif i == slot_rows:
                placed[8 + rows : 16 + rows, lanes] = cells[image, 0:16, :].astype(F32)[0:8]
            else:
                placed[8 + 64 * i : 72 + 64 * i, lanes] = cells[image].astype(F32)
    placed[16 + rows :, :] = jnp.zeros((placed.shape[0] - 16 - rows, placed.shape[1]), F32)

    at_row = lax.broadcasted_iota(jnp.int32, (CB, 384), 1) - BLUR_HALF
    row_ok = (at_row >= place[0]) & (at_row < place[1])
    at_col = lax.broadcasted_iota(jnp.int32, (CB, 384), 0) - BLUR_HALF
    for b in range(NB):
        edge = acc[NB, :, EDGE_AT[b] : EDGE_AT[b] + EDGE_OUT]
        part = jnp.concatenate(
            [acc[b, :, 0:MAIN], edge, jnp.zeros((CB, 384 - MAIN - EDGE_OUT), F32)], axis=1
        )
        here = at_col + b * CB
        keep = row_ok & (here >= place[2]) & (here < place[3])
        flat[b * CB : (b + 1) * CB, :] = jnp.where(keep, part, 0.0).astype(BF16)
    flat[NB * CB :, :] = jnp.zeros((flat.shape[0] - NB * CB, 384), BF16)

    for j in range(cols // 128):
        image = flat[128 * j : 128 * j + 256, :]
        cell = placed[:, 128 * j : 128 * j + 384].astype(BF16)
        part = dot_nn(g_hi[...], image) + dot_nn(g_lo[...], image)
        part += dot_nt(g2_hi[...], cell) + dot_nt(g2_lo[...], cell)
        high = part.astype(BF16)
        blurred[0, 128 * j : 128 * j + 128, :] = high
        blurred[1, 128 * j : 128 * j + 128, :] = (part - high.astype(F32)).astype(BF16)
    for i in range(rows // 128):
        lanes = slice(128 * i, 128 * i + 256)
        high, low = blurred[0, :, lanes], blurred[1, :, lanes]
        out[128 * i : 128 * i + 128, :] = (
            dot_nt(g_hi[...], high) + dot_nt(g_lo[...], high) + dot_nt(g_hi[...], low)
        )


def shape(dims, dtype):
    return jax.ShapeDtypeStruct(dims, dtype)


def on_device(
    mask_pixels, across_taps, down_taps, kernel_weights, library, cell_ids, cell_slots, cell_count
):
    rows, cols = mask_pixels.shape
    pairs = across_taps.shape[0] * 2
    taps = across_taps.shape[-1]
    entries = cell_ids.shape[-1]
    per = library.shape[0]
    n_row, n_col = lax.axis_size("row"), lax.axis_size("col")
    row, col = lax.axis_index("row"), lax.axis_index("col")
    table = jnp.concatenate([cell_ids.reshape(-1), cell_slots.reshape(-1), cell_count.reshape(-1)])
    table = jnp.pad(table.astype(BF16)[None, :], ((0, 15), (0, 256 - 2 * entries - 1)))

    first, last, pixels = pl.pallas_call(
        prep_kernel,
        out_shape=(
            shape((STRIP + 16, rows), BF16),
            shape((STRIP + 16, rows), BF16),
            shape((rows, cols), F32),
        ),
        in_specs=[VMEM] * 2,
        out_specs=(VMEM,) * 3,
        compiler_params=PARAMS,
        name="prep",
    )(mask_pixels, table)

    up = lambda n: [(i, i + 1) for i in range(n - 1)]
    down = lambda n: [(i + 1, i) for i in range(n - 1)]
    left = lax.ppermute(last, "col", up(n_col))
    right = lax.ppermute(first, "col", down(n_col))

    shards = [library]
    for shift in range(1, n_col):
        shards.append(lax.ppermute(library, "col", [(i, (i + shift) % n_col) for i in range(n_col)]))

    top, bottom, wide = pl.pallas_call(
        mid_kernel,
        out_shape=(
            shape((STRIP + 16, WIDE), BF16),
            shape((STRIP + 16, WIDE), BF16),
            shape((rows, WIDE), F32),
        ),
        in_specs=[VMEM] * 4,
        out_specs=(VMEM,) * 3,
        compiler_params=PARAMS,
        name="mid",
    )(pixels, left, right, table)
    above = lax.ppermute(bottom, "row", up(n_row))
    below = lax.ppermute(top, "row", down(n_row))

    pad_taps = lambda x: jnp.pad(x.reshape(pairs, taps).astype(F32), ((0, 0), (0, 128 - taps)))
    b1, d_main, d_edge, g_hi, g_lo, g2_hi, g2_lo = pl.pallas_call(
        bands_kernel,
        out_shape=(
            shape((pairs, CB, 256), BF16),
            shape((pairs, 256, 256), BF16),
            shape((pairs, 256, 256), BF16),
            shape((128, 256), BF16),
            shape((128, 256), BF16),
            shape((128, 384), BF16),
            shape((128, 384), BF16),
        ),
        in_specs=[VMEM] * 2,
        out_specs=(VMEM,) * 7,
        compiler_params=PARAMS,
        cost_estimate=pl.CostEstimate(flops=2 * 10**9, bytes_accessed=8 * 10**6, transcendentals=0),
        name="bands",
    )(pad_taps(across_taps), pad_taps(down_taps))

    acc = pl.pallas_call(
        socs_kernel,
        out_shape=shape((NB + 1, CB, 256), F32),
        in_specs=[SMEM] + [VMEM] * 6,
        out_specs=VMEM,
        scratch_shapes=[
            pltpu.VMEM((NB + 1, 256, 256), BF16),
            pltpu.VMEM((2, NB + 1, CB, 256), BF16),
        ],
        compiler_params=PARAMS,
        cost_estimate=pl.CostEstimate(flops=5 * 10**9, bytes_accessed=8 * 10**6, transcendentals=0),
        name="socs",
    )(kernel_weights, wide, above, below, b1, d_main, d_edge)

    def three(x):
        line = x[STRIP, 0:384].reshape(3, 128)
        return line

    here = jnp.stack([left[STRIP, 0:128], table[0, 0:128], right[STRIP, 0:128]])
    tables = jnp.concatenate([three(above), here, three(below)]).astype(jnp.int32)
    far = 1 << 20
    place = jnp.stack(
        [
            jnp.where(row == 0, 0, -far),
            jnp.where(row == n_row - 1, rows, far),
            jnp.where(col == 0, 0, -far),
            jnp.where(col == n_col - 1, cols, far),
            col,
        ]
    ).astype(jnp.int32)

    return pl.pallas_call(
        functools.partial(final_kernel, entries, per),
        out_shape=shape((rows, cols), F32),
        in_specs=[SMEM] * 2 + [VMEM] * (5 + len(shards)),
        out_specs=VMEM,
        scratch_shapes=[
            pltpu.VMEM((per * len(shards) + 1, 64, 128), BF16),
            pltpu.SMEM((9 * 17,), jnp.int32),
            pltpu.VMEM((384, cols + 256), F32),
            pltpu.VMEM((cols + 128, 384), BF16),
            pltpu.VMEM((2, cols, 384), BF16),
        ],
        compiler_params=PARAMS,
        name="final",
    )(tables, place, acc, g_hi, g_lo, g2_hi, g2_lo, *shards)


def solution(mesh):
    placed = (
        P(("frames", "row"), "col"),
        P(),
        P(),
        P(),
        P("col", None, None),
        P(("frames", "row"), "col", None),
        P(("frames", "row"), "col", None),
        P(("frames", "row"), "col"),
    )
    return jax.shard_map(
        on_device,
        mesh=mesh,
        in_specs=placed,
        out_specs=P(("frames", "row"), "col"),
        check_vma=False,
    )
```

time: 99.3 us -> 51 us (0.51)
  the two profiles are of different devices: /device:TPU:0 before, /device:TPU:1 now
where the time goes in v1:
time: 51 us; the launch traced here: 50.7 us
  Pallas kernels  17.5 us (34%)
  starting transfers between devices  17 us (33%)
  local copies, waits for them, and re-layouts  11.4 us (22%)
  waiting for transfers between devices  2.57 us (5%)
  other arithmetic  1.48 us (3%)
  between operations  0.81 us (2%)
    unnamed x18, local copies, waits for them, and re-layouts  11.1 us
    pallas_call x1, Pallas kernels, on_device(): pl.pallas_call(socs_kernel, out_shape=shape((NB + 1, CB, 256), F32), in_s...  7.71 us
    ppermute x1, starting transfers between devices, on_device(): above = lax.ppermute(bottom, 'row', up(n_row))  5.95 us
    pallas_call x1, Pallas kernels, on_device(): pl.pallas_call(bands_kernel, out_shape=(shape((pairs, CB, 256), BF16), sh...  5.55 us
    ppermute x3, starting transfers between devices, on_device(): lax.ppermute(library, 'col', [(i, (i + shift) % n_col) for i in range(n_c...  5.5 us
    pallas_call x1, Pallas kernels, on_device(): pl.pallas_call(functools.partial(final_kernel, entries, per), out_shape=s...  3.79 us
    ppermute x1, waiting for transfers between devices, on_device(): right = lax.ppermute(first, 'col', down(n_col))  2.55 us
    ppermute x1, starting transfers between devices, on_device(): left = lax.ppermute(last, 'col', up(n_col))  2.3 us
  transfers between devices with their start and end apart: 7, of which 1 were waited for; matrix products, arithmetic and copies ran while one was open for 3% of the time, Pallas kernels for 27%

profile of v1, /device:TPU:1, one launch (start us, length us, event | category | flops | bytes accessed | tf_op | source)
XLA Modules:
  0.0 50.7 jit_solution(7809705049050336371)
XLA Ops:
  0.0 2.1 %collective-permute-start.4 = (bf16[8,64,128]{2,1,0:T(8,128)(2,1)}, bf16[8,64,128]{2,1,0:T(8,128)(2,1)S(1)}, u32[]{:S(2)}, u32[]{:S(2)}) collective-permute-start(bf16[8,64,128]{2,1,0:T(8,128)(2,1)} %rest_0_.1), channel_id=1, source_target_pairs={{0,1},{1,2},{2,3},{3,0},{4,5},{5,6},{6,7},{7,4},{8,9},{9,10},{10,1... | collective-permute-start | bytes 393224 | tf_op jit(solution)/shard_map/ppermute | solution.py:263
  2.1 2.3 %collective-permute-start.5 = (bf16[8,64,128]{2,1,0:T(8,128)(2,1)}, bf16[8,64,128]{2,1,0:T(8,128)(2,1)S(1)}, u32[]{:S(2)}, u32[]{:S(2)}) collective-permute-start(bf16[8,64,128]{2,1,0:T(8,128)(2,1)} %rest_0_.1), channel_id=1, source_target_pairs={{0,2},{1,3},{2,0},{3,1},{4,6},{5,7},{6,4},{7,5},{8,10},{9,11},{10,... | collective-permute-start | bytes 393224 | tf_op jit(solution)/shard_map/ppermute | solution.py:263
  4.4 1.1 %collective-permute-start.6 = (bf16[8,64,128]{2,1,0:T(8,128)(2,1)}, bf16[8,64,128]{2,1,0:T(8,128)(2,1)S(1)}, u32[]{:S(2)}, u32[]{:S(2)}) collective-permute-start(bf16[8,64,128]{2,1,0:T(8,128)(2,1)} %rest_0_.1), channel_id=1, source_target_pairs={{0,3},{1,0},{2,1},{3,2},{4,7},{5,4},{6,5},{7,6},{8,11},{9,8},{10,9... | collective-permute-start | bytes 393224 | tf_op jit(solution)/shard_map/ppermute | solution.py:263
  6.2 0.7 %convert_bitcast_fusion = (bf16[1,8]{1,0:T(2,128)(2,1)S(1)}, bf16[1,8]{1,0:T(2,128)(2,1)S(1)}) fusion(s32[1,1,8]{2,1,0:T(1,128)} %param.14, s32[1,1,8]{2,1,0:T(1,128)} %param.13), kind=kLoop, calls=%fused_computation.15 | loop fusion | flops 16 | bytes 96 | tf_op jit(solution)/shard_map/concatenate | solution.py:240
  6.9 1.0 %copy-done = s32[256,512]{1,0:T(8,128)S(1)} copy-done((s32[256,512]{1,0:T(8,128)S(1)}, s32[256,512]{1,0:T(8,128)}, u32[]{:S(2)}) %copy-start) | copy-done | bytes 524312
  8.0 0.1 prep.1
  8.1 2.3 %collective-permute-start = (bf16[48,256]{1,0:T(8,128)(2,1)S(1)}, bf16[48,256]{1,0:T(8,128)(2,1)S(1)}, u32[]{:S(2)}, u32[]{:S(2)}) collective-permute-start(bf16[48,256]{1,0:T(8,128)(2,1)S(1)} %get-tuple-element.19), channel_id=1, source_target_pairs={{0,1},{1,2},{2,3},{4,5},{5,6},{6,7},{8,9},{9,10},{10,11},{12,13},{... | collective-permute-start | bytes 73736 | tf_op jit(solution)/shard_map/ppermute | solution.py:258
  10.4 1.3 %collective-permute-start.1 = (bf16[48,256]{1,0:T(8,128)(2,1)S(1)}, bf16[48,256]{1,0:T(8,128)(2,1)S(1)}, u32[]{:S(2)}, u32[]{:S(2)}) collective-permute-start(bf16[48,256]{1,0:T(8,128)(2,1)S(1)} %get-tuple-element.20), channel_id=1, source_target_pairs={{1,0},{2,1},{3,2},{5,4},{6,5},{7,6},{9,8},{10,9},{11,10},{13,12},{... | collective-permute-start | bytes 73736 | tf_op jit(solution)/shard_map/ppermute | solution.py:259
  11.7 0.7 %pad_convert_fusion = (f32[24,128]{1,0:T(8,128)S(1)}, f32[24,128]{1,0:T(8,128)S(1)}) fusion(bf16[24,33]{1,0:T(8,128)(2,1)} %bitcast.13, bf16[24,33]{1,0:T(8,128)(2,1)} %bitcast.14), kind=kLoop, calls=%fused_computation.11 | loop fusion | flops 6144 | bytes 27744 | tf_op jit(solution)/shard_map/jit(_pad)/pad | solution.py:280
  12.4 2.6 %collective-permute-done.1.right = bf16[48,256]{1,0:T(8,128)(2,1)S(1)} collective-permute-done((bf16[48,256]{1,0:T(8,128)(2,1)S(1)}, bf16[48,256]{1,0:T(8,128)(2,1)S(1)}, u32[]{:S(2)}, u32[]{:S(2)}) %collective-permute-start.1) | collective-permute-done | bytes 24608 | tf_op jit(solution)/shard_map/ppermute | solution.py:259
  15.0 0.3 mid.1
  15.3 5.9 %collective-permute-start.2 = (bf16[48,640]{1,0:T(8,128)(2,1)S(1)}, bf16[48,640]{1,0:T(8,128)(2,1)S(1)}, u32[]{:S(2)}, u32[]{:S(2)}) collective-permute-start(bf16[48,640]{1,0:T(8,128)(2,1)S(1)} %get-tuple-element.21), channel_id=1, source_target_pairs={{0,4},{4,8},{8,12},{1,5},{5,9},{9,13},{2,6},{6,10},{10,14},{3,7},{... | collective-permute-start | bytes 184328 | tf_op jit(solution)/shard_map/ppermute | solution.py:277
  21.2 1.9 %collective-permute-start.3 = (bf16[48,640]{1,0:T(8,128)(2,1)S(1)}, bf16[48,640]{1,0:T(8,128)(2,1)S(1)}, u32[]{:S(2)}, u32[]{:S(2)}) collective-permute-start(bf16[48,640]{1,0:T(8,128)(2,1)S(1)} %get-tuple-element.22), channel_id=1, source_target_pairs={{4,0},{8,4},{12,8},{5,1},{9,5},{13,9},{6,2},{10,6},{14,10},{7,3},{... | collective-permute-start | bytes 184328 | tf_op jit(solution)/shard_map/ppermute | solution.py:278
  23.2 5.6 %bands.1 = (bf16[24,176,256]{2,1,0:T(8,128)(2,1)S(1)}, bf16[24,256,256]{2,1,0:T(8,128)(2,1)S(1)}, bf16[24,256,256]{2,1,0:T(8,128)(2,1)S(1)}, bf16[128,256]{1,0:T...) custom-call(f32[24,128]{1,0:T(8,128)S(1)} %get-tuple-element.34.across, ...), custom_call_target="tpu_custom_call" | custom-call | flops 2000000000 | bytes 8000000 | tf_op jit(solution)/shard_map/bands/pallas_call | solution.py:281
  28.7 1.6 %copy-done.3 = bf16[24,256,256]{2,1,0:T(8,128)(2,1)} copy-done((bf16[24,256,256]{2,1,0:T(8,128)(2,1)}, bf16[24,256,256]{2,1,0:T(8,128)(2,1)S(1)}, u32[]{:S(2)}) %copy-start.3) | copy-done | bytes 3145752
  30.4 1.7 %copy-done.5 = bf16[24,256,256]{2,1,0:T(8,128)(2,1)} copy-done((bf16[24,256,256]{2,1,0:T(8,128)(2,1)}, bf16[24,256,256]{2,1,0:T(8,128)(2,1)S(1)}, u32[]{:S(2)}) %copy-start.5) | copy-done | bytes 3145752
  32.1 1.4 %copy-done.7 = bf16[24,176,256]{2,1,0:T(8,128)(2,1)} copy-done((bf16[24,176,256]{2,1,0:T(8,128)(2,1)}, bf16[24,176,256]{2,1,0:T(8,128)(2,1)S(1)}, u32[]{:S(2)}) %copy-start.7) | copy-done | bytes 2162712
  33.4 0.1 stack.23.place
  33.5 1.9 %copy-done.4 = bf16[24,256,256]{2,1,0:T(8,128)(2,1)S(1)} copy-done((bf16[24,256,256]{2,1,0:T(8,128)(2,1)S(1)}, bf16[24,256,256]{2,1,0:T(8,128)(2,1)}, u32[]{:S(2)}) %copy-start.4) | copy-done | bytes 3145752
  35.4 1.9 %copy-done.6 = bf16[24,256,256]{2,1,0:T(8,128)(2,1)S(1)} copy-done((bf16[24,256,256]{2,1,0:T(8,128)(2,1)S(1)}, bf16[24,256,256]{2,1,0:T(8,128)(2,1)}, u32[]{:S(2)}) %copy-start.6) | copy-done | bytes 3145752
  37.3 1.6 %copy-done.8 = bf16[24,176,256]{2,1,0:T(8,128)(2,1)S(1)} copy-done((bf16[24,176,256]{2,1,0:T(8,128)(2,1)S(1)}, bf16[24,176,256]{2,1,0:T(8,128)(2,1)}, u32[]{:S(2)}) %copy-start.8) | copy-done | bytes 2162712
  38.9 7.7 %socs.1.acc = f32[4,176,256]{2,1,0:T(8,128)S(1)} custom-call(f32[12]{0:T(128)S(1)} %copy-done.2, f32[256,640]{1,0:T(8,128)S(1)} %get-tuple-element.23.wide, bf16[48,640]{1,0:T(8,128)(2,1)S(1)} %collective-permute-done.2.above, bf16[48,640]{1,0:T(8,128)(2,1)S(1)} %collective-permute-done.3.below, bf16[24,176,256]{2,1,0:T(8,128)(2,1)S(1)} %copy-done.8, ...), custom_call_target="tpu_custom_call" | custom-call | flops 5000000000 | bytes 8000000 | tf_op jit(solution)/shard_map/socs/pallas_call | solution.py:299
  46.7 0.1 concatenate.21
  46.9 3.8 %final.1 = f32[256,512]{1,0:T(8,128)} custom-call(s32[9,128]{1,0:T(8,128)S(1)} %convert_element_type.24.tables, s32[5]{0:T(128)S(1)} %stack.23.place, f32[4,176,256]{2,1,0:T(8,128)S(1)} %socs.1.acc, bf16[128,256]{1,0:T(8,128)(2,1)S(1)} %get-tuple-element.27.g_hi, bf16[128,256]{1,0:T(8,128)(2,1)S(1)} %get-tuple-element.28.g_lo, ...), custom_call_target="tpu_custom_call" | custom-call | tf_op jit(solution)/shard_map/final/pallas_call | solution.py:330
  (24 shorter events, 0.2 us)
Async XLA Ops:
  0.0 46.8 %collective-permute-start.4 = (bf16[8,64,128]{2,1,0:T(8,128)(2,1)}, bf16[8,64,128]{2,1,0:T(8,128)(2,1)S(1)}, u32[]{:S(2)}, u32[]{:S(2)}) collective-permute-start(bf16[8,64,128]{2,1,0:T(8,128)(2,1)} %rest_0_.1), channel_id=1, source_target_pairs={{0,1},{1,2},{2,3},{3,0},{4,5},{5,6},{6,7},{7,4},{8,9},{9,10},{10,1... | collective-permute-start | bytes 393224 | tf_op jit(solution)/shard_map/ppermute | solution.py:263
  2.1 44.7 %collective-permute-start.5 = (bf16[8,64,128]{2,1,0:T(8,128)(2,1)}, bf16[8,64,128]{2,1,0:T(8,128)(2,1)S(1)}, u32[]{:S(2)}, u32[]{:S(2)}) collective-permute-start(bf16[8,64,128]{2,1,0:T(8,128)(2,1)} %rest_0_.1), channel_id=1, source_target_pairs={{0,2},{1,3},{2,0},{3,1},{4,6},{5,7},{6,4},{7,5},{8,10},{9,11},{10,... | collective-permute-start | bytes 393224 | tf_op jit(solution)/shard_map/ppermute | solution.py:263
  4.4 42.4 %collective-permute-start.6 = (bf16[8,64,128]{2,1,0:T(8,128)(2,1)}, bf16[8,64,128]{2,1,0:T(8,128)(2,1)S(1)}, u32[]{:S(2)}, u32[]{:S(2)}) collective-permute-start(bf16[8,64,128]{2,1,0:T(8,128)(2,1)} %rest_0_.1), channel_id=1, source_target_pairs={{0,3},{1,0},{2,1},{3,2},{4,7},{5,4},{6,5},{7,6},{8,11},{9,8},{10,9... | collective-permute-start | bytes 393224 | tf_op jit(solution)/shard_map/ppermute | solution.py:263
  6.9 1.0 %copy-start = (s32[256,512]{1,0:T(8,128)S(1)}, s32[256,512]{1,0:T(8,128)}, u32[]{:S(2)}) copy-start(s32[256,512]{1,0:T(8,128)} %mask.1) | copy-start | bytes 1572868
  8.1 4.3 %collective-permute-start = (bf16[48,256]{1,0:T(8,128)(2,1)S(1)}, bf16[48,256]{1,0:T(8,128)(2,1)S(1)}, u32[]{:S(2)}, u32[]{:S(2)}) collective-permute-start(bf16[48,256]{1,0:T(8,128)(2,1)S(1)} %get-tuple-element.19), channel_id=1, source_target_pairs={{0,1},{1,2},{2,3},{4,5},{5,6},{6,7},{8,9},{9,10},{10,11},{12,13},{... | collective-permute-start | bytes 73736 | tf_op jit(solution)/shard_map/ppermute | solution.py:258
  10.4 4.6 %collective-permute-start.1 = (bf16[48,256]{1,0:T(8,128)(2,1)S(1)}, bf16[48,256]{1,0:T(8,128)(2,1)S(1)}, u32[]{:S(2)}, u32[]{:S(2)}) collective-permute-start(bf16[48,256]{1,0:T(8,128)(2,1)S(1)} %get-tuple-element.20), channel_id=1, source_target_pairs={{1,0},{2,1},{3,2},{5,4},{6,5},{7,6},{9,8},{10,9},{11,10},{13,12},{... | collective-permute-start | bytes 73736 | tf_op jit(solution)/shard_map/ppermute | solution.py:259
  15.3 18.2 %collective-permute-start.2 = (bf16[48,640]{1,0:T(8,128)(2,1)S(1)}, bf16[48,640]{1,0:T(8,128)(2,1)S(1)}, u32[]{:S(2)}, u32[]{:S(2)}) collective-permute-start(bf16[48,640]{1,0:T(8,128)(2,1)S(1)} %get-tuple-element.21), channel_id=1, source_target_pairs={{0,4},{4,8},{8,12},{1,5},{5,9},{9,13},{2,6},{6,10},{10,14},{3,7},{... | collective-permute-start | bytes 184328 | tf_op jit(solution)/shard_map/ppermute | solution.py:277
  21.2 12.3 %collective-permute-start.3 = (bf16[48,640]{1,0:T(8,128)(2,1)S(1)}, bf16[48,640]{1,0:T(8,128)(2,1)S(1)}, u32[]{:S(2)}, u32[]{:S(2)}) collective-permute-start(bf16[48,640]{1,0:T(8,128)(2,1)S(1)} %get-tuple-element.22), channel_id=1, source_target_pairs={{4,0},{8,4},{12,8},{5,1},{9,5},{13,9},{6,2},{10,6},{14,10},{7,3},{... | collective-permute-start | bytes 184328 | tf_op jit(solution)/shard_map/ppermute | solution.py:278
  23.2 10.4 %copy-start.2 = (f32[12]{0:T(128)S(1)}, f32[12]{0:T(128)}, u32[]{:S(2)}) copy-start(f32[12]{0:T(128)} %weights.1) | copy-start | bytes 148
  28.7 1.6 %copy-start.3 = (bf16[24,256,256]{2,1,0:T(8,128)(2,1)}, bf16[24,256,256]{2,1,0:T(8,128)(2,1)S(1)}, u32[]{:S(2)}) copy-start(bf16[24,256,256]{2,1,0:T(8,128)(2,1)S(1)} %get-tuple-element.25.d_main) | copy-start | bytes 9437188
  30.4 1.7 %copy-start.5 = (bf16[24,256,256]{2,1,0:T(8,128)(2,1)}, bf16[24,256,256]{2,1,0:T(8,128)(2,1)S(1)}, u32[]{:S(2)}) copy-start(bf16[24,256,256]{2,1,0:T(8,128)(2,1)S(1)} %get-tuple-element.26.d_edge) | copy-start | bytes 9437188
  32.0 1.4 %copy-start.7 = (bf16[24,176,256]{2,1,0:T(8,128)(2,1)}, bf16[24,176,256]{2,1,0:T(8,128)(2,1)S(1)}, u32[]{:S(2)}) copy-start(bf16[24,176,256]{2,1,0:T(8,128)(2,1)S(1)} %get-tuple-element.24.b1) | copy-start | bytes 6488068
  33.5 1.9 %copy-start.4 = (bf16[24,256,256]{2,1,0:T(8,128)(2,1)S(1)}, bf16[24,256,256]{2,1,0:T(8,128)(2,1)}, u32[]{:S(2)}) copy-start(bf16[24,256,256]{2,1,0:T(8,128)(2,1)} %copy-done.3) | copy-start | bytes 9437188
  35.4 1.9 %copy-start.6 = (bf16[24,256,256]{2,1,0:T(8,128)(2,1)S(1)}, bf16[24,256,256]{2,1,0:T(8,128)(2,1)}, u32[]{:S(2)}) copy-start(bf16[24,256,256]{2,1,0:T(8,128)(2,1)} %copy-done.5) | copy-start | bytes 9437188
  37.3 1.6 %copy-start.8 = (bf16[24,176,256]{2,1,0:T(8,128)(2,1)S(1)}, bf16[24,176,256]{2,1,0:T(8,128)(2,1)}, u32[]{:S(2)}) copy-start(bf16[24,176,256]{2,1,0:T(8,128)(2,1)} %copy-done.7) | copy-start | bytes 6488068
  38.9 7.9 %copy-start.1 = (bf16[8,64,128]{2,1,0:T(8,128)(2,1)S(1)}, bf16[8,64,128]{2,1,0:T(8,128)(2,1)}, u32[]{:S(2)}) copy-start(bf16[8,64,128]{2,1,0:T(8,128)(2,1)} %rest_0_.1) | copy-start | bytes 393220

commit v2 on v1

v2 whole, which is shorter than its diff:
```python
import functools
import math

import jax
import jax.numpy as jnp
from jax import lax
from jax.experimental import pallas as pl
from jax.experimental.pallas import tpu as pltpu
from jax.sharding import PartitionSpec as P

BLUR_HALF = 8
BLUR_SIGMA = 4.0
HALF = 16
RIM = HALF + BLUR_HALF
STRIP = 32
CB = 176
NB = 3
MAIN = 224
EDGE_IN = 80
EDGE_OUT = 48
EDGE_AT = (0, 48, 128)
WIDE = 640
F32 = jnp.float32
BF16 = jnp.bfloat16
VMEM = pl.BlockSpec(memory_space=pltpu.VMEM)
SMEM = pl.BlockSpec(memory_space=pltpu.SMEM)
HBM = pl.BlockSpec(memory_space=pltpu.HBM)
PARAMS = pltpu.CompilerParams(vmem_limit_bytes=16 * 1024 * 1024)


def dot_nt(a, b):
    return lax.dot_general(a, b, (((1,), (1,)), ((), ())), preferred_element_type=F32)


def dot_nn(a, b):
    return lax.dot_general(a, b, (((1,), (0,)), ((), ())), preferred_element_type=F32)


def prep_kernel(
    mask, ids, slots, count, across, down, first, last, ahead, back, ends, a_ids, a_slots, a_count, tap, sems
):
    rows, cols = mask.shape
    copies = [
        pltpu.make_async_copy(mask.at[:, 0:128], ends.at[0], sems.at[0]),
        pltpu.make_async_copy(mask.at[:, cols - 128 : cols], ends.at[1], sems.at[1]),
        pltpu.make_async_copy(ids, a_ids, sems.at[2]),
        pltpu.make_async_copy(slots, a_slots, sems.at[3]),
        pltpu.make_async_copy(count, a_count, sems.at[4]),
        pltpu.make_async_copy(across, tap.at[0], sems.at[5]),
        pltpu.make_async_copy(down, tap.at[1], sems.at[6]),
    ]
    for copy in copies:
        copy.start()
    for copy in copies[2:5]:
        copy.wait()
    line = lax.broadcasted_iota(jnp.int32, (16, 128), 0)
    lane = lax.broadcasted_iota(jnp.int32, (16, 128), 1)

    def spread(x):
        x = x.astype(F32)
        x = jnp.concatenate([x, jnp.zeros((1, 128 - x.shape[1]), F32)], axis=1)
        return jnp.broadcast_to(x, (16, 128))

    table = jnp.where(line == 1, spread(a_slots[0]), spread(a_count[...]))
    table = jnp.where(line == 0, spread(a_ids[0]), table)
    width = jnp.where(line == 2, 1, ids.shape[2])
    table = jnp.where((lane < width) & (line < 3), table, 0.0).astype(BF16)
    for strip in (first, last):
        strip[STRIP:, 0:128] = table
        strip[STRIP:, 128:] = jnp.zeros((16, rows - 128), BF16)
    copies[0].wait()
    first[0:STRIP, :] = ends[0].astype(F32).T[0:STRIP].astype(BF16)
    copies[1].wait()
    last[0:STRIP, :] = ends[1].astype(F32).T[128 - STRIP :].astype(BF16)
    copies[5].wait()
    copies[6].wait()
    taps = across.shape[2]
    flip = lax.broadcasted_iota(jnp.int32, (128, 128), 0) + lax.broadcasted_iota(jnp.int32, (128, 128), 1)
    flip = jnp.where(flip % 128 == 0, 1.0, 0.0).astype(BF16)
    pad = jnp.zeros((8, 128 - taps), F32)
    more = jnp.zeros((6, taps), F32)
    for k in range(across.shape[0]):
        line = jnp.concatenate([tap[0, k].astype(F32), more], axis=0)
        ahead[k] = jnp.concatenate([line, pad], axis=1)
        line = jnp.concatenate([tap[1, k].astype(F32), more], axis=0)
        back[k] = dot_nn(jnp.concatenate([line, pad], axis=1).astype(BF16), flip)


def mid_kernel(mask, left, right, own, top, bottom, ends, sems):
    rows, cols = mask.shape
    copies = [
        pltpu.make_async_copy(mask.at[0:STRIP], ends.at[0], sems.at[0]),
        pltpu.make_async_copy(mask.at[rows - STRIP : rows], ends.at[1], sems.at[1]),
    ]
    for copy in copies:
        copy.start()
    fill = jnp.zeros((128 - STRIP, 128), F32)

    def turned(strip, at):
        return jnp.concatenate([strip[0:STRIP, at : at + 128].astype(F32), fill], axis=0).T

    tables = jnp.concatenate(
        [left[STRIP:, 0:128], own[STRIP:, 0:128], right[STRIP:, 0:128], jnp.zeros((16, 256), BF16)],
        axis=1,
    )
    for i, out in enumerate((top, bottom)):
        at = 0 if i == 0 else rows - 128
        cut = slice(0, STRIP) if i == 0 else slice(128 - STRIP, 128)
        lhs = turned(left, at)[cut, STRIP - RIM : STRIP]
        rhs = turned(right, at)[cut, 0 : WIDE - RIM - cols]
        copies[i].wait()
        out[0:STRIP, :] = jnp.concatenate([lhs, ends[i].astype(F32), rhs], axis=1).astype(BF16)
        out[STRIP:, :] = tables


def window_kernel(mask, left, right, windows):
    rows, cols = mask.shape
    fill = jnp.zeros((128 - STRIP, rows), F32)
    lhs = jnp.concatenate([left[0:STRIP, :].astype(F32), fill], axis=0).T
    rhs = jnp.concatenate([right[0:STRIP, :].astype(F32), fill], axis=0).T
    full = jnp.concatenate(
        [lhs[:, STRIP - RIM : STRIP], mask[...].astype(F32), rhs[:, 0 : WIDE - RIM - cols]], axis=1
    )
    for b in range(NB):
        windows[b] = full[:, CB * b : CB * b + 256]


def socs_kernel(weights, windows, above, below, ahead, back, acc, x_win, *scratch):
    across = scratch[0:2]
    d_main = scratch[2:4]
    d_edge = scratch[4:6]
    first = scratch[6:8]
    kernels = ahead.shape[0]
    upper_rows = above[0:STRIP, :].astype(F32)[STRIP - RIM :]
    lower_rows = below[0:STRIP, :].astype(F32)[0:RIM]
    edge_rows = []
    for b in range(NB):
        lanes = slice(CB * b, CB * b + 256)
        own = windows[b]
        x_win[b] = jnp.concatenate([upper_rows[:, lanes], own[0 : 256 - RIM]], axis=0).astype(BF16)
        edge_rows += [own[MAIN - RIM :], lower_rows[:, lanes]]
    edge_rows.append(jnp.zeros((256 - NB * EDGE_IN, 256), F32))
    x_win[NB] = jnp.concatenate(edge_rows, axis=0).astype(BF16)
    acc[...] = jnp.zeros(acc.shape, F32)
    for ref in across + d_main + d_edge:
        ref[...] = jnp.zeros(ref.shape, BF16)

    row = lax.broadcasted_iota(jnp.int32, (32, 128), 0)
    lane = lax.broadcasted_iota(jnp.int32, (32, 128), 1)
    low = lane >= row + 96
    narrow = lax.broadcasted_iota(jnp.int32, (EDGE_IN, 128), 1) < EDGE_OUT

    def cycled(x):
        return pltpu.roll(jnp.broadcast_to(x, (128, 128)), 0, 1, stride=1, stride_axis=0)

    def build_across(k, s):
        for p in range(2):
            cyc = cycled(ahead[k, p : p + 1, :])
            head = cyc[0:96].astype(BF16)
            tail = cyc[96:128]
            over = jnp.where(low, 0.0, tail)
            across[s][p, 0:96, 0:128] = head
            across[s][p, 128:CB, 128:256] = head[0 : CB - 128]
            across[s][p, 96:128, 0:128] = jnp.where(low, tail, 0.0).astype(BF16)
            across[s][p, 96:128, 128:256] = over.astype(BF16)

    def build_down(k, s):
        for p in range(2):
            cyc = cycled(back[k, p : p + 1, :])
            head = cyc[0:32]
            over = jnp.where(low, head, 0.0).astype(BF16)
            head = jnp.where(low, 0.0, head)
            same = jnp.concatenate([head, cyc[32:128]], axis=0)
            edge = jnp.where(narrow, same[0:EDGE_IN], 0.0)
            same = same.astype(BF16)
            d_main[s][p, 0:128, 0:128] = same
            d_main[s][p, 128:256, 128:256] = same
            d_main[s][p, 128:160, 0:128] = over
            moved = pltpu.roll(edge, EDGE_AT[1], 1).astype(BF16)
            edge = edge.astype(BF16)
            d_edge[s][p, 0:EDGE_IN, 0:128] = edge
            d_edge[s][p, EDGE_IN : 2 * EDGE_IN, 0:128] = moved
            d_edge[s][p, 2 * EDGE_IN : 3 * EDGE_IN, 128:256] = edge

    def pass_one(s):
        taps = across[s][...].reshape(2 * CB, 256)
        for j in range(NB + 1):
            part = dot_nt(taps, x_win[j]).astype(BF16)
            first[s][0, j] = part[0:CB]
            first[s][1, j] = part[CB:]

    def pass_two(k, s):
        weight = weights[k]
        total = None
        for p in range(2):
            second = dot_nn(first[s][p, 0:NB].reshape(NB * CB, 256), d_main[s][p])
            total = second * second if total is None else total + second * second
        acc[0:NB] += (weight * total).reshape(NB, CB, 256)
        total = None
        for p in range(2):
            second = dot_nn(first[s][p, NB], d_edge[s][p])
            total = second * second if total is None else total + second * second
        acc[NB] += weight * total

    def stage(k, s):
        pass_one(s)
        build_down(k, s)
        build_across(jnp.minimum(k + 1, kernels - 1), 1 - s)
        pass_two(k - 1, 1 - s)

    build_across(0, 0)
    pass_one(0)
    build_down(0, 0)
    build_across(1, 1)

    def step(m, carry):
        stage(2 * m + 1, 1)
        stage(2 * m + 2, 0)
        return carry

    lax.fori_loop(0, kernels // 2 - 1, step, 0)
    stage(kernels - 1, 1)
    pass_two(kernels - 1, 1)


def blur_matrix(shape, axis):
    lag = lax.broadcasted_iota(jnp.int32, shape, axis) - lax.broadcasted_iota(jnp.int32, shape, 1 - axis)
    total = sum(math.exp(-(t * t) / (2 * BLUR_SIGMA**2)) for t in range(-BLUR_HALF, BLUR_HALF + 1))
    off = (lag - BLUR_HALF).astype(F32)
    g = jnp.exp(-off * off / (2.0 * BLUR_SIGMA * BLUR_SIGMA)) * (1.0 / total)
    g = jnp.where((lag >= 0) & (lag <= 2 * BLUR_HALF), g, 0.0)
    high = g.astype(BF16)
    return high, (g - high.astype(F32)).astype(BF16)


def final_kernel(entries, per, n_row, n_col, acc, above, left, own, right, below, *rest):
    shards = rest[:-9]
    out, cells, tab, tables, slots, placed, flat, blurred, sem = rest[-9:]
    count = len(shards)
    rows, cols = out.shape
    row, col = lax.axis_index("row"), lax.axis_index("col")

    for i, strip in enumerate((above, below)):
        tab[:, 768 * i : 768 * i + 384] = strip[STRIP:, 0:384].astype(F32).astype(jnp.int32)[0:8]
    for i, strip in enumerate((left, own, right)):
        tab[:, 384 + 128 * i : 512 + 128 * i] = strip[STRIP:, 0:128].astype(F32).astype(jnp.int32)[0:8]
    fetch = pltpu.make_async_copy(tab, tables, sem)
    fetch.start()
    for i, shard in enumerate(shards):
        cells[pl.ds(i * per, per)] = shard[...]
    empty = count * per
    cells[empty] = jnp.zeros(cells.shape[1:], BF16)

    far = 1 << 20
    at_row = lax.broadcasted_iota(jnp.int32, (CB, 384), 1) - BLUR_HALF
    row_ok = (at_row >= jnp.where(row == 0, 0, -far)) & (at_row < jnp.where(row == n_row - 1, rows, far))
    at_col = lax.broadcasted_iota(jnp.int32, (CB, 384), 0) - BLUR_HALF
    for b in range(NB):
        edge = acc[NB, :, EDGE_AT[b] : EDGE_AT[b] + EDGE_OUT]
        part = jnp.concatenate(
            [acc[b, :, 0:MAIN], edge, jnp.zeros((CB, 384 - MAIN - EDGE_OUT), F32)], axis=1
        )
        here = at_col + b * CB
        keep = row_ok & (here >= jnp.where(col == 0, 0, -far))
        keep = keep & (here < jnp.where(col == n_col - 1, cols, far))
        flat[b * CB : (b + 1) * CB, :] = jnp.where(keep, part, 0.0).astype(BF16)
    flat[NB * CB :, :] = jnp.zeros((flat.shape[0] - NB * CB, 384), BF16)

    fetch.wait()
    for t in range(9):
        for s in range(16):
            slots[t * 17 + s] = empty
        live = tables[2, 128 * t]
        for n in range(entries):
            cell = tables[0, 128 * t + n]
            owner = cell // per
            behind = jnp.where(owner <= col, col - owner, col - owner + count)
            at = jnp.where(n < live, tables[1, 128 * t + n], 16)
            slots[t * 17 + at] = behind * per + cell - owner * per

    slot_rows, slot_cols = rows // 64, cols // 128
    for i in range(-1, slot_rows + 1):
        for j in range(-1, slot_cols + 1):
            ti = 0 if i < 0 else (2 if i == slot_rows else 1)
            tj = 0 if j < 0 else (2 if j == slot_cols else 1)
            image = slots[(3 * ti + tj) * 17 + (i % slot_rows) * slot_cols + j % slot_cols]
            lanes = slice(128 + 128 * j, 256 + 128 * j)
            if i < 0:
                placed[0:8, lanes] = cells[image, 48:64, :].astype(F32)[8:16]
            elif i == slot_rows:
                placed[8 + rows : 16 + rows, lanes] = cells[image, 0:16, :].astype(F32)[0:8]
            else:
                placed[8 + 64 * i : 72 + 64 * i, lanes] = cells[image].astype(F32)
    placed[16 + rows :, :] = jnp.zeros((placed.shape[0] - 16 - rows, placed.shape[1]), F32)

    g_high, g_low = blur_matrix((128, 256), 1)
    g_both = jnp.concatenate([g_high, g_low], axis=0)
    for i in range(rows // 128):
        part = dot_nt(g_both, flat[:, 128 * i : 128 * i + 256])
        cell = dot_nn(g_both, placed[128 * i : 128 * i + 256, :].astype(BF16))
        part = part[0:128] + part[128:]
        cell = cell[0:128] + cell[128:]
        part += cell[:, 128 - BLUR_HALF : 128 - BLUR_HALF + part.shape[1]]
        high = part.astype(BF16)
        blurred[0, 128 * i : 128 * i + 128, :] = high
        blurred[1, 128 * i : 128 * i + 128, :] = (part - high.astype(F32)).astype(BF16)
    g_high, g_low = blur_matrix((256, 128), 0)
    g_both = jnp.concatenate([g_high, g_low], axis=1)
    for j in range(cols // 128):
        lanes = slice(128 * j, 128 * j + 256)
        part = dot_nn(blurred[0, :, lanes], g_both)
        out[:, 128 * j : 128 * j + 128] = (
            part[:, 0:128] + part[:, 128:] + dot_nn(blurred[1, :, lanes], g_high)
        )


def shape(dims, dtype):
    return jax.ShapeDtypeStruct(dims, dtype)


def on_device(
    mask_pixels, across_taps, down_taps, kernel_weights, library, cell_ids, cell_slots, cell_count
):
    rows, cols = mask_pixels.shape
    kernels = across_taps.shape[0]
    entries = cell_ids.shape[-1]
    per = library.shape[0]
    n_row, n_col = lax.axis_size("row"), lax.axis_size("col")

    first, last, ahead, back = pl.pallas_call(
        prep_kernel,
        out_shape=(shape((STRIP + 16, rows), BF16),) * 2 + (shape((kernels, 8, 128), F32),) * 2,
        in_specs=[HBM] * 6,
        out_specs=(VMEM,) * 4,
        scratch_shapes=[
            pltpu.VMEM((2, rows, 128), jnp.int32),
            pltpu.VMEM(cell_ids.shape, jnp.int32),
            pltpu.VMEM(cell_slots.shape, jnp.int32),
            pltpu.VMEM(cell_count.shape, jnp.int32),
            pltpu.VMEM((2,) + across_taps.shape, BF16),
            pltpu.SemaphoreType.DMA((7,)),
        ],
        compiler_params=PARAMS,
        name="prep",
    )(mask_pixels, cell_ids, cell_slots, cell_count, across_taps, down_taps)
    library, first, last = lax.optimization_barrier((library, first, last))

    up = lambda n: [(i, i + 1) for i in range(n - 1)]
    down = lambda n: [(i + 1, i) for i in range(n - 1)]
    left = lax.ppermute(last, "col", up(n_col))
    right = lax.ppermute(first, "col", down(n_col))

    shards = [library]
    for shift in range(1, n_col):
        shards.append(lax.ppermute(library, "col", [(i, (i + shift) % n_col) for i in range(n_col)]))

    top, bottom = pl.pallas_call(
        mid_kernel,
        out_shape=(shape((STRIP + 16, WIDE), BF16),) * 2,
        in_specs=[HBM] + [VMEM] * 3,
        out_specs=(VMEM,) * 2,
        scratch_shapes=[pltpu.VMEM((2, STRIP, cols), jnp.int32), pltpu.SemaphoreType.DMA((2,))],
        compiler_params=PARAMS,
        name="mid",
    )(mask_pixels, left, right, first)
    above = lax.ppermute(bottom, "row", up(n_row))
    below = lax.ppermute(top, "row", down(n_row))

    windows = pl.pallas_call(
        window_kernel,
        out_shape=shape((NB, rows, 256), F32),
        in_specs=[VMEM] * 3,
        out_specs=VMEM,
        compiler_params=PARAMS,
        cost_estimate=pl.CostEstimate(flops=10**6, bytes_accessed=10**6, transcendentals=0),
        name="window",
    )(mask_pixels, left, right)

    acc = pl.pallas_call(
        socs_kernel,
        out_shape=shape((NB + 1, CB, 256), F32),
        in_specs=[SMEM] + [VMEM] * 5,
        out_specs=VMEM,
        scratch_shapes=[pltpu.VMEM((NB + 1, 256, 256), BF16)]
        + [pltpu.VMEM((2, CB, 256), BF16)] * 2
        + [pltpu.VMEM((2, 256, 256), BF16)] * 4
        + [pltpu.VMEM((2, NB + 1, CB, 256), BF16)] * 2,
        compiler_params=PARAMS,
        cost_estimate=pl.CostEstimate(flops=5 * 10**9, bytes_accessed=8 * 10**6, transcendentals=0),
        name="socs",
    )(kernel_weights, windows, above, below, ahead, back)

    return pl.pallas_call(
        functools.partial(final_kernel, entries, per, n_row, n_col),
        out_shape=shape((rows, cols), F32),
        in_specs=[VMEM] * (6 + len(shards)),
        out_specs=VMEM,
        scratch_shapes=[
            pltpu.VMEM((per * len(shards) + 1, 64, 128), BF16),
            pltpu.VMEM((8, 9 * 128), jnp.int32),
            pltpu.SMEM((8, 9 * 128), jnp.int32),
            pltpu.SMEM((9 * 17,), jnp.int32),
            pltpu.VMEM((384, cols + 256), F32),
            pltpu.VMEM((WIDE, 384), BF16),
            pltpu.VMEM((2, rows, WIDE), BF16),
            pltpu.SemaphoreType.DMA,
        ],
        compiler_params=PARAMS,
        name="final",
    )(acc, above, left, first, right, below, *shards)


def solution(mesh):
    placed = (
        P(("frames", "row"), "col"),
        P(),
        P(),
        P(),
        P("col", None, None),
        P(("frames", "row"), "col", None),
        P(("frames", "row"), "col", None),
        P(("frames", "row"), "col"),
    )
    return jax.shard_map(
        on_device,
        mesh=mesh,
        in_specs=placed,
        out_specs=P(("frames", "row"), "col"),
        check_vma=False,
    )
```

time: 51 us -> 36 us (0.71)
  local copies, waits for them, and re-layouts: 11.4 us -> 3.08 us
  Pallas kernels: 17.5 us -> 12.3 us
  waiting for transfers between devices: 2.57 us -> 0.93 us
  other arithmetic: 1.48 us -> 0 us
  starting transfers between devices: 17 us -> 18.4 us
    unnamed x18 -> x14, local copies, waits for them, and re-layouts: 11.1 us -> 3.08 us
    pallas_call x4, Pallas kernels: 9.76 us -> 5.22 us  [the longest x1 3.74 us: on_device(): pl.pallas_call(functools.partial(final_kernel, entries, per, n_row, n_col...]
    ppermute x1, waiting for transfers between devices: 2.55 us -> 0.01 us  [on_device(): right = lax.ppermute(first, 'col', down(n_col))]
    ppermute x1, starting transfers between devices: 2.3 us -> 4.66 us  [on_device(): left = lax.ppermute(last, 'col', up(n_col))]
    ppermute x1, starting transfers between devices: 5.95 us -> 4.97 us  [on_device(): above = lax.ppermute(bottom, 'row', up(n_row))]
    ppermute x1, waiting for transfers between devices: 0.01 us -> 0.92 us  [on_device(): left = lax.ppermute(last, 'col', up(n_col))]
    concatenate x2 -> x0, other arithmetic: 0.76 us -> none  [on_device(): jnp.concatenate([cell_ids.reshape(-1), cell_slots.reshape(-1), cell_count...]
    pad x1 -> x0, other arithmetic: 0.72 us -> none  [on_device(): jnp.pad(x.reshape(pairs, taps).astype(F32), ((0, 0), (0, 128 - taps)))]
  transfers between devices with their start and end apart: 7 -> 7, of which waited for: 1 -> 1; matrix products, arithmetic and copies ran while one was open for 3% -> 0% of each run, Pallas kernels for 27% -> 21%
where the time goes in v2:
time: 36 us; the launch traced here: 35.6 us
  starting transfers between devices  18.4 us (51%)
  Pallas kernels  12.3 us (34%)
  local copies, waits for them, and re-layouts  3.08 us (9%)
  waiting for transfers between devices  0.93 us (3%)
  between operations  0.84 us (2%)
    pallas_call x1, Pallas kernels, on_device(): pl.pallas_call(socs_kernel, out_shape=shape((NB + 1, CB, 256), F32), in_s...  7.13 us
    ppermute x3, starting transfers between devices, on_device(): lax.ppermute(library, 'col', [(i, (i + shift) % n_col) for i in range(n_c...  5.46 us
    ppermute x1, starting transfers between devices, on_device(): above = lax.ppermute(bottom, 'row', up(n_row))  4.97 us
    ppermute x1, starting transfers between devices, on_device(): left = lax.ppermute(last, 'col', up(n_col))  4.66 us
    pallas_call x1, Pallas kernels, on_device(): pl.pallas_call(functools.partial(final_kernel, entries, per, n_row, n_col...  3.74 us
    unnamed x14, local copies, waits for them, and re-layouts  3.08 us
    ppermute x1, starting transfers between devices, on_device(): below = lax.ppermute(top, 'row', down(n_row))  1.92 us
    ppermute x1, starting transfers between devices, on_device(): right = lax.ppermute(first, 'col', down(n_col))  1.42 us
  transfers between devices with their start and end apart: 7, of which 1 were waited for; matrix products, arithmetic and copies ran while one was open for 0% of the time, Pallas kernels for 21%

profile of v2, /device:TPU:1, one launch (start us, length us, event | category | flops | bytes accessed | tf_op | source)
XLA Modules:
  0.0 35.6 jit_solution(16668476105679708715)
XLA Ops:
  0.7 1.0 %copy-done = s32[256,512]{1,0:T(8,128)S(1)} copy-done((s32[256,512]{1,0:T(8,128)S(1)}, s32[256,512]{1,0:T(8,128)}, u32[]{:S(2)}) %copy-start) | copy-done | bytes 524312
  1.7 0.7 %copy-done.2 = bf16[12,2,33]{2,1,0:T(2,128)(2,1)S(1)} copy-done((bf16[12,2,33]{2,1,0:T(2,128)(2,1)S(1)}, bf16[12,2,33]{2,1,0:T(2,128)(2,1)}, u32[]{:S(2)}) %copy-start.2) | copy-done | bytes 1608
  2.4 0.7 %copy-done.3 = bf16[12,2,33]{2,1,0:T(2,128)(2,1)S(1)} copy-done((bf16[12,2,33]{2,1,0:T(2,128)(2,1)S(1)}, bf16[12,2,33]{2,1,0:T(2,128)(2,1)}, u32[]{:S(2)}) %copy-start.3) | copy-done | bytes 1608
  3.1 0.5 %prep.1 = (bf16[48,256]{1,0:T(8,128)(2,1)S(1)}, bf16[48,256]{1,0:T(8,128)(2,1)S(1)}, f32[12,8,128]{2,1,0:T(8,128)S(1)}, f32[12,8,128]{2,1,0:T(8,128)S(1)}) custom-call(s32[256,512]{1,0:T(8,128)S(1)} %copy-done, s32[1,1,8]{2,1,0:T(1,128)S(1)} %copy-done.4, s32[1,1,8]{2,1,0:T(1,128)S(1)} %copy-done.5, s32[1,1]{1,0:T(1,128)S(6)} %copy.9.count, ...), custom_call_target="tpu_custom_call" | custom-call | tf_op jit(solution)/shard_map/prep/pallas_call | solution.py:330
  3.7 0.0 copy-start.1
  3.7 1.4 %collective-permute-start.1 = (bf16[48,256]{1,0:T(8,128)(2,1)S(1)}, bf16[48,256]{1,0:T(8,128)(2,1)S(1)}, u32[]{:S(2)}, u32[]{:S(2)}) collective-permute-start(bf16[48,256]{1,0:T(8,128)(2,1)S(1)} %get-tuple-element.17.own), channel_id=1, source_target_pairs={{1,0},{2,1},{3,2},{5,4},{6,5},{7,6},{9,8},{10,9},{11,10},{13,12},{... | collective-permute-start | bytes 73736 | tf_op jit(solution)/shard_map/ppermute | solution.py:351
  5.1 4.7 %collective-permute-start = (bf16[48,256]{1,0:T(8,128)(2,1)S(1)}, bf16[48,256]{1,0:T(8,128)(2,1)S(1)}, u32[]{:S(2)}, u32[]{:S(2)}) collective-permute-start(bf16[48,256]{1,0:T(8,128)(2,1)S(1)} %get-tuple-element.16), channel_id=1, source_target_pairs={{0,1},{1,2},{2,3},{4,5},{5,6},{6,7},{8,9},{9,10},{10,11},{12,13},{... | collective-permute-start | bytes 73736 | tf_op jit(solution)/shard_map/ppermute | solution.py:350
  9.8 0.0 collective-permute-done.1.right
  9.8 0.9 %collective-permute-done.left = bf16[48,256]{1,0:T(8,128)(2,1)S(1)} collective-permute-done((bf16[48,256]{1,0:T(8,128)(2,1)S(1)}, bf16[48,256]{1,0:T(8,128)(2,1)S(1)}, u32[]{:S(2)}, u32[]{:S(2)}) %collective-permute-start) | collective-permute-done | bytes 24608 | tf_op jit(solution)/shard_map/ppermute | solution.py:350
  10.7 0.4 %mid.1 = (bf16[48,640]{1,0:T(8,128)(2,1)S(1)}, bf16[48,640]{1,0:T(8,128)(2,1)S(1)}) custom-call(s32[256,512]{1,0:T(8,128)S(1)} %copy-done, bf16[48,256]{1,0:T(8,128)(2,1)S(1)} %collective-permute-done.left, bf16[48,256]{1,0:T(8,128)(2,1)S(1)} %collective-permute-done.1.right, bf16[48,256]{1,0:T(8,128)(2,1)S(1)} %get-tuple-element.17.own), custom_call_target="tpu_custom_call" | custom-call | tf_op jit(solution)/shard_map/mid/pallas_call | solution.py:357
  11.2 5.0 %collective-permute-start.2 = (bf16[48,640]{1,0:T(8,128)(2,1)S(1)}, bf16[48,640]{1,0:T(8,128)(2,1)S(1)}, u32[]{:S(2)}, u32[]{:S(2)}) collective-permute-start(bf16[48,640]{1,0:T(8,128)(2,1)S(1)} %get-tuple-element.18), channel_id=1, source_target_pairs={{0,4},{4,8},{8,12},{1,5},{5,9},{9,13},{2,6},{6,10},{10,14},{3,7},{... | collective-permute-start | bytes 184328 | tf_op jit(solution)/shard_map/ppermute | solution.py:366
  16.1 1.9 %collective-permute-start.3 = (bf16[48,640]{1,0:T(8,128)(2,1)S(1)}, bf16[48,640]{1,0:T(8,128)(2,1)S(1)}, u32[]{:S(2)}, u32[]{:S(2)}) collective-permute-start(bf16[48,640]{1,0:T(8,128)(2,1)S(1)} %get-tuple-element.19), channel_id=1, source_target_pairs={{4,0},{8,4},{12,8},{5,1},{9,5},{13,9},{6,2},{10,6},{14,10},{7,3},{... | collective-permute-start | bytes 184328 | tf_op jit(solution)/shard_map/ppermute | solution.py:367
  18.1 2.1 %collective-permute-start.4 = (bf16[8,64,128]{2,1,0:T(8,128)(2,1)S(1)}, bf16[8,64,128]{2,1,0:T(8,128)(2,1)S(1)}, u32[]{:S(2)}, u32[]{:S(2)}) collective-permute-start(bf16[8,64,128]{2,1,0:T(8,128)(2,1)S(1)} %copy-done.1), channel_id=1, source_target_pairs={{0,1},{1,2},{2,3},{3,0},{4,5},{5,6},{6,7},{7,4},{8,9},{9,10},{10,1... | collective-permute-start | bytes 393224 | tf_op jit(solution)/shard_map/ppermute | solution.py:355
  20.2 2.3 %collective-permute-start.5 = (bf16[8,64,128]{2,1,0:T(8,128)(2,1)S(1)}, bf16[8,64,128]{2,1,0:T(8,128)(2,1)S(1)}, u32[]{:S(2)}, u32[]{:S(2)}) collective-permute-start(bf16[8,64,128]{2,1,0:T(8,128)(2,1)S(1)} %copy-done.1), channel_id=1, source_target_pairs={{0,2},{1,3},{2,0},{3,1},{4,6},{5,7},{6,4},{7,5},{8,10},{9,11},{10,... | collective-permute-start | bytes 393224 | tf_op jit(solution)/shard_map/ppermute | solution.py:355
  22.5 1.1 %collective-permute-start.6 = (bf16[8,64,128]{2,1,0:T(8,128)(2,1)S(1)}, bf16[8,64,128]{2,1,0:T(8,128)(2,1)S(1)}, u32[]{:S(2)}, u32[]{:S(2)}) collective-permute-start(bf16[8,64,128]{2,1,0:T(8,128)(2,1)S(1)} %copy-done.1), channel_id=1, source_target_pairs={{0,3},{1,0},{2,1},{3,2},{4,7},{5,4},{6,5},{7,6},{8,11},{9,8},{10,9... | collective-permute-start | bytes 393224 | tf_op jit(solution)/shard_map/ppermute | solution.py:355
  23.5 0.5 %window.1.windows = f32[3,256,256]{2,1,0:T(8,128)S(1)} custom-call(s32[256,512]{1,0:T(8,128)S(1)} %copy-done, bf16[48,256]{1,0:T(8,128)(2,1)S(1)} %collective-permute-done.left, bf16[48,256]{1,0:T(8,128)(2,1)S(1)} %collective-permute-done.1.right), custom_call_target="tpu_custom_call" | custom-call | flops 1000000 | bytes 1000000 | tf_op jit(solution)/shard_map/window/pallas_call | solution.py:369
  24.1 0.0 collective-permute-done.2.above
  24.1 0.0 collective-permute-done.3.below
  24.1 0.0 copy-start.6
  24.1 0.6 %copy-done.6 = f32[12]{0:T(128)S(1)} copy-done((f32[12]{0:T(128)S(1)}, f32[12]{0:T(128)}, u32[]{:S(2)}) %copy-start.6) | copy-done | bytes 72
  24.7 7.1 %socs.1.acc = f32[4,176,256]{2,1,0:T(8,128)S(1)} custom-call(f32[12]{0:T(128)S(1)} %copy-done.6, f32[3,256,256]{2,1,0:T(8,128)S(1)} %window.1.windows, bf16[48,640]{1,0:T(8,128)(2,1)S(1)} %collective-permute-done.2.above, bf16[48,640]{1,0:T(8,128)(2,1)S(1)} %collective-permute-done.3.below, f32[12,8,128]{2,1,0:T(8,128)S(1)} %get-tuple-element.20.ahead, ...), custom_call_target="tpu_custom_call" | custom-call | flops 5000000000 | bytes 8000000 | tf_op jit(solution)/shard_map/socs/pallas_call | solution.py:379
  31.9 0.0 collective-permute-done.5.rest_2_
  31.9 0.0 collective-permute-done.6.rest_3_
  31.9 3.7 %final.1 = f32[256,512]{1,0:T(8,128)} custom-call(f32[4,176,256]{2,1,0:T(8,128)S(1)} %socs.1.acc, bf16[48,640]{1,0:T(8,128)(2,1)S(1)} %collective-permute-done.2.above, bf16[48,256]{1,0:T(8,128)(2,1)S(1)} %collective-permute-done.left, bf16[48,256]{1,0:T(8,128)(2,1)S(1)} %get-tuple-element.17.own, bf16[48,256]{1,0:T(8,128)(2,1)S(1)} %collective-permute-done.1.right, ...), custom_call_target="tpu_custom_call" | custom-call | tf_op jit(solution)/shard_map/final/pallas_call | solution.py:393
  (9 shorter events, 0.0 us)
Async XLA Ops:
  0.0 0.7 %copy-start.4 = (s32[1,1,8]{2,1,0:T(1,128)S(1)}, s32[1,1,8]{2,1,0:T(1,128)}, u32[]{:S(2)}) copy-start(s32[1,1,8]{2,1,0:T(1,128)} %ids.1) | copy-start | bytes 100
  0.0 0.7 %copy-start.5 = (s32[1,1,8]{2,1,0:T(1,128)S(1)}, s32[1,1,8]{2,1,0:T(1,128)}, u32[]{:S(2)}) copy-start(s32[1,1,8]{2,1,0:T(1,128)} %slots.1) | copy-start | bytes 100
  0.7 1.0 %copy-start = (s32[256,512]{1,0:T(8,128)S(1)}, s32[256,512]{1,0:T(8,128)}, u32[]{:S(2)}) copy-start(s32[256,512]{1,0:T(8,128)} %mask.5) | copy-start | bytes 1572868
  1.7 0.7 %copy-start.2 = (bf16[12,2,33]{2,1,0:T(2,128)(2,1)S(1)}, bf16[12,2,33]{2,1,0:T(2,128)(2,1)}, u32[]{:S(2)}) copy-start(bf16[12,2,33]{2,1,0:T(2,128)(2,1)} %across.1) | copy-start | bytes 4756
  2.4 0.7 %copy-start.3 = (bf16[12,2,33]{2,1,0:T(2,128)(2,1)S(1)}, bf16[12,2,33]{2,1,0:T(2,128)(2,1)}, u32[]{:S(2)}) copy-start(bf16[12,2,33]{2,1,0:T(2,128)(2,1)} %down.1) | copy-start | bytes 4756
  3.7 14.4 %copy-start.1 = (bf16[8,64,128]{2,1,0:T(8,128)(2,1)S(1)}, bf16[8,64,128]{2,1,0:T(8,128)(2,1)}, u32[]{:S(2)}) copy-start(bf16[8,64,128]{2,1,0:T(8,128)(2,1)} %rest_0_) | copy-start | bytes 393220
  3.7 6.1 %collective-permute-start.1 = (bf16[48,256]{1,0:T(8,128)(2,1)S(1)}, bf16[48,256]{1,0:T(8,128)(2,1)S(1)}, u32[]{:S(2)}, u32[]{:S(2)}) collective-permute-start(bf16[48,256]{1,0:T(8,128)(2,1)S(1)} %get-tuple-element.17.own), channel_id=1, source_target_pairs={{1,0},{2,1},{3,2},{5,4},{6,5},{7,6},{9,8},{10,9},{11,10},{13,12},{... | collective-permute-start | bytes 73736 | tf_op jit(solution)/shard_map/ppermute | solution.py:351
  5.1 5.6 %collective-permute-start = (bf16[48,256]{1,0:T(8,128)(2,1)S(1)}, bf16[48,256]{1,0:T(8,128)(2,1)S(1)}, u32[]{:S(2)}, u32[]{:S(2)}) collective-permute-start(bf16[48,256]{1,0:T(8,128)(2,1)S(1)} %get-tuple-element.16), channel_id=1, source_target_pairs={{0,1},{1,2},{2,3},{4,5},{5,6},{6,7},{8,9},{9,10},{10,11},{12,13},{... | collective-permute-start | bytes 73736 | tf_op jit(solution)/shard_map/ppermute | solution.py:350
  11.2 12.9 %collective-permute-start.2 = (bf16[48,640]{1,0:T(8,128)(2,1)S(1)}, bf16[48,640]{1,0:T(8,128)(2,1)S(1)}, u32[]{:S(2)}, u32[]{:S(2)}) collective-permute-start(bf16[48,640]{1,0:T(8,128)(2,1)S(1)} %get-tuple-element.18), channel_id=1, source_target_pairs={{0,4},{4,8},{8,12},{1,5},{5,9},{9,13},{2,6},{6,10},{10,14},{3,7},{... | collective-permute-start | bytes 184328 | tf_op jit(solution)/shard_map/ppermute | solution.py:366
  16.1 7.9 %collective-permute-start.3 = (bf16[48,640]{1,0:T(8,128)(2,1)S(1)}, bf16[48,640]{1,0:T(8,128)(2,1)S(1)}, u32[]{:S(2)}, u32[]{:S(2)}) collective-permute-start(bf16[48,640]{1,0:T(8,128)(2,1)S(1)} %get-tuple-element.19), channel_id=1, source_target_pairs={{4,0},{8,4},{12,8},{5,1},{9,5},{13,9},{6,2},{10,6},{14,10},{7,3},{... | collective-permute-start | bytes 184328 | tf_op jit(solution)/shard_map/ppermute | solution.py:367
  18.1 13.8 %collective-permute-start.4 = (bf16[8,64,128]{2,1,0:T(8,128)(2,1)S(1)}, bf16[8,64,128]{2,1,0:T(8,128)(2,1)S(1)}, u32[]{:S(2)}, u32[]{:S(2)}) collective-permute-start(bf16[8,64,128]{2,1,0:T(8,128)(2,1)S(1)} %copy-done.1), channel_id=1, source_target_pairs={{0,1},{1,2},{2,3},{3,0},{4,5},{5,6},{6,7},{7,4},{8,9},{9,10},{10,1... | collective-permute-start | bytes 393224 | tf_op jit(solution)/shard_map/ppermute | solution.py:355
  20.2 11.7 %collective-permute-start.5 = (bf16[8,64,128]{2,1,0:T(8,128)(2,1)S(1)}, bf16[8,64,128]{2,1,0:T(8,128)(2,1)S(1)}, u32[]{:S(2)}, u32[]{:S(2)}) collective-permute-start(bf16[8,64,128]{2,1,0:T(8,128)(2,1)S(1)} %copy-done.1), channel_id=1, source_target_pairs={{0,2},{1,3},{2,0},{3,1},{4,6},{5,7},{6,4},{7,5},{8,10},{9,11},{10,... | collective-permute-start | bytes 393224 | tf_op jit(solution)/shard_map/ppermute | solution.py:355
  22.5 9.4 %collective-permute-start.6 = (bf16[8,64,128]{2,1,0:T(8,128)(2,1)S(1)}, bf16[8,64,128]{2,1,0:T(8,128)(2,1)S(1)}, u32[]{:S(2)}, u32[]{:S(2)}) collective-permute-start(bf16[8,64,128]{2,1,0:T(8,128)(2,1)S(1)} %copy-done.1), channel_id=1, source_target_pairs={{0,3},{1,0},{2,1},{3,2},{4,7},{5,4},{6,5},{7,6},{8,11},{9,8},{10,9... | collective-permute-start | bytes 393224 | tf_op jit(solution)/shard_map/ppermute | solution.py:355
  24.1 0.7 %copy-start.6 = (f32[12]{0:T(128)S(1)}, f32[12]{0:T(128)}, u32[]{:S(2)}) copy-start(f32[12]{0:T(128)} %weights.1) | copy-start | bytes 148

commit v3 on v2

--- a/solution.py
+++ b/solution.py
@@ -20,6 +20,7 @@
 EDGE_OUT = 48
 EDGE_AT = (0, 48, 128)
 WIDE = 640
+SLOTS = 16
 F32 = jnp.float32
 BF16 = jnp.bfloat16
 VMEM = pl.BlockSpec(memory_space=pltpu.VMEM)
@@ -37,7 +38,7 @@
 
 
 def prep_kernel(
-    mask, ids, slots, count, across, down, first, last, ahead, back, ends, a_ids, a_slots, a_count, tap, sems
+    mask, ids, slots, count, first, last, ends, a_ids, a_slots, sems
 ):
     rows, cols = mask.shape
     copies = [
@@ -45,13 +46,10 @@
         pltpu.make_async_copy(mask.at[:, cols - 128 : cols], ends.at[1], sems.at[1]),
         pltpu.make_async_copy(ids, a_ids, sems.at[2]),
         pltpu.make_async_copy(slots, a_slots, sems.at[3]),
-        pltpu.make_async_copy(count, a_count, sems.at[4]),
-        pltpu.make_async_copy(across, tap.at[0], sems.at[5]),
-        pltpu.make_async_copy(down, tap.at[1], sems.at[6]),
     ]
     for copy in copies:
         copy.start()
-    for copy in copies[2:5]:
+    for copy in copies[2:4]:
         copy.wait()
     line = lax.broadcasted_iota(jnp.int32, (16, 128), 0)
     lane = lax.broadcasted_iota(jnp.int32, (16, 128), 1)
@@ -61,7 +59,7 @@
         x = jnp.concatenate([x, jnp.zeros((1, 128 - x.shape[1]), F32)], axis=1)
         return jnp.broadcast_to(x, (16, 128))
 
-    table = jnp.where(line == 1, spread(a_slots[0]), spread(a_count[...]))
+    table = jnp.where(line == 1, spread(a_slots[0]), count[0, 0].astype(F32))
     table = jnp.where(line == 0, spread(a_ids[0]), table)
     width = jnp.where(line == 2, 1, ids.shape[2])
     table = jnp.where((lane < width) & (line < 3), table, 0.0).astype(BF16)
@@ -72,18 +70,6 @@
     first[0:STRIP, :] = ends[0].astype(F32).T[0:STRIP].astype(BF16)
     copies[1].wait()
     last[0:STRIP, :] = ends[1].astype(F32).T[128 - STRIP :].astype(BF16)
-    copies[5].wait()
-    copies[6].wait()
-    taps = across.shape[2]
-    flip = lax.broadcasted_iota(jnp.int32, (128, 128), 0) + lax.broadcasted_iota(jnp.int32, (128, 128), 1)
-    flip = jnp.where(flip % 128 == 0, 1.0, 0.0).astype(BF16)
-    pad = jnp.zeros((8, 128 - taps), F32)
-    more = jnp.zeros((6, taps), F32)
-    for k in range(across.shape[0]):
-        line = jnp.concatenate([tap[0, k].astype(F32), more], axis=0)
-        ahead[k] = jnp.concatenate([line, pad], axis=1)
-        line = jnp.concatenate([tap[1, k].astype(F32), more], axis=0)
-        back[k] = dot_nn(jnp.concatenate([line, pad], axis=1).astype(BF16), flip)
 
 
 def mid_kernel(mask, left, right, own, top, bottom, ends, sems):
@@ -113,19 +99,49 @@
         out[STRIP:, :] = tables
 
 
-def window_kernel(mask, left, right, windows):
+def window_kernel(
+    mask, left, right, across, down, weights, windows, ahead, back, scale, own, tap, line, sems
+):
     rows, cols = mask.shape
+    copies = [
+        pltpu.make_async_copy(mask, own, sems.at[0]),
+        pltpu.make_async_copy(across, tap.at[0], sems.at[1]),
+        pltpu.make_async_copy(down, tap.at[1], sems.at[2]),
+        pltpu.make_async_copy(weights, line, sems.at[3]),
+    ]
+    for copy in copies:
+        copy.start()
     fill = jnp.zeros((128 - STRIP, rows), F32)
+    copies[0].wait()
     lhs = jnp.concatenate([left[0:STRIP, :].astype(F32), fill], axis=0).T
     rhs = jnp.concatenate([right[0:STRIP, :].astype(F32), fill], axis=0).T
     full = jnp.concatenate(
-        [lhs[:, STRIP - RIM : STRIP], mask[...].astype(F32), rhs[:, 0 : WIDE - RIM - cols]], axis=1
+        [lhs[:, STRIP - RIM : STRIP], own[...].astype(F32), rhs[:, 0 : WIDE - RIM - cols]], axis=1
     )
     for b in range(NB):
         windows[b] = full[:, CB * b : CB * b + 256]
-
-
-def socs_kernel(weights, windows, above, below, ahead, back, acc, x_win, *scratch):
+    for copy in copies[1:]:
+        copy.wait()
+    taps = across.shape[2]
+    flip = lax.broadcasted_iota(jnp.int32, (128, 128), 0) + lax.broadcasted_iota(jnp.int32, (128, 128), 1)
+    flip = jnp.where(flip % 128 == 0, 1.0, 0.0).astype(BF16)
+    pad = jnp.zeros((8, 128 - taps), F32)
+    more = jnp.zeros((6, taps), F32)
+    at = lax.broadcasted_iota(jnp.int32, (8, 128), 1)
+    every = jnp.broadcast_to(line[...].reshape(1, -1), (8, line.shape[0]))
+    every = jnp.concatenate([every, jnp.zeros((8, 128 - line.shape[0]), F32)], axis=1)
+    for k in range(across.shape[0]):
+        part = jnp.concatenate([tap[0, k].astype(F32), more], axis=0)
+        ahead[k] = jnp.concatenate([part, pad], axis=1)
+        part = jnp.concatenate([tap[1, k].astype(F32), more], axis=0)
+        back[k] = dot_nn(jnp.concatenate([part, pad], axis=1).astype(BF16), flip)
+        weight = jnp.sum(jnp.where(at == k, every, 0.0), axis=1, keepdims=True)
+        scale[k] = jnp.broadcast_to(weight, (8, 256))
+
+
+def socs_kernel(
+    entries, windows, above, left, own, right, below, ahead, back, scale, acc, images, x_win, *scratch
+):
     across = scratch[0:2]
     d_main = scratch[2:4]
     d_edge = scratch[4:6]
@@ -136,14 +152,27 @@
     edge_rows = []
     for b in range(NB):
         lanes = slice(CB * b, CB * b + 256)
-        own = windows[b]
-        x_win[b] = jnp.concatenate([upper_rows[:, lanes], own[0 : 256 - RIM]], axis=0).astype(BF16)
-        edge_rows += [own[MAIN - RIM :], lower_rows[:, lanes]]
+        part = windows[b]
+        x_win[b] = jnp.concatenate([upper_rows[:, lanes], part[0 : 256 - RIM]], axis=0).astype(BF16)
+        edge_rows += [part[MAIN - RIM :], lower_rows[:, lanes]]
     edge_rows.append(jnp.zeros((256 - NB * EDGE_IN, 256), F32))
     x_win[NB] = jnp.concatenate(edge_rows, axis=0).astype(BF16)
     acc[...] = jnp.zeros(acc.shape, F32)
     for ref in across + d_main + d_edge:
         ref[...] = jnp.zeros(ref.shape, BF16)
+
+    slot = lax.broadcasted_iota(jnp.int32, (SLOTS, 128), 0).astype(F32)
+    lane = lax.broadcasted_iota(jnp.int32, (SLOTS, 128), 1)
+    found = jnp.zeros((SLOTS, 128), F32)
+    strips = [above] * 3 + [left, own, right] + [below] * 3
+    for t, strip in enumerate(strips):
+        at = 0 if t in (3, 4, 5) else 128 * (t % 3)
+        table = strip[STRIP:, at : at + 128].astype(F32)
+        live = lane.astype(F32) < table[2:3, 0:1]
+        hit = live & (table[1:2] == slot) & (lane < entries)
+        image = jnp.sum(jnp.where(hit, table[0:1] + 1.0, 0.0), axis=1, keepdims=True)
+        found = jnp.where(lane == t, image, found)
+    images[...] = found.astype(jnp.int32)
 
     row = lax.broadcasted_iota(jnp.int32, (32, 128), 0)
     lane = lax.broadcasted_iota(jnp.int32, (32, 128), 1)
@@ -190,7 +219,7 @@
             first[s][1, j] = part[CB:]
 
     def pass_two(k, s):
-        weight = weights[k]
+        weight = scale[k, 0:1, :]
         total = None
         for p in range(2):
             second = dot_nn(first[s][p, 0:NB].reshape(NB * CB, 256), d_main[s][p])
@@ -233,64 +262,44 @@
     return high, (g - high.astype(F32)).astype(BF16)
 
 
-def final_kernel(entries, per, n_row, n_col, acc, above, left, own, right, below, *rest):
-    shards = rest[:-9]
-    out, cells, tab, tables, slots, placed, flat, blurred, sem = rest[-9:]
-    count = len(shards)
+def final_kernel(n_row, n_col, acc, images, cells, out, table, placed, flat, blurred, sem):
     rows, cols = out.shape
     row, col = lax.axis_index("row"), lax.axis_index("col")
-
-    for i, strip in enumerate((above, below)):
-        tab[:, 768 * i : 768 * i + 384] = strip[STRIP:, 0:384].astype(F32).astype(jnp.int32)[0:8]
-    for i, strip in enumerate((left, own, right)):
-        tab[:, 384 + 128 * i : 512 + 128 * i] = strip[STRIP:, 0:128].astype(F32).astype(jnp.int32)[0:8]
-    fetch = pltpu.make_async_copy(tab, tables, sem)
+    fetch = pltpu.make_async_copy(images, table, sem)
     fetch.start()
-    for i, shard in enumerate(shards):
-        cells[pl.ds(i * per, per)] = shard[...]
-    empty = count * per
-    cells[empty] = jnp.zeros(cells.shape[1:], BF16)
-
-    far = 1 << 20
-    at_row = lax.broadcasted_iota(jnp.int32, (CB, 384), 1) - BLUR_HALF
-    row_ok = (at_row >= jnp.where(row == 0, 0, -far)) & (at_row < jnp.where(row == n_row - 1, rows, far))
-    at_col = lax.broadcasted_iota(jnp.int32, (CB, 384), 0) - BLUR_HALF
+
+    at_row = lax.broadcasted_iota(jnp.int32, (8, 384), 1) - BLUR_HALF
+    row_ok = ((row > 0) | (at_row >= 0)) & ((row < n_row - 1) | (at_row < rows))
+    row_ok = jnp.where(row_ok, 1.0, 0.0)
     for b in range(NB):
         edge = acc[NB, :, EDGE_AT[b] : EDGE_AT[b] + EDGE_OUT]
         part = jnp.concatenate(
             [acc[b, :, 0:MAIN], edge, jnp.zeros((CB, 384 - MAIN - EDGE_OUT), F32)], axis=1
         )
-        here = at_col + b * CB
-        keep = row_ok & (here >= jnp.where(col == 0, 0, -far))
-        keep = keep & (here < jnp.where(col == n_col - 1, cols, far))
-        flat[b * CB : (b + 1) * CB, :] = jnp.where(keep, part, 0.0).astype(BF16)
+        part = part * row_ok[0:1]
+        if b == 0:
+            part = jnp.concatenate([jnp.where(col > 0, part[0:8], 0.0), part[8:]], axis=0)
+        if b == NB - 1:
+            part = jnp.concatenate([part[0 : CB - 8], jnp.where(col < n_col - 1, part[CB - 8 :], 0.0)], axis=0)
+        flat[b * CB : (b + 1) * CB, :] = part.astype(BF16)
     flat[NB * CB :, :] = jnp.zeros((flat.shape[0] - NB * CB, 384), BF16)
 
     fetch.wait()
-    for t in range(9):
-        for s in range(16):
-            slots[t * 17 + s] = empty
-        live = tables[2, 128 * t]
-        for n in range(entries):
-            cell = tables[0, 128 * t + n]
-            owner = cell // per
-            behind = jnp.where(owner <= col, col - owner, col - owner + count)
-            at = jnp.where(n < live, tables[1, 128 * t + n], 16)
-            slots[t * 17 + at] = behind * per + cell - owner * per
-
     slot_rows, slot_cols = rows // 64, cols // 128
     for i in range(-1, slot_rows + 1):
         for j in range(-1, slot_cols + 1):
             ti = 0 if i < 0 else (2 if i == slot_rows else 1)
             tj = 0 if j < 0 else (2 if j == slot_cols else 1)
-            image = slots[(3 * ti + tj) * 17 + (i % slot_rows) * slot_cols + j % slot_cols]
+            found = table[(i % slot_rows) * slot_cols + j % slot_cols, 3 * ti + tj]
+            image = jnp.maximum(found - 1, 0)
             lanes = slice(128 + 128 * j, 256 + 128 * j)
+            show = lambda x: jnp.where(found > 0, x.astype(F32), 0.0)
             if i < 0:
-                placed[0:8, lanes] = cells[image, 48:64, :].astype(F32)[8:16]
+                placed[0:8, lanes] = show(cells[image, 48:64, :])[8:16]
             elif i == slot_rows:
-                placed[8 + rows : 16 + rows, lanes] = cells[image, 0:16, :].astype(F32)[0:8]
+                placed[8 + rows : 16 + rows, lanes] = show(cells[image, 0:16, :])[0:8]
             else:
-                placed[8 + 64 * i : 72 + 64 * i, lanes] = cells[image].astype(F32)
+                placed[8 + 64 * i : 72 + 64 * i, lanes] = show(cells[image])
     placed[16 + rows :, :] = jnp.zeros((placed.shape[0] - 16 - rows, placed.shape[1]), F32)
 
     g_high, g_low = blur_matrix((128, 256), 1)
@@ -326,23 +335,23 @@
     entries = cell_ids.shape[-1]
     per = library.shape[0]
     n_row, n_col = lax.axis_size("row"), lax.axis_size("col")
-
-    first, last, ahead, back = pl.pallas_call(
+    in_hbm = lambda x: pltpu.with_memory_space_constraint(x, pltpu.HBM)
+    mask_hbm = in_hbm(mask_pixels)
+
+    first, last = pl.pallas_call(
         prep_kernel,
-        out_shape=(shape((STRIP + 16, rows), BF16),) * 2 + (shape((kernels, 8, 128), F32),) * 2,
-        in_specs=[HBM] * 6,
-        out_specs=(VMEM,) * 4,
+        out_shape=(shape((STRIP + 16, rows), BF16),) * 2,
+        in_specs=[HBM] * 3 + [SMEM],
+        out_specs=(VMEM,) * 2,
         scratch_shapes=[
             pltpu.VMEM((2, rows, 128), jnp.int32),
             pltpu.VMEM(cell_ids.shape, jnp.int32),
             pltpu.VMEM(cell_slots.shape, jnp.int32),
-            pltpu.VMEM(cell_count.shape, jnp.int32),
-            pltpu.VMEM((2,) + across_taps.shape, BF16),
-            pltpu.SemaphoreType.DMA((7,)),
+            pltpu.SemaphoreType.DMA((4,)),
         ],
         compiler_params=PARAMS,
         name="prep",
-    )(mask_pixels, cell_ids, cell_slots, cell_count, across_taps, down_taps)
+    )(mask_hbm, in_hbm(cell_ids), in_hbm(cell_slots), cell_count)
     library, first, last = lax.optimization_barrier((library, first, last))
 
     up = lambda n: [(i, i + 1) for i in range(n - 1)]
@@ -350,9 +359,8 @@
     left = lax.ppermute(last, "col", up(n_col))
     right = lax.ppermute(first, "col", down(n_col))
 
-    shards = [library]
-    for shift in range(1, n_col):
-        shards.append(lax.ppermute(library, "col", [(i, (i + shift) % n_col) for i in range(n_col)]))
+    cells = lax.all_to_all(jnp.broadcast_to(library[None], (n_col,) + library.shape), "col", 0, 0)
+    cells = cells.reshape((n_col * per,) + library.shape[1:])
 
     top, bottom = pl.pallas_call(
         mid_kernel,
@@ -362,25 +370,36 @@
         scratch_shapes=[pltpu.VMEM((2, STRIP, cols), jnp.int32), pltpu.SemaphoreType.DMA((2,))],
         compiler_params=PARAMS,
         name="mid",
-    )(mask_pixels, left, right, first)
+    )(mask_hbm, left, right, first)
     above = lax.ppermute(bottom, "row", up(n_row))
     below = lax.ppermute(top, "row", down(n_row))
 
-    windows = pl.pallas_call(
+    windows, ahead, back, scale = pl.pallas_call(
         window_kernel,
-        out_shape=shape((NB, rows, 256), F32),
-        in_specs=[VMEM] * 3,
-        out_specs=VMEM,
+        out_shape=(
+            shape((NB, rows, 256), F32),
+            shape((kernels, 8, 128), F32),
+            shape((kernels, 8, 128), F32),
+            shape((kernels, 8, 256), F32),
+        ),
+        in_specs=[HBM] + [VMEM] * 2 + [HBM] * 3,
+        out_specs=(VMEM,) * 4,
+        scratch_shapes=[
+            pltpu.VMEM(mask_pixels.shape, jnp.int32),
+            pltpu.VMEM((2,) + across_taps.shape, BF16),
+            pltpu.VMEM(kernel_weights.shape, F32),
+            pltpu.SemaphoreType.DMA((4,)),
+        ],
         compiler_params=PARAMS,
         cost_estimate=pl.CostEstimate(flops=10**6, bytes_accessed=10**6, transcendentals=0),
         name="window",
-    )(mask_pixels, left, right)
-
-    acc = pl.pallas_call(
-        socs_kernel,
-        out_shape=shape((NB + 1, CB, 256), F32),
-        in_specs=[SMEM] + [VMEM] * 5,
-        out_specs=VMEM,
+    )(mask_hbm, left, right, in_hbm(across_taps), in_hbm(down_taps), in_hbm(kernel_weights))
+
+    acc, images = pl.pallas_call(
+        functools.partial(socs_kernel, entries),
+        out_shape=(shape((NB + 1, CB, 256), F32), shape((SLOTS, 128), jnp.int32)),
+        in_specs=[VMEM] * 9,
+        out_specs=(VMEM,) * 2,
         scratch_shapes=[pltpu.VMEM((NB + 1, 256, 256), BF16)]
         + [pltpu.VMEM((2, CB, 256), BF16)] * 2
         + [pltpu.VMEM((2, 256, 256), BF16)] * 4
@@ -388,18 +407,15 @@
         compiler_params=PARAMS,
         cost_estimate=pl.CostEstimate(flops=5 * 10**9, bytes_accessed=8 * 10**6, transcendentals=0),
         name="socs",
-    )(kernel_weights, windows, above, below, ahead, back)
+    )(windows, above, left, first, right, below, ahead, back, scale)
 
     return pl.pallas_call(
-        functools.partial(final_kernel, entries, per, n_row, n_col),
+        functools.partial(final_kernel, n_row, n_col),
         out_shape=shape((rows, cols), F32),
-        in_specs=[VMEM] * (6 + len(shards)),
+        in_specs=[VMEM] * 3,
         out_specs=VMEM,
         scratch_shapes=[
-            pltpu.VMEM((per * len(shards) + 1, 64, 128), BF16),
-            pltpu.VMEM((8, 9 * 128), jnp.int32),
-            pltpu.SMEM((8, 9 * 128), jnp.int32),
-            pltpu.SMEM((9 * 17,), jnp.int32),
+            pltpu.SMEM((SLOTS, 128), jnp.int32),
             pltpu.VMEM((384, cols + 256), F32),
             pltpu.VMEM((WIDE, 384), BF16),
             pltpu.VMEM((2, rows, WIDE), BF16),
@@ -407,7 +423,7 @@
         ],
         compiler_params=PARAMS,
         name="final",
-    )(acc, above, left, first, right, below, *shards)
+    )(acc, images, cells)
 
 
 def solution(mesh):

time: 36 us -> 41.4 us (1.15)
  the two profiles are of different devices: /device:TPU:1 before, /device:TPU:9 now
where the time goes in v3:
time: 41.4 us; the launch traced here: 41.1 us
  starting transfers between devices  16.7 us (40%)
  Pallas kernels  13.2 us (32%)
  waiting for transfers between devices  9.54 us (23%)
  local copies, waits for them, and re-layouts  0.92 us (2%)
  between operations  0.75 us (2%)
    ppermute x1, waiting for transfers between devices, on_device(): right = lax.ppermute(first, 'col', down(n_col))  7.76 us
    pallas_call x1, Pallas kernels, on_device(): pl.pallas_call(functools.partial(socs_kernel, entries), out_shape=(shape(...  6.57 us
    all_to_all x1, starting transfers between devices, on_device(): lax.all_to_all(jnp.broadcast_to(library[None], (n_col,) + library.shape),...  4.76 us
    ppermute x1, starting transfers between devices, on_device(): above = lax.ppermute(bottom, 'row', up(n_row))  4.75 us
    ppermute x1, starting transfers between devices, on_device(): left = lax.ppermute(last, 'col', up(n_col))  3.36 us
    pallas_call x1, Pallas kernels, on_device(): pl.pallas_call(functools.partial(final_kernel, n_row, n_col), out_shape=s...  2.54 us
    ppermute x1, starting transfers between devices, on_device(): below = lax.ppermute(top, 'row', down(n_row))  1.92 us
    ppermute x1, starting transfers between devices, on_device(): right = lax.ppermute(first, 'col', down(n_col))  1.91 us
  transfers between devices with their start and end apart: 5, of which 2 were waited for; matrix products, arithmetic and copies ran while one was open for 0% of the time, Pallas kernels for 23%

profile of v3, /device:TPU:9, one launch (start us, length us, event | category | flops | bytes accessed | tf_op | source)
XLA Modules:
  0.0 41.1 jit_solution(3360235849355530712)
XLA Ops:
  0.7 0.0 copy-start
  0.7 1.2 %prep.1 = (bf16[48,256]{1,0:T(8,128)(2,1)S(1)}, bf16[48,256]{1,0:T(8,128)(2,1)S(1)}) custom-call(s32[256,512]{1,0:T(8,128)} %mask.5, s32[1,1,8]{2,1,0:T(1,128)} %ids.1, s32[1,1,8]{2,1,0:T(1,128)} %slots.1, s32[1,1]{1,0:T(1,128)S(6)} %copy.9.count), custom_call_target="tpu_custom_call" | custom-call | tf_op jit(solution)/shard_map/prep/pallas_call | solution.py:341
  1.8 0.0 copy-done
  1.8 0.9 %broadcast_in_dim.2 = bf16[4,8,64,128]{3,2,1,0:T(8,128)(2,1)} broadcast(bf16[8,64,128]{2,1,0:T(8,128)(2,1)S(1)} %copy-done), dimensions={1,2,3} | broadcast | bytes 655360 | tf_op jit(solution)/shard_map/broadcast_in_dim | solution.py:362
  2.8 4.8 %all-to-all-start = ((bf16[4,8,64,128]{3,2,1,0:T(8,128)(2,1)}), bf16[4,8,64,128]{3,2,1,0:T(8,128)(2,1)S(1)}, u32[]{:S(2)}, u32[]{:S(2)}) async-start(bf16[4,8,64,128]{3,2,1,0:T(8,128)(2,1)} %broadcast_in_dim.2), calls=%async_computation | async-start | bytes 1048576 | tf_op jit(solution)/shard_map/all_to_all | solution.py:362
  7.5 1.9 %collective-permute-start.1 = (bf16[48,256]{1,0:T(8,128)(2,1)S(1)}, bf16[48,256]{1,0:T(8,128)(2,1)S(1)}, u32[]{:S(2)}, u32[]{:S(2)}) collective-permute-start(bf16[48,256]{1,0:T(8,128)(2,1)S(1)} %get-tuple-element.21.own), channel_id=1, source_target_pairs={{1,0},{2,1},{3,2},{5,4},{6,5},{7,6},{9,8},{10,9},{11,10},{13,12},{... | collective-permute-start | bytes 73736 | tf_op jit(solution)/shard_map/ppermute | solution.py:360
  9.4 3.4 %collective-permute-start = (bf16[48,256]{1,0:T(8,128)(2,1)S(1)}, bf16[48,256]{1,0:T(8,128)(2,1)S(1)}, u32[]{:S(2)}, u32[]{:S(2)}) collective-permute-start(bf16[48,256]{1,0:T(8,128)(2,1)S(1)} %get-tuple-element.20), channel_id=1, source_target_pairs={{0,1},{1,2},{2,3},{4,5},{5,6},{6,7},{8,9},{9,10},{10,11},{12,13},{... | collective-permute-start | bytes 73736 | tf_op jit(solution)/shard_map/ppermute | solution.py:359
  12.8 7.8 %collective-permute-done.1.right = bf16[48,256]{1,0:T(8,128)(2,1)S(1)} collective-permute-done((bf16[48,256]{1,0:T(8,128)(2,1)S(1)}, bf16[48,256]{1,0:T(8,128)(2,1)S(1)}, u32[]{:S(2)}, u32[]{:S(2)}) %collective-permute-start.1) | collective-permute-done | bytes 24608 | tf_op jit(solution)/shard_map/ppermute | solution.py:360
  20.6 0.0 collective-permute-done.left
  20.6 1.1 %mid.1 = (bf16[48,640]{1,0:T(8,128)(2,1)S(1)}, bf16[48,640]{1,0:T(8,128)(2,1)S(1)}) custom-call(s32[256,512]{1,0:T(8,128)} %mask.5, bf16[48,256]{1,0:T(8,128)(2,1)S(1)} %collective-permute-done.left, bf16[48,256]{1,0:T(8,128)(2,1)S(1)} %collective-permute-done.1.right, bf16[48,256]{1,0:T(8,128)(2,1)S(1)} %get-tuple-element.21.own), custom_call_target="tpu_custom_call" | custom-call | tf_op jit(solution)/shard_map/mid/pallas_call | solution.py:365
  21.6 4.7 %collective-permute-start.2 = (bf16[48,640]{1,0:T(8,128)(2,1)S(1)}, bf16[48,640]{1,0:T(8,128)(2,1)S(1)}, u32[]{:S(2)}, u32[]{:S(2)}) collective-permute-start(bf16[48,640]{1,0:T(8,128)(2,1)S(1)} %get-tuple-element.23), channel_id=1, source_target_pairs={{0,4},{4,8},{8,12},{1,5},{5,9},{9,13},{2,6},{6,10},{10,14},{3,7},{... | collective-permute-start | bytes 184328 | tf_op jit(solution)/shard_map/ppermute | solution.py:374
  26.4 1.9 %collective-permute-start.3 = (bf16[48,640]{1,0:T(8,128)(2,1)S(1)}, bf16[48,640]{1,0:T(8,128)(2,1)S(1)}, u32[]{:S(2)}, u32[]{:S(2)}) collective-permute-start(bf16[48,640]{1,0:T(8,128)(2,1)S(1)} %get-tuple-element.24), channel_id=1, source_target_pairs={{4,0},{8,4},{12,8},{5,1},{9,5},{13,9},{6,2},{10,6},{14,10},{7,3},{... | collective-permute-start | bytes 184328 | tf_op jit(solution)/shard_map/ppermute | solution.py:375
  28.3 1.8 %window.1 = (f32[3,256,256]{2,1,0:T(8,128)S(1)}, f32[12,8,128]{2,1,0:T(8,128)S(1)}, f32[12,8,128]{2,1,0:T(8,128)S(1)}, f32[12,8,256]{2,1,0:T(8,128)S(1)}) custom-call(s32[256,512]{1,0:T(8,128)} %mask.5, bf16[48,256]{1,0:T(8,128)(2,1)S(1)} %collective-permute-done.left, bf16[48,256]{1,0:T(8,128)(2,1)S(1)} %collective-permute-done.1.right, ...), custom_call_target="tpu_custom_call" | custom-call | flops 1000000 | bytes 1000000 | tf_op jit(solution)/shard_map/window/pallas_call | solution.py:377
  30.2 0.0 collective-permute-done.2.above
  30.2 1.8 %collective-permute-done.3.below = bf16[48,640]{1,0:T(8,128)(2,1)S(1)} collective-permute-done((bf16[48,640]{1,0:T(8,128)(2,1)S(1)}, bf16[48,640]{1,0:T(8,128)(2,1)S(1)}, u32[]{:S(2)}, u32[]{:S(2)}) %collective-permute-start.3) | collective-permute-done | bytes 61472 | tf_op jit(solution)/shard_map/ppermute | solution.py:375
  31.9 6.6 %socs.1 = (f32[4,176,256]{2,1,0:T(8,128)S(1)}, s32[16,128]{1,0:T(8,128)S(1)}) custom-call(f32[3,256,256]{2,1,0:T(8,128)S(1)} %get-tuple-element.22.windows, bf16[48,640]{1,0:T(8,128)(2,1)S(1)} %collective-permute-done.2.above, bf16[48,256]{1,0:T(8,128)(2,1)S(1)} %collective-permute-done.left, bf16[48,256]{1,0:T(8,128)(2,1)S(1)} %get-tuple-element.21.own, ...), custom_call_target="tpu_custom_call" | custom-call | flops 5000000000 | bytes 8000000 | tf_op jit(solution)/shard_map/socs/pallas_call | solution.py:398
  38.5 0.0 all-to-all-done
  38.5 2.5 %final.1 = f32[256,512]{1,0:T(8,128)} custom-call(f32[4,176,256]{2,1,0:T(8,128)S(1)} %get-tuple-element.28.acc, s32[16,128]{1,0:T(8,128)S(1)} %get-tuple-element.29.images, bf16[32,64,128]{2,1,0:T(8,128)(2,1)S(1)} %bitcast.1), custom_call_target="tpu_custom_call" | custom-call | tf_op jit(solution)/shard_map/final/pallas_call | solution.py:412
Async XLA Ops:
  0.7 1.2 %copy-start = (bf16[8,64,128]{2,1,0:T(8,128)(2,1)S(1)}, bf16[8,64,128]{2,1,0:T(8,128)(2,1)}, u32[]{:S(2)}) copy-start(bf16[8,64,128]{2,1,0:T(8,128)(2,1)} %param.12) | copy-start | bytes 393220
  2.8 35.8 %all-to-all-start = ((bf16[4,8,64,128]{3,2,1,0:T(8,128)(2,1)}), bf16[4,8,64,128]{3,2,1,0:T(8,128)(2,1)S(1)}, u32[]{:S(2)}, u32[]{:S(2)}) async-start(bf16[4,8,64,128]{3,2,1,0:T(8,128)(2,1)} %broadcast_in_dim.2), calls=%async_computation | async-start | bytes 1048576 | tf_op jit(solution)/shard_map/all_to_all | solution.py:362
  7.5 13.0 %collective-permute-start.1 = (bf16[48,256]{1,0:T(8,128)(2,1)S(1)}, bf16[48,256]{1,0:T(8,128)(2,1)S(1)}, u32[]{:S(2)}, u32[]{:S(2)}) collective-permute-start(bf16[48,256]{1,0:T(8,128)(2,1)S(1)} %get-tuple-element.21.own), channel_id=1, source_target_pairs={{1,0},{2,1},{3,2},{5,4},{6,5},{7,6},{9,8},{10,9},{11,10},{13,12},{... | collective-permute-start | bytes 73736 | tf_op jit(solution)/shard_map/ppermute | solution.py:360
  9.4 11.1 %collective-permute-start = (bf16[48,256]{1,0:T(8,128)(2,1)S(1)}, bf16[48,256]{1,0:T(8,128)(2,1)S(1)}, u32[]{:S(2)}, u32[]{:S(2)}) collective-permute-start(bf16[48,256]{1,0:T(8,128)(2,1)S(1)} %get-tuple-element.20), channel_id=1, source_target_pairs={{0,1},{1,2},{2,3},{4,5},{5,6},{6,7},{8,9},{9,10},{10,11},{12,13},{... | collective-permute-start | bytes 73736 | tf_op jit(solution)/shard_map/ppermute | solution.py:359
  21.6 8.5 %collective-permute-start.2 = (bf16[48,640]{1,0:T(8,128)(2,1)S(1)}, bf16[48,640]{1,0:T(8,128)(2,1)S(1)}, u32[]{:S(2)}, u32[]{:S(2)}) collective-permute-start(bf16[48,640]{1,0:T(8,128)(2,1)S(1)} %get-tuple-element.23), channel_id=1, source_target_pairs={{0,4},{4,8},{8,12},{1,5},{5,9},{9,13},{2,6},{6,10},{10,14},{3,7},{... | collective-permute-start | bytes 184328 | tf_op jit(solution)/shard_map/ppermute | solution.py:374
  26.4 5.5 %collective-permute-start.3 = (bf16[48,640]{1,0:T(8,128)(2,1)S(1)}, bf16[48,640]{1,0:T(8,128)(2,1)S(1)}, u32[]{:S(2)}, u32[]{:S(2)}) collective-permute-start(bf16[48,640]{1,0:T(8,128)(2,1)S(1)} %get-tuple-element.24), channel_id=1, source_target_pairs={{4,0},{8,4},{12,8},{5,1},{9,5},{13,9},{6,2},{10,6},{14,10},{7,3},{... | collective-permute-start | bytes 184328 | tf_op jit(solution)/shard_map/ppermute | solution.py:375

commit v4 on v3

v4 whole, which is shorter than its diff:
```python
import functools
import math

import jax
import jax.numpy as jnp
from jax import lax
from jax.experimental import pallas as pl
from jax.experimental.pallas import tpu as pltpu
from jax.sharding import PartitionSpec as P

BLUR_HALF = 8
BLUR_SIGMA = 4.0
HALF = 16
RIM = HALF + BLUR_HALF
STRIP = 32
CB = 176
NB = 3
MAIN = 224
EDGE_IN = 80
EDGE_OUT = 48
GROUP = 2
WIDE = 640
SLOTS = 16
F32 = jnp.float32
BF16 = jnp.bfloat16
VMEM = pl.BlockSpec(memory_space=pltpu.VMEM)
SMEM = pl.BlockSpec(memory_space=pltpu.SMEM)
HBM = pl.BlockSpec(memory_space=pltpu.HBM)
PARAMS = pltpu.CompilerParams(vmem_limit_bytes=16 * 1024 * 1024)


def dot_nt(a, b):
    return lax.dot_general(a, b, (((1,), (1,)), ((), ())), preferred_element_type=F32)


def dot_nn(a, b):
    return lax.dot_general(a, b, (((1,), (0,)), ((), ())), preferred_element_type=F32)


def eye(rows, cols, shift):
    at = lax.broadcasted_iota(jnp.int32, (rows, cols), 1) - lax.broadcasted_iota(jnp.int32, (rows, cols), 0)
    return jnp.where(at == shift, 1.0, 0.0).astype(BF16)


def sides(axis, first_swap, second_swap):
    even = lax.rem(lax.axis_index(axis), 2) == 0
    return jnp.where(even, second_swap, first_swap), jnp.where(even, first_swap, second_swap)


def prep_kernel(
    mask, ids, slots, count, across, down, to_first, to_second, edges, taps, ends, a_ids, a_slots, sems
):
    rows, cols = mask.shape
    copies = [
        pltpu.make_async_copy(mask.at[:, 0:128], ends.at[0], sems.at[0]),
        pltpu.make_async_copy(mask.at[:, cols - 128 : cols], ends.at[1], sems.at[1]),
        pltpu.make_async_copy(ids, a_ids, sems.at[2]),
        pltpu.make_async_copy(slots, a_slots, sems.at[3]),
        pltpu.make_async_copy(mask.at[0:STRIP], edges.at[0], sems.at[4]),
        pltpu.make_async_copy(mask.at[rows - STRIP : rows], edges.at[1], sems.at[5]),
        pltpu.make_async_copy(across, taps.at[0], sems.at[6]),
        pltpu.make_async_copy(down, taps.at[1], sems.at[7]),
    ]
    for copy in copies:
        copy.start()
    for copy in copies[2:4]:
        copy.wait()
    line = lax.broadcasted_iota(jnp.int32, (16, 128), 0)
    lane = lax.broadcasted_iota(jnp.int32, (16, 128), 1)

    def spread(x):
        x = x.astype(F32)
        x = jnp.concatenate([x, jnp.zeros((1, 128 - x.shape[1]), F32)], axis=1)
        return jnp.broadcast_to(x, (16, 128))

    table = jnp.where(line == 1, spread(a_slots[0]), count[0, 0].astype(F32))
    table = jnp.where(line == 0, spread(a_ids[0]), table)
    width = jnp.where(line == 2, 1, ids.shape[2])
    table = jnp.where((lane < width) & (line < 3), table, 0.0).astype(BF16)
    for strip in (to_first, to_second):
        strip[STRIP:, 0:128] = table
        strip[STRIP:, 128:] = jnp.zeros((16, rows - 128), BF16)
    even = lax.rem(lax.axis_index("col"), 2) == 0
    copies[0].wait()
    first = dot_nt(eye(STRIP, 128, 0), ends[0].astype(F32).astype(BF16))
    copies[1].wait()
    last = dot_nt(eye(STRIP, 128, 128 - STRIP), ends[1].astype(F32).astype(BF16))
    to_first[0:STRIP, :] = jnp.where(even, last, first).astype(BF16)
    to_second[0:STRIP, :] = jnp.where(even, first, last).astype(BF16)
    for copy in copies[4:]:
        copy.wait()


def mid_kernel(edges, from_first, from_second, own, to_first, to_second):
    cols = edges.shape[2]
    rows = from_first.shape[1]
    left, right = sides("col", from_first[...].astype(F32), from_second[...].astype(F32))
    tables = jnp.concatenate(
        [left[STRIP:, 0:128], own[STRIP:, 0:128].astype(F32), right[STRIP:, 0:128], jnp.zeros((16, 256), F32)],
        axis=1,
    ).astype(BF16)
    fill = jnp.zeros((128 - STRIP, 128), F32)
    strips = []
    for i in range(2):
        at = 0 if i == 0 else rows - 128
        pick = eye(STRIP, 128, 0 if i == 0 else 128 - STRIP)

        def turned(strip):
            return dot_nt(pick, jnp.concatenate([strip[0:STRIP, at : at + 128], fill], axis=0).astype(BF16))

        parts = [turned(left)[:, STRIP - RIM : STRIP], edges[i].astype(F32), turned(right)[:, 0 : WIDE - RIM - cols]]
        strips.append(jnp.concatenate(parts, axis=1))
    even = lax.rem(lax.axis_index("row"), 2) == 0
    to_first[0:STRIP, :] = jnp.where(even, strips[1], strips[0]).astype(BF16)
    to_second[0:STRIP, :] = jnp.where(even, strips[0], strips[1]).astype(BF16)
    to_first[STRIP:, :] = tables
    to_second[STRIP:, :] = tables


def window_kernel(mask, from_first, from_second, taps, windows, ahead, back):
    rows, cols = mask.shape
    fill = jnp.zeros((128 - STRIP, rows), F32)
    left, right = sides("col", from_first[0:STRIP, :].astype(F32), from_second[0:STRIP, :].astype(F32))
    lhs = jnp.concatenate([left, fill], axis=0).T
    rhs = jnp.concatenate([right, fill], axis=0).T
    full = jnp.concatenate(
        [lhs[:, STRIP - RIM : STRIP], mask[...].astype(F32), rhs[:, 0 : WIDE - RIM - cols]], axis=1
    )
    for b in range(NB):
        windows[b] = full[:, CB * b : CB * b + 256]
    kernels, _, count = taps.shape[1:]
    flip = lax.broadcasted_iota(jnp.int32, (128, 128), 0) + lax.broadcasted_iota(jnp.int32, (128, 128), 1)
    flip = jnp.where(flip % 128 == 0, 1.0, 0.0).astype(BF16)
    ahead[...] = jnp.zeros(ahead.shape, F32)
    back[...] = jnp.zeros(back.shape, F32)
    for k in range(kernels):
        ahead[k, 0:2, 0:count] = taps[0, k].astype(F32)
        back[k, 0:2, 0:count] = taps[1, k].astype(F32)
    back[...] = dot_nn(back[...].reshape(kernels * 8, 128).astype(BF16), flip).reshape(kernels, 8, 128)


def socs_kernel(
    entries,
    per,
    weights,
    windows,
    row_first,
    row_second,
    col_first,
    col_second,
    own,
    ahead,
    back,
    acc,
    images,
    x_win,
    scale,
    sem,
    *scratch,
):
    across = scratch[0:2]
    down = scratch[2:4]
    first = scratch[4:6]
    groups = ahead.shape[0] // GROUP
    fetch = pltpu.make_async_copy(weights, scale, sem)
    fetch.start()
    above, below = sides("row", row_first[...].astype(F32), row_second[...].astype(F32))
    left, right = sides("col", col_first[STRIP:, 0:128].astype(F32), col_second[STRIP:, 0:128].astype(F32))
    upper_rows = above[STRIP - RIM : STRIP]
    lower_rows = below[0:RIM]
    edge_rows = []
    for b in range(NB):
        lanes = slice(CB * b, CB * b + 256)
        part = windows[b]
        x_win[b] = jnp.concatenate([upper_rows[:, lanes], part[0 : 256 - RIM]], axis=0).astype(BF16)
        edge_rows += [part[MAIN - RIM :], lower_rows[:, lanes]]
    edge_rows.append(jnp.zeros((256 - NB * EDGE_IN, 256), F32))
    x_win[NB] = jnp.concatenate(edge_rows, axis=0).astype(BF16)
    acc[...] = jnp.zeros(acc.shape, F32)
    for ref in across + down:
        ref[...] = jnp.zeros(ref.shape, BF16)

    slot = lax.broadcasted_iota(jnp.int32, (SLOTS, 128), 0).astype(F32)
    lane = lax.broadcasted_iota(jnp.int32, (SLOTS, 128), 1)
    found = jnp.zeros((SLOTS, 128), F32)
    col = lax.axis_index("col")
    tables = [above[STRIP:, 128 * t : 128 * t + 128] for t in range(3)]
    tables += [left, own[STRIP:, 0:128].astype(F32), right]
    tables += [below[STRIP:, 128 * t : 128 * t + 128] for t in range(3)]
    for t, table in enumerate(tables):
        live = lane.astype(F32) < table[2:3, 0:1]
        hit = live & (table[1:2] == slot) & (lane < entries)
        image = jnp.sum(jnp.where(hit, table[0:1] + 1.0, 0.0), axis=1, keepdims=True)
        found = jnp.where(lane == t, image, found)
    cell = found.astype(jnp.int32) - 1
    images[...] = jnp.where(cell >= 0, ((cell // per) ^ col) * per + cell % per + 1, 0)

    row = lax.broadcasted_iota(jnp.int32, (32, 128), 0)
    lane = lax.broadcasted_iota(jnp.int32, (32, 128), 1)
    low = lane >= row + 96

    def cycled(x):
        return pltpu.roll(jnp.broadcast_to(x, (128, 128)), 0, 1, stride=1, stride_axis=0)

    def build_across(m, s):
        for q in range(2 * GROUP):
            cyc = cycled(ahead[GROUP * m + q // 2, q % 2 : q % 2 + 1, :])
            head = cyc[0:96].astype(BF16)
            tail = cyc[96:128]
            over = jnp.where(low, 0.0, tail)
            across[s][q, 0:96, 0:128] = head
            across[s][q, 128:CB, 128:256] = head[0 : CB - 128]
            across[s][q, 96:128, 0:128] = jnp.where(low, tail, 0.0).astype(BF16)
            across[s][q, 96:128, 128:256] = over.astype(BF16)

    def build_down(m, s):
        for q in range(2 * GROUP):
            cyc = cycled(back[GROUP * m + q // 2, q % 2 : q % 2 + 1, :])
            head = cyc[0:32]
            over = jnp.where(low, head, 0.0).astype(BF16)
            head = jnp.where(low, 0.0, head)
            same = jnp.concatenate([head, cyc[32:128]], axis=0).astype(BF16)
            down[s][q, 0:128, 0:128] = same
            down[s][q, 128:256, 128:256] = same
            down[s][q, 128:160, 0:128] = over

    def pass_one(s):
        taps = across[s][...].reshape(2 * GROUP * CB, 256)
        for j in range(NB + 1):
            part = dot_nt(taps, x_win[j]).astype(BF16)
            for q in range(2 * GROUP):
                first[s][q, j] = part[q * CB : (q + 1) * CB]

    def pass_two(m, s):
        for g in range(GROUP):
            total = None
            for q in (2 * g, 2 * g + 1):
                second = dot_nn(first[s][q].reshape((NB + 1) * CB, 256), down[s][q])
                total = second * second if total is None else total + second * second
            acc[...] += (scale[GROUP * m + g] * total).reshape(acc.shape)

    def stage(m, s):
        pass_one(s)
        build_down(m, s)
        build_across(jnp.minimum(m + 1, groups - 1), 1 - s)
        pass_two(m - 1, 1 - s)

    build_across(0, 0)
    pass_one(0)
    build_down(0, 0)
    build_across(1, 1)
    fetch.wait()

    def step(i, carry):
        stage(2 * i + 1, 1)
        stage(2 * i + 2, 0)
        return carry

    lax.fori_loop(0, groups // 2 - 1, step, 0)
    stage(groups - 1, 1)
    pass_two(groups - 1, 1)


def blur_matrix(shape, axis):
    lag = lax.broadcasted_iota(jnp.int32, shape, axis) - lax.broadcasted_iota(jnp.int32, shape, 1 - axis)
    total = sum(math.exp(-(t * t) / (2 * BLUR_SIGMA**2)) for t in range(-BLUR_HALF, BLUR_HALF + 1))
    off = (lag - BLUR_HALF).astype(F32)
    g = jnp.exp(-off * off / (2.0 * BLUR_SIGMA * BLUR_SIGMA)) * (1.0 / total)
    g = jnp.where((lag >= 0) & (lag <= 2 * BLUR_HALF), g, 0.0)
    high = g.astype(BF16)
    return high, (g - high.astype(F32)).astype(BF16)


def final_kernel(n_row, n_col, acc, images, *rest):
    shards = rest[:-7]
    out, cells, table, placed, flat, blurred, sem = rest[-7:]
    per = shards[0].shape[0]
    rows, cols = out.shape
    row, col = lax.axis_index("row"), lax.axis_index("col")
    fetch = pltpu.make_async_copy(images, table, sem)
    fetch.start()
    for i, shard in enumerate(shards):
        cells[pl.ds(i * per, per)] = shard[...]

    at_row = lax.broadcasted_iota(jnp.int32, (8, 384), 1) - BLUR_HALF
    row_ok = ((row > 0) | (at_row >= 0)) & ((row < n_row - 1) | (at_row < rows))
    row_ok = jnp.where(row_ok, 1.0, 0.0)
    for b in range(NB):
        edge = acc[NB, :, EDGE_IN * b : EDGE_IN * b + EDGE_OUT]
        part = jnp.concatenate(
            [acc[b, :, 0:MAIN], edge, jnp.zeros((CB, 384 - MAIN - EDGE_OUT), F32)], axis=1
        )
        part = part * row_ok[0:1]
        if b == 0:
            part = jnp.concatenate([jnp.where(col > 0, part[0:8], 0.0), part[8:]], axis=0)
        if b == NB - 1:
            part = jnp.concatenate([part[0 : CB - 8], jnp.where(col < n_col - 1, part[CB - 8 :], 0.0)], axis=0)
        flat[b * CB : (b + 1) * CB, :] = part.astype(BF16)
    flat[NB * CB :, :] = jnp.zeros((flat.shape[0] - NB * CB, 384), BF16)

    fetch.wait()
    slot_rows, slot_cols = rows // 64, cols // 128
    for i in range(-1, slot_rows + 1):
        for j in range(-1, slot_cols + 1):
            ti = 0 if i < 0 else (2 if i == slot_rows else 1)
            tj = 0 if j < 0 else (2 if j == slot_cols else 1)
            found = table[(i % slot_rows) * slot_cols + j % slot_cols, 3 * ti + tj]
            image = jnp.maximum(found - 1, 0)
            lanes = slice(128 + 128 * j, 256 + 128 * j)
            show = lambda x: jnp.where(found > 0, x.astype(F32), 0.0)
            if i < 0:
                placed[0:8, lanes] = show(cells[image, 48:64, :])[8:16]
            elif i == slot_rows:
                placed[8 + rows : 16 + rows, lanes] = show(cells[image, 0:16, :])[0:8]
            else:
                placed[8 + 64 * i : 72 + 64 * i, lanes] = show(cells[image])
    placed[16 + rows :, :] = jnp.zeros((placed.shape[0] - 16 - rows, placed.shape[1]), F32)

    g_high, g_low = blur_matrix((128, 256), 1)
    g_both = jnp.concatenate([g_high, g_low], axis=0)
    for i in range(rows // 128):
        part = dot_nt(g_both, flat[:, 128 * i : 128 * i + 256])
        cell = dot_nn(g_both, placed[128 * i : 128 * i + 256, :].astype(BF16))
        part = part[0:128] + part[128:]
        cell = cell[0:128] + cell[128:]
        part += cell[:, 128 - BLUR_HALF : 128 - BLUR_HALF + part.shape[1]]
        high = part.astype(BF16)
        blurred[0, 128 * i : 128 * i + 128, :] = high
        blurred[1, 128 * i : 128 * i + 128, :] = (part - high.astype(F32)).astype(BF16)
    g_high, g_low = blur_matrix((256, 128), 0)
    g_both = jnp.concatenate([g_high, g_low], axis=1)
    for j in range(cols // 128):
        lanes = slice(128 * j, 128 * j + 256)
        part = dot_nn(blurred[0, :, lanes], g_both)
        out[:, 128 * j : 128 * j + 128] = (
            part[:, 0:128] + part[:, 128:] + dot_nn(blurred[1, :, lanes], g_high)
        )


def shape(dims, dtype):
    return jax.ShapeDtypeStruct(dims, dtype)


def on_device(
    mask_pixels, across_taps, down_taps, kernel_weights, library, cell_ids, cell_slots, cell_count
):
    rows, cols = mask_pixels.shape
    kernels = across_taps.shape[0]
    entries = cell_ids.shape[-1]
    per = library.shape[0]
    n_row, n_col = lax.axis_size("row"), lax.axis_size("col")
    in_hbm = lambda x: pltpu.with_memory_space_constraint(x, pltpu.HBM)
    mask_hbm = in_hbm(mask_pixels)

    to_first, to_second, edges, taps = pl.pallas_call(
        prep_kernel,
        out_shape=(
            shape((STRIP + 16, rows), BF16),
            shape((STRIP + 16, rows), BF16),
            shape((2, STRIP, cols), jnp.int32),
            shape((2,) + across_taps.shape, BF16),
        ),
        in_specs=[HBM] * 3 + [SMEM] + [HBM] * 2,
        out_specs=(VMEM,) * 4,
        scratch_shapes=[
            pltpu.VMEM((2, rows, 128), jnp.int32),
            pltpu.VMEM(cell_ids.shape, jnp.int32),
            pltpu.VMEM(cell_slots.shape, jnp.int32),
            pltpu.SemaphoreType.DMA((8,)),
        ],
        compiler_params=PARAMS,
        name="prep",
    )(mask_hbm, in_hbm(cell_ids), in_hbm(cell_slots), cell_count, in_hbm(across_taps), in_hbm(down_taps))
    library, to_first, to_second = lax.optimization_barrier((library, to_first, to_second))

    def swaps(n):
        rounds = []
        for start in (0, 1):
            pairs = [(i, i + 1) for i in range(start, n - 1, 2)]
            rounds.append(pairs + [(b, a) for a, b in pairs])
        return rounds

    col_first, col_second = (
        lax.ppermute(x, "col", pairs) for x, pairs in zip((to_first, to_second), swaps(n_col))
    )
    shards = [library]
    for d in range(1, n_col):
        shards.append(lax.ppermute(library, "col", [(i, i ^ d) for i in range(n_col)]))

    to_above, to_below = pl.pallas_call(
        mid_kernel,
        out_shape=(shape((STRIP + 16, WIDE), BF16),) * 2,
        in_specs=[VMEM] * 4,
        out_specs=(VMEM,) * 2,
        compiler_params=PARAMS,
        name="mid",
    )(edges, col_first, col_second, to_first)
    row_first, row_second = (
        lax.ppermute(x, "row", pairs) for x, pairs in zip((to_above, to_below), swaps(n_row))
    )

    windows, ahead, back = pl.pallas_call(
        window_kernel,
        out_shape=(
            shape((NB, rows, 256), F32),
            shape((kernels, 8, 128), F32),
            shape((kernels, 8, 128), F32),
        ),
        in_specs=[VMEM] * 4,
        out_specs=(VMEM,) * 3,
        compiler_params=PARAMS,
        cost_estimate=pl.CostEstimate(flops=10**6, bytes_accessed=10**6, transcendentals=0),
        name="window",
    )(mask_pixels, col_first, col_second, taps)

    acc, images = pl.pallas_call(
        functools.partial(socs_kernel, entries, per),
        out_shape=(shape((NB + 1, CB, 256), F32), shape((SLOTS, 128), jnp.int32)),
        in_specs=[HBM] + [VMEM] * 8,
        out_specs=(VMEM,) * 2,
        scratch_shapes=[
            pltpu.VMEM((NB + 1, 256, 256), BF16),
            pltpu.SMEM(kernel_weights.shape, F32),
            pltpu.SemaphoreType.DMA,
        ]
        + [pltpu.VMEM((2 * GROUP, CB, 256), BF16)] * 2
        + [pltpu.VMEM((2 * GROUP, 256, 256), BF16)] * 2
        + [pltpu.VMEM((2 * GROUP, NB + 1, CB, 256), BF16)] * 2,
        compiler_params=PARAMS,
        cost_estimate=pl.CostEstimate(flops=5 * 10**9, bytes_accessed=8 * 10**6, transcendentals=0),
        name="socs",
    )(in_hbm(kernel_weights), windows, row_first, row_second, col_first, col_second, to_first, ahead, back)

    return pl.pallas_call(
        functools.partial(final_kernel, n_row, n_col),
        out_shape=shape((rows, cols), F32),
        in_specs=[VMEM] * (2 + n_col),
        out_specs=VMEM,
        scratch_shapes=[
            pltpu.VMEM((n_col * per,) + library.shape[1:], BF16),
            pltpu.SMEM((SLOTS, 128), jnp.int32),
            pltpu.VMEM((384, cols + 256), F32),
            pltpu.VMEM((WIDE, 384), BF16),
            pltpu.VMEM((2, rows, WIDE), BF16),
            pltpu.SemaphoreType.DMA,
        ],
        compiler_params=PARAMS,
        name="final",
    )(acc, images, *shards)


def solution(mesh):
    placed = (
        P(("frames", "row"), "col"),
        P(),
        P(),
        P(),
        P("col", None, None),
        P(("frames", "row"), "col", None),
        P(("frames", "row"), "col", None),
        P(("frames", "row"), "col"),
    )
    return jax.shard_map(
        on_device,
        mesh=mesh,
        in_specs=placed,
        out_specs=P(("frames", "row"), "col"),
        check_vma=False,
    )
```

time: 41.4 us -> 29.4 us (0.71)
  the two profiles are of different devices: /device:TPU:9 before, /device:TPU:1 now
where the time goes in v4:
time: 29.4 us; the launch traced here: 29.2 us
  starting transfers between devices  14.9 us (51%)
  Pallas kernels  11 us (37%)
  waiting for transfers between devices  2.55 us (9%)
  between operations  0.8 us (3%)
    ppermute x3, starting transfers between devices, on_device(): lax.ppermute(library, 'col', [(i, i ^ d) for i in range(n_col)])  7.01 us
    pallas_call x1, Pallas kernels, on_device(): pl.pallas_call(functools.partial(socs_kernel, entries, per), out_shape=(s...  6.35 us
    ppermute x2, starting transfers between devices, on_device(): lax.ppermute(x, 'row', pairs)  5.07 us
    ppermute x2, starting transfers between devices, on_device(): lax.ppermute(x, 'col', pairs)  2.84 us
    pallas_call x1, Pallas kernels, on_device(): pl.pallas_call(functools.partial(final_kernel, n_row, n_col), out_shape=s...  2.54 us
    ppermute x3, waiting for transfers between devices, on_device(): lax.ppermute(library, 'col', [(i, i ^ d) for i in range(n_col)])  1.99 us
    pallas_call x1, Pallas kernels, on_device(): pl.pallas_call(prep_kernel, out_shape=(shape((STRIP + 16, rows), BF16), s...  1.3 us
  transfers between devices with their start and end apart: 7, of which 2 were waited for; matrix products, arithmetic and copies ran while one was open for 0% of the time, Pallas kernels for 24%

profile of v4, /device:TPU:1, one launch (start us, length us, event | category | flops | bytes accessed | tf_op | source)
XLA Modules:
  0.0 29.2 jit_solution(4108087500104839419)
XLA Ops:
  0.0 0.0 copy-start
  0.7 1.3 %prep.1 = (bf16[48,256]{1,0:T(8,128)(2,1)S(1)}, bf16[48,256]{1,0:T(8,128)(2,1)S(1)}, s32[2,32,512]{2,1,0:T(8,128)S(1)}, bf16[2,12,2,33]{3,2,1,0:T(2,128)(2,1)S(1)}) custom-call(s32[256,512]{1,0:T(8,128)} %mask.3, s32[1,1,8]{2,1,0:T(1,128)} %ids.1, s32[1,1,8]{2,1,0:T(1,128)} %slots.1, s32[1,1]{1,0:T(1,128)S(6)} %copy.9.count, bf16[12,2,33]{2,1,0:T(2,128)(2,1)} %across.1, ...), custom_call_target="tpu_custom_call" | custom-call | tf_op jit(solution)/shard_map/prep/pallas_call | solution.py:355
  2.0 0.0 copy-start.1
  2.0 2.2 %collective-permute-start = (bf16[48,256]{1,0:T(8,128)(2,1)S(1)}, bf16[48,256]{1,0:T(8,128)(2,1)S(1)}, u32[]{:S(2)}, u32[]{:S(2)}) collective-permute-start(bf16[48,256]{1,0:T(8,128)(2,1)S(1)} %get-tuple-element.21.own), channel_id=1, source_target_pairs={{0,1},{2,3},{1,0},{3,2},{4,5},{6,7},{5,4},{7,6},{8,9},{10,11},{9,8... | collective-permute-start | bytes 73736 | tf_op jit(solution)/shard_map/ppermute | solution.py:384
  4.2 0.7 %collective-permute-start.1 = (bf16[48,256]{1,0:T(8,128)(2,1)S(1)}, bf16[48,256]{1,0:T(8,128)(2,1)S(1)}, u32[]{:S(2)}, u32[]{:S(2)}) collective-permute-start(bf16[48,256]{1,0:T(8,128)(2,1)S(1)} %get-tuple-element.22), channel_id=1, source_target_pairs={{1,2},{2,1},{5,6},{6,5},{9,10},{10,9},{13,14},{14,13},{17,18},{18,... | collective-permute-start | bytes 73736 | tf_op jit(solution)/shard_map/ppermute | solution.py:384
  4.9 0.6 %collective-permute-done.from_first.col_first = bf16[48,256]{1,0:T(8,128)(2,1)S(1)} collective-permute-done((bf16[48,256]{1,0:T(8,128)(2,1)S(1)}, bf16[48,256]{1,0:T(8,128)(2,1)S(1)}, u32[]{:S(2)}, u32[]{:S(2)}) %collective-permute-start) | collective-permute-done | bytes 24608 | tf_op jit(solution)/shard_map/ppermute | solution.py:384
  5.4 0.0 collective-permute-done.1.from_second.col_second
  5.4 0.2 mid.1
  5.7 1.6 %collective-permute-start.2 = (bf16[48,640]{1,0:T(8,128)(2,1)S(1)}, bf16[48,640]{1,0:T(8,128)(2,1)S(1)}, u32[]{:S(2)}, u32[]{:S(2)}) collective-permute-start(bf16[48,640]{1,0:T(8,128)(2,1)S(1)} %get-tuple-element.26), channel_id=1, source_target_pairs={{0,4},{8,12},{4,0},{12,8},{1,5},{9,13},{5,1},{13,9},{2,6},{10,14},... | collective-permute-start | bytes 184328 | tf_op jit(solution)/shard_map/ppermute | solution.py:399
  7.3 3.5 %collective-permute-start.3 = (bf16[48,640]{1,0:T(8,128)(2,1)S(1)}, bf16[48,640]{1,0:T(8,128)(2,1)S(1)}, u32[]{:S(2)}, u32[]{:S(2)}) collective-permute-start(bf16[48,640]{1,0:T(8,128)(2,1)S(1)} %get-tuple-element.27), channel_id=1, source_target_pairs={{4,8},{8,4},{5,9},{9,5},{6,10},{10,6},{7,11},{11,7},{20,24},{24,20... | collective-permute-start | bytes 184328 | tf_op jit(solution)/shard_map/ppermute | solution.py:399
  10.8 0.0 copy-done.1
  10.8 4.4 %collective-permute-start.4 = (bf16[8,64,128]{2,1,0:T(8,128)(2,1)S(1)}, bf16[8,64,128]{2,1,0:T(8,128)(2,1)S(1)}, u32[]{:S(2)}, u32[]{:S(2)}) collective-permute-start(bf16[8,64,128]{2,1,0:T(8,128)(2,1)S(1)} %copy-done.1), channel_id=1, source_target_pairs={{0,1},{1,0},{2,3},{3,2},{4,5},{5,4},{6,7},{7,6},{8,9},{9,8},{10,11... | collective-permute-start | bytes 393224 | tf_op jit(solution)/shard_map/ppermute | solution.py:388
  15.1 1.5 %collective-permute-start.5 = (bf16[8,64,128]{2,1,0:T(8,128)(2,1)S(1)}, bf16[8,64,128]{2,1,0:T(8,128)(2,1)S(1)}, u32[]{:S(2)}, u32[]{:S(2)}) collective-permute-start(bf16[8,64,128]{2,1,0:T(8,128)(2,1)S(1)} %copy-done.1), channel_id=1, source_target_pairs={{0,2},{1,3},{2,0},{3,1},{4,6},{5,7},{6,4},{7,5},{8,10},{9,11},{10,... | collective-permute-start | bytes 393224 | tf_op jit(solution)/shard_map/ppermute | solution.py:388
  16.7 1.1 %collective-permute-start.6 = (bf16[8,64,128]{2,1,0:T(8,128)(2,1)S(1)}, bf16[8,64,128]{2,1,0:T(8,128)(2,1)S(1)}, u32[]{:S(2)}, u32[]{:S(2)}) collective-permute-start(bf16[8,64,128]{2,1,0:T(8,128)(2,1)S(1)} %copy-done.1), channel_id=1, source_target_pairs={{0,3},{1,2},{2,1},{3,0},{4,7},{5,6},{6,5},{7,4},{8,11},{9,10},{10,... | collective-permute-start | bytes 393224 | tf_op jit(solution)/shard_map/ppermute | solution.py:388
  17.8 0.0 copy-done
  17.8 0.5 %window.1 = (f32[3,256,256]{2,1,0:T(8,128)S(1)}, f32[12,8,128]{2,1,0:T(8,128)S(1)}, f32[12,8,128]{2,1,0:T(8,128)S(1)}) custom-call(s32[256,512]{1,0:T(8,128)S(1)} %copy-done, bf16[48,256]{1,0:T(8,128)(2,1)S(1)} %collective-permute-done.from_first.col_first, bf16[48,256]{1,0:T(8,128)(2,1)S(1)} %collective-permute-done.1.from_second.col_second, ...), custom_call_target="tpu_custom_call" | custom-call | flops 1000000 | bytes 1000000 | tf_op jit(solution)/shard_map/window/pallas_call | solution.py:402
  18.3 0.0 collective-permute-done.2.row_first
  18.3 0.0 collective-permute-done.3.row_second
  18.3 6.4 %socs.1 = (f32[4,176,256]{2,1,0:T(8,128)S(1)}, s32[16,128]{1,0:T(8,128)S(1)}) custom-call(f32[12]{0:T(128)} %weights.1, f32[3,256,256]{2,1,0:T(8,128)S(1)} %get-tuple-element.24.windows, bf16[48,640]{1,0:T(8,128)(2,1)S(1)} %collective-permute-done.2.row_first, bf16[48,640]{1,0:T(8,128)(2,1)S(1)} %collective-permute-done.3.row_second, ...), custom_call_target="tpu_custom_call" | custom-call | flops 5000000000 | bytes 8000000 | tf_op jit(solution)/shard_map/socs/pallas_call | solution.py:416
  24.7 0.0 collective-permute-done.4.rest_1_
  24.7 2.0 %collective-permute-done.5.rest_2_ = bf16[8,64,128]{2,1,0:T(8,128)(2,1)S(1)} collective-permute-done((bf16[8,64,128]{2,1,0:T(8,128)(2,1)S(1)}, bf16[8,64,128]{2,1,0:T(8,128)(2,1)S(1)}, u32[]{:S(2)}, u32[]{:S(2)}) %collective-permute-start.5) | collective-permute-done | bytes 131104 | tf_op jit(solution)/shard_map/ppermute | solution.py:388
  26.7 0.0 collective-permute-done.6.rest_3_
  26.7 2.5 %final.1 = f32[256,512]{1,0:T(8,128)} custom-call(f32[4,176,256]{2,1,0:T(8,128)S(1)} %get-tuple-element.30.acc, s32[16,128]{1,0:T(8,128)S(1)} %get-tuple-element.31.images, bf16[8,64,128]{2,1,0:T(8,128)(2,1)S(1)} %copy-done.1, bf16[8,64,128]{2,1,0:T(8,128)(2,1)S(1)} %collective-permute-done.4.rest_1_, ...), custom_call_target="tpu_custom_call" | custom-call | tf_op jit(solution)/shard_map/final/pallas_call | solution.py:434
Async XLA Ops:
  0.0 17.8 %copy-start = (s32[256,512]{1,0:T(8,128)S(1)}, s32[256,512]{1,0:T(8,128)}, u32[]{:S(2)}) copy-start(s32[256,512]{1,0:T(8,128)} %mask.3) | copy-start | bytes 1572868
  2.0 8.7 %copy-start.1 = (bf16[8,64,128]{2,1,0:T(8,128)(2,1)S(1)}, bf16[8,64,128]{2,1,0:T(8,128)(2,1)}, u32[]{:S(2)}) copy-start(bf16[8,64,128]{2,1,0:T(8,128)(2,1)} %rest_0_) | copy-start | bytes 393220
  2.0 3.4 %collective-permute-start = (bf16[48,256]{1,0:T(8,128)(2,1)S(1)}, bf16[48,256]{1,0:T(8,128)(2,1)S(1)}, u32[]{:S(2)}, u32[]{:S(2)}) collective-permute-start(bf16[48,256]{1,0:T(8,128)(2,1)S(1)} %get-tuple-element.21.own), channel_id=1, source_target_pairs={{0,1},{2,3},{1,0},{3,2},{4,5},{6,7},{5,4},{7,6},{8,9},{10,11},{9,8... | collective-permute-start | bytes 73736 | tf_op jit(solution)/shard_map/ppermute | solution.py:384
  4.2 1.2 %collective-permute-start.1 = (bf16[48,256]{1,0:T(8,128)(2,1)S(1)}, bf16[48,256]{1,0:T(8,128)(2,1)S(1)}, u32[]{:S(2)}, u32[]{:S(2)}) collective-permute-start(bf16[48,256]{1,0:T(8,128)(2,1)S(1)} %get-tuple-element.22), channel_id=1, source_target_pairs={{1,2},{2,1},{5,6},{6,5},{9,10},{10,9},{13,14},{14,13},{17,18},{18,... | collective-permute-start | bytes 73736 | tf_op jit(solution)/shard_map/ppermute | solution.py:384
  5.7 12.7 %collective-permute-start.2 = (bf16[48,640]{1,0:T(8,128)(2,1)S(1)}, bf16[48,640]{1,0:T(8,128)(2,1)S(1)}, u32[]{:S(2)}, u32[]{:S(2)}) collective-permute-start(bf16[48,640]{1,0:T(8,128)(2,1)S(1)} %get-tuple-element.26), channel_id=1, source_target_pairs={{0,4},{8,12},{4,0},{12,8},{1,5},{9,13},{5,1},{13,9},{2,6},{10,14},... | collective-permute-start | bytes 184328 | tf_op jit(solution)/shard_map/ppermute | solution.py:399
  7.3 11.1 %collective-permute-start.3 = (bf16[48,640]{1,0:T(8,128)(2,1)S(1)}, bf16[48,640]{1,0:T(8,128)(2,1)S(1)}, u32[]{:S(2)}, u32[]{:S(2)}) collective-permute-start(bf16[48,640]{1,0:T(8,128)(2,1)S(1)} %get-tuple-element.27), channel_id=1, source_target_pairs={{4,8},{8,4},{5,9},{9,5},{6,10},{10,6},{7,11},{11,7},{20,24},{24,20... | collective-permute-start | bytes 184328 | tf_op jit(solution)/shard_map/ppermute | solution.py:399
  10.8 13.9 %collective-permute-start.4 = (bf16[8,64,128]{2,1,0:T(8,128)(2,1)S(1)}, bf16[8,64,128]{2,1,0:T(8,128)(2,1)S(1)}, u32[]{:S(2)}, u32[]{:S(2)}) collective-permute-start(bf16[8,64,128]{2,1,0:T(8,128)(2,1)S(1)} %copy-done.1), channel_id=1, source_target_pairs={{0,1},{1,0},{2,3},{3,2},{4,5},{5,4},{6,7},{7,6},{8,9},{9,8},{10,11... | collective-permute-start | bytes 393224 | tf_op jit(solution)/shard_map/ppermute | solution.py:388
  15.1 11.6 %collective-permute-start.5 = (bf16[8,64,128]{2,1,0:T(8,128)(2,1)S(1)}, bf16[8,64,128]{2,1,0:T(8,128)(2,1)S(1)}, u32[]{:S(2)}, u32[]{:S(2)}) collective-permute-start(bf16[8,64,128]{2,1,0:T(8,128)(2,1)S(1)} %copy-done.1), channel_id=1, source_target_pairs={{0,2},{1,3},{2,0},{3,1},{4,6},{5,7},{6,4},{7,5},{8,10},{9,11},{10,... | collective-permute-start | bytes 393224 | tf_op jit(solution)/shard_map/ppermute | solution.py:388
  16.7 10.0 %collective-permute-start.6 = (bf16[8,64,128]{2,1,0:T(8,128)(2,1)S(1)}, bf16[8,64,128]{2,1,0:T(8,128)(2,1)S(1)}, u32[]{:S(2)}, u32[]{:S(2)}) collective-permute-start(bf16[8,64,128]{2,1,0:T(8,128)(2,1)S(1)} %copy-done.1), channel_id=1, source_target_pairs={{0,3},{1,2},{2,1},{3,0},{4,7},{5,6},{6,5},{7,4},{8,11},{9,10},{10,... | collective-permute-start | bytes 393224 | tf_op jit(solution)/shard_map/ppermute | solution.py:388

commit v5 on v4

--- a/solution.py
+++ b/solution.py
@@ -18,6 +18,7 @@
 MAIN = 224
 EDGE_IN = 80
 EDGE_OUT = 48
+RIGHT_AT = 56
 GROUP = 2
 WIDE = 640
 SLOTS = 16
@@ -117,14 +118,20 @@
     to_second[STRIP:, :] = tables
 
 
-def window_kernel(mask, from_first, from_second, taps, windows, ahead, back):
+def blur_matrix(shape, axis):
+    lag = lax.broadcasted_iota(jnp.int32, shape, axis) - lax.broadcasted_iota(jnp.int32, shape, 1 - axis)
+    total = sum(math.exp(-(t * t) / (2 * BLUR_SIGMA**2)) for t in range(-BLUR_HALF, BLUR_HALF + 1))
+    off = (lag - BLUR_HALF).astype(F32)
+    g = jnp.exp(-off * off / (2.0 * BLUR_SIGMA * BLUR_SIGMA)) * (1.0 / total)
+    g = jnp.where((lag >= 0) & (lag <= 2 * BLUR_HALF), g, 0.0)
+    high = g.astype(BF16)
+    return high, (g - high.astype(F32)).astype(BF16)
+
+
+def own_kernel(mask, taps, windows, ahead, back, g_row, g_col):
     rows, cols = mask.shape
-    fill = jnp.zeros((128 - STRIP, rows), F32)
-    left, right = sides("col", from_first[0:STRIP, :].astype(F32), from_second[0:STRIP, :].astype(F32))
-    lhs = jnp.concatenate([left, fill], axis=0).T
-    rhs = jnp.concatenate([right, fill], axis=0).T
     full = jnp.concatenate(
-        [lhs[:, STRIP - RIM : STRIP], mask[...].astype(F32), rhs[:, 0 : WIDE - RIM - cols]], axis=1
+        [jnp.zeros((rows, RIM), F32), mask[...].astype(F32), jnp.zeros((rows, WIDE - RIM - cols), F32)], axis=1
     )
     for b in range(NB):
         windows[b] = full[:, CB * b : CB * b + 256]
@@ -137,6 +144,8 @@
         ahead[k, 0:2, 0:count] = taps[0, k].astype(F32)
         back[k, 0:2, 0:count] = taps[1, k].astype(F32)
     back[...] = dot_nn(back[...].reshape(kernels * 8, 128).astype(BF16), flip).reshape(kernels, 8, 128)
+    g_row[0:128], g_row[128:256] = blur_matrix((128, 256), 1)
+    g_col[:, 0:128], g_col[:, 128:256] = blur_matrix((256, 128), 0)
 
 
 def socs_kernel(
@@ -165,13 +174,29 @@
     fetch = pltpu.make_async_copy(weights, scale, sem)
     fetch.start()
     above, below = sides("row", row_first[...].astype(F32), row_second[...].astype(F32))
-    left, right = sides("col", col_first[STRIP:, 0:128].astype(F32), col_second[STRIP:, 0:128].astype(F32))
+    left, right = sides("col", col_first[...].astype(F32), col_second[...].astype(F32))
+    rows = windows.shape[1]
+    turned = jnp.concatenate(
+        [
+            left[STRIP - RIM : STRIP],
+            jnp.zeros((128 - RIM + RIGHT_AT, rows), F32),
+            right[0:RIM],
+            jnp.zeros((128 - RIM - RIGHT_AT, rows), F32),
+        ],
+        axis=0,
+    )
+    turned = dot_nt(eye(rows, rows, 0), turned.astype(BF16))
+    left, right = left[STRIP:, 0:128], right[STRIP:, 0:128]
     upper_rows = above[STRIP - RIM : STRIP]
     lower_rows = below[0:RIM]
     edge_rows = []
     for b in range(NB):
         lanes = slice(CB * b, CB * b + 256)
         part = windows[b]
+        if b == 0:
+            part = jnp.concatenate([part[:, 0:128] + turned[:, 0:128], part[:, 128:256]], axis=1)
+        if b == NB - 1:
+            part = jnp.concatenate([part[:, 0:128], part[:, 128:256] + turned[:, 128:256]], axis=1)
         x_win[b] = jnp.concatenate([upper_rows[:, lanes], part[0 : 256 - RIM]], axis=0).astype(BF16)
         edge_rows += [part[MAIN - RIM :], lower_rows[:, lanes]]
     edge_rows.append(jnp.zeros((256 - NB * EDGE_IN, 256), F32))
@@ -232,12 +257,9 @@
                 first[s][q, j] = part[q * CB : (q + 1) * CB]
 
     def pass_two(m, s):
-        for g in range(GROUP):
-            total = None
-            for q in (2 * g, 2 * g + 1):
-                second = dot_nn(first[s][q].reshape((NB + 1) * CB, 256), down[s][q])
-                total = second * second if total is None else total + second * second
-            acc[...] += (scale[GROUP * m + g] * total).reshape(acc.shape)
+        for q in range(2 * GROUP):
+            second = dot_nn(first[s][q].reshape((NB + 1) * CB, 256), down[s][q])
+            acc[...] += (scale[GROUP * m + q // 2] * (second * second)).reshape(acc.shape)
 
     def stage(m, s):
         pass_one(s)
@@ -261,19 +283,10 @@
     pass_two(groups - 1, 1)
 
 
-def blur_matrix(shape, axis):
-    lag = lax.broadcasted_iota(jnp.int32, shape, axis) - lax.broadcasted_iota(jnp.int32, shape, 1 - axis)
-    total = sum(math.exp(-(t * t) / (2 * BLUR_SIGMA**2)) for t in range(-BLUR_HALF, BLUR_HALF + 1))
-    off = (lag - BLUR_HALF).astype(F32)
-    g = jnp.exp(-off * off / (2.0 * BLUR_SIGMA * BLUR_SIGMA)) * (1.0 / total)
-    g = jnp.where((lag >= 0) & (lag <= 2 * BLUR_HALF), g, 0.0)
-    high = g.astype(BF16)
-    return high, (g - high.astype(F32)).astype(BF16)
-
-
-def final_kernel(n_row, n_col, acc, images, *rest):
+def final_kernel(n_row, n_col, acc, images, g_row, g_col, *rest):
     shards = rest[:-7]
     out, cells, table, placed, flat, blurred, sem = rest[-7:]
+    g_high = g_col[:, 0:128]
     per = shards[0].shape[0]
     rows, cols = out.shape
     row, col = lax.axis_index("row"), lax.axis_index("col")
@@ -297,6 +310,11 @@
             part = jnp.concatenate([part[0 : CB - 8], jnp.where(col < n_col - 1, part[CB - 8 :], 0.0)], axis=0)
         flat[b * CB : (b + 1) * CB, :] = part.astype(BF16)
     flat[NB * CB :, :] = jnp.zeros((flat.shape[0] - NB * CB, 384), BF16)
+
+    halves = []
+    for i in range(rows // 128):
+        part = dot_nt(g_row[...], flat[:, 128 * i : 128 * i + 256])
+        halves.append(part[0:128] + part[128:])
 
     fetch.wait()
     slot_rows, slot_cols = rows // 64, cols // 128
@@ -316,22 +334,16 @@
                 placed[8 + 64 * i : 72 + 64 * i, lanes] = show(cells[image])
     placed[16 + rows :, :] = jnp.zeros((placed.shape[0] - 16 - rows, placed.shape[1]), F32)
 
-    g_high, g_low = blur_matrix((128, 256), 1)
-    g_both = jnp.concatenate([g_high, g_low], axis=0)
-    for i in range(rows // 128):
-        part = dot_nt(g_both, flat[:, 128 * i : 128 * i + 256])
-        cell = dot_nn(g_both, placed[128 * i : 128 * i + 256, :].astype(BF16))
-        part = part[0:128] + part[128:]
+    for i, part in enumerate(halves):
+        cell = dot_nn(g_row[...], placed[128 * i : 128 * i + 256, :].astype(BF16))
         cell = cell[0:128] + cell[128:]
         part += cell[:, 128 - BLUR_HALF : 128 - BLUR_HALF + part.shape[1]]
         high = part.astype(BF16)
         blurred[0, 128 * i : 128 * i + 128, :] = high
         blurred[1, 128 * i : 128 * i + 128, :] = (part - high.astype(F32)).astype(BF16)
-    g_high, g_low = blur_matrix((256, 128), 0)
-    g_both = jnp.concatenate([g_high, g_low], axis=1)
     for j in range(cols // 128):
         lanes = slice(128 * j, 128 * j + 256)
-        part = dot_nn(blurred[0, :, lanes], g_both)
+        part = dot_nn(blurred[0, :, lanes], g_col[...])
         out[:, 128 * j : 128 * j + 128] = (
             part[:, 0:128] + part[:, 128:] + dot_nn(blurred[1, :, lanes], g_high)
         )
@@ -371,7 +383,6 @@
         compiler_params=PARAMS,
         name="prep",
     )(mask_hbm, in_hbm(cell_ids), in_hbm(cell_slots), cell_count, in_hbm(across_taps), in_hbm(down_taps))
-    library, to_first, to_second = lax.optimization_barrier((library, to_first, to_second))
 
     def swaps(n):
         rounds = []
@@ -383,10 +394,6 @@
     col_first, col_second = (
         lax.ppermute(x, "col", pairs) for x, pairs in zip((to_first, to_second), swaps(n_col))
     )
-    shards = [library]
-    for d in range(1, n_col):
-        shards.append(lax.ppermute(library, "col", [(i, i ^ d) for i in range(n_col)]))
-
     to_above, to_below = pl.pallas_call(
         mid_kernel,
         out_shape=(shape((STRIP + 16, WIDE), BF16),) * 2,
@@ -395,23 +402,29 @@
         compiler_params=PARAMS,
         name="mid",
     )(edges, col_first, col_second, to_first)
+    library, to_above, to_below = lax.optimization_barrier((library, to_above, to_below))
+    shards = [library]
+    for d in range(1, n_col):
+        shards.append(lax.ppermute(library, "col", [(i, i ^ d) for i in range(n_col)]))
     row_first, row_second = (
         lax.ppermute(x, "row", pairs) for x, pairs in zip((to_above, to_below), swaps(n_row))
     )
 
-    windows, ahead, back = pl.pallas_call(
-        window_kernel,
+    windows, ahead, back, g_row, g_col = pl.pallas_call(
+        own_kernel,
         out_shape=(
             shape((NB, rows, 256), F32),
             shape((kernels, 8, 128), F32),
             shape((kernels, 8, 128), F32),
+            shape((256, 256), BF16),
+            shape((256, 256), BF16),
         ),
-        in_specs=[VMEM] * 4,
-        out_specs=(VMEM,) * 3,
+        in_specs=[VMEM] * 2,
+        out_specs=(VMEM,) * 5,
         compiler_params=PARAMS,
         cost_estimate=pl.CostEstimate(flops=10**6, bytes_accessed=10**6, transcendentals=0),
-        name="window",
-    )(mask_pixels, col_first, col_second, taps)
+        name="own",
+    )(mask_pixels, taps)
 
     acc, images = pl.pallas_call(
         functools.partial(socs_kernel, entries, per),
@@ -427,14 +440,14 @@
         + [pltpu.VMEM((2 * GROUP, 256, 256), BF16)] * 2
         + [pltpu.VMEM((2 * GROUP, NB + 1, CB, 256), BF16)] * 2,
         compiler_params=PARAMS,
-        cost_estimate=pl.CostEstimate(flops=5 * 10**9, bytes_accessed=8 * 10**6, transcendentals=0),
+        cost_estimate=pl.CostEstimate(flops=10**6, bytes_accessed=10**5, transcendentals=0),
         name="socs",
     )(in_hbm(kernel_weights), windows, row_first, row_second, col_first, col_second, to_first, ahead, back)
 
     return pl.pallas_call(
         functools.partial(final_kernel, n_row, n_col),
         out_shape=shape((rows, cols), F32),
-        in_specs=[VMEM] * (2 + n_col),
+        in_specs=[VMEM] * (4 + n_col),
         out_specs=VMEM,
         scratch_shapes=[
             pltpu.VMEM((n_col * per,) + library.shape[1:], BF16),
@@ -446,7 +459,7 @@
         ],
         compiler_params=PARAMS,
         name="final",
-    )(acc, images, *shards)
+    )(acc, images, g_row, g_col, *shards)
 
 
 def solution(mesh):

time: 29.4 us -> 30 us (1.020)
  starting transfers between devices: 14.9 us -> 15.4 us
  waiting for transfers between devices: 2.55 us -> 2.94 us
  Pallas kernels: 11 us -> 10.7 us
    ppermute x2, waiting for transfers between devices: 0.01 us -> 2.37 us  [on_device(): lax.ppermute(x, 'row', pairs)]
    ppermute x3, waiting for transfers between devices: 1.99 us -> 0.01 us  [on_device(): lax.ppermute(library, 'col', [(i, i ^ d) for i in range(n_col)])]
    ppermute x2, starting transfers between devices: 5.07 us -> 5.66 us  [on_device(): lax.ppermute(x, 'row', pairs)]
  transfers between devices with their start and end apart: 7 -> 7, of which waited for: 2 -> 2; matrix products, arithmetic and copies ran while one was open for 0% -> 0% of each run, Pallas kernels for 24% -> 23%
where the time goes in v5:
time: 30 us; the launch traced here: 29.8 us
  starting transfers between devices  15.4 us (51%)
  Pallas kernels  10.7 us (36%)
  waiting for transfers between devices  2.94 us (10%)
  between operations  0.81 us (3%)
    ppermute x3, starting transfers between devices, on_device(): lax.ppermute(library, 'col', [(i, i ^ d) for i in range(n_col)])  6.9 us
    pallas_call x1, Pallas kernels, on_device(): pl.pallas_call(functools.partial(socs_kernel, entries, per), out_shape=(s...  6.35 us
    ppermute x2, starting transfers between devices, on_device(): lax.ppermute(x, 'row', pairs)  5.66 us
    ppermute x2, starting transfers between devices, on_device(): lax.ppermute(x, 'col', pairs)  2.84 us
    pallas_call x1, Pallas kernels, on_device(): pl.pallas_call(functools.partial(final_kernel, n_row, n_col), out_shape=s...  2.38 us
    ppermute x2, waiting for transfers between devices, on_device(): lax.ppermute(x, 'row', pairs)  2.37 us
    pallas_call x1, Pallas kernels, on_device(): pl.pallas_call(prep_kernel, out_shape=(shape((STRIP + 16, rows), BF16), s...  1.3 us
  transfers between devices with their start and end apart: 7, of which 2 were waited for; matrix products, arithmetic and copies ran while one was open for 0% of the time, Pallas kernels for 23%

profile of v5, /device:TPU:1, one launch (start us, length us, event | category | flops | bytes accessed | tf_op | source)
XLA Modules:
  0.0 29.8 jit_solution(14460170686497511818)
XLA Ops:
  0.0 0.0 copy-start
  0.7 1.3 %prep.1 = (bf16[48,256]{1,0:T(8,128)(2,1)S(1)}, bf16[48,256]{1,0:T(8,128)(2,1)S(1)}, s32[2,32,512]{2,1,0:T(8,128)S(1)}, bf16[2,12,2,33]{3,2,1,0:T(2,128)(2,1)S(1)}) custom-call(s32[256,512]{1,0:T(8,128)} %mask.3, s32[1,1,8]{2,1,0:T(1,128)} %ids.1, s32[1,1,8]{2,1,0:T(1,128)} %slots.1, s32[1,1]{1,0:T(1,128)S(6)} %copy.9.count, bf16[12,2,33]{2,1,0:T(2,128)(2,1)} %across.1, ...), custom_call_target="tpu_custom_call" | custom-call | tf_op jit(solution)/shard_map/prep/pallas_call | solution.py:367
  2.0 0.0 copy-start.1
  2.0 2.2 %collective-permute-start = (bf16[48,256]{1,0:T(8,128)(2,1)S(1)}, bf16[48,256]{1,0:T(8,128)(2,1)S(1)}, u32[]{:S(2)}, u32[]{:S(2)}) collective-permute-start(bf16[48,256]{1,0:T(8,128)(2,1)S(1)} %get-tuple-element.24.own), channel_id=1, source_target_pairs={{0,1},{2,3},{1,0},{3,2},{4,5},{6,7},{5,4},{7,6},{8,9},{10,11},{9,8... | collective-permute-start | bytes 73736 | tf_op jit(solution)/shard_map/ppermute | solution.py:395
  4.2 0.7 %collective-permute-start.1 = (bf16[48,256]{1,0:T(8,128)(2,1)S(1)}, bf16[48,256]{1,0:T(8,128)(2,1)S(1)}, u32[]{:S(2)}, u32[]{:S(2)}) collective-permute-start(bf16[48,256]{1,0:T(8,128)(2,1)S(1)} %get-tuple-element.25), channel_id=1, source_target_pairs={{1,2},{2,1},{5,6},{6,5},{9,10},{10,9},{13,14},{14,13},{17,18},{18,... | collective-permute-start | bytes 73736 | tf_op jit(solution)/shard_map/ppermute | solution.py:395
  4.9 0.6 %collective-permute-done.from_first.col_first = bf16[48,256]{1,0:T(8,128)(2,1)S(1)} collective-permute-done((bf16[48,256]{1,0:T(8,128)(2,1)S(1)}, bf16[48,256]{1,0:T(8,128)(2,1)S(1)}, u32[]{:S(2)}, u32[]{:S(2)}) %collective-permute-start) | collective-permute-done | bytes 24608 | tf_op jit(solution)/shard_map/ppermute | solution.py:395
  5.4 0.0 collective-permute-done.1.from_second.col_second
  5.4 0.2 mid.1
  5.7 0.0 copy-done.1
  5.7 4.5 %collective-permute-start.4 = (bf16[8,64,128]{2,1,0:T(8,128)(2,1)S(1)}, bf16[8,64,128]{2,1,0:T(8,128)(2,1)S(1)}, u32[]{:S(2)}, u32[]{:S(2)}) collective-permute-start(bf16[8,64,128]{2,1,0:T(8,128)(2,1)S(1)} %copy-done.1), channel_id=1, source_target_pairs={{0,1},{1,0},{2,3},{3,2},{4,5},{5,4},{6,7},{7,6},{8,9},{9,8},{10,11... | collective-permute-start | bytes 393224 | tf_op jit(solution)/shard_map/ppermute | solution.py:408
  10.2 1.2 %collective-permute-start.5 = (bf16[8,64,128]{2,1,0:T(8,128)(2,1)S(1)}, bf16[8,64,128]{2,1,0:T(8,128)(2,1)S(1)}, u32[]{:S(2)}, u32[]{:S(2)}) collective-permute-start(bf16[8,64,128]{2,1,0:T(8,128)(2,1)S(1)} %copy-done.1), channel_id=1, source_target_pairs={{0,2},{1,3},{2,0},{3,1},{4,6},{5,7},{6,4},{7,5},{8,10},{9,11},{10,... | collective-permute-start | bytes 393224 | tf_op jit(solution)/shard_map/ppermute | solution.py:408
  11.5 1.1 %collective-permute-start.6 = (bf16[8,64,128]{2,1,0:T(8,128)(2,1)S(1)}, bf16[8,64,128]{2,1,0:T(8,128)(2,1)S(1)}, u32[]{:S(2)}, u32[]{:S(2)}) collective-permute-start(bf16[8,64,128]{2,1,0:T(8,128)(2,1)S(1)} %copy-done.1), channel_id=1, source_target_pairs={{0,3},{1,2},{2,1},{3,0},{4,7},{5,6},{6,5},{7,4},{8,11},{9,10},{10,... | collective-permute-start | bytes 393224 | tf_op jit(solution)/shard_map/ppermute | solution.py:408
  12.6 2.7 %collective-permute-start.2 = (bf16[48,640]{1,0:T(8,128)(2,1)S(1)}, bf16[48,640]{1,0:T(8,128)(2,1)S(1)}, u32[]{:S(2)}, u32[]{:S(2)}) collective-permute-start(bf16[48,640]{1,0:T(8,128)(2,1)S(1)} %get-tuple-element.28), channel_id=1, source_target_pairs={{0,4},{8,12},{4,0},{12,8},{1,5},{9,13},{5,1},{13,9},{2,6},{10,14},... | collective-permute-start | bytes 184328 | tf_op jit(solution)/shard_map/ppermute | solution.py:410
  15.2 3.0 %collective-permute-start.3 = (bf16[48,640]{1,0:T(8,128)(2,1)S(1)}, bf16[48,640]{1,0:T(8,128)(2,1)S(1)}, u32[]{:S(2)}, u32[]{:S(2)}) collective-permute-start(bf16[48,640]{1,0:T(8,128)(2,1)S(1)} %get-tuple-element.29), channel_id=1, source_target_pairs={{4,8},{8,4},{5,9},{9,5},{6,10},{10,6},{7,11},{11,7},{20,24},{24,20... | collective-permute-start | bytes 184328 | tf_op jit(solution)/shard_map/ppermute | solution.py:410
  18.2 0.0 copy-done
  18.3 0.4 %own.1 = (f32[3,256,256]{2,1,0:T(8,128)S(1)}, f32[12,8,128]{2,1,0:T(8,128)S(1)}, f32[12,8,128]{2,1,0:T(8,128)S(1)}, bf16[256,256]{1,0:T(8,128)(2,1)S(1)}, bf16[256,256]{1,0:T(8,128)(2,1)S(1)}) custom-call(s32[256,512]{1,0:T(8,128)S(1)} %copy-done, bf16[2,12,2,33]{3,2,1,0:T(2,128)(2,1)S(1)} %get-tuple-element.21.taps), custom_call_target="tpu_custom_call" | custom-call | flops 1000000 | bytes 1000000 | tf_op jit(solution)/shard_map/own/pallas_call | solution.py:413
  18.7 0.0 collective-permute-done.2.row_first
  18.7 2.4 %collective-permute-done.3.row_second = bf16[48,640]{1,0:T(8,128)(2,1)S(1)} collective-permute-done((bf16[48,640]{1,0:T(8,128)(2,1)S(1)}, bf16[48,640]{1,0:T(8,128)(2,1)S(1)}, u32[]{:S(2)}, u32[]{:S(2)}) %collective-permute-start.3) | collective-permute-done | bytes 61472 | tf_op jit(solution)/shard_map/ppermute | solution.py:410
  21.1 6.3 %socs.1 = (f32[4,176,256]{2,1,0:T(8,128)S(1)}, s32[16,128]{1,0:T(8,128)S(1)}) custom-call(f32[12]{0:T(128)} %weights.1, f32[3,256,256]{2,1,0:T(8,128)S(1)} %get-tuple-element.22.windows, bf16[48,640]{1,0:T(8,128)(2,1)S(1)} %collective-permute-done.2.row_first, bf16[48,640]{1,0:T(8,128)(2,1)S(1)} %collective-permute-done.3.row_second, ...), custom_call_target="tpu_custom_call" | custom-call | flops 1000000 | bytes 100000 | tf_op jit(solution)/shard_map/socs/pallas_call | solution.py:429
  27.4 0.0 collective-permute-done.4.rest_1_
  27.4 0.0 collective-permute-done.5.rest_2_
  27.4 0.0 collective-permute-done.6.rest_3_
  27.5 2.4 %final.1 = f32[256,512]{1,0:T(8,128)} custom-call(f32[4,176,256]{2,1,0:T(8,128)S(1)} %get-tuple-element.32.acc, s32[16,128]{1,0:T(8,128)S(1)} %get-tuple-element.33.images, bf16[256,256]{1,0:T(8,128)(2,1)S(1)} %get-tuple-element.34.g_row, bf16[256,256]{1,0:T(8,128)(2,1)S(1)} %get-tuple-element.35.g_col, bf16[8,64,128]{2,1,0:T(8,128)(2,1)S(1)} %copy-done.1, ...), custom_call_target="tpu_custom_call" | custom-call | tf_op jit(solution)/shard_map/final/pallas_call | solution.py:447
Async XLA Ops:
  0.0 18.3 %copy-start = (s32[256,512]{1,0:T(8,128)S(1)}, s32[256,512]{1,0:T(8,128)}, u32[]{:S(2)}) copy-start(s32[256,512]{1,0:T(8,128)} %mask.3) | copy-start | bytes 1572868
  2.0 3.7 %copy-start.1 = (bf16[8,64,128]{2,1,0:T(8,128)(2,1)S(1)}, bf16[8,64,128]{2,1,0:T(8,128)(2,1)}, u32[]{:S(2)}) copy-start(bf16[8,64,128]{2,1,0:T(8,128)(2,1)} %rest_0_) | copy-start | bytes 393220
  2.0 3.4 %collective-permute-start = (bf16[48,256]{1,0:T(8,128)(2,1)S(1)}, bf16[48,256]{1,0:T(8,128)(2,1)S(1)}, u32[]{:S(2)}, u32[]{:S(2)}) collective-permute-start(bf16[48,256]{1,0:T(8,128)(2,1)S(1)} %get-tuple-element.24.own), channel_id=1, source_target_pairs={{0,1},{2,3},{1,0},{3,2},{4,5},{6,7},{5,4},{7,6},{8,9},{10,11},{9,8... | collective-permute-start | bytes 73736 | tf_op jit(solution)/shard_map/ppermute | solution.py:395
  4.2 1.2 %collective-permute-start.1 = (bf16[48,256]{1,0:T(8,128)(2,1)S(1)}, bf16[48,256]{1,0:T(8,128)(2,1)S(1)}, u32[]{:S(2)}, u32[]{:S(2)}) collective-permute-start(bf16[48,256]{1,0:T(8,128)(2,1)S(1)} %get-tuple-element.25), channel_id=1, source_target_pairs={{1,2},{2,1},{5,6},{6,5},{9,10},{10,9},{13,14},{14,13},{17,18},{18,... | collective-permute-start | bytes 73736 | tf_op jit(solution)/shard_map/ppermute | solution.py:395
  5.7 21.7 %collective-permute-start.4 = (bf16[8,64,128]{2,1,0:T(8,128)(2,1)S(1)}, bf16[8,64,128]{2,1,0:T(8,128)(2,1)S(1)}, u32[]{:S(2)}, u32[]{:S(2)}) collective-permute-start(bf16[8,64,128]{2,1,0:T(8,128)(2,1)S(1)} %copy-done.1), channel_id=1, source_target_pairs={{0,1},{1,0},{2,3},{3,2},{4,5},{5,4},{6,7},{7,6},{8,9},{9,8},{10,11... | collective-permute-start | bytes 393224 | tf_op jit(solution)/shard_map/ppermute | solution.py:408
  10.2 17.2 %collective-permute-start.5 = (bf16[8,64,128]{2,1,0:T(8,128)(2,1)S(1)}, bf16[8,64,128]{2,1,0:T(8,128)(2,1)S(1)}, u32[]{:S(2)}, u32[]{:S(2)}) collective-permute-start(bf16[8,64,128]{2,1,0:T(8,128)(2,1)S(1)} %copy-done.1), channel_id=1, source_target_pairs={{0,2},{1,3},{2,0},{3,1},{4,6},{5,7},{6,4},{7,5},{8,10},{9,11},{10,... | collective-permute-start | bytes 393224 | tf_op jit(solution)/shard_map/ppermute | solution.py:408
  11.5 16.0 %collective-permute-start.6 = (bf16[8,64,128]{2,1,0:T(8,128)(2,1)S(1)}, bf16[8,64,128]{2,1,0:T(8,128)(2,1)S(1)}, u32[]{:S(2)}, u32[]{:S(2)}) collective-permute-start(bf16[8,64,128]{2,1,0:T(8,128)(2,1)S(1)} %copy-done.1), channel_id=1, source_target_pairs={{0,3},{1,2},{2,1},{3,0},{4,7},{5,6},{6,5},{7,4},{8,11},{9,10},{10,... | collective-permute-start | bytes 393224 | tf_op jit(solution)/shard_map/ppermute | solution.py:408
  12.6 6.1 %collective-permute-start.2 = (bf16[48,640]{1,0:T(8,128)(2,1)S(1)}, bf16[48,640]{1,0:T(8,128)(2,1)S(1)}, u32[]{:S(2)}, u32[]{:S(2)}) collective-permute-start(bf16[48,640]{1,0:T(8,128)(2,1)S(1)} %get-tuple-element.28), channel_id=1, source_target_pairs={{0,4},{8,12},{4,0},{12,8},{1,5},{9,13},{5,1},{13,9},{2,6},{10,14},... | collective-permute-start | bytes 184328 | tf_op jit(solution)/shard_map/ppermute | solution.py:410
  15.2 5.8 %collective-permute-start.3 = (bf16[48,640]{1,0:T(8,128)(2,1)S(1)}, bf16[48,640]{1,0:T(8,128)(2,1)S(1)}, u32[]{:S(2)}, u32[]{:S(2)}) collective-permute-start(bf16[48,640]{1,0:T(8,128)(2,1)S(1)} %get-tuple-element.29), channel_id=1, source_target_pairs={{4,8},{8,4},{5,9},{9,5},{6,10},{10,6},{7,11},{11,7},{20,24},{24,20... | collective-permute-start | bytes 184328 | tf_op jit(solution)/shard_map/ppermute | solution.py:410

commit v6 on v5

--- a/solution.py
+++ b/solution.py
@@ -19,6 +19,7 @@
 EDGE_IN = 80
 EDGE_OUT = 48
 RIGHT_AT = 56
+HALF_STRIP = STRIP + 16
 GROUP = 2
 WIDE = 640
 SLOTS = 16
@@ -38,6 +39,11 @@
     return lax.dot_general(a, b, (((1,), (0,)), ((), ())), preferred_element_type=F32)
 
 
+def join(strip):
+    halves = [strip[0:HALF_STRIP, :], strip[HALF_STRIP : 2 * HALF_STRIP, :]]
+    return jnp.concatenate(halves, axis=1).astype(F32)
+
+
 def eye(rows, cols, shift):
     at = lax.broadcasted_iota(jnp.int32, (rows, cols), 1) - lax.broadcasted_iota(jnp.int32, (rows, cols), 0)
     return jnp.where(at == shift, 1.0, 0.0).astype(BF16)
@@ -49,7 +55,7 @@
 
 
 def prep_kernel(
-    mask, ids, slots, count, across, down, to_first, to_second, edges, taps, ends, a_ids, a_slots, sems
+    mask, ids, slots, count, across, down, library, to_first, to_second, edges, taps, ends, a_ids, a_slots, sems
 ):
     rows, cols = mask.shape
     copies = [
@@ -61,6 +67,7 @@
         pltpu.make_async_copy(mask.at[rows - STRIP : rows], edges.at[1], sems.at[5]),
         pltpu.make_async_copy(across, taps.at[0], sems.at[6]),
         pltpu.make_async_copy(down, taps.at[1], sems.at[7]),
+        pltpu.make_async_copy(library, to_first.at[2 * HALF_STRIP :], sems.at[8]),
     ]
     for copy in copies:
         copy.start()
@@ -79,25 +86,26 @@
     width = jnp.where(line == 2, 1, ids.shape[2])
     table = jnp.where((lane < width) & (line < 3), table, 0.0).astype(BF16)
     for strip in (to_first, to_second):
-        strip[STRIP:, 0:128] = table
-        strip[STRIP:, 128:] = jnp.zeros((16, rows - 128), BF16)
+        strip[STRIP:HALF_STRIP, :] = table
+        strip[HALF_STRIP + STRIP : 2 * HALF_STRIP, :] = jnp.zeros((16, 128), BF16)
     even = lax.rem(lax.axis_index("col"), 2) == 0
     copies[0].wait()
     first = dot_nt(eye(STRIP, 128, 0), ends[0].astype(F32).astype(BF16))
     copies[1].wait()
     last = dot_nt(eye(STRIP, 128, 128 - STRIP), ends[1].astype(F32).astype(BF16))
-    to_first[0:STRIP, :] = jnp.where(even, last, first).astype(BF16)
-    to_second[0:STRIP, :] = jnp.where(even, first, last).astype(BF16)
+    for strip, part in ((to_first, jnp.where(even, last, first)), (to_second, jnp.where(even, first, last))):
+        strip[0:STRIP, :] = part[:, 0:128].astype(BF16)
+        strip[HALF_STRIP : HALF_STRIP + STRIP, :] = part[:, 128:256].astype(BF16)
     for copy in copies[4:]:
         copy.wait()
 
 
 def mid_kernel(edges, from_first, from_second, own, to_first, to_second):
     cols = edges.shape[2]
-    rows = from_first.shape[1]
-    left, right = sides("col", from_first[...].astype(F32), from_second[...].astype(F32))
+    rows = 256
+    left, right = sides("col", join(from_first), join(from_second))
     tables = jnp.concatenate(
-        [left[STRIP:, 0:128], own[STRIP:, 0:128].astype(F32), right[STRIP:, 0:128], jnp.zeros((16, 256), F32)],
+        [left[STRIP:, 0:128], own[STRIP:HALF_STRIP, :].astype(F32), right[STRIP:, 0:128], jnp.zeros((16, 256), F32)],
         axis=1,
     ).astype(BF16)
     fill = jnp.zeros((128 - STRIP, 128), F32)
@@ -174,7 +182,7 @@
     fetch = pltpu.make_async_copy(weights, scale, sem)
     fetch.start()
     above, below = sides("row", row_first[...].astype(F32), row_second[...].astype(F32))
-    left, right = sides("col", col_first[...].astype(F32), col_second[...].astype(F32))
+    left, right = sides("col", join(col_first), join(col_second))
     rows = windows.shape[1]
     turned = jnp.concatenate(
         [
@@ -210,7 +218,7 @@
     found = jnp.zeros((SLOTS, 128), F32)
     col = lax.axis_index("col")
     tables = [above[STRIP:, 128 * t : 128 * t + 128] for t in range(3)]
-    tables += [left, own[STRIP:, 0:128].astype(F32), right]
+    tables += [left, own[STRIP:HALF_STRIP, :].astype(F32), right]
     tables += [below[STRIP:, 128 * t : 128 * t + 128] for t in range(3)]
     for t, table in enumerate(tables):
         live = lane.astype(F32) < table[2:3, 0:1]
@@ -287,13 +295,14 @@
     shards = rest[:-7]
     out, cells, table, placed, flat, blurred, sem = rest[-7:]
     g_high = g_col[:, 0:128]
-    per = shards[0].shape[0]
+    per = cells.shape[0] // len(shards)
     rows, cols = out.shape
     row, col = lax.axis_index("row"), lax.axis_index("col")
     fetch = pltpu.make_async_copy(images, table, sem)
     fetch.start()
     for i, shard in enumerate(shards):
-        cells[pl.ds(i * per, per)] = shard[...]
+        rows_of = shard.shape[0] - per * 64
+        cells[pl.ds(i * per, per)] = shard[rows_of:, :].reshape(per, 64, 128)
 
     at_row = lax.broadcasted_iota(jnp.int32, (8, 384), 1) - BLUR_HALF
     row_ok = ((row > 0) | (at_row >= 0)) & ((row < n_row - 1) | (at_row < rows))
@@ -361,28 +370,29 @@
     entries = cell_ids.shape[-1]
     per = library.shape[0]
     n_row, n_col = lax.axis_size("row"), lax.axis_size("col")
+    library = library.reshape(per * 64, 128)
     in_hbm = lambda x: pltpu.with_memory_space_constraint(x, pltpu.HBM)
     mask_hbm = in_hbm(mask_pixels)
 
     to_first, to_second, edges, taps = pl.pallas_call(
         prep_kernel,
         out_shape=(
-            shape((STRIP + 16, rows), BF16),
-            shape((STRIP + 16, rows), BF16),
+            shape((2 * HALF_STRIP + per * 64, 128), BF16),
+            shape((2 * HALF_STRIP, 128), BF16),
             shape((2, STRIP, cols), jnp.int32),
             shape((2,) + across_taps.shape, BF16),
         ),
-        in_specs=[HBM] * 3 + [SMEM] + [HBM] * 2,
+        in_specs=[HBM] * 3 + [SMEM] + [HBM] * 3,
         out_specs=(VMEM,) * 4,
         scratch_shapes=[
             pltpu.VMEM((2, rows, 128), jnp.int32),
             pltpu.VMEM(cell_ids.shape, jnp.int32),
             pltpu.VMEM(cell_slots.shape, jnp.int32),
-            pltpu.SemaphoreType.DMA((8,)),
+            pltpu.SemaphoreType.DMA((9,)),
         ],
         compiler_params=PARAMS,
         name="prep",
-    )(mask_hbm, in_hbm(cell_ids), in_hbm(cell_slots), cell_count, in_hbm(across_taps), in_hbm(down_taps))
+    )(mask_hbm, in_hbm(cell_ids), in_hbm(cell_slots), cell_count, in_hbm(across_taps), in_hbm(down_taps), in_hbm(library))
 
     def swaps(n):
         rounds = []
@@ -391,9 +401,10 @@
             rounds.append(pairs + [(b, a) for a, b in pairs])
         return rounds
 
-    col_first, col_second = (
-        lax.ppermute(x, "col", pairs) for x, pairs in zip((to_first, to_second), swaps(n_col))
-    )
+    pairs = swaps(n_col)
+    col_second = lax.ppermute(to_second, "col", pairs[1])
+    col_first = lax.ppermute(to_first, "col", pairs[0])
+    shards = [library, col_first]
     to_above, to_below = pl.pallas_call(
         mid_kernel,
         out_shape=(shape((STRIP + 16, WIDE), BF16),) * 2,
@@ -402,10 +413,12 @@
         compiler_params=PARAMS,
         name="mid",
     )(edges, col_first, col_second, to_first)
-    library, to_above, to_below = lax.optimization_barrier((library, to_above, to_below))
-    shards = [library]
-    for d in range(1, n_col):
-        shards.append(lax.ppermute(library, "col", [(i, i ^ d) for i in range(n_col)]))
+    for d in range(2, n_col):
+        if d == 2:
+            block, col_second = lax.optimization_barrier((library, col_second))
+        if d == 3:
+            block, to_above, to_below = lax.optimization_barrier((library, to_above, to_below))
+        shards.append(lax.ppermute(block, "col", [(i, i ^ d) for i in range(n_col)]))
     row_first, row_second = (
         lax.ppermute(x, "row", pairs) for x, pairs in zip((to_above, to_below), swaps(n_row))
     )
@@ -450,7 +463,7 @@
         in_specs=[VMEM] * (4 + n_col),
         out_specs=VMEM,
         scratch_shapes=[
-            pltpu.VMEM((n_col * per,) + library.shape[1:], BF16),
+            pltpu.VMEM((n_col * per, 64, 128), BF16),
             pltpu.SMEM((SLOTS, 128), jnp.int32),
             pltpu.VMEM((384, cols + 256), F32),
             pltpu.VMEM((WIDE, 384), BF16),

time: 30 us -> 29.5 us (0.983)
  waiting for transfers between devices: 2.94 us -> 2.38 us
    ppermute x2, starting transfers between devices: 5.66 us -> 5.09 us  [on_device(): lax.ppermute(x, 'row', pairs)]
    ppermute x5 -> x4, starting transfers between devices: 9.74 us -> 10.3 us  [the longest x2 7.46 us: on_device(): lax.ppermute(block, 'col', [(i, i ^ d) for i in range(n_col)])]
    ppermute x5 -> x4, waiting for transfers between devices: 0.57 us -> 0.01 us  [the longest x2 0.01 us: on_device(): lax.ppermute(block, 'col', [(i, i ^ d) for i in range(n_col)])]
  transfers between devices with their start and end apart: 7 -> 6, of which waited for: 2 -> 1; matrix products, arithmetic and copies ran while one was open for 0% -> 0% of each run, Pallas kernels for 23% -> 24%
where the time goes in v6:
time: 29.5 us; the launch traced here: 29.3 us
  starting transfers between devices  15.4 us (52%)
  Pallas kernels  10.7 us (36%)
  waiting for transfers between devices  2.38 us (8%)
  between operations  0.76 us (3%)
    ppermute x2, starting transfers between devices, on_device(): lax.ppermute(block, 'col', [(i, i ^ d) for i in range(n_col)])  7.46 us
    pallas_call x1, Pallas kernels, on_device(): pl.pallas_call(functools.partial(socs_kernel, entries, per), out_shape=(s...  6.34 us
    ppermute x2, starting transfers between devices, on_device(): lax.ppermute(x, 'row', pairs)  5.09 us
    pallas_call x1, Pallas kernels, on_device(): pl.pallas_call(functools.partial(final_kernel, n_row, n_col), out_shape=s...  2.38 us
    ppermute x2, waiting for transfers between devices, on_device(): lax.ppermute(x, 'row', pairs)  2.37 us
    ppermute x1, starting transfers between devices, on_device(): col_first = lax.ppermute(to_first, 'col', pairs[0])  2.19 us
    pallas_call x1, Pallas kernels, on_device(): pl.pallas_call(prep_kernel, out_shape=(shape((2 * HALF_STRIP + per * 64,...  1.37 us
    ppermute x1, starting transfers between devices, on_device(): col_second = lax.ppermute(to_second, 'col', pairs[1])  0.65 us
  transfers between devices with their start and end apart: 6, of which 1 were waited for; matrix products, arithmetic and copies ran while one was open for 0% of the time, Pallas kernels for 24%

profile of v6, /device:TPU:1, one launch (start us, length us, event | category | flops | bytes accessed | tf_op | source)
XLA Modules:
  0.0 29.3 jit_solution(15581385799258435755)
XLA Ops:
  0.7 0.0 copy-start.1
  0.7 0.0 copy-start
  0.7 1.4 %prep.1 = (bf16[608,128]{1,0:T(8,128)(2,1)S(1)}, bf16[96,128]{1,0:T(8,128)(2,1)S(1)}, s32[2,32,512]{2,1,0:T(8,128)S(1)}, bf16[2,12,2,33]{3,2,1,0:T(2,128)(2,1)S(1)}) custom-call(s32[256,512]{1,0:T(8,128)} %mask.3, s32[1,1,8]{2,1,0:T(1,128)} %ids.1, s32[1,1,8]{2,1,0:T(1,128)} %slots.1, s32[1,1]{1,0:T(1,128)S(6)} %copy.9.count, bf16[12,2,33]{2,1,0:T(2,128)(2,1)} %across.1, ...), custom_call_target="tpu_custom_call" | custom-call | tf_op jit(solution)/shard_map/prep/pallas_call | solution.py:377
  2.1 2.2 %collective-permute-start = (bf16[608,128]{1,0:T(8,128)(2,1)S(1)}, bf16[608,128]{1,0:T(8,128)(2,1)S(1)}, u32[]{:S(2)}, u32[]{:S(2)}) collective-permute-start(bf16[608,128]{1,0:T(8,128)(2,1)S(1)} %get-tuple-element.26.own), channel_id=1, source_target_pairs={{0,1},{2,3},{1,0},{3,2},{4,5},{6,7},{5,4},{7,6},{8,9},{10,11},{9,8... | collective-permute-start | bytes 466952 | tf_op jit(solution)/shard_map/ppermute | solution.py:406
  4.2 0.7 %collective-permute-start.1 = (bf16[96,128]{1,0:T(8,128)(2,1)S(1)}, bf16[96,128]{1,0:T(8,128)(2,1)S(1)}, u32[]{:S(2)}, u32[]{:S(2)}) collective-permute-start(bf16[96,128]{1,0:T(8,128)(2,1)S(1)} %get-tuple-element.27), channel_id=1, source_target_pairs={{1,2},{2,1},{5,6},{6,5},{9,10},{10,9},{13,14},{14,13},{17,18},{18,... | collective-permute-start | bytes 73736 | tf_op jit(solution)/shard_map/ppermute | solution.py:405
  4.9 0.0 collective-permute-done.1.from_second.col_second
  4.9 0.0 copy-done.1
  4.9 6.4 %collective-permute-start.4 = (bf16[512,128]{1,0:T(8,128)(2,1)S(1)}, bf16[512,128]{1,0:T(8,128)(2,1)S(1)}, u32[]{:S(2)}, u32[]{:S(2)}) collective-permute-start(bf16[512,128]{1,0:T(8,128)(2,1)S(1)} %bitcast.2), channel_id=1, source_target_pairs={{0,2},{1,3},{2,0},{3,1},{4,6},{5,7},{6,4},{7,5},{8,10},{9,11},{10,... | collective-permute-start | bytes 393224 | tf_op jit(solution)/shard_map/ppermute | solution.py:421
  11.3 0.0 collective-permute-done.from_first.col_first.rest_1_
  11.3 0.2 mid.1
  11.5 1.1 %collective-permute-start.5 = (bf16[512,128]{1,0:T(8,128)(2,1)S(1)}, bf16[512,128]{1,0:T(8,128)(2,1)S(1)}, u32[]{:S(2)}, u32[]{:S(2)}) collective-permute-start(bf16[512,128]{1,0:T(8,128)(2,1)S(1)} %bitcast.3), channel_id=1, source_target_pairs={{0,3},{1,2},{2,1},{3,0},{4,7},{5,6},{6,5},{7,4},{8,11},{9,10},{10,... | collective-permute-start | bytes 393224 | tf_op jit(solution)/shard_map/ppermute | solution.py:421
  12.6 2.1 %collective-permute-start.2 = (bf16[48,640]{1,0:T(8,128)(2,1)S(1)}, bf16[48,640]{1,0:T(8,128)(2,1)S(1)}, u32[]{:S(2)}, u32[]{:S(2)}) collective-permute-start(bf16[48,640]{1,0:T(8,128)(2,1)S(1)} %get-tuple-element.30), channel_id=1, source_target_pairs={{0,4},{8,12},{4,0},{12,8},{1,5},{9,13},{5,1},{13,9},{2,6},{10,14},... | collective-permute-start | bytes 184328 | tf_op jit(solution)/shard_map/ppermute | solution.py:423
  14.7 3.0 %collective-permute-start.3 = (bf16[48,640]{1,0:T(8,128)(2,1)S(1)}, bf16[48,640]{1,0:T(8,128)(2,1)S(1)}, u32[]{:S(2)}, u32[]{:S(2)}) collective-permute-start(bf16[48,640]{1,0:T(8,128)(2,1)S(1)} %get-tuple-element.31), channel_id=1, source_target_pairs={{4,8},{8,4},{5,9},{9,5},{6,10},{10,6},{7,11},{11,7},{20,24},{24,20... | collective-permute-start | bytes 184328 | tf_op jit(solution)/shard_map/ppermute | solution.py:423
  17.7 0.0 copy-done
  17.7 0.4 %own.1 = (f32[3,256,256]{2,1,0:T(8,128)S(1)}, f32[12,8,128]{2,1,0:T(8,128)S(1)}, f32[12,8,128]{2,1,0:T(8,128)S(1)}, bf16[256,256]{1,0:T(8,128)(2,1)S(1)}, bf16[256,256]{1,0:T(8,128)(2,1)S(1)}) custom-call(s32[256,512]{1,0:T(8,128)S(1)} %copy-done, bf16[2,12,2,33]{3,2,1,0:T(2,128)(2,1)S(1)} %get-tuple-element.23.taps), custom_call_target="tpu_custom_call" | custom-call | flops 1000000 | bytes 1000000 | tf_op jit(solution)/shard_map/own/pallas_call | solution.py:426
  18.2 0.0 collective-permute-done.2.row_first
  18.2 2.4 %collective-permute-done.3.row_second = bf16[48,640]{1,0:T(8,128)(2,1)S(1)} collective-permute-done((bf16[48,640]{1,0:T(8,128)(2,1)S(1)}, bf16[48,640]{1,0:T(8,128)(2,1)S(1)}, u32[]{:S(2)}, u32[]{:S(2)}) %collective-permute-start.3) | collective-permute-done | bytes 61472 | tf_op jit(solution)/shard_map/ppermute | solution.py:423
  20.5 6.3 %socs.1 = (f32[4,176,256]{2,1,0:T(8,128)S(1)}, s32[16,128]{1,0:T(8,128)S(1)}) custom-call(f32[12]{0:T(128)} %weights.1, f32[3,256,256]{2,1,0:T(8,128)S(1)} %get-tuple-element.24.windows, bf16[48,640]{1,0:T(8,128)(2,1)S(1)} %collective-permute-done.2.row_first, bf16[48,640]{1,0:T(8,128)(2,1)S(1)} %collective-permute-done.3.row_second, ...), custom_call_target="tpu_custom_call" | custom-call | flops 1000000 | bytes 100000 | tf_op jit(solution)/shard_map/socs/pallas_call | solution.py:442
  26.9 0.0 collective-permute-done.4.rest_2_
  26.9 0.0 collective-permute-done.5.rest_3_
  26.9 2.4 %final.1 = f32[256,512]{1,0:T(8,128)} custom-call(f32[4,176,256]{2,1,0:T(8,128)S(1)} %get-tuple-element.35.acc, s32[16,128]{1,0:T(8,128)S(1)} %get-tuple-element.36.images, bf16[256,256]{1,0:T(8,128)(2,1)S(1)} %get-tuple-element.37.g_row, bf16[256,256]{1,0:T(8,128)(2,1)S(1)} %get-tuple-element.38.g_col, bf16[512,128]{1,0:T(8,128)(2,1)S(1)} %bitcast.4, ...), custom_call_target="tpu_custom_call" | custom-call | tf_op jit(solution)/shard_map/final/pallas_call | solution.py:460
Async XLA Ops:
  0.7 4.3 %copy-start.1 = (bf16[8,64,128]{2,1,0:T(8,128)(2,1)S(1)}, bf16[8,64,128]{2,1,0:T(8,128)(2,1)}, u32[]{:S(2)}) copy-start(bf16[8,64,128]{2,1,0:T(8,128)(2,1)} %param.12) | copy-start | bytes 393220
  0.7 17.1 %copy-start = (s32[256,512]{1,0:T(8,128)S(1)}, s32[256,512]{1,0:T(8,128)}, u32[]{:S(2)}) copy-start(s32[256,512]{1,0:T(8,128)} %mask.3) | copy-start | bytes 1572868
  2.1 9.3 %collective-permute-start = (bf16[608,128]{1,0:T(8,128)(2,1)S(1)}, bf16[608,128]{1,0:T(8,128)(2,1)S(1)}, u32[]{:S(2)}, u32[]{:S(2)}) collective-permute-start(bf16[608,128]{1,0:T(8,128)(2,1)S(1)} %get-tuple-element.26.own), channel_id=1, source_target_pairs={{0,1},{2,3},{1,0},{3,2},{4,5},{6,7},{5,4},{7,6},{8,9},{10,11},{9,8... | collective-permute-start | bytes 466952 | tf_op jit(solution)/shard_map/ppermute | solution.py:406
  4.2 0.7 %collective-permute-start.1 = (bf16[96,128]{1,0:T(8,128)(2,1)S(1)}, bf16[96,128]{1,0:T(8,128)(2,1)S(1)}, u32[]{:S(2)}, u32[]{:S(2)}) collective-permute-start(bf16[96,128]{1,0:T(8,128)(2,1)S(1)} %get-tuple-element.27), channel_id=1, source_target_pairs={{1,2},{2,1},{5,6},{6,5},{9,10},{10,9},{13,14},{14,13},{17,18},{18,... | collective-permute-start | bytes 73736 | tf_op jit(solution)/shard_map/ppermute | solution.py:405
  4.9 22.0 %collective-permute-start.4 = (bf16[512,128]{1,0:T(8,128)(2,1)S(1)}, bf16[512,128]{1,0:T(8,128)(2,1)S(1)}, u32[]{:S(2)}, u32[]{:S(2)}) collective-permute-start(bf16[512,128]{1,0:T(8,128)(2,1)S(1)} %bitcast.2), channel_id=1, source_target_pairs={{0,2},{1,3},{2,0},{3,1},{4,6},{5,7},{6,4},{7,5},{8,10},{9,11},{10,... | collective-permute-start | bytes 393224 | tf_op jit(solution)/shard_map/ppermute | solution.py:421
  11.5 15.4 %collective-permute-start.5 = (bf16[512,128]{1,0:T(8,128)(2,1)S(1)}, bf16[512,128]{1,0:T(8,128)(2,1)S(1)}, u32[]{:S(2)}, u32[]{:S(2)}) collective-permute-start(bf16[512,128]{1,0:T(8,128)(2,1)S(1)} %bitcast.3), channel_id=1, source_target_pairs={{0,3},{1,2},{2,1},{3,0},{4,7},{5,6},{6,5},{7,4},{8,11},{9,10},{10,... | collective-permute-start | bytes 393224 | tf_op jit(solution)/shard_map/ppermute | solution.py:421
  12.6 5.5 %collective-permute-start.2 = (bf16[48,640]{1,0:T(8,128)(2,1)S(1)}, bf16[48,640]{1,0:T(8,128)(2,1)S(1)}, u32[]{:S(2)}, u32[]{:S(2)}) collective-permute-start(bf16[48,640]{1,0:T(8,128)(2,1)S(1)} %get-tuple-element.30), channel_id=1, source_target_pairs={{0,4},{8,12},{4,0},{12,8},{1,5},{9,13},{5,1},{13,9},{2,6},{10,14},... | collective-permute-start | bytes 184328 | tf_op jit(solution)/shard_map/ppermute | solution.py:423
  14.7 5.8 %collective-permute-start.3 = (bf16[48,640]{1,0:T(8,128)(2,1)S(1)}, bf16[48,640]{1,0:T(8,128)(2,1)S(1)}, u32[]{:S(2)}, u32[]{:S(2)}) collective-permute-start(bf16[48,640]{1,0:T(8,128)(2,1)S(1)} %get-tuple-element.31), channel_id=1, source_target_pairs={{4,8},{8,4},{5,9},{9,5},{6,10},{10,6},{7,11},{11,7},{20,24},{24,20... | collective-permute-start | bytes 184328 | tf_op jit(solution)/shard_map/ppermute | solution.py:423

commit v7 on v6

--- a/solution.py
+++ b/solution.py
@@ -50,8 +50,11 @@
 
 
 def sides(axis, first_swap, second_swap):
-    even = lax.rem(lax.axis_index(axis), 2) == 0
-    return jnp.where(even, second_swap, first_swap), jnp.where(even, first_swap, second_swap)
+    index, count = lax.axis_index(axis), lax.axis_size(axis)
+    even = lax.rem(index, 2) == 0
+    lower = jnp.where(even, second_swap, first_swap)
+    upper = jnp.where(even, first_swap, second_swap)
+    return jnp.where(index > 0, lower, 0.0), jnp.where(index < count - 1, upper, 0.0)
 
 
 def prep_kernel(
@@ -272,7 +275,8 @@
     def stage(m, s):
         pass_one(s)
         build_down(m, s)
-        build_across(jnp.minimum(m + 1, groups - 1), 1 - s)
+        if m + 1 < groups:
+            build_across(m + 1, 1 - s)
         pass_two(m - 1, 1 - s)
 
     build_across(0, 0)
@@ -281,14 +285,9 @@
     build_across(1, 1)
     fetch.wait()
 
-    def step(i, carry):
-        stage(2 * i + 1, 1)
-        stage(2 * i + 2, 0)
-        return carry
-
-    lax.fori_loop(0, groups // 2 - 1, step, 0)
-    stage(groups - 1, 1)
-    pass_two(groups - 1, 1)
+    for m in range(1, groups):
+        stage(m, m % 2)
+    pass_two(groups - 1, (groups - 1) % 2)
 
 
 def final_kernel(n_row, n_col, acc, images, g_row, g_col, *rest):
@@ -397,7 +396,7 @@
     def swaps(n):
         rounds = []
         for start in (0, 1):
-            pairs = [(i, i + 1) for i in range(start, n - 1, 2)]
+            pairs = [(i, (i + 1) % n) for i in range(start, n, 2)]
             rounds.append(pairs + [(b, a) for a, b in pairs])
         return rounds
 

time: 29.5 us -> 26.3 us (0.89)
  the two profiles are of different devices: /device:TPU:1 before, /device:TPU:0 now
where the time goes in v7:
time: 26.3 us; the launch traced here: 25.8 us
  Pallas kernels  10.4 us (40%)
  starting transfers between devices  8.8 us (33%)
  waiting for transfers between devices  5.87 us (22%)
  between operations  0.72 us (3%)
    pallas_call x1, Pallas kernels, on_device(): pl.pallas_call(functools.partial(socs_kernel, entries, per), out_shape=(s...  6.02 us
    ppermute x1, waiting for transfers between devices, on_device(): col_second = lax.ppermute(to_second, 'col', pairs[1])  4.26 us
    ppermute x1, starting transfers between devices, on_device(): col_first = lax.ppermute(to_first, 'col', pairs[0])  3.09 us
    ppermute x1, starting transfers between devices, on_device(): col_second = lax.ppermute(to_second, 'col', pairs[1])  2.47 us
    pallas_call x1, Pallas kernels, on_device(): pl.pallas_call(functools.partial(final_kernel, n_row, n_col), out_shape=s...  2.38 us
    ppermute x2, starting transfers between devices, on_device(): lax.ppermute(block, 'col', [(i, i ^ d) for i in range(n_col)])  1.63 us
    ppermute x2, starting transfers between devices, on_device(): lax.ppermute(x, 'row', pairs)  1.61 us
    ppermute x2, waiting for transfers between devices, on_device(): lax.ppermute(x, 'row', pairs)  1.6 us
  transfers between devices with their start and end apart: 6, of which 2 were waited for; matrix products, arithmetic and copies ran while one was open for 0% of the time, Pallas kernels for 26%

profile of v7, /device:TPU:0, one launch (start us, length us, event | category | flops | bytes accessed | tf_op | source)
XLA Modules:
  0.0 25.8 jit_solution(16091313227866887616)
XLA Ops:
  0.7 0.0 copy-start.1
  0.7 0.0 copy-start
  0.7 1.4 %prep.1 = (bf16[608,128]{1,0:T(8,128)(2,1)S(1)}, bf16[96,128]{1,0:T(8,128)(2,1)S(1)}, s32[2,32,512]{2,1,0:T(8,128)S(1)}, bf16[2,12,2,33]{3,2,1,0:T(2,128)(2,1)S(1)}) custom-call(s32[256,512]{1,0:T(8,128)} %mask.3, s32[1,1,8]{2,1,0:T(1,128)} %ids.1, s32[1,1,8]{2,1,0:T(1,128)} %slots.1, s32[1,1]{1,0:T(1,128)S(6)} %copy.9.count, bf16[12,2,33]{2,1,0:T(2,128)(2,1)} %across.1, ...), custom_call_target="tpu_custom_call" | custom-call | tf_op jit(solution)/shard_map/prep/pallas_call | solution.py:376
  2.1 3.1 %collective-permute-start = (bf16[608,128]{1,0:T(8,128)(2,1)S(1)}, bf16[608,128]{1,0:T(8,128)(2,1)S(1)}, u32[]{:S(2)}, u32[]{:S(2)}) collective-permute-start(bf16[608,128]{1,0:T(8,128)(2,1)S(1)} %get-tuple-element.26.own), channel_id=1, source_target_pairs={{0,1},{2,3},{1,0},{3,2},{4,5},{6,7},{5,4},{7,6},{8,9},{10,11},{9,8... | collective-permute-start | bytes 466952 | tf_op jit(solution)/shard_map/ppermute | solution.py:405
  5.1 2.5 %collective-permute-start.1 = (bf16[96,128]{1,0:T(8,128)(2,1)S(1)}, bf16[96,128]{1,0:T(8,128)(2,1)S(1)}, u32[]{:S(2)}, u32[]{:S(2)}) collective-permute-start(bf16[96,128]{1,0:T(8,128)(2,1)S(1)} %get-tuple-element.27), channel_id=1, source_target_pairs={{1,2},{3,0},{2,1},{0,3},{5,6},{7,4},{6,5},{4,7},{9,10},{11,8},{10,... | collective-permute-start | bytes 73736 | tf_op jit(solution)/shard_map/ppermute | solution.py:404
  7.6 4.3 %collective-permute-done.1.from_second.col_second = bf16[96,128]{1,0:T(8,128)(2,1)S(1)} collective-permute-done((bf16[96,128]{1,0:T(8,128)(2,1)S(1)}, bf16[96,128]{1,0:T(8,128)(2,1)S(1)}, u32[]{:S(2)}, u32[]{:S(2)}) %collective-permute-start.1) | collective-permute-done | bytes 24608 | tf_op jit(solution)/shard_map/ppermute | solution.py:404
  11.9 0.0 copy-done.1
  11.9 0.0 collective-permute-start.4
  11.9 0.0 collective-permute-done.from_first.col_first.rest_1_
  11.9 0.2 mid.1
  12.1 1.6 %collective-permute-start.5 = (bf16[512,128]{1,0:T(8,128)(2,1)S(1)}, bf16[512,128]{1,0:T(8,128)(2,1)S(1)}, u32[]{:S(2)}, u32[]{:S(2)}) collective-permute-start(bf16[512,128]{1,0:T(8,128)(2,1)S(1)} %bitcast.3), channel_id=1, source_target_pairs={{0,3},{1,2},{2,1},{3,0},{4,7},{5,6},{6,5},{7,4},{8,11},{9,10},{10,... | collective-permute-start | bytes 393224 | tf_op jit(solution)/shard_map/ppermute | solution.py:420
  13.8 0.0 collective-permute-start.2
  13.8 1.6 %collective-permute-start.3 = (bf16[48,640]{1,0:T(8,128)(2,1)S(1)}, bf16[48,640]{1,0:T(8,128)(2,1)S(1)}, u32[]{:S(2)}, u32[]{:S(2)}) collective-permute-start(bf16[48,640]{1,0:T(8,128)(2,1)S(1)} %get-tuple-element.31), channel_id=1, source_target_pairs={{4,8},{12,0},{8,4},{0,12},{5,9},{13,1},{9,5},{1,13},{6,10},{14,2},... | collective-permute-start | bytes 184328 | tf_op jit(solution)/shard_map/ppermute | solution.py:422
  15.4 0.0 copy-done
  15.4 0.4 %own.1 = (f32[3,256,256]{2,1,0:T(8,128)S(1)}, f32[12,8,128]{2,1,0:T(8,128)S(1)}, f32[12,8,128]{2,1,0:T(8,128)S(1)}, bf16[256,256]{1,0:T(8,128)(2,1)S(1)}, bf16[256,256]{1,0:T(8,128)(2,1)S(1)}) custom-call(s32[256,512]{1,0:T(8,128)S(1)} %copy-done, bf16[2,12,2,33]{3,2,1,0:T(2,128)(2,1)S(1)} %get-tuple-element.23.taps), custom_call_target="tpu_custom_call" | custom-call | flops 1000000 | bytes 1000000 | tf_op jit(solution)/shard_map/own/pallas_call | solution.py:425
  15.8 0.0 collective-permute-done.2.row_first
  15.8 1.6 %collective-permute-done.3.row_second = bf16[48,640]{1,0:T(8,128)(2,1)S(1)} collective-permute-done((bf16[48,640]{1,0:T(8,128)(2,1)S(1)}, bf16[48,640]{1,0:T(8,128)(2,1)S(1)}, u32[]{:S(2)}, u32[]{:S(2)}) %collective-permute-start.3) | collective-permute-done | bytes 61472 | tf_op jit(solution)/shard_map/ppermute | solution.py:422
  17.4 6.0 %socs.1 = (f32[4,176,256]{2,1,0:T(8,128)S(1)}, s32[16,128]{1,0:T(8,128)S(1)}) custom-call(f32[12]{0:T(128)} %weights.1, f32[3,256,256]{2,1,0:T(8,128)S(1)} %get-tuple-element.24.windows, bf16[48,640]{1,0:T(8,128)(2,1)S(1)} %collective-permute-done.2.row_first, bf16[48,640]{1,0:T(8,128)(2,1)S(1)} %collective-permute-done.3.row_second, ...), custom_call_target="tpu_custom_call" | custom-call | flops 1000000 | bytes 100000 | tf_op jit(solution)/shard_map/socs/pallas_call | solution.py:441
  23.4 0.0 collective-permute-done.4.rest_2_
  23.4 0.0 collective-permute-done.5.rest_3_
  23.5 2.4 %final.1 = f32[256,512]{1,0:T(8,128)} custom-call(f32[4,176,256]{2,1,0:T(8,128)S(1)} %get-tuple-element.35.acc, s32[16,128]{1,0:T(8,128)S(1)} %get-tuple-element.36.images, bf16[256,256]{1,0:T(8,128)(2,1)S(1)} %get-tuple-element.37.g_row, bf16[256,256]{1,0:T(8,128)(2,1)S(1)} %get-tuple-element.38.g_col, bf16[512,128]{1,0:T(8,128)(2,1)S(1)} %bitcast.4, ...), custom_call_target="tpu_custom_call" | custom-call | tf_op jit(solution)/shard_map/final/pallas_call | solution.py:459
Async XLA Ops:
  0.7 11.2 %copy-start.1 = (bf16[8,64,128]{2,1,0:T(8,128)(2,1)S(1)}, bf16[8,64,128]{2,1,0:T(8,128)(2,1)}, u32[]{:S(2)}) copy-start(bf16[8,64,128]{2,1,0:T(8,128)(2,1)} %param.12) | copy-start | bytes 393220
  0.7 14.7 %copy-start = (s32[256,512]{1,0:T(8,128)S(1)}, s32[256,512]{1,0:T(8,128)}, u32[]{:S(2)}) copy-start(s32[256,512]{1,0:T(8,128)} %mask.3) | copy-start | bytes 1572868
  2.1 9.8 %collective-permute-start = (bf16[608,128]{1,0:T(8,128)(2,1)S(1)}, bf16[608,128]{1,0:T(8,128)(2,1)S(1)}, u32[]{:S(2)}, u32[]{:S(2)}) collective-permute-start(bf16[608,128]{1,0:T(8,128)(2,1)S(1)} %get-tuple-element.26.own), channel_id=1, source_target_pairs={{0,1},{2,3},{1,0},{3,2},{4,5},{6,7},{5,4},{7,6},{8,9},{10,11},{9,8... | collective-permute-start | bytes 466952 | tf_op jit(solution)/shard_map/ppermute | solution.py:405
  5.1 6.7 %collective-permute-start.1 = (bf16[96,128]{1,0:T(8,128)(2,1)S(1)}, bf16[96,128]{1,0:T(8,128)(2,1)S(1)}, u32[]{:S(2)}, u32[]{:S(2)}) collective-permute-start(bf16[96,128]{1,0:T(8,128)(2,1)S(1)} %get-tuple-element.27), channel_id=1, source_target_pairs={{1,2},{3,0},{2,1},{0,3},{5,6},{7,4},{6,5},{4,7},{9,10},{11,8},{10,... | collective-permute-start | bytes 73736 | tf_op jit(solution)/shard_map/ppermute | solution.py:404
  11.9 11.6 %collective-permute-start.4 = (bf16[512,128]{1,0:T(8,128)(2,1)S(1)}, bf16[512,128]{1,0:T(8,128)(2,1)S(1)}, u32[]{:S(2)}, u32[]{:S(2)}) collective-permute-start(bf16[512,128]{1,0:T(8,128)(2,1)S(1)} %bitcast.2), channel_id=1, source_target_pairs={{0,2},{1,3},{2,0},{3,1},{4,6},{5,7},{6,4},{7,5},{8,10},{9,11},{10,... | collective-permute-start | bytes 393224 | tf_op jit(solution)/shard_map/ppermute | solution.py:420
  12.1 11.3 %collective-permute-start.5 = (bf16[512,128]{1,0:T(8,128)(2,1)S(1)}, bf16[512,128]{1,0:T(8,128)(2,1)S(1)}, u32[]{:S(2)}, u32[]{:S(2)}) collective-permute-start(bf16[512,128]{1,0:T(8,128)(2,1)S(1)} %bitcast.3), channel_id=1, source_target_pairs={{0,3},{1,2},{2,1},{3,0},{4,7},{5,6},{6,5},{7,4},{8,11},{9,10},{10,... | collective-permute-start | bytes 393224 | tf_op jit(solution)/shard_map/ppermute | solution.py:420
  13.8 2.0 %collective-permute-start.2 = (bf16[48,640]{1,0:T(8,128)(2,1)S(1)}, bf16[48,640]{1,0:T(8,128)(2,1)S(1)}, u32[]{:S(2)}, u32[]{:S(2)}) collective-permute-start(bf16[48,640]{1,0:T(8,128)(2,1)S(1)} %get-tuple-element.30), channel_id=1, source_target_pairs={{0,4},{8,12},{4,0},{12,8},{1,5},{9,13},{5,1},{13,9},{2,6},{10,14},... | collective-permute-start | bytes 184328 | tf_op jit(solution)/shard_map/ppermute | solution.py:422
  13.8 3.6 %collective-permute-start.3 = (bf16[48,640]{1,0:T(8,128)(2,1)S(1)}, bf16[48,640]{1,0:T(8,128)(2,1)S(1)}, u32[]{:S(2)}, u32[]{:S(2)}) collective-permute-start(bf16[48,640]{1,0:T(8,128)(2,1)S(1)} %get-tuple-element.31), channel_id=1, source_target_pairs={{4,8},{12,0},{8,4},{0,12},{5,9},{13,1},{9,5},{1,13},{6,10},{14,2},... | collective-permute-start | bytes 184328 | tf_op jit(solution)/shard_map/ppermute | solution.py:422

commit v8 on v7

--- a/solution.py
+++ b/solution.py
@@ -20,7 +20,7 @@
 EDGE_OUT = 48
 RIGHT_AT = 56
 HALF_STRIP = STRIP + 16
-GROUP = 2
+GROUP = 4
 WIDE = 640
 SLOTS = 16
 F32 = jnp.float32
@@ -412,12 +412,9 @@
         compiler_params=PARAMS,
         name="mid",
     )(edges, col_first, col_second, to_first)
+    library, to_first, to_second = lax.optimization_barrier((library, to_first, to_second))
     for d in range(2, n_col):
-        if d == 2:
-            block, col_second = lax.optimization_barrier((library, col_second))
-        if d == 3:
-            block, to_above, to_below = lax.optimization_barrier((library, to_above, to_below))
-        shards.append(lax.ppermute(block, "col", [(i, i ^ d) for i in range(n_col)]))
+        shards.append(lax.ppermute(library, "col", [(i, i ^ d) for i in range(n_col)]))
     row_first, row_second = (
         lax.ppermute(x, "row", pairs) for x, pairs in zip((to_above, to_below), swaps(n_row))
     )
@@ -452,7 +449,7 @@
         + [pltpu.VMEM((2 * GROUP, 256, 256), BF16)] * 2
         + [pltpu.VMEM((2 * GROUP, NB + 1, CB, 256), BF16)] * 2,
         compiler_params=PARAMS,
-        cost_estimate=pl.CostEstimate(flops=10**6, bytes_accessed=10**5, transcendentals=0),
+        cost_estimate=pl.CostEstimate(flops=6 * 10**8, bytes_accessed=10**5, transcendentals=0),
         name="socs",
     )(in_hbm(kernel_weights), windows, row_first, row_second, col_first, col_second, to_first, ahead, back)
 

time: 26.3 us -> 26.2 us (level)
  waiting for transfers between devices: 5.87 us -> 4.23 us
  starting transfers between devices: 8.8 us -> 10.3 us
    ppermute x1, waiting for transfers between devices: 4.26 us -> 2.47 us  [on_device(): col_second = lax.ppermute(to_second, 'col', pairs[1])]
    ppermute x2, starting transfers between devices: 1.63 us -> 3.04 us  [on_device(): lax.ppermute(library, 'col', [(i, i ^ d) for i in range(n_col)])]
where the time goes in v8:
time: 26.2 us; the launch traced here: 25.8 us
  Pallas kernels  10.6 us (40%)
  starting transfers between devices  10.3 us (39%)
  waiting for transfers between devices  4.23 us (16%)
  between operations  0.73 us (3%)
    pallas_call x1, Pallas kernels, on_device(): pl.pallas_call(functools.partial(socs_kernel, entries, per), out_shape=(s...  6.15 us
    ppermute x1, starting transfers between devices, on_device(): col_first = lax.ppermute(to_first, 'col', pairs[0])  3.09 us
    ppermute x2, starting transfers between devices, on_device(): lax.ppermute(library, 'col', [(i, i ^ d) for i in range(n_col)])  3.04 us
    ppermute x1, starting transfers between devices, on_device(): col_second = lax.ppermute(to_second, 'col', pairs[1])  2.47 us
    ppermute x1, waiting for transfers between devices, on_device(): col_second = lax.ppermute(to_second, 'col', pairs[1])  2.47 us
    pallas_call x1, Pallas kernels, on_device(): pl.pallas_call(functools.partial(final_kernel, n_row, n_col), out_shape=s...  2.38 us
    ppermute x2, waiting for transfers between devices, on_device(): lax.ppermute(x, 'row', pairs)  1.75 us
    ppermute x2, starting transfers between devices, on_device(): lax.ppermute(x, 'row', pairs)  1.68 us
  transfers between devices with their start and end apart: 6, of which 2 were waited for; matrix products, arithmetic and copies ran while one was open for 0% of the time, Pallas kernels for 26%

profile of v8, /device:TPU:0, one launch (start us, length us, event | category | flops | bytes accessed | tf_op | source)
XLA Modules:
  0.0 25.8 jit_solution(1522189579894173748)
XLA Ops:
  0.7 0.0 copy-start.1
  0.7 0.0 copy-start
  0.7 1.4 %prep.1 = (bf16[608,128]{1,0:T(8,128)(2,1)S(1)}, bf16[96,128]{1,0:T(8,128)(2,1)S(1)}, s32[2,32,512]{2,1,0:T(8,128)S(1)}, bf16[2,12,2,33]{3,2,1,0:T(2,128)(2,1)S(1)}) custom-call(s32[256,512]{1,0:T(8,128)} %mask.3, s32[1,1,8]{2,1,0:T(1,128)} %ids.1, s32[1,1,8]{2,1,0:T(1,128)} %slots.1, s32[1,1]{1,0:T(1,128)S(6)} %copy.9.count, bf16[12,2,33]{2,1,0:T(2,128)(2,1)} %across.1, ...), custom_call_target="tpu_custom_call" | custom-call | tf_op jit(solution)/shard_map/prep/pallas_call | solution.py:376
  2.1 3.1 %collective-permute-start = (bf16[608,128]{1,0:T(8,128)(2,1)S(1)}, bf16[608,128]{1,0:T(8,128)(2,1)S(1)}, u32[]{:S(2)}, u32[]{:S(2)}) collective-permute-start(bf16[608,128]{1,0:T(8,128)(2,1)S(1)} %get-tuple-element.27.own), channel_id=1, source_target_pairs={{0,1},{2,3},{1,0},{3,2},{4,5},{6,7},{5,4},{7,6},{8,9},{10,11},{9,8... | collective-permute-start | bytes 466952 | tf_op jit(solution)/shard_map/ppermute | solution.py:405
  5.1 2.5 %collective-permute-start.1 = (bf16[96,128]{1,0:T(8,128)(2,1)S(1)}, bf16[96,128]{1,0:T(8,128)(2,1)S(1)}, u32[]{:S(2)}, u32[]{:S(2)}) collective-permute-start(bf16[96,128]{1,0:T(8,128)(2,1)S(1)} %get-tuple-element.24), channel_id=1, source_target_pairs={{1,2},{3,0},{2,1},{0,3},{5,6},{7,4},{6,5},{4,7},{9,10},{11,8},{10,... | collective-permute-start | bytes 73736 | tf_op jit(solution)/shard_map/ppermute | solution.py:404
  7.6 0.0 copy-done.1
  7.6 0.1 collective-permute-start.4
  7.7 2.9 %collective-permute-start.5 = (bf16[512,128]{1,0:T(8,128)(2,1)S(1)}, bf16[512,128]{1,0:T(8,128)(2,1)S(1)}, u32[]{:S(2)}, u32[]{:S(2)}) collective-permute-start(bf16[512,128]{1,0:T(8,128)(2,1)S(1)} %bitcast.3), channel_id=1, source_target_pairs={{0,3},{1,2},{2,1},{3,0},{4,7},{5,6},{6,5},{7,4},{8,11},{9,10},{10,... | collective-permute-start | bytes 393224 | tf_op jit(solution)/shard_map/ppermute | solution.py:417
  10.7 2.5 %collective-permute-done.1.from_second.col_second = bf16[96,128]{1,0:T(8,128)(2,1)S(1)} collective-permute-done((bf16[96,128]{1,0:T(8,128)(2,1)S(1)}, bf16[96,128]{1,0:T(8,128)(2,1)S(1)}, u32[]{:S(2)}, u32[]{:S(2)}) %collective-permute-start.1) | collective-permute-done | bytes 24608 | tf_op jit(solution)/shard_map/ppermute | solution.py:404
  13.1 0.0 collective-permute-done.from_first.col_first.rest_1_
  13.1 0.2 mid.1
  13.4 0.1 collective-permute-start.2
  13.4 1.6 %collective-permute-start.3 = (bf16[48,640]{1,0:T(8,128)(2,1)S(1)}, bf16[48,640]{1,0:T(8,128)(2,1)S(1)}, u32[]{:S(2)}, u32[]{:S(2)}) collective-permute-start(bf16[48,640]{1,0:T(8,128)(2,1)S(1)} %get-tuple-element.26), channel_id=1, source_target_pairs={{4,8},{12,0},{8,4},{0,12},{5,9},{13,1},{9,5},{1,13},{6,10},{14,2},... | collective-permute-start | bytes 184328 | tf_op jit(solution)/shard_map/ppermute | solution.py:419
  15.0 0.0 copy-done
  15.0 0.4 %own.1 = (f32[3,256,256]{2,1,0:T(8,128)S(1)}, f32[12,8,128]{2,1,0:T(8,128)S(1)}, f32[12,8,128]{2,1,0:T(8,128)S(1)}, bf16[256,256]{1,0:T(8,128)(2,1)S(1)}, bf16[256,256]{1,0:T(8,128)(2,1)S(1)}) custom-call(s32[256,512]{1,0:T(8,128)S(1)} %copy-done, bf16[2,12,2,33]{3,2,1,0:T(2,128)(2,1)S(1)} %get-tuple-element.20.taps), custom_call_target="tpu_custom_call" | custom-call | flops 1000000 | bytes 1000000 | tf_op jit(solution)/shard_map/own/pallas_call | solution.py:422
  15.5 0.0 collective-permute-done.2.row_first
  15.5 1.7 %collective-permute-done.3.row_second = bf16[48,640]{1,0:T(8,128)(2,1)S(1)} collective-permute-done((bf16[48,640]{1,0:T(8,128)(2,1)S(1)}, bf16[48,640]{1,0:T(8,128)(2,1)S(1)}, u32[]{:S(2)}, u32[]{:S(2)}) %collective-permute-start.3) | collective-permute-done | bytes 61472 | tf_op jit(solution)/shard_map/ppermute | solution.py:419
  17.2 6.2 %socs.1 = (f32[4,176,256]{2,1,0:T(8,128)S(1)}, s32[16,128]{1,0:T(8,128)S(1)}) custom-call(f32[12]{0:T(128)} %weights.1, f32[3,256,256]{2,1,0:T(8,128)S(1)} %get-tuple-element.21.windows, bf16[48,640]{1,0:T(8,128)(2,1)S(1)} %collective-permute-done.2.row_first, bf16[48,640]{1,0:T(8,128)(2,1)S(1)} %collective-permute-done.3.row_second, ...), custom_call_target="tpu_custom_call" | custom-call | flops 600000000 | bytes 100000 | tf_op jit(solution)/shard_map/socs/pallas_call | solution.py:438
  23.4 0.0 collective-permute-done.4.rest_2_
  23.4 0.0 collective-permute-done.5.rest_3_
  23.4 2.4 %final.1 = f32[256,512]{1,0:T(8,128)} custom-call(f32[4,176,256]{2,1,0:T(8,128)S(1)} %get-tuple-element.30.acc, s32[16,128]{1,0:T(8,128)S(1)} %get-tuple-element.31.images, bf16[256,256]{1,0:T(8,128)(2,1)S(1)} %get-tuple-element.32.g_row, bf16[256,256]{1,0:T(8,128)(2,1)S(1)} %get-tuple-element.33.g_col, bf16[512,128]{1,0:T(8,128)(2,1)S(1)} %bitcast.4, ...), custom_call_target="tpu_custom_call" | custom-call | tf_op jit(solution)/shard_map/final/pallas_call | solution.py:456
Async XLA Ops:
  0.7 7.0 %copy-start.1 = (bf16[8,64,128]{2,1,0:T(8,128)(2,1)S(1)}, bf16[8,64,128]{2,1,0:T(8,128)(2,1)}, u32[]{:S(2)}) copy-start(bf16[8,64,128]{2,1,0:T(8,128)(2,1)} %param.12) | copy-start | bytes 393220
  0.7 14.4 %copy-start = (s32[256,512]{1,0:T(8,128)S(1)}, s32[256,512]{1,0:T(8,128)}, u32[]{:S(2)}) copy-start(s32[256,512]{1,0:T(8,128)} %mask.3) | copy-start | bytes 1572868
  2.1 11.1 %collective-permute-start = (bf16[608,128]{1,0:T(8,128)(2,1)S(1)}, bf16[608,128]{1,0:T(8,128)(2,1)S(1)}, u32[]{:S(2)}, u32[]{:S(2)}) collective-permute-start(bf16[608,128]{1,0:T(8,128)(2,1)S(1)} %get-tuple-element.27.own), channel_id=1, source_target_pairs={{0,1},{2,3},{1,0},{3,2},{4,5},{6,7},{5,4},{7,6},{8,9},{10,11},{9,8... | collective-permute-start | bytes 466952 | tf_op jit(solution)/shard_map/ppermute | solution.py:405
  5.1 8.0 %collective-permute-start.1 = (bf16[96,128]{1,0:T(8,128)(2,1)S(1)}, bf16[96,128]{1,0:T(8,128)(2,1)S(1)}, u32[]{:S(2)}, u32[]{:S(2)}) collective-permute-start(bf16[96,128]{1,0:T(8,128)(2,1)S(1)} %get-tuple-element.24), channel_id=1, source_target_pairs={{1,2},{3,0},{2,1},{0,3},{5,6},{7,4},{6,5},{4,7},{9,10},{11,8},{10,... | collective-permute-start | bytes 73736 | tf_op jit(solution)/shard_map/ppermute | solution.py:404
  7.6 15.8 %collective-permute-start.4 = (bf16[512,128]{1,0:T(8,128)(2,1)S(1)}, bf16[512,128]{1,0:T(8,128)(2,1)S(1)}, u32[]{:S(2)}, u32[]{:S(2)}) collective-permute-start(bf16[512,128]{1,0:T(8,128)(2,1)S(1)} %bitcast.2), channel_id=1, source_target_pairs={{0,2},{1,3},{2,0},{3,1},{4,6},{5,7},{6,4},{7,5},{8,10},{9,11},{10,... | collective-permute-start | bytes 393224 | tf_op jit(solution)/shard_map/ppermute | solution.py:417
  7.7 15.7 %collective-permute-start.5 = (bf16[512,128]{1,0:T(8,128)(2,1)S(1)}, bf16[512,128]{1,0:T(8,128)(2,1)S(1)}, u32[]{:S(2)}, u32[]{:S(2)}) collective-permute-start(bf16[512,128]{1,0:T(8,128)(2,1)S(1)} %bitcast.3), channel_id=1, source_target_pairs={{0,3},{1,2},{2,1},{3,0},{4,7},{5,6},{6,5},{7,4},{8,11},{9,10},{10,... | collective-permute-start | bytes 393224 | tf_op jit(solution)/shard_map/ppermute | solution.py:417
  13.4 2.1 %collective-permute-start.2 = (bf16[48,640]{1,0:T(8,128)(2,1)S(1)}, bf16[48,640]{1,0:T(8,128)(2,1)S(1)}, u32[]{:S(2)}, u32[]{:S(2)}) collective-permute-start(bf16[48,640]{1,0:T(8,128)(2,1)S(1)} %get-tuple-element.25), channel_id=1, source_target_pairs={{0,4},{8,12},{4,0},{12,8},{1,5},{9,13},{5,1},{13,9},{2,6},{10,14},... | collective-permute-start | bytes 184328 | tf_op jit(solution)/shard_map/ppermute | solution.py:419
  13.4 3.8 %collective-permute-start.3 = (bf16[48,640]{1,0:T(8,128)(2,1)S(1)}, bf16[48,640]{1,0:T(8,128)(2,1)S(1)}, u32[]{:S(2)}, u32[]{:S(2)}) collective-permute-start(bf16[48,640]{1,0:T(8,128)(2,1)S(1)} %get-tuple-element.26), channel_id=1, source_target_pairs={{4,8},{12,0},{8,4},{0,12},{5,9},{13,1},{9,5},{1,13},{6,10},{14,2},... | collective-permute-start | bytes 184328 | tf_op jit(solution)/shard_map/ppermute | solution.py:419

commit v9 on v8

--- a/solution.py
+++ b/solution.py
@@ -58,7 +58,7 @@
 
 
 def prep_kernel(
-    mask, ids, slots, count, across, down, library, to_first, to_second, edges, taps, ends, a_ids, a_slots, sems
+    mask, ids, slots, count, across, down, library, to_first, to_second, taps, ends, a_ids, a_slots, sems
 ):
     rows, cols = mask.shape
     copies = [
@@ -66,11 +66,9 @@
         pltpu.make_async_copy(mask.at[:, cols - 128 : cols], ends.at[1], sems.at[1]),
         pltpu.make_async_copy(ids, a_ids, sems.at[2]),
         pltpu.make_async_copy(slots, a_slots, sems.at[3]),
-        pltpu.make_async_copy(mask.at[0:STRIP], edges.at[0], sems.at[4]),
-        pltpu.make_async_copy(mask.at[rows - STRIP : rows], edges.at[1], sems.at[5]),
-        pltpu.make_async_copy(across, taps.at[0], sems.at[6]),
-        pltpu.make_async_copy(down, taps.at[1], sems.at[7]),
-        pltpu.make_async_copy(library, to_first.at[2 * HALF_STRIP :], sems.at[8]),
+        pltpu.make_async_copy(across, taps.at[0], sems.at[4]),
+        pltpu.make_async_copy(down, taps.at[1], sems.at[5]),
+        pltpu.make_async_copy(library, to_first.at[2 * HALF_STRIP :], sems.at[6]),
     ]
     for copy in copies:
         copy.start()
@@ -84,7 +82,7 @@
         x = jnp.concatenate([x, jnp.zeros((1, 128 - x.shape[1]), F32)], axis=1)
         return jnp.broadcast_to(x, (16, 128))
 
-    table = jnp.where(line == 1, spread(a_slots[0]), count[0, 0].astype(F32))
+    table = jnp.where(line == 1, spread(a_slots[0]), jnp.broadcast_to(count[...].astype(F32), (16, 128)))
     table = jnp.where(line == 0, spread(a_ids[0]), table)
     width = jnp.where(line == 2, 1, ids.shape[2])
     table = jnp.where((lane < width) & (line < 3), table, 0.0).astype(BF16)
@@ -103,9 +101,8 @@
         copy.wait()
 
 
-def mid_kernel(edges, from_first, from_second, own, to_first, to_second):
-    cols = edges.shape[2]
-    rows = 256
+def mid_kernel(mask, from_first, from_second, own, to_first, to_second):
+    rows, cols = mask.shape
     left, right = sides("col", join(from_first), join(from_second))
     tables = jnp.concatenate(
         [left[STRIP:, 0:128], own[STRIP:HALF_STRIP, :].astype(F32), right[STRIP:, 0:128], jnp.zeros((16, 256), F32)],
@@ -120,7 +117,7 @@
         def turned(strip):
             return dot_nt(pick, jnp.concatenate([strip[0:STRIP, at : at + 128], fill], axis=0).astype(BF16))
 
-        parts = [turned(left)[:, STRIP - RIM : STRIP], edges[i].astype(F32), turned(right)[:, 0 : WIDE - RIM - cols]]
+        parts = [turned(left)[:, STRIP - RIM : STRIP], mask[(rows - STRIP) * i : (rows - STRIP) * i + STRIP, :].astype(F32), turned(right)[:, 0 : WIDE - RIM - cols]]
         strips.append(jnp.concatenate(parts, axis=1))
     even = lax.rem(lax.axis_index("row"), 2) == 0
     to_first[0:STRIP, :] = jnp.where(even, strips[1], strips[0]).astype(BF16)
@@ -373,21 +370,20 @@
     in_hbm = lambda x: pltpu.with_memory_space_constraint(x, pltpu.HBM)
     mask_hbm = in_hbm(mask_pixels)
 
-    to_first, to_second, edges, taps = pl.pallas_call(
+    to_first, to_second, taps = pl.pallas_call(
         prep_kernel,
         out_shape=(
             shape((2 * HALF_STRIP + per * 64, 128), BF16),
             shape((2 * HALF_STRIP, 128), BF16),
-            shape((2, STRIP, cols), jnp.int32),
             shape((2,) + across_taps.shape, BF16),
         ),
-        in_specs=[HBM] * 3 + [SMEM] + [HBM] * 3,
-        out_specs=(VMEM,) * 4,
+        in_specs=[HBM] * 3 + [VMEM] + [HBM] * 3,
+        out_specs=(VMEM,) * 3,
         scratch_shapes=[
             pltpu.VMEM((2, rows, 128), jnp.int32),
             pltpu.VMEM(cell_ids.shape, jnp.int32),
             pltpu.VMEM(cell_slots.shape, jnp.int32),
-            pltpu.SemaphoreType.DMA((9,)),
+            pltpu.SemaphoreType.DMA((7,)),
         ],
         compiler_params=PARAMS,
         name="prep",
@@ -396,8 +392,10 @@
     def swaps(n):
         rounds = []
         for start in (0, 1):
-            pairs = [(i, (i + 1) % n) for i in range(start, n, 2)]
-            rounds.append(pairs + [(b, a) for a, b in pairs])
+            pairs = [(i, i + 1) for i in range(start, n - 1, 2)]
+            pairs += [(b, a) for a, b in pairs]
+            rest = set(range(n)) - {a for a, b in pairs}
+            rounds.append(pairs + [(i, i) for i in sorted(rest)])
         return rounds
 
     pairs = swaps(n_col)
@@ -411,10 +409,11 @@
         out_specs=(VMEM,) * 2,
         compiler_params=PARAMS,
         name="mid",
-    )(edges, col_first, col_second, to_first)
-    library, to_first, to_second = lax.optimization_barrier((library, to_first, to_second))
+    )(mask_pixels, col_first, col_second, to_first)
+    late, to_above, to_below = lax.optimization_barrier((library, to_above, to_below))
     for d in range(2, n_col):
-        shards.append(lax.ppermute(library, "col", [(i, i ^ d) for i in range(n_col)]))
+        block = to_first if d < n_col - 1 else late
+        shards.append(lax.ppermute(block, "col", [(i, i ^ d) for i in range(n_col)]))
     row_first, row_second = (
         lax.ppermute(x, "row", pairs) for x, pairs in zip((to_above, to_below), swaps(n_row))
     )
@@ -449,7 +448,7 @@
         + [pltpu.VMEM((2 * GROUP, 256, 256), BF16)] * 2
         + [pltpu.VMEM((2 * GROUP, NB + 1, CB, 256), BF16)] * 2,
         compiler_params=PARAMS,
-        cost_estimate=pl.CostEstimate(flops=6 * 10**8, bytes_accessed=10**5, transcendentals=0),
+        cost_estimate=pl.CostEstimate(flops=8 * 10**8, bytes_accessed=10**5, transcendentals=0),
         name="socs",
     )(in_hbm(kernel_weights), windows, row_first, row_second, col_first, col_second, to_first, ahead, back)
 

time: 26.2 us -> 28.2 us (1.076)
  the two profiles are of different devices: /device:TPU:0 before, /device:TPU:17 now
where the time goes in v9:
time: 28.2 us; the launch traced here: 28.1 us
  starting transfers between devices  12 us (43%)
  Pallas kernels  10.5 us (37%)
  waiting for transfers between devices  4.77 us (17%)
  between operations  0.8 us (3%)
    ppermute x2, starting transfers between devices, on_device(): lax.ppermute(x, 'row', pairs)  8.47 us
    pallas_call x1, Pallas kernels, on_device(): pl.pallas_call(functools.partial(socs_kernel, entries, per), out_shape=(s...  6.15 us
    ppermute x1, waiting for transfers between devices, on_device(): col_second = lax.ppermute(to_second, 'col', pairs[1])  2.62 us
    pallas_call x1, Pallas kernels, on_device(): pl.pallas_call(functools.partial(final_kernel, n_row, n_col), out_shape=s...  2.38 us
    ppermute x2, waiting for transfers between devices, on_device(): lax.ppermute(x, 'row', pairs)  2.14 us
    ppermute x1, starting transfers between devices, on_device(): col_second = lax.ppermute(to_second, 'col', pairs[1])  2.04 us
    ppermute x1, starting transfers between devices, on_device(): col_first = lax.ppermute(to_first, 'col', pairs[0])  1.36 us
    pallas_call x1, Pallas kernels, on_device(): pl.pallas_call(prep_kernel, out_shape=(shape((2 * HALF_STRIP + per * 64,...  1.29 us
  transfers between devices with their start and end apart: 6, of which 2 were waited for; matrix products, arithmetic and copies ran while one was open for 0% of the time, Pallas kernels for 24%

profile of v9, /device:TPU:17, one launch (start us, length us, event | category | flops | bytes accessed | tf_op | source)
XLA Modules:
  0.0 28.1 jit_solution(16570591747151218381)
XLA Ops:
  0.0 0.0 copy-start
  0.7 1.3 %prep.1 = (bf16[608,128]{1,0:T(8,128)(2,1)S(1)}, bf16[96,128]{1,0:T(8,128)(2,1)S(1)}, bf16[2,12,2,33]{3,2,1,0:T(2,128)(2,1)S(1)}) custom-call(s32[256,512]{1,0:T(8,128)} %mask.5, s32[1,1,8]{2,1,0:T(1,128)} %ids.1, s32[1,1,8]{2,1,0:T(1,128)} %slots.1, s32[1,1]{1,0:T(1,128)S(6)} %copy.9.count, bf16[12,2,33]{2,1,0:T(2,128)(2,1)} %across.1, ...), custom_call_target="tpu_custom_call" | custom-call | tf_op jit(solution)/shard_map/prep/pallas_call | solution.py:373
  2.0 1.4 %collective-permute-start = (bf16[608,128]{1,0:T(8,128)(2,1)S(1)}, bf16[608,128]{1,0:T(8,128)(2,1)S(1)}, u32[]{:S(2)}, u32[]{:S(2)}) collective-permute-start(bf16[608,128]{1,0:T(8,128)(2,1)S(1)} %get-tuple-element.22.own), channel_id=1, source_target_pairs={{0,1},{2,3},{1,0},{3,2},{4,5},{6,7},{5,4},{7,6},{8,9},{10,11},{9,8... | collective-permute-start | bytes 466952 | tf_op jit(solution)/shard_map/ppermute | solution.py:403
  3.4 0.0 copy-start.1
  3.4 2.0 %collective-permute-start.1 = (bf16[96,128]{1,0:T(8,128)(2,1)S(1)}, bf16[96,128]{1,0:T(8,128)(2,1)S(1)}, u32[]{:S(2)}, u32[]{:S(2)}) collective-permute-start(bf16[96,128]{1,0:T(8,128)(2,1)S(1)} %get-tuple-element.23), channel_id=1, source_target_pairs={{1,2},{2,1},{0,0},{3,3},{5,6},{6,5},{4,4},{7,7},{9,10},{10,9},{8,8... | collective-permute-start | bytes 73736 | tf_op jit(solution)/shard_map/ppermute | solution.py:402
  5.4 0.1 collective-permute-start.4
  5.5 2.6 %collective-permute-done.1.from_second.col_second = bf16[96,128]{1,0:T(8,128)(2,1)S(1)} collective-permute-done((bf16[96,128]{1,0:T(8,128)(2,1)S(1)}, bf16[96,128]{1,0:T(8,128)(2,1)S(1)}, u32[]{:S(2)}, u32[]{:S(2)}) %collective-permute-start.1) | collective-permute-done | bytes 24608 | tf_op jit(solution)/shard_map/ppermute | solution.py:402
  8.1 0.0 collective-permute-done.from_first.col_first.rest_1_
  8.1 0.0 copy-done
  8.1 0.2 mid.1
  8.4 5.5 %collective-permute-start.2 = (bf16[48,640]{1,0:T(8,128)(2,1)S(1)}, bf16[48,640]{1,0:T(8,128)(2,1)S(1)}, u32[]{:S(2)}, u32[]{:S(2)}) collective-permute-start(bf16[48,640]{1,0:T(8,128)(2,1)S(1)} %get-tuple-element.26), channel_id=1, source_target_pairs={{0,4},{8,12},{4,0},{12,8},{1,5},{9,13},{5,1},{13,9},{2,6},{10,14},... | collective-permute-start | bytes 184328 | tf_op jit(solution)/shard_map/ppermute | solution.py:418
  13.8 3.0 %collective-permute-start.3 = (bf16[48,640]{1,0:T(8,128)(2,1)S(1)}, bf16[48,640]{1,0:T(8,128)(2,1)S(1)}, u32[]{:S(2)}, u32[]{:S(2)}) collective-permute-start(bf16[48,640]{1,0:T(8,128)(2,1)S(1)} %get-tuple-element.27), channel_id=1, source_target_pairs={{4,8},{8,4},{0,0},{12,12},{5,9},{9,5},{1,1},{13,13},{6,10},{10,6},... | collective-permute-start | bytes 184328 | tf_op jit(solution)/shard_map/ppermute | solution.py:418
  16.8 0.0 copy-done.1
  16.8 0.1 collective-permute-start.5
  16.9 0.4 %own.1 = (f32[3,256,256]{2,1,0:T(8,128)S(1)}, f32[12,8,128]{2,1,0:T(8,128)S(1)}, f32[12,8,128]{2,1,0:T(8,128)S(1)}, bf16[256,256]{1,0:T(8,128)(2,1)S(1)}, bf16[256,256]{1,0:T(8,128)(2,1)S(1)}) custom-call(s32[256,512]{1,0:T(8,128)S(1)} %copy-done, bf16[2,12,2,33]{3,2,1,0:T(2,128)(2,1)S(1)} %get-tuple-element.20.taps), custom_call_target="tpu_custom_call" | custom-call | flops 1000000 | bytes 1000000 | tf_op jit(solution)/shard_map/own/pallas_call | solution.py:421
  17.4 0.0 collective-permute-done.2.row_first
  17.4 2.1 %collective-permute-done.3.row_second = bf16[48,640]{1,0:T(8,128)(2,1)S(1)} collective-permute-done((bf16[48,640]{1,0:T(8,128)(2,1)S(1)}, bf16[48,640]{1,0:T(8,128)(2,1)S(1)}, u32[]{:S(2)}, u32[]{:S(2)}) %collective-permute-start.3) | collective-permute-done | bytes 61472 | tf_op jit(solution)/shard_map/ppermute | solution.py:418
  19.5 6.2 %socs.1 = (f32[4,176,256]{2,1,0:T(8,128)S(1)}, s32[16,128]{1,0:T(8,128)S(1)}) custom-call(f32[12]{0:T(128)} %weights.1, f32[3,256,256]{2,1,0:T(8,128)S(1)} %get-tuple-element.21.windows, bf16[48,640]{1,0:T(8,128)(2,1)S(1)} %collective-permute-done.2.row_first, bf16[48,640]{1,0:T(8,128)(2,1)S(1)} %collective-permute-done.3.row_second, ...), custom_call_target="tpu_custom_call" | custom-call | flops 800000000 | bytes 100000 | tf_op jit(solution)/shard_map/socs/pallas_call | solution.py:437
  25.7 0.0 collective-permute-done.4.rest_2_
  25.7 0.0 collective-permute-done.5.rest_3_
  25.7 2.4 %final.1 = f32[256,512]{1,0:T(8,128)} custom-call(f32[4,176,256]{2,1,0:T(8,128)S(1)} %get-tuple-element.30.acc, s32[16,128]{1,0:T(8,128)S(1)} %get-tuple-element.31.images, bf16[256,256]{1,0:T(8,128)(2,1)S(1)} %get-tuple-element.32.g_row, bf16[256,256]{1,0:T(8,128)(2,1)S(1)} %get-tuple-element.33.g_col, bf16[512,128]{1,0:T(8,128)(2,1)S(1)} %bitcast.3, ...), custom_call_target="tpu_custom_call" | custom-call | tf_op jit(solution)/shard_map/final/pallas_call | solution.py:455
Async XLA Ops:
  0.0 8.1 %copy-start = (s32[256,512]{1,0:T(8,128)S(1)}, s32[256,512]{1,0:T(8,128)}, u32[]{:S(2)}) copy-start(s32[256,512]{1,0:T(8,128)} %mask.5) | copy-start | bytes 1572868
  2.0 6.1 %collective-permute-start = (bf16[608,128]{1,0:T(8,128)(2,1)S(1)}, bf16[608,128]{1,0:T(8,128)(2,1)S(1)}, u32[]{:S(2)}, u32[]{:S(2)}) collective-permute-start(bf16[608,128]{1,0:T(8,128)(2,1)S(1)} %get-tuple-element.22.own), channel_id=1, source_target_pairs={{0,1},{2,3},{1,0},{3,2},{4,5},{6,7},{5,4},{7,6},{8,9},{10,11},{9,8... | collective-permute-start | bytes 466952 | tf_op jit(solution)/shard_map/ppermute | solution.py:403
  3.4 13.5 %copy-start.1 = (bf16[8,64,128]{2,1,0:T(8,128)(2,1)S(1)}, bf16[8,64,128]{2,1,0:T(8,128)(2,1)}, u32[]{:S(2)}) copy-start(bf16[8,64,128]{2,1,0:T(8,128)(2,1)} %param.12) | copy-start | bytes 393220
  3.4 4.7 %collective-permute-start.1 = (bf16[96,128]{1,0:T(8,128)(2,1)S(1)}, bf16[96,128]{1,0:T(8,128)(2,1)S(1)}, u32[]{:S(2)}, u32[]{:S(2)}) collective-permute-start(bf16[96,128]{1,0:T(8,128)(2,1)S(1)} %get-tuple-element.23), channel_id=1, source_target_pairs={{1,2},{2,1},{0,0},{3,3},{5,6},{6,5},{4,4},{7,7},{9,10},{10,9},{8,8... | collective-permute-start | bytes 73736 | tf_op jit(solution)/shard_map/ppermute | solution.py:402
  5.4 20.2 %collective-permute-start.4 = (bf16[608,128]{1,0:T(8,128)(2,1)S(1)}, bf16[608,128]{1,0:T(8,128)(2,1)S(1)}, u32[]{:S(2)}, u32[]{:S(2)}) collective-permute-start(bf16[608,128]{1,0:T(8,128)(2,1)S(1)} %get-tuple-element.22.own), channel_id=1, source_target_pairs={{0,2},{1,3},{2,0},{3,1},{4,6},{5,7},{6,4},{7,5},{8,10},{9,11},{10,... | collective-permute-start | bytes 466952 | tf_op jit(solution)/shard_map/ppermute | solution.py:416
  8.4 9.0 %collective-permute-start.2 = (bf16[48,640]{1,0:T(8,128)(2,1)S(1)}, bf16[48,640]{1,0:T(8,128)(2,1)S(1)}, u32[]{:S(2)}, u32[]{:S(2)}) collective-permute-start(bf16[48,640]{1,0:T(8,128)(2,1)S(1)} %get-tuple-element.26), channel_id=1, source_target_pairs={{0,4},{8,12},{4,0},{12,8},{1,5},{9,13},{5,1},{13,9},{2,6},{10,14},... | collective-permute-start | bytes 184328 | tf_op jit(solution)/shard_map/ppermute | solution.py:418
  13.8 5.7 %collective-permute-start.3 = (bf16[48,640]{1,0:T(8,128)(2,1)S(1)}, bf16[48,640]{1,0:T(8,128)(2,1)S(1)}, u32[]{:S(2)}, u32[]{:S(2)}) collective-permute-start(bf16[48,640]{1,0:T(8,128)(2,1)S(1)} %get-tuple-element.27), channel_id=1, source_target_pairs={{4,8},{8,4},{0,0},{12,12},{5,9},{9,5},{1,1},{13,13},{6,10},{10,6},... | collective-permute-start | bytes 184328 | tf_op jit(solution)/shard_map/ppermute | solution.py:418
  16.8 8.8 %collective-permute-start.5 = (bf16[512,128]{1,0:T(8,128)(2,1)S(1)}, bf16[512,128]{1,0:T(8,128)(2,1)S(1)}, u32[]{:S(2)}, u32[]{:S(2)}) collective-permute-start(bf16[512,128]{1,0:T(8,128)(2,1)S(1)} %bitcast.2), channel_id=1, source_target_pairs={{0,3},{1,2},{2,1},{3,0},{4,7},{5,6},{6,5},{7,4},{8,11},{9,10},{10,... | collective-permute-start | bytes 393224 | tf_op jit(solution)/shard_map/ppermute | solution.py:416

commit v10 on v9

--- a/solution.py
+++ b/solution.py
@@ -392,15 +392,17 @@
     def swaps(n):
         rounds = []
         for start in (0, 1):
-            pairs = [(i, i + 1) for i in range(start, n - 1, 2)]
-            pairs += [(b, a) for a, b in pairs]
-            rest = set(range(n)) - {a for a, b in pairs}
-            rounds.append(pairs + [(i, i) for i in sorted(rest)])
+            pairs = [(i, (i + 1) % n) for i in range(start, n, 2)]
+            rounds.append(pairs + [(b, a) for a, b in pairs])
         return rounds
 
-    pairs = swaps(n_col)
-    col_second = lax.ppermute(to_second, "col", pairs[1])
-    col_first = lax.ppermute(to_first, "col", pairs[0])
+    second = []
+    for r in range(n_row):
+        second += [(r * n_col + a, r * n_col + b) for a, b in swaps(n_col)[1] if abs(a - b) == 1]
+        second += [(r * n_col + a, (r ^ 1) * n_col + a) for a in (0, n_col - 1)]
+
+    col_second = lax.ppermute(to_second, ("row", "col"), second)
+    col_first = lax.ppermute(to_first, "col", swaps(n_col)[0])
     shards = [library, col_first]
     to_above, to_below = pl.pallas_call(
         mid_kernel,

time: 28.2 us -> 24.9 us (0.88)
  the two profiles are of different devices: /device:TPU:17 before, /device:TPU:0 now
where the time goes in v10:
time: 24.9 us; the launch traced here: 24.7 us
  starting transfers between devices  11.8 us (47%)
  Pallas kernels  10.5 us (42%)
  waiting for transfers between devices  1.7 us (7%)
  between operations  0.78 us (3%)
    ppermute x2, starting transfers between devices, on_device(): lax.ppermute(block, 'col', [(i, i ^ d) for i in range(n_col)])  6.8 us
    pallas_call x1, Pallas kernels, on_device(): pl.pallas_call(functools.partial(socs_kernel, entries, per), out_shape=(s...  6.15 us
    ppermute x1, starting transfers between devices, on_device(): col_first = lax.ppermute(to_first, 'col', swaps(n_col)[0])  3.09 us
    pallas_call x1, Pallas kernels, on_device(): pl.pallas_call(functools.partial(final_kernel, n_row, n_col), out_shape=s...  2.38 us
    ppermute x2, starting transfers between devices, on_device(): lax.ppermute(x, 'row', pairs)  1.89 us
    ppermute x1, waiting for transfers between devices, on_device(): col_first = lax.ppermute(to_first, 'col', swaps(n_col)[0])  1.68 us
    pallas_call x1, Pallas kernels, on_device(): pl.pallas_call(prep_kernel, out_shape=(shape((2 * HALF_STRIP + per * 64,...  1.29 us
  transfers between devices with their start and end apart: 6, of which 1 were waited for; matrix products, arithmetic and copies ran while one was open for 0% of the time, Pallas kernels for 28%

profile of v10, /device:TPU:0, one launch (start us, length us, event | category | flops | bytes accessed | tf_op | source)
XLA Modules:
  0.0 24.7 jit_solution(11905916168638029549)
XLA Ops:
  0.0 0.0 copy-start
  0.7 1.3 %prep.1 = (bf16[608,128]{1,0:T(8,128)(2,1)S(1)}, bf16[96,128]{1,0:T(8,128)(2,1)S(1)}, bf16[2,12,2,33]{3,2,1,0:T(2,128)(2,1)S(1)}) custom-call(s32[256,512]{1,0:T(8,128)} %mask.5, s32[1,1,8]{2,1,0:T(1,128)} %ids.1, s32[1,1,8]{2,1,0:T(1,128)} %slots.1, s32[1,1]{1,0:T(1,128)S(6)} %copy.9.count, bf16[12,2,33]{2,1,0:T(2,128)(2,1)} %across.1, ...), custom_call_target="tpu_custom_call" | custom-call | tf_op jit(solution)/shard_map/prep/pallas_call | solution.py:373
  2.0 3.1 %collective-permute-start = (bf16[608,128]{1,0:T(8,128)(2,1)S(1)}, bf16[608,128]{1,0:T(8,128)(2,1)S(1)}, u32[]{:S(2)}, u32[]{:S(2)}) collective-permute-start(bf16[608,128]{1,0:T(8,128)(2,1)S(1)} %get-tuple-element.22.own), channel_id=1, source_target_pairs={{0,1},{2,3},{1,0},{3,2},{4,5},{6,7},{5,4},{7,6},{8,9},{10,11},{9,8... | collective-permute-start | bytes 466952 | tf_op jit(solution)/shard_map/ppermute | solution.py:405
  5.1 0.0 copy-start.1
  5.1 0.0 collective-permute-start.1
  5.1 2.6 %collective-permute-start.4 = (bf16[608,128]{1,0:T(8,128)(2,1)S(1)}, bf16[608,128]{1,0:T(8,128)(2,1)S(1)}, u32[]{:S(2)}, u32[]{:S(2)}) collective-permute-start(bf16[608,128]{1,0:T(8,128)(2,1)S(1)} %get-tuple-element.22.own), channel_id=1, source_target_pairs={{0,2},{1,3},{2,0},{3,1},{4,6},{5,7},{6,4},{7,5},{8,10},{9,11},{10,... | collective-permute-start | bytes 466952 | tf_op jit(solution)/shard_map/ppermute | solution.py:418
  7.7 0.0 collective-permute-done.1.from_second.col_second
  7.7 1.7 %collective-permute-done.from_first.col_first.rest_1_ = bf16[608,128]{1,0:T(8,128)(2,1)S(1)} collective-permute-done((bf16[608,128]{1,0:T(8,128)(2,1)S(1)}, bf16[608,128]{1,0:T(8,128)(2,1)S(1)}, u32[]{:S(2)}, u32[]{:S(2)}) %collective-permute-start) | collective-permute-done | bytes 155680 | tf_op jit(solution)/shard_map/ppermute | solution.py:405
  9.4 0.0 copy-done
  9.4 0.2 mid.1
  9.6 0.1 collective-permute-start.2
  9.7 1.8 %collective-permute-start.3 = (bf16[48,640]{1,0:T(8,128)(2,1)S(1)}, bf16[48,640]{1,0:T(8,128)(2,1)S(1)}, u32[]{:S(2)}, u32[]{:S(2)}) collective-permute-start(bf16[48,640]{1,0:T(8,128)(2,1)S(1)} %get-tuple-element.27), channel_id=1, source_target_pairs={{4,8},{12,0},{8,4},{0,12},{5,9},{13,1},{9,5},{1,13},{6,10},{14,2},... | collective-permute-start | bytes 184328 | tf_op jit(solution)/shard_map/ppermute | solution.py:420
  11.5 0.0 copy-done.1
  11.5 4.2 %collective-permute-start.5 = (bf16[512,128]{1,0:T(8,128)(2,1)S(1)}, bf16[512,128]{1,0:T(8,128)(2,1)S(1)}, u32[]{:S(2)}, u32[]{:S(2)}) collective-permute-start(bf16[512,128]{1,0:T(8,128)(2,1)S(1)} %bitcast.2), channel_id=1, source_target_pairs={{0,3},{1,2},{2,1},{3,0},{4,7},{5,6},{6,5},{7,4},{8,11},{9,10},{10,... | collective-permute-start | bytes 393224 | tf_op jit(solution)/shard_map/ppermute | solution.py:418
  15.7 0.4 %own.1 = (f32[3,256,256]{2,1,0:T(8,128)S(1)}, f32[12,8,128]{2,1,0:T(8,128)S(1)}, f32[12,8,128]{2,1,0:T(8,128)S(1)}, bf16[256,256]{1,0:T(8,128)(2,1)S(1)}, bf16[256,256]{1,0:T(8,128)(2,1)S(1)}) custom-call(s32[256,512]{1,0:T(8,128)S(1)} %copy-done, bf16[2,12,2,33]{3,2,1,0:T(2,128)(2,1)S(1)} %get-tuple-element.20.taps), custom_call_target="tpu_custom_call" | custom-call | flops 1000000 | bytes 1000000 | tf_op jit(solution)/shard_map/own/pallas_call | solution.py:423
  16.2 0.0 collective-permute-done.2.row_first
  16.2 0.0 collective-permute-done.3.row_second
  16.2 6.2 %socs.1 = (f32[4,176,256]{2,1,0:T(8,128)S(1)}, s32[16,128]{1,0:T(8,128)S(1)}) custom-call(f32[12]{0:T(128)} %weights.1, f32[3,256,256]{2,1,0:T(8,128)S(1)} %get-tuple-element.21.windows, bf16[48,640]{1,0:T(8,128)(2,1)S(1)} %collective-permute-done.2.row_first, bf16[48,640]{1,0:T(8,128)(2,1)S(1)} %collective-permute-done.3.row_second, ...), custom_call_target="tpu_custom_call" | custom-call | flops 800000000 | bytes 100000 | tf_op jit(solution)/shard_map/socs/pallas_call | solution.py:439
  22.3 0.0 collective-permute-done.4.rest_2_
  22.4 0.0 collective-permute-done.5.rest_3_
  22.4 2.4 %final.1 = f32[256,512]{1,0:T(8,128)} custom-call(f32[4,176,256]{2,1,0:T(8,128)S(1)} %get-tuple-element.30.acc, s32[16,128]{1,0:T(8,128)S(1)} %get-tuple-element.31.images, bf16[256,256]{1,0:T(8,128)(2,1)S(1)} %get-tuple-element.32.g_row, bf16[256,256]{1,0:T(8,128)(2,1)S(1)} %get-tuple-element.33.g_col, bf16[512,128]{1,0:T(8,128)(2,1)S(1)} %bitcast.3, ...), custom_call_target="tpu_custom_call" | custom-call | tf_op jit(solution)/shard_map/final/pallas_call | solution.py:457
Async XLA Ops:
  0.0 9.4 %copy-start = (s32[256,512]{1,0:T(8,128)S(1)}, s32[256,512]{1,0:T(8,128)}, u32[]{:S(2)}) copy-start(s32[256,512]{1,0:T(8,128)} %mask.5) | copy-start | bytes 1572868
  2.0 7.4 %collective-permute-start = (bf16[608,128]{1,0:T(8,128)(2,1)S(1)}, bf16[608,128]{1,0:T(8,128)(2,1)S(1)}, u32[]{:S(2)}, u32[]{:S(2)}) collective-permute-start(bf16[608,128]{1,0:T(8,128)(2,1)S(1)} %get-tuple-element.22.own), channel_id=1, source_target_pairs={{0,1},{2,3},{1,0},{3,2},{4,5},{6,7},{5,4},{7,6},{8,9},{10,11},{9,8... | collective-permute-start | bytes 466952 | tf_op jit(solution)/shard_map/ppermute | solution.py:405
  5.1 6.4 %copy-start.1 = (bf16[8,64,128]{2,1,0:T(8,128)(2,1)S(1)}, bf16[8,64,128]{2,1,0:T(8,128)(2,1)}, u32[]{:S(2)}) copy-start(bf16[8,64,128]{2,1,0:T(8,128)(2,1)} %param.12) | copy-start | bytes 393220
  5.1 2.6 %collective-permute-start.1 = (bf16[96,128]{1,0:T(8,128)(2,1)S(1)}, bf16[96,128]{1,0:T(8,128)(2,1)S(1)}, u32[]{:S(2)}, u32[]{:S(2)}) collective-permute-start(bf16[96,128]{1,0:T(8,128)(2,1)S(1)} %get-tuple-element.23), channel_id=1, source_target_pairs={{1,2},{2,1},{0,4},{3,7},{5,6},{6,5},{4,0},{7,3},{9,10},{10,9},{8,1... | collective-permute-start | bytes 73736 | tf_op jit(solution)/shard_map/ppermute | solution.py:404
  5.1 17.2 %collective-permute-start.4 = (bf16[608,128]{1,0:T(8,128)(2,1)S(1)}, bf16[608,128]{1,0:T(8,128)(2,1)S(1)}, u32[]{:S(2)}, u32[]{:S(2)}) collective-permute-start(bf16[608,128]{1,0:T(8,128)(2,1)S(1)} %get-tuple-element.22.own), channel_id=1, source_target_pairs={{0,2},{1,3},{2,0},{3,1},{4,6},{5,7},{6,4},{7,5},{8,10},{9,11},{10,... | collective-permute-start | bytes 466952 | tf_op jit(solution)/shard_map/ppermute | solution.py:418
  9.6 6.6 %collective-permute-start.2 = (bf16[48,640]{1,0:T(8,128)(2,1)S(1)}, bf16[48,640]{1,0:T(8,128)(2,1)S(1)}, u32[]{:S(2)}, u32[]{:S(2)}) collective-permute-start(bf16[48,640]{1,0:T(8,128)(2,1)S(1)} %get-tuple-element.26), channel_id=1, source_target_pairs={{0,4},{8,12},{4,0},{12,8},{1,5},{9,13},{5,1},{13,9},{2,6},{10,14},... | collective-permute-start | bytes 184328 | tf_op jit(solution)/shard_map/ppermute | solution.py:420
  9.7 6.5 %collective-permute-start.3 = (bf16[48,640]{1,0:T(8,128)(2,1)S(1)}, bf16[48,640]{1,0:T(8,128)(2,1)S(1)}, u32[]{:S(2)}, u32[]{:S(2)}) collective-permute-start(bf16[48,640]{1,0:T(8,128)(2,1)S(1)} %get-tuple-element.27), channel_id=1, source_target_pairs={{4,8},{12,0},{8,4},{0,12},{5,9},{13,1},{9,5},{1,13},{6,10},{14,2},... | collective-permute-start | bytes 184328 | tf_op jit(solution)/shard_map/ppermute | solution.py:420
  11.5 10.8 %collective-permute-start.5 = (bf16[512,128]{1,0:T(8,128)(2,1)S(1)}, bf16[512,128]{1,0:T(8,128)(2,1)S(1)}, u32[]{:S(2)}, u32[]{:S(2)}) collective-permute-start(bf16[512,128]{1,0:T(8,128)(2,1)S(1)} %bitcast.2), channel_id=1, source_target_pairs={{0,3},{1,2},{2,1},{3,0},{4,7},{5,6},{6,5},{7,4},{8,11},{9,10},{10,... | collective-permute-start | bytes 393224 | tf_op jit(solution)/shard_map/ppermute | solution.py:418

commit v11 on v10

--- a/solution.py
+++ b/solution.py
@@ -20,7 +20,7 @@
 EDGE_OUT = 48
 RIGHT_AT = 56
 HALF_STRIP = STRIP + 16
-GROUP = 4
+GROUP = 2
 WIDE = 640
 SLOTS = 16
 F32 = jnp.float32
@@ -58,7 +58,7 @@
 
 
 def prep_kernel(
-    mask, ids, slots, count, across, down, library, to_first, to_second, taps, ends, a_ids, a_slots, sems
+    mask, ids, slots, count, across, down, library, to_first, to_second, block, taps, ends, a_ids, a_slots, sems
 ):
     rows, cols = mask.shape
     copies = [
@@ -68,7 +68,7 @@
         pltpu.make_async_copy(slots, a_slots, sems.at[3]),
         pltpu.make_async_copy(across, taps.at[0], sems.at[4]),
         pltpu.make_async_copy(down, taps.at[1], sems.at[5]),
-        pltpu.make_async_copy(library, to_first.at[2 * HALF_STRIP :], sems.at[6]),
+        pltpu.make_async_copy(library, block.at[2 * HALF_STRIP :], sems.at[6]),
     ]
     for copy in copies:
         copy.start()
@@ -89,6 +89,7 @@
     for strip in (to_first, to_second):
         strip[STRIP:HALF_STRIP, :] = table
         strip[HALF_STRIP + STRIP : 2 * HALF_STRIP, :] = jnp.zeros((16, 128), BF16)
+    block[0 : 2 * HALF_STRIP, :] = jnp.zeros((2 * HALF_STRIP, 128), BF16)
     even = lax.rem(lax.axis_index("col"), 2) == 0
     copies[0].wait()
     first = dot_nt(eye(STRIP, 128, 0), ends[0].astype(F32).astype(BF16))
@@ -126,8 +127,8 @@
     to_second[STRIP:, :] = tables
 
 
-def blur_matrix(shape, axis):
-    lag = lax.broadcasted_iota(jnp.int32, shape, axis) - lax.broadcasted_iota(jnp.int32, shape, 1 - axis)
+def blur_matrix(shape, axis, start=0):
+    lag = lax.broadcasted_iota(jnp.int32, shape, axis) - lax.broadcasted_iota(jnp.int32, shape, 1 - axis) - start
     total = sum(math.exp(-(t * t) / (2 * BLUR_SIGMA**2)) for t in range(-BLUR_HALF, BLUR_HALF + 1))
     off = (lag - BLUR_HALF).astype(F32)
     g = jnp.exp(-off * off / (2.0 * BLUR_SIGMA * BLUR_SIGMA)) * (1.0 / total)
@@ -136,7 +137,7 @@
     return high, (g - high.astype(F32)).astype(BF16)
 
 
-def own_kernel(mask, taps, windows, ahead, back, g_row, g_col):
+def own_kernel(mask, taps, windows, ahead, back, g_row, g_far, g_col):
     rows, cols = mask.shape
     full = jnp.concatenate(
         [jnp.zeros((rows, RIM), F32), mask[...].astype(F32), jnp.zeros((rows, WIDE - RIM - cols), F32)], axis=1
@@ -153,12 +154,14 @@
         back[k, 0:2, 0:count] = taps[1, k].astype(F32)
     back[...] = dot_nn(back[...].reshape(kernels * 8, 128).astype(BF16), flip).reshape(kernels, 8, 128)
     g_row[0:128], g_row[128:256] = blur_matrix((128, 256), 1)
+    g_far[0:128], g_far[128:256] = blur_matrix((128, 256), 1, 16 - BLUR_HALF)
     g_col[:, 0:128], g_col[:, 128:256] = blur_matrix((256, 128), 0)
 
 
 def socs_kernel(
     entries,
     per,
+    empty,
     weights,
     windows,
     row_first,
@@ -226,7 +229,7 @@
         image = jnp.sum(jnp.where(hit, table[0:1] + 1.0, 0.0), axis=1, keepdims=True)
         found = jnp.where(lane == t, image, found)
     cell = found.astype(jnp.int32) - 1
-    images[...] = jnp.where(cell >= 0, ((cell // per) ^ col) * per + cell % per + 1, 0)
+    images[...] = jnp.where(cell >= 0, ((cell // per) ^ col) * per + cell % per, empty)
 
     row = lax.broadcasted_iota(jnp.int32, (32, 128), 0)
     lane = lax.broadcasted_iota(jnp.int32, (32, 128), 1)
@@ -287,18 +290,18 @@
     pass_two(groups - 1, (groups - 1) % 2)
 
 
-def final_kernel(n_row, n_col, acc, images, g_row, g_col, *rest):
+def final_kernel(n_row, n_col, acc, images, g_row, g_far, g_col, *rest):
     shards = rest[:-7]
     out, cells, table, placed, flat, blurred, sem = rest[-7:]
-    g_high = g_col[:, 0:128]
-    per = cells.shape[0] // len(shards)
+    per = (cells.shape[0] - 1) // len(shards)
     rows, cols = out.shape
     row, col = lax.axis_index("row"), lax.axis_index("col")
     fetch = pltpu.make_async_copy(images, table, sem)
     fetch.start()
     for i, shard in enumerate(shards):
         rows_of = shard.shape[0] - per * 64
-        cells[pl.ds(i * per, per)] = shard[rows_of:, :].reshape(per, 64, 128)
+        cells[i * per : (i + 1) * per] = shard[rows_of:, :].reshape(per, 64, 128)
+    cells[len(shards) * per] = jnp.zeros((64, 128), BF16)
 
     at_row = lax.broadcasted_iota(jnp.int32, (8, 384), 1) - BLUR_HALF
     row_ok = ((row > 0) | (at_row >= 0)) & ((row < n_row - 1) | (at_row < rows))
@@ -327,31 +330,31 @@
         for j in range(-1, slot_cols + 1):
             ti = 0 if i < 0 else (2 if i == slot_rows else 1)
             tj = 0 if j < 0 else (2 if j == slot_cols else 1)
-            found = table[(i % slot_rows) * slot_cols + j % slot_cols, 3 * ti + tj]
-            image = jnp.maximum(found - 1, 0)
+            image = table[(i % slot_rows) * slot_cols + j % slot_cols, 3 * ti + tj]
             lanes = slice(128 + 128 * j, 256 + 128 * j)
-            show = lambda x: jnp.where(found > 0, x.astype(F32), 0.0)
             if i < 0:
-                placed[0:8, lanes] = show(cells[image, 48:64, :])[8:16]
+                placed[0:16, lanes] = cells[image, 48:64, :]
             elif i == slot_rows:
-                placed[8 + rows : 16 + rows, lanes] = show(cells[image, 0:16, :])[0:8]
+                placed[16 + rows : 32 + rows, lanes] = cells[image, 0:16, :]
             else:
-                placed[8 + 64 * i : 72 + 64 * i, lanes] = show(cells[image])
-    placed[16 + rows :, :] = jnp.zeros((placed.shape[0] - 16 - rows, placed.shape[1]), F32)
+                placed[16 + 64 * i : 80 + 64 * i, lanes] = cells[image]
+    placed[32 + rows :, :] = jnp.zeros((placed.shape[0] - 32 - rows, placed.shape[1]), BF16)
 
     for i, part in enumerate(halves):
-        cell = dot_nn(g_row[...], placed[128 * i : 128 * i + 256, :].astype(BF16))
+        cell = dot_nn(g_far[...], placed[128 * i : 128 * i + 256, :])
         cell = cell[0:128] + cell[128:]
         part += cell[:, 128 - BLUR_HALF : 128 - BLUR_HALF + part.shape[1]]
         high = part.astype(BF16)
         blurred[0, 128 * i : 128 * i + 128, :] = high
         blurred[1, 128 * i : 128 * i + 128, :] = (part - high.astype(F32)).astype(BF16)
-    for j in range(cols // 128):
-        lanes = slice(128 * j, 128 * j + 256)
-        part = dot_nn(blurred[0, :, lanes], g_col[...])
-        out[:, 128 * j : 128 * j + 128] = (
-            part[:, 0:128] + part[:, 128:] + dot_nn(blurred[1, :, lanes], g_high)
-        )
+    count = cols // 128
+    stacked = [
+        jnp.concatenate([blurred[p, :, 128 * j : 128 * j + 256] for j in range(count)], axis=0) for p in range(2)
+    ]
+    part = dot_nn(stacked[0], g_col[...])
+    part = part[:, 0:128] + part[:, 128:] + dot_nn(stacked[1], g_col[:, 0:128])
+    for j in range(count):
+        out[:, 128 * j : 128 * j + 128] = part[rows * j : rows * j + rows]
 
 
 def shape(dims, dtype):
@@ -370,15 +373,16 @@
     in_hbm = lambda x: pltpu.with_memory_space_constraint(x, pltpu.HBM)
     mask_hbm = in_hbm(mask_pixels)
 
-    to_first, to_second, taps = pl.pallas_call(
+    to_first, to_second, block, taps = pl.pallas_call(
         prep_kernel,
         out_shape=(
+            shape((2 * HALF_STRIP, 128), BF16),
+            shape((2 * HALF_STRIP, 128), BF16),
             shape((2 * HALF_STRIP + per * 64, 128), BF16),
-            shape((2 * HALF_STRIP, 128), BF16),
             shape((2,) + across_taps.shape, BF16),
         ),
         in_specs=[HBM] * 3 + [VMEM] + [HBM] * 3,
-        out_specs=(VMEM,) * 3,
+        out_specs=(VMEM,) * 4,
         scratch_shapes=[
             pltpu.VMEM((2, rows, 128), jnp.int32),
             pltpu.VMEM(cell_ids.shape, jnp.int32),
@@ -403,7 +407,7 @@
 
     col_second = lax.ppermute(to_second, ("row", "col"), second)
     col_first = lax.ppermute(to_first, "col", swaps(n_col)[0])
-    shards = [library, col_first]
+
     to_above, to_below = pl.pallas_call(
         mid_kernel,
         out_shape=(shape((STRIP + 16, WIDE), BF16),) * 2,
@@ -413,14 +417,15 @@
         name="mid",
     )(mask_pixels, col_first, col_second, to_first)
     late, to_above, to_below = lax.optimization_barrier((library, to_above, to_below))
-    for d in range(2, n_col):
-        block = to_first if d < n_col - 1 else late
-        shards.append(lax.ppermute(block, "col", [(i, i ^ d) for i in range(n_col)]))
+    shards = [library]
+    for d in range(1, n_col):
+        part = late if d in (1, n_col - 1) else block
+        shards.append(lax.ppermute(part, "col", [(i, i ^ d) for i in range(n_col)]))
     row_first, row_second = (
         lax.ppermute(x, "row", pairs) for x, pairs in zip((to_above, to_below), swaps(n_row))
     )
 
-    windows, ahead, back, g_row, g_col = pl.pallas_call(
+    windows, ahead, back, g_row, g_far, g_col = pl.pallas_call(
         own_kernel,
         out_shape=(
             shape((NB, rows, 256), F32),
@@ -428,16 +433,17 @@
             shape((kernels, 8, 128), F32),
             shape((256, 256), BF16),
             shape((256, 256), BF16),
+            shape((256, 256), BF16),
         ),
         in_specs=[VMEM] * 2,
-        out_specs=(VMEM,) * 5,
+        out_specs=(VMEM,) * 6,
         compiler_params=PARAMS,
         cost_estimate=pl.CostEstimate(flops=10**6, bytes_accessed=10**6, transcendentals=0),
         name="own",
     )(mask_pixels, taps)
 
     acc, images = pl.pallas_call(
-        functools.partial(socs_kernel, entries, per),
+        functools.partial(socs_kernel, entries, per, n_col * per),
         out_shape=(shape((NB + 1, CB, 256), F32), shape((SLOTS, 128), jnp.int32)),
         in_specs=[HBM] + [VMEM] * 8,
         out_specs=(VMEM,) * 2,
@@ -457,19 +463,19 @@
     return pl.pallas_call(
         functools.partial(final_kernel, n_row, n_col),
         out_shape=shape((rows, cols), F32),
-        in_specs=[VMEM] * (4 + n_col),
+        in_specs=[VMEM] * (5 + n_col),
         out_specs=VMEM,
         scratch_shapes=[
-            pltpu.VMEM((n_col * per, 64, 128), BF16),
+            pltpu.VMEM((n_col * per + 1, 64, 128), BF16),
             pltpu.SMEM((SLOTS, 128), jnp.int32),
-            pltpu.VMEM((384, cols + 256), F32),
+            pltpu.VMEM((384, cols + 256), BF16),
             pltpu.VMEM((WIDE, 384), BF16),
             pltpu.VMEM((2, rows, WIDE), BF16),
             pltpu.SemaphoreType.DMA,
         ],
         compiler_params=PARAMS,
         name="final",
-    )(acc, images, g_row, g_col, *shards)
+    )(acc, images, g_row, g_far, g_col, *shards)
 
 
 def solution(mesh):

time: 24.9 us -> 27.3 us (1.096)
  starting transfers between devices: 11.8 us -> 15.8 us
  waiting for transfers between devices: 1.7 us -> 0.02 us
    ppermute x2 -> x3, starting transfers between devices: 6.8 us -> 11 us  [on_device(): shards.append(lax.ppermute(part, 'col', [(i, i ^ d) for i in range(n_col)]))]
    ppermute x1, waiting for transfers between devices: 1.68 us -> 0.01 us  [on_device(): col_first = lax.ppermute(to_first, 'col', swaps(n_col)[0])]
  transfers between devices with their start and end apart: 6 -> 7, of which waited for: 1 -> 0; matrix products, arithmetic and copies ran while one was open for 0% -> 0% of each run, Pallas kernels for 28% -> 25%
where the time goes in v11:
time: 27.3 us; the launch traced here: 27.1 us
  starting transfers between devices  15.8 us (58%)
  Pallas kernels  10.5 us (38%)
  between operations  0.79 us (3%)
    ppermute x3, starting transfers between devices, on_device(): shards.append(lax.ppermute(part, 'col', [(i, i ^ d) for i in range(n_col)]))  11 us
    pallas_call x1, Pallas kernels, on_device(): pl.pallas_call(functools.partial(socs_kernel, entries, per, n_col * per),...  6.07 us
    ppermute x1, starting transfers between devices, on_device(): col_first = lax.ppermute(to_first, 'col', swaps(n_col)[0])  3.09 us
    pallas_call x1, Pallas kernels, on_device(): pl.pallas_call(functools.partial(final_kernel, n_row, n_col), out_shape=s...  2.4 us
    ppermute x2, starting transfers between devices, on_device(): lax.ppermute(x, 'row', pairs)  1.68 us
    pallas_call x1, Pallas kernels, on_device(): pl.pallas_call(prep_kernel, out_shape=(shape((2 * HALF_STRIP, 128), BF16)...  1.29 us
  transfers between devices with their start and end apart: 7, of which 0 were waited for; matrix products, arithmetic and copies ran while one was open for 0% of the time, Pallas kernels for 25%

profile of v11, /device:TPU:0, one launch (start us, length us, event | category | flops | bytes accessed | tf_op | source)
XLA Modules:
  0.0 27.1 jit_solution(4627158562914347285)
XLA Ops:
  0.0 0.0 copy-start
  0.7 1.3 %prep.1 = (bf16[96,128]{1,0:T(8,128)(2,1)S(1)}, bf16[96,128]{1,0:T(8,128)(2,1)S(1)}, bf16[608,128]{1,0:T(8,128)(2,1)S(1)}, bf16[2,12,2,33]{3,2,1,0:T(2,128)(2,1)S(1)}) custom-call(s32[256,512]{1,0:T(8,128)} %mask.5, s32[1,1,8]{2,1,0:T(1,128)} %ids.1, s32[1,1,8]{2,1,0:T(1,128)} %slots.1, s32[1,1]{1,0:T(1,128)S(6)} %copy.9.count, bf16[12,2,33]{2,1,0:T(2,128)(2,1)} %across.1, ...), custom_call_target="tpu_custom_call" | custom-call | tf_op jit(solution)/shard_map/prep/pallas_call | solution.py:376
  2.0 3.1 %collective-permute-start = (bf16[96,128]{1,0:T(8,128)(2,1)S(1)}, bf16[96,128]{1,0:T(8,128)(2,1)S(1)}, u32[]{:S(2)}, u32[]{:S(2)}) collective-permute-start(bf16[96,128]{1,0:T(8,128)(2,1)S(1)} %get-tuple-element.24.own), channel_id=1, source_target_pairs={{0,1},{2,3},{1,0},{3,2},{4,5},{6,7},{5,4},{7,6},{8,9},{10,11},{9,8... | collective-permute-start | bytes 73736 | tf_op jit(solution)/shard_map/ppermute | solution.py:409
  5.1 0.0 collective-permute-start.1
  5.1 0.0 copy-start.1
  5.1 2.6 %collective-permute-start.5 = (bf16[608,128]{1,0:T(8,128)(2,1)S(1)}, bf16[608,128]{1,0:T(8,128)(2,1)S(1)}, u32[]{:S(2)}, u32[]{:S(2)}) collective-permute-start(bf16[608,128]{1,0:T(8,128)(2,1)S(1)} %get-tuple-element.38), channel_id=1, source_target_pairs={{0,2},{1,3},{2,0},{3,1},{4,6},{5,7},{6,4},{7,5},{8,10},{9,11},{10,... | collective-permute-start | bytes 466952 | tf_op jit(solution)/shard_map/ppermute | solution.py:423
  7.7 0.0 collective-permute-done.from_first.col_first
  7.7 0.0 collective-permute-done.1.from_second.col_second
  7.7 0.0 copy-done
  7.7 0.2 mid.1
  7.9 0.1 collective-permute-start.2
  8.0 1.6 %collective-permute-start.3 = (bf16[48,640]{1,0:T(8,128)(2,1)S(1)}, bf16[48,640]{1,0:T(8,128)(2,1)S(1)}, u32[]{:S(2)}, u32[]{:S(2)}) collective-permute-start(bf16[48,640]{1,0:T(8,128)(2,1)S(1)} %get-tuple-element.29), channel_id=1, source_target_pairs={{4,8},{12,0},{8,4},{0,12},{5,9},{13,1},{9,5},{1,13},{6,10},{14,2},... | collective-permute-start | bytes 184328 | tf_op jit(solution)/shard_map/ppermute | solution.py:425
  9.6 0.0 copy-done.1
  9.6 4.9 %collective-permute-start.4 = (bf16[512,128]{1,0:T(8,128)(2,1)S(1)}, bf16[512,128]{1,0:T(8,128)(2,1)S(1)}, u32[]{:S(2)}, u32[]{:S(2)}) collective-permute-start(bf16[512,128]{1,0:T(8,128)(2,1)S(1)} %bitcast.2), channel_id=1, source_target_pairs={{0,1},{1,0},{2,3},{3,2},{4,5},{5,4},{6,7},{7,6},{8,9},{9,8},{10,11... | collective-permute-start | bytes 393224 | tf_op jit(solution)/shard_map/ppermute | solution.py:423
  14.6 3.5 %collective-permute-start.6 = (bf16[512,128]{1,0:T(8,128)(2,1)S(1)}, bf16[512,128]{1,0:T(8,128)(2,1)S(1)}, u32[]{:S(2)}, u32[]{:S(2)}) collective-permute-start(bf16[512,128]{1,0:T(8,128)(2,1)S(1)} %bitcast.3), channel_id=1, source_target_pairs={{0,3},{1,2},{2,1},{3,0},{4,7},{5,6},{6,5},{7,4},{8,11},{9,10},{10,... | collective-permute-start | bytes 393224 | tf_op jit(solution)/shard_map/ppermute | solution.py:423
  18.1 0.5 %own.1 = (f32[3,256,256]{2,1,0:T(8,128)S(1)}, f32[12,8,128]{2,1,0:T(8,128)S(1)}, f32[12,8,128]{2,1,0:T(8,128)S(1)}, bf16[256,256]{1,0:T(8,128)(2,1)S(1)}, bf16[2...) custom-call(s32[256,512]{1,0:T(8,128)S(1)} %copy-done, bf16[2,12,2,33]{3,2,1,0:T(2,128)(2,1)S(1)} %get-tuple-element.22.taps), custom_call_target="tpu_custom_call" | custom-call | flops 1000000 | bytes 1000000 | tf_op jit(solution)/shard_map/own/pallas_call | solution.py:428
  18.6 0.0 collective-permute-done.2.row_first
  18.6 0.0 collective-permute-done.3.row_second
  18.6 6.1 %socs.1 = (f32[4,176,256]{2,1,0:T(8,128)S(1)}, s32[16,128]{1,0:T(8,128)S(1)}) custom-call(f32[12]{0:T(128)} %weights.1, f32[3,256,256]{2,1,0:T(8,128)S(1)} %get-tuple-element.23.windows, bf16[48,640]{1,0:T(8,128)(2,1)S(1)} %collective-permute-done.2.row_first, bf16[48,640]{1,0:T(8,128)(2,1)S(1)} %collective-permute-done.3.row_second, ...), custom_call_target="tpu_custom_call" | custom-call | flops 800000000 | bytes 100000 | tf_op jit(solution)/shard_map/socs/pallas_call | solution.py:445
  24.7 0.0 collective-permute-done.4.rest_1_
  24.7 0.0 collective-permute-done.6.rest_3_
  24.7 0.0 collective-permute-done.5.rest_2_
  24.7 2.4 %final.1 = f32[256,512]{1,0:T(8,128)} custom-call(f32[4,176,256]{2,1,0:T(8,128)S(1)} %get-tuple-element.32.acc, s32[16,128]{1,0:T(8,128)S(1)} %get-tuple-element.33.images, bf16[256,256]{1,0:T(8,128)(2,1)S(1)} %get-tuple-element.34.g_row, bf16[256,256]{1,0:T(8,128)(2,1)S(1)} %get-tuple-element.35.g_far, bf16[256,256]{1,0:T(8,128)(2,1)S(1)} %get-tuple-element.36.g_col, ...), custom_call_target="tpu_custom_call" | custom-call | tf_op jit(solution)/shard_map/final/pallas_call | solution.py:463
Async XLA Ops:
  0.0 7.7 %copy-start = (s32[256,512]{1,0:T(8,128)S(1)}, s32[256,512]{1,0:T(8,128)}, u32[]{:S(2)}) copy-start(s32[256,512]{1,0:T(8,128)} %mask.5) | copy-start | bytes 1572868
  2.0 5.7 %collective-permute-start = (bf16[96,128]{1,0:T(8,128)(2,1)S(1)}, bf16[96,128]{1,0:T(8,128)(2,1)S(1)}, u32[]{:S(2)}, u32[]{:S(2)}) collective-permute-start(bf16[96,128]{1,0:T(8,128)(2,1)S(1)} %get-tuple-element.24.own), channel_id=1, source_target_pairs={{0,1},{2,3},{1,0},{3,2},{4,5},{6,7},{5,4},{7,6},{8,9},{10,11},{9,8... | collective-permute-start | bytes 73736 | tf_op jit(solution)/shard_map/ppermute | solution.py:409
  5.1 2.6 %collective-permute-start.1 = (bf16[96,128]{1,0:T(8,128)(2,1)S(1)}, bf16[96,128]{1,0:T(8,128)(2,1)S(1)}, u32[]{:S(2)}, u32[]{:S(2)}) collective-permute-start(bf16[96,128]{1,0:T(8,128)(2,1)S(1)} %get-tuple-element.25), channel_id=1, source_target_pairs={{1,2},{2,1},{0,4},{3,7},{5,6},{6,5},{4,0},{7,3},{9,10},{10,9},{8,1... | collective-permute-start | bytes 73736 | tf_op jit(solution)/shard_map/ppermute | solution.py:408
  5.1 4.5 %copy-start.1 = (bf16[8,64,128]{2,1,0:T(8,128)(2,1)S(1)}, bf16[8,64,128]{2,1,0:T(8,128)(2,1)}, u32[]{:S(2)}) copy-start(bf16[8,64,128]{2,1,0:T(8,128)(2,1)} %param.12) | copy-start | bytes 393220
  5.1 19.6 %collective-permute-start.5 = (bf16[608,128]{1,0:T(8,128)(2,1)S(1)}, bf16[608,128]{1,0:T(8,128)(2,1)S(1)}, u32[]{:S(2)}, u32[]{:S(2)}) collective-permute-start(bf16[608,128]{1,0:T(8,128)(2,1)S(1)} %get-tuple-element.38), channel_id=1, source_target_pairs={{0,2},{1,3},{2,0},{3,1},{4,6},{5,7},{6,4},{7,5},{8,10},{9,11},{10,... | collective-permute-start | bytes 466952 | tf_op jit(solution)/shard_map/ppermute | solution.py:423
  7.9 10.6 %collective-permute-start.2 = (bf16[48,640]{1,0:T(8,128)(2,1)S(1)}, bf16[48,640]{1,0:T(8,128)(2,1)S(1)}, u32[]{:S(2)}, u32[]{:S(2)}) collective-permute-start(bf16[48,640]{1,0:T(8,128)(2,1)S(1)} %get-tuple-element.28), channel_id=1, source_target_pairs={{0,4},{8,12},{4,0},{12,8},{1,5},{9,13},{5,1},{13,9},{2,6},{10,14},... | collective-permute-start | bytes 184328 | tf_op jit(solution)/shard_map/ppermute | solution.py:425
  8.0 10.6 %collective-permute-start.3 = (bf16[48,640]{1,0:T(8,128)(2,1)S(1)}, bf16[48,640]{1,0:T(8,128)(2,1)S(1)}, u32[]{:S(2)}, u32[]{:S(2)}) collective-permute-start(bf16[48,640]{1,0:T(8,128)(2,1)S(1)} %get-tuple-element.29), channel_id=1, source_target_pairs={{4,8},{12,0},{8,4},{0,12},{5,9},{13,1},{9,5},{1,13},{6,10},{14,2},... | collective-permute-start | bytes 184328 | tf_op jit(solution)/shard_map/ppermute | solution.py:425
  9.6 15.0 %collective-permute-start.4 = (bf16[512,128]{1,0:T(8,128)(2,1)S(1)}, bf16[512,128]{1,0:T(8,128)(2,1)S(1)}, u32[]{:S(2)}, u32[]{:S(2)}) collective-permute-start(bf16[512,128]{1,0:T(8,128)(2,1)S(1)} %bitcast.2), channel_id=1, source_target_pairs={{0,1},{1,0},{2,3},{3,2},{4,5},{5,4},{6,7},{7,6},{8,9},{9,8},{10,11... | collective-permute-start | bytes 393224 | tf_op jit(solution)/shard_map/ppermute | solution.py:423
  14.6 10.1 %collective-permute-start.6 = (bf16[512,128]{1,0:T(8,128)(2,1)S(1)}, bf16[512,128]{1,0:T(8,128)(2,1)S(1)}, u32[]{:S(2)}, u32[]{:S(2)}) collective-permute-start(bf16[512,128]{1,0:T(8,128)(2,1)S(1)} %bitcast.3), channel_id=1, source_target_pairs={{0,3},{1,2},{2,1},{3,0},{4,7},{5,6},{6,5},{7,4},{8,11},{9,10},{10,... | collective-permute-start | bytes 393224 | tf_op jit(solution)/shard_map/ppermute | solution.py:423

commit v12 on v11

--- a/solution.py
+++ b/solution.py
@@ -90,6 +90,7 @@
         strip[STRIP:HALF_STRIP, :] = table
         strip[HALF_STRIP + STRIP : 2 * HALF_STRIP, :] = jnp.zeros((16, 128), BF16)
     block[0 : 2 * HALF_STRIP, :] = jnp.zeros((2 * HALF_STRIP, 128), BF16)
+    to_second[2 * HALF_STRIP :, :] = jnp.zeros((128 - 2 * HALF_STRIP, 128), BF16)
     even = lax.rem(lax.axis_index("col"), 2) == 0
     copies[0].wait()
     first = dot_nt(eye(STRIP, 128, 0), ends[0].astype(F32).astype(BF16))
@@ -377,7 +378,7 @@
         prep_kernel,
         out_shape=(
             shape((2 * HALF_STRIP, 128), BF16),
-            shape((2 * HALF_STRIP, 128), BF16),
+            shape((128, 128), BF16),
             shape((2 * HALF_STRIP + per * 64, 128), BF16),
             shape((2,) + across_taps.shape, BF16),
         ),

time: 27.3 us -> 24 us (0.88)
  starting transfers between devices: 15.8 us -> 11 us
  waiting for transfers between devices: 0.02 us -> 1.89 us
  Pallas kernels: 10.5 us -> 10.2 us
    ppermute x3, starting transfers between devices: 11 us -> 4.64 us  [on_device(): shards.append(lax.ppermute(part, 'col', [(i, i ^ d) for i in range(n_col)]))]
    ppermute x3, waiting for transfers between devices: 0.01 us -> 1.17 us  [on_device(): shards.append(lax.ppermute(part, 'col', [(i, i ^ d) for i in range(n_col)]))]
    ppermute x1, starting transfers between devices: 3.09 us -> 4.15 us  [on_device(): col_first = lax.ppermute(to_first, 'col', swaps(n_col)[0])]
    ppermute x1, waiting for transfers between devices: 0.01 us -> 0.71 us  [on_device(): col_first = lax.ppermute(to_first, 'col', swaps(n_col)[0])]
    ppermute x1, starting transfers between devices: 0.01 us -> 0.52 us  [on_device(): col_second = lax.ppermute(to_second, ('row', 'col'), second)]
  transfers between devices with their start and end apart: 7 -> 7, of which waited for: 0 -> 2; matrix products, arithmetic and copies ran while one was open for 0% -> 0% of each run, Pallas kernels for 25% -> 27%
where the time goes in v12:
time: 24 us; the launch traced here: 23.9 us
  starting transfers between devices  11 us (46%)
  Pallas kernels  10.2 us (42%)
  waiting for transfers between devices  1.89 us (8%)
  between operations  0.77 us (3%)
    pallas_call x1, Pallas kernels, on_device(): pl.pallas_call(functools.partial(socs_kernel, entries, per, n_col * per),...  5.82 us
    ppermute x3, starting transfers between devices, on_device(): shards.append(lax.ppermute(part, 'col', [(i, i ^ d) for i in range(n_col)]))  4.64 us
    ppermute x1, starting transfers between devices, on_device(): col_first = lax.ppermute(to_first, 'col', swaps(n_col)[0])  4.15 us
    pallas_call x1, Pallas kernels, on_device(): pl.pallas_call(functools.partial(final_kernel, n_row, n_col), out_shape=s...  2.41 us
    ppermute x2, starting transfers between devices, on_device(): lax.ppermute(x, 'row', pairs)  1.68 us
    pallas_call x1, Pallas kernels, on_device(): pl.pallas_call(prep_kernel, out_shape=(shape((2 * HALF_STRIP, 128), BF16)...  1.29 us
    ppermute x3, waiting for transfers between devices, on_device(): shards.append(lax.ppermute(part, 'col', [(i, i ^ d) for i in range(n_col)]))  1.17 us
    ppermute x1, waiting for transfers between devices, on_device(): col_first = lax.ppermute(to_first, 'col', swaps(n_col)[0])  0.71 us
  transfers between devices with their start and end apart: 7, of which 2 were waited for; matrix products, arithmetic and copies ran while one was open for 0% of the time, Pallas kernels for 27%

profile of v12, /device:TPU:0, one launch (start us, length us, event | category | flops | bytes accessed | tf_op | source)
XLA Modules:
  0.0 23.9 jit_solution(11356134374871727333)
XLA Ops:
  0.0 0.0 copy-start
  0.7 1.3 %prep.1 = (bf16[96,128]{1,0:T(8,128)(2,1)S(1)}, bf16[128,128]{1,0:T(8,128)(2,1)S(1)}, bf16[608,128]{1,0:T(8,128)(2,1)S(1)}, bf16[2,12,2,33]{3,2,1,0:T(2,128)(2,1)S(1)}) custom-call(s32[256,512]{1,0:T(8,128)} %mask.5, s32[1,1,8]{2,1,0:T(1,128)} %ids.1, s32[1,1,8]{2,1,0:T(1,128)} %slots.1, s32[1,1]{1,0:T(1,128)S(6)} %copy.9.count, bf16[12,2,33]{2,1,0:T(2,128)(2,1)} %across.1, ...), custom_call_target="tpu_custom_call" | custom-call | tf_op jit(solution)/shard_map/prep/pallas_call | solution.py:377
  2.0 0.5 %collective-permute-start.1 = (bf16[128,128]{1,0:T(8,128)(2,1)S(1)}, bf16[128,128]{1,0:T(8,128)(2,1)S(1)}, u32[]{:S(2)}, u32[]{:S(2)}) collective-permute-start(bf16[128,128]{1,0:T(8,128)(2,1)S(1)} %get-tuple-element.25), channel_id=1, source_target_pairs={{1,2},{2,1},{0,4},{3,7},{5,6},{6,5},{4,0},{7,3},{9,10},{10,9},{8,1... | collective-permute-start | bytes 98312 | tf_op jit(solution)/shard_map/ppermute | solution.py:409
  2.5 4.1 %collective-permute-start = (bf16[96,128]{1,0:T(8,128)(2,1)S(1)}, bf16[96,128]{1,0:T(8,128)(2,1)S(1)}, u32[]{:S(2)}, u32[]{:S(2)}) collective-permute-start(bf16[96,128]{1,0:T(8,128)(2,1)S(1)} %get-tuple-element.24.own), channel_id=1, source_target_pairs={{0,1},{2,3},{1,0},{3,2},{4,5},{6,7},{5,4},{7,6},{8,9},{10,11},{9,8... | collective-permute-start | bytes 73736 | tf_op jit(solution)/shard_map/ppermute | solution.py:410
  6.7 0.0 copy-start.1
  6.7 1.1 %collective-permute-start.5 = (bf16[608,128]{1,0:T(8,128)(2,1)S(1)}, bf16[608,128]{1,0:T(8,128)(2,1)S(1)}, u32[]{:S(2)}, u32[]{:S(2)}) collective-permute-start(bf16[608,128]{1,0:T(8,128)(2,1)S(1)} %get-tuple-element.38), channel_id=1, source_target_pairs={{0,2},{1,3},{2,0},{3,1},{4,6},{5,7},{6,4},{7,5},{8,10},{9,11},{10,... | collective-permute-start | bytes 466952 | tf_op jit(solution)/shard_map/ppermute | solution.py:424
  7.8 0.7 %collective-permute-done.from_first.col_first = bf16[96,128]{1,0:T(8,128)(2,1)S(1)} collective-permute-done((bf16[96,128]{1,0:T(8,128)(2,1)S(1)}, bf16[96,128]{1,0:T(8,128)(2,1)S(1)}, u32[]{:S(2)}, u32[]{:S(2)}) %collective-permute-start) | collective-permute-done | bytes 24608 | tf_op jit(solution)/shard_map/ppermute | solution.py:410
  8.5 0.0 collective-permute-done.1.from_second.col_second
  8.5 0.0 copy-done
  8.5 0.2 mid.1
  8.7 0.1 collective-permute-start.2
  8.8 1.6 %collective-permute-start.3 = (bf16[48,640]{1,0:T(8,128)(2,1)S(1)}, bf16[48,640]{1,0:T(8,128)(2,1)S(1)}, u32[]{:S(2)}, u32[]{:S(2)}) collective-permute-start(bf16[48,640]{1,0:T(8,128)(2,1)S(1)} %get-tuple-element.29), channel_id=1, source_target_pairs={{4,8},{12,0},{8,4},{0,12},{5,9},{13,1},{9,5},{1,13},{6,10},{14,2},... | collective-permute-start | bytes 184328 | tf_op jit(solution)/shard_map/ppermute | solution.py:426
  10.4 0.0 copy-done.1
  10.4 2.0 %collective-permute-start.4 = (bf16[512,128]{1,0:T(8,128)(2,1)S(1)}, bf16[512,128]{1,0:T(8,128)(2,1)S(1)}, u32[]{:S(2)}, u32[]{:S(2)}) collective-permute-start(bf16[512,128]{1,0:T(8,128)(2,1)S(1)} %bitcast.2), channel_id=1, source_target_pairs={{0,1},{1,0},{2,3},{3,2},{4,5},{5,4},{6,7},{7,6},{8,9},{9,8},{10,11... | collective-permute-start | bytes 393224 | tf_op jit(solution)/shard_map/ppermute | solution.py:424
  12.4 1.5 %collective-permute-start.6 = (bf16[512,128]{1,0:T(8,128)(2,1)S(1)}, bf16[512,128]{1,0:T(8,128)(2,1)S(1)}, u32[]{:S(2)}, u32[]{:S(2)}) collective-permute-start(bf16[512,128]{1,0:T(8,128)(2,1)S(1)} %bitcast.3), channel_id=1, source_target_pairs={{0,3},{1,2},{2,1},{3,0},{4,7},{5,6},{6,5},{7,4},{8,11},{9,10},{10,... | collective-permute-start | bytes 393224 | tf_op jit(solution)/shard_map/ppermute | solution.py:424
  13.9 0.5 %own.1 = (f32[3,256,256]{2,1,0:T(8,128)S(1)}, f32[12,8,128]{2,1,0:T(8,128)S(1)}, f32[12,8,128]{2,1,0:T(8,128)S(1)}, bf16[256,256]{1,0:T(8,128)(2,1)S(1)}, bf16[2...) custom-call(s32[256,512]{1,0:T(8,128)S(1)} %copy-done, bf16[2,12,2,33]{3,2,1,0:T(2,128)(2,1)S(1)} %get-tuple-element.22.taps), custom_call_target="tpu_custom_call" | custom-call | flops 1000000 | bytes 1000000 | tf_op jit(solution)/shard_map/own/pallas_call | solution.py:429
  14.4 0.0 collective-permute-done.2.row_first
  14.4 0.0 collective-permute-done.3.row_second
  14.4 5.8 %socs.1 = (f32[4,176,256]{2,1,0:T(8,128)S(1)}, s32[16,128]{1,0:T(8,128)S(1)}) custom-call(f32[12]{0:T(128)} %weights.1, f32[3,256,256]{2,1,0:T(8,128)S(1)} %get-tuple-element.23.windows, bf16[48,640]{1,0:T(8,128)(2,1)S(1)} %collective-permute-done.2.row_first, bf16[48,640]{1,0:T(8,128)(2,1)S(1)} %collective-permute-done.3.row_second, ...), custom_call_target="tpu_custom_call" | custom-call | flops 800000000 | bytes 100000 | tf_op jit(solution)/shard_map/socs/pallas_call | solution.py:446
  20.3 0.0 collective-permute-done.5.rest_2_
  20.3 1.2 %collective-permute-done.4.rest_1_ = bf16[512,128]{1,0:T(8,128)(2,1)S(1)} collective-permute-done((bf16[512,128]{1,0:T(8,128)(2,1)S(1)}, bf16[512,128]{1,0:T(8,128)(2,1)S(1)}, u32[]{:S(2)}, u32[]{:S(2)}) %collective-permute-start.4) | collective-permute-done | bytes 131104 | tf_op jit(solution)/shard_map/ppermute | solution.py:424
  21.5 0.0 collective-permute-done.6.rest_3_
  21.5 2.4 %final.1 = f32[256,512]{1,0:T(8,128)} custom-call(f32[4,176,256]{2,1,0:T(8,128)S(1)} %get-tuple-element.32.acc, s32[16,128]{1,0:T(8,128)S(1)} %get-tuple-element.33.images, bf16[256,256]{1,0:T(8,128)(2,1)S(1)} %get-tuple-element.34.g_row, bf16[256,256]{1,0:T(8,128)(2,1)S(1)} %get-tuple-element.35.g_far, bf16[256,256]{1,0:T(8,128)(2,1)S(1)} %get-tuple-element.36.g_col, ...), custom_call_target="tpu_custom_call" | custom-call | tf_op jit(solution)/shard_map/final/pallas_call | solution.py:464
Async XLA Ops:
  0.0 8.5 %copy-start = (s32[256,512]{1,0:T(8,128)S(1)}, s32[256,512]{1,0:T(8,128)}, u32[]{:S(2)}) copy-start(s32[256,512]{1,0:T(8,128)} %mask.5) | copy-start | bytes 1572868
  2.0 6.5 %collective-permute-start.1 = (bf16[128,128]{1,0:T(8,128)(2,1)S(1)}, bf16[128,128]{1,0:T(8,128)(2,1)S(1)}, u32[]{:S(2)}, u32[]{:S(2)}) collective-permute-start(bf16[128,128]{1,0:T(8,128)(2,1)S(1)} %get-tuple-element.25), channel_id=1, source_target_pairs={{1,2},{2,1},{0,4},{3,7},{5,6},{6,5},{4,0},{7,3},{9,10},{10,9},{8,1... | collective-permute-start | bytes 98312 | tf_op jit(solution)/shard_map/ppermute | solution.py:409
  2.5 6.0 %collective-permute-start = (bf16[96,128]{1,0:T(8,128)(2,1)S(1)}, bf16[96,128]{1,0:T(8,128)(2,1)S(1)}, u32[]{:S(2)}, u32[]{:S(2)}) collective-permute-start(bf16[96,128]{1,0:T(8,128)(2,1)S(1)} %get-tuple-element.24.own), channel_id=1, source_target_pairs={{0,1},{2,3},{1,0},{3,2},{4,5},{6,7},{5,4},{7,6},{8,9},{10,11},{9,8... | collective-permute-start | bytes 73736 | tf_op jit(solution)/shard_map/ppermute | solution.py:410
  6.7 3.7 %copy-start.1 = (bf16[8,64,128]{2,1,0:T(8,128)(2,1)S(1)}, bf16[8,64,128]{2,1,0:T(8,128)(2,1)}, u32[]{:S(2)}) copy-start(bf16[8,64,128]{2,1,0:T(8,128)(2,1)} %param.12) | copy-start | bytes 393220
  6.7 13.6 %collective-permute-start.5 = (bf16[608,128]{1,0:T(8,128)(2,1)S(1)}, bf16[608,128]{1,0:T(8,128)(2,1)S(1)}, u32[]{:S(2)}, u32[]{:S(2)}) collective-permute-start(bf16[608,128]{1,0:T(8,128)(2,1)S(1)} %get-tuple-element.38), channel_id=1, source_target_pairs={{0,2},{1,3},{2,0},{3,1},{4,6},{5,7},{6,4},{7,5},{8,10},{9,11},{10,... | collective-permute-start | bytes 466952 | tf_op jit(solution)/shard_map/ppermute | solution.py:424
  8.7 5.7 %collective-permute-start.2 = (bf16[48,640]{1,0:T(8,128)(2,1)S(1)}, bf16[48,640]{1,0:T(8,128)(2,1)S(1)}, u32[]{:S(2)}, u32[]{:S(2)}) collective-permute-start(bf16[48,640]{1,0:T(8,128)(2,1)S(1)} %get-tuple-element.28), channel_id=1, source_target_pairs={{0,4},{8,12},{4,0},{12,8},{1,5},{9,13},{5,1},{13,9},{2,6},{10,14},... | collective-permute-start | bytes 184328 | tf_op jit(solution)/shard_map/ppermute | solution.py:426
  8.8 5.6 %collective-permute-start.3 = (bf16[48,640]{1,0:T(8,128)(2,1)S(1)}, bf16[48,640]{1,0:T(8,128)(2,1)S(1)}, u32[]{:S(2)}, u32[]{:S(2)}) collective-permute-start(bf16[48,640]{1,0:T(8,128)(2,1)S(1)} %get-tuple-element.29), channel_id=1, source_target_pairs={{4,8},{12,0},{8,4},{0,12},{5,9},{13,1},{9,5},{1,13},{6,10},{14,2},... | collective-permute-start | bytes 184328 | tf_op jit(solution)/shard_map/ppermute | solution.py:426
  10.4 11.0 %collective-permute-start.4 = (bf16[512,128]{1,0:T(8,128)(2,1)S(1)}, bf16[512,128]{1,0:T(8,128)(2,1)S(1)}, u32[]{:S(2)}, u32[]{:S(2)}) collective-permute-start(bf16[512,128]{1,0:T(8,128)(2,1)S(1)} %bitcast.2), channel_id=1, source_target_pairs={{0,1},{1,0},{2,3},{3,2},{4,5},{5,4},{6,7},{7,6},{8,9},{9,8},{10,11... | collective-permute-start | bytes 393224 | tf_op jit(solution)/shard_map/ppermute | solution.py:424
  12.4 9.0 %collective-permute-start.6 = (bf16[512,128]{1,0:T(8,128)(2,1)S(1)}, bf16[512,128]{1,0:T(8,128)(2,1)S(1)}, u32[]{:S(2)}, u32[]{:S(2)}) collective-permute-start(bf16[512,128]{1,0:T(8,128)(2,1)S(1)} %bitcast.3), channel_id=1, source_target_pairs={{0,3},{1,2},{2,1},{3,0},{4,7},{5,6},{6,5},{7,4},{8,11},{9,10},{10,... | collective-permute-start | bytes 393224 | tf_op jit(solution)/shard_map/ppermute | solution.py:424

commit v13 on v12

--- a/solution.py
+++ b/solution.py
@@ -20,6 +20,7 @@
 EDGE_OUT = 48
 RIGHT_AT = 56
 HALF_STRIP = STRIP + 16
+SPARE = 16
 GROUP = 2
 WIDE = 640
 SLOTS = 16
@@ -68,7 +69,7 @@
         pltpu.make_async_copy(slots, a_slots, sems.at[3]),
         pltpu.make_async_copy(across, taps.at[0], sems.at[4]),
         pltpu.make_async_copy(down, taps.at[1], sems.at[5]),
-        pltpu.make_async_copy(library, block.at[2 * HALF_STRIP :], sems.at[6]),
+        pltpu.make_async_copy(library, block.at[SPARE:], sems.at[6]),
     ]
     for copy in copies:
         copy.start()
@@ -89,7 +90,7 @@
     for strip in (to_first, to_second):
         strip[STRIP:HALF_STRIP, :] = table
         strip[HALF_STRIP + STRIP : 2 * HALF_STRIP, :] = jnp.zeros((16, 128), BF16)
-    block[0 : 2 * HALF_STRIP, :] = jnp.zeros((2 * HALF_STRIP, 128), BF16)
+    block[0:SPARE, :] = jnp.zeros((SPARE, 128), BF16)
     to_second[2 * HALF_STRIP :, :] = jnp.zeros((128 - 2 * HALF_STRIP, 128), BF16)
     even = lax.rem(lax.axis_index("col"), 2) == 0
     copies[0].wait()
@@ -291,19 +292,10 @@
     pass_two(groups - 1, (groups - 1) % 2)
 
 
-def final_kernel(n_row, n_col, acc, images, g_row, g_far, g_col, *rest):
-    shards = rest[:-7]
-    out, cells, table, placed, flat, blurred, sem = rest[-7:]
-    per = (cells.shape[0] - 1) // len(shards)
-    rows, cols = out.shape
+def rows_kernel(n_row, n_col, acc, g_row, out, flat):
+    rows = out.shape[0]
+    cols = CB * NB - 2 * BLUR_HALF
     row, col = lax.axis_index("row"), lax.axis_index("col")
-    fetch = pltpu.make_async_copy(images, table, sem)
-    fetch.start()
-    for i, shard in enumerate(shards):
-        rows_of = shard.shape[0] - per * 64
-        cells[i * per : (i + 1) * per] = shard[rows_of:, :].reshape(per, 64, 128)
-    cells[len(shards) * per] = jnp.zeros((64, 128), BF16)
-
     at_row = lax.broadcasted_iota(jnp.int32, (8, 384), 1) - BLUR_HALF
     row_ok = ((row > 0) | (at_row >= 0)) & ((row < n_row - 1) | (at_row < rows))
     row_ok = jnp.where(row_ok, 1.0, 0.0)
@@ -320,10 +312,22 @@
         flat[b * CB : (b + 1) * CB, :] = part.astype(BF16)
     flat[NB * CB :, :] = jnp.zeros((flat.shape[0] - NB * CB, 384), BF16)
 
-    halves = []
     for i in range(rows // 128):
         part = dot_nt(g_row[...], flat[:, 128 * i : 128 * i + 256])
-        halves.append(part[0:128] + part[128:])
+        out[128 * i : 128 * i + 128, :] = part[0:128] + part[128:]
+
+
+def final_kernel(images, blurred_rows, g_far, g_col, *rest):
+    shards = rest[:-6]
+    out, cells, table, placed, blurred, sem = rest[-6:]
+    per = (cells.shape[0] - 1) // len(shards)
+    rows, cols = out.shape
+    fetch = pltpu.make_async_copy(images, table, sem)
+    fetch.start()
+    for i, shard in enumerate(shards):
+        rows_of = shard.shape[0] - per * 64
+        cells[i * per : (i + 1) * per] = shard[rows_of:, :].reshape(per, 64, 128)
+    cells[len(shards) * per] = jnp.zeros((64, 128), BF16)
 
     fetch.wait()
     slot_rows, slot_cols = rows // 64, cols // 128
@@ -341,7 +345,8 @@
                 placed[16 + 64 * i : 80 + 64 * i, lanes] = cells[image]
     placed[32 + rows :, :] = jnp.zeros((placed.shape[0] - 32 - rows, placed.shape[1]), BF16)
 
-    for i, part in enumerate(halves):
+    for i in range(rows // 128):
+        part = blurred_rows[128 * i : 128 * i + 128, :]
         cell = dot_nn(g_far[...], placed[128 * i : 128 * i + 256, :])
         cell = cell[0:128] + cell[128:]
         part += cell[:, 128 - BLUR_HALF : 128 - BLUR_HALF + part.shape[1]]
@@ -379,7 +384,7 @@
         out_shape=(
             shape((2 * HALF_STRIP, 128), BF16),
             shape((128, 128), BF16),
-            shape((2 * HALF_STRIP + per * 64, 128), BF16),
+            shape((SPARE + per * 64, 128), BF16),
             shape((2,) + across_taps.shape, BF16),
         ),
         in_specs=[HBM] * 3 + [VMEM] + [HBM] * 3,
@@ -418,10 +423,11 @@
         name="mid",
     )(mask_pixels, col_first, col_second, to_first)
     late, to_above, to_below = lax.optimization_barrier((library, to_above, to_below))
-    shards = [library]
-    for d in range(1, n_col):
-        part = late if d in (1, n_col - 1) else block
-        shards.append(lax.ppermute(part, "col", [(i, i ^ d) for i in range(n_col)]))
+    blocks = {0: library}
+    for d in sorted(range(1, n_col), key=lambda d: (d == n_col - 1, -(d & -d))):
+        part = late if d == n_col - 1 else block
+        blocks[d] = lax.ppermute(part, "col", [(i, i ^ d) for i in range(n_col)])
+    shards = [blocks[d] for d in range(n_col)]
     row_first, row_second = (
         lax.ppermute(x, "row", pairs) for x, pairs in zip((to_above, to_below), swaps(n_row))
     )
@@ -457,26 +463,36 @@
         + [pltpu.VMEM((2 * GROUP, 256, 256), BF16)] * 2
         + [pltpu.VMEM((2 * GROUP, NB + 1, CB, 256), BF16)] * 2,
         compiler_params=PARAMS,
-        cost_estimate=pl.CostEstimate(flops=8 * 10**8, bytes_accessed=10**5, transcendentals=0),
+        cost_estimate=pl.CostEstimate(flops=75 * 10**7, bytes_accessed=10**5, transcendentals=0),
         name="socs",
     )(in_hbm(kernel_weights), windows, row_first, row_second, col_first, col_second, to_first, ahead, back)
 
+    blurred_rows = pl.pallas_call(
+        functools.partial(rows_kernel, n_row, n_col),
+        out_shape=shape((rows, WIDE), F32),
+        in_specs=[VMEM] * 2,
+        out_specs=VMEM,
+        scratch_shapes=[pltpu.VMEM((WIDE, 384), BF16)],
+        compiler_params=PARAMS,
+        cost_estimate=pl.CostEstimate(flops=10**6, bytes_accessed=10**5, transcendentals=0),
+        name="rows",
+    )(acc, g_row)
+
     return pl.pallas_call(
-        functools.partial(final_kernel, n_row, n_col),
+        final_kernel,
         out_shape=shape((rows, cols), F32),
-        in_specs=[VMEM] * (5 + n_col),
+        in_specs=[VMEM] * (4 + n_col),
         out_specs=VMEM,
         scratch_shapes=[
             pltpu.VMEM((n_col * per + 1, 64, 128), BF16),
             pltpu.SMEM((SLOTS, 128), jnp.int32),
             pltpu.VMEM((384, cols + 256), BF16),
-            pltpu.VMEM((WIDE, 384), BF16),
             pltpu.VMEM((2, rows, WIDE), BF16),
             pltpu.SemaphoreType.DMA,
         ],
         compiler_params=PARAMS,
         name="final",
-    )(acc, images, g_row, g_far, g_col, *shards)
+    )(images, blurred_rows, g_far, g_col, *shards)
 
 
 def solution(mesh):

time: 24 us -> 22.5 us (0.938)
  waiting for transfers between devices: 1.89 us -> 0.02 us
  Pallas kernels: 10.2 us -> 10.6 us
    ppermute x3, waiting for transfers between devices: 1.17 us -> 0.01 us  [on_device(): blocks[d] = lax.ppermute(part, 'col', [(i, i ^ d) for i in range(n_col)])]
    ppermute x1, waiting for transfers between devices: 0.71 us -> 0.01 us  [on_device(): col_first = lax.ppermute(to_first, 'col', swaps(n_col)[0])]
    pallas_call x1 -> x2, Pallas kernels: 2.41 us -> 2.81 us  [the longest x1 2.33 us: on_device(): pl.pallas_call(final_kernel, out_shape=shape((rows, cols), F32), in_specs...]
  transfers between devices with their start and end apart: 7 -> 7, of which waited for: 2 -> 0; matrix products, arithmetic and copies ran while one was open for 0% -> 0% of each run, Pallas kernels for 27% -> 31%
where the time goes in v13:
time: 22.5 us; the launch traced here: 22.3 us
  starting transfers between devices  10.9 us (48%)
  Pallas kernels  10.6 us (47%)
  between operations  0.79 us (4%)
    pallas_call x1, Pallas kernels, on_device(): pl.pallas_call(functools.partial(socs_kernel, entries, per, n_col * per),...  5.83 us
    ppermute x3, starting transfers between devices, on_device(): blocks[d] = lax.ppermute(part, 'col', [(i, i ^ d) for i in range(n_col)])  4.53 us
    ppermute x1, starting transfers between devices, on_device(): col_first = lax.ppermute(to_first, 'col', swaps(n_col)[0])  4.15 us
    pallas_call x1, Pallas kernels, on_device(): pl.pallas_call(final_kernel, out_shape=shape((rows, cols), F32), in_specs...  2.33 us
    ppermute x2, starting transfers between devices, on_device(): lax.ppermute(x, 'row', pairs)  1.68 us
    pallas_call x1, Pallas kernels, on_device(): pl.pallas_call(prep_kernel, out_shape=(shape((2 * HALF_STRIP, 128), BF16)...  1.29 us
    ppermute x1, starting transfers between devices, on_device(): col_second = lax.ppermute(to_second, ('row', 'col'), second)  0.52 us
    pallas_call x1, Pallas kernels, on_device(): pl.pallas_call(functools.partial(rows_kernel, n_row, n_col), out_shape=sh...  0.48 us
  transfers between devices with their start and end apart: 7, of which 0 were waited for; matrix products, arithmetic and copies ran while one was open for 0% of the time, Pallas kernels for 31%

profile of v13, /device:TPU:0, one launch (start us, length us, event | category | flops | bytes accessed | tf_op | source)
XLA Modules:
  0.0 22.3 jit_solution(3496602785839835729)
XLA Ops:
  0.0 0.0 copy-start
  0.7 1.3 %prep.1 = (bf16[96,128]{1,0:T(8,128)(2,1)S(1)}, bf16[128,128]{1,0:T(8,128)(2,1)S(1)}, bf16[528,128]{1,0:T(8,128)(2,1)S(1)}, bf16[2,12,2,33]{3,2,1,0:T(2,128)(2,1)S(1)}) custom-call(s32[256,512]{1,0:T(8,128)} %mask.5, s32[1,1,8]{2,1,0:T(1,128)} %ids.1, s32[1,1,8]{2,1,0:T(1,128)} %slots.1, s32[1,1]{1,0:T(1,128)S(6)} %copy.9.count, bf16[12,2,33]{2,1,0:T(2,128)(2,1)} %across.1, ...), custom_call_target="tpu_custom_call" | custom-call | tf_op jit(solution)/shard_map/prep/pallas_call | solution.py:382
  2.0 0.5 %collective-permute-start.1 = (bf16[128,128]{1,0:T(8,128)(2,1)S(1)}, bf16[128,128]{1,0:T(8,128)(2,1)S(1)}, u32[]{:S(2)}, u32[]{:S(2)}) collective-permute-start(bf16[128,128]{1,0:T(8,128)(2,1)S(1)} %get-tuple-element.25), channel_id=1, source_target_pairs={{1,2},{2,1},{0,4},{3,7},{5,6},{6,5},{4,0},{7,3},{9,10},{10,9},{8,1... | collective-permute-start | bytes 98312 | tf_op jit(solution)/shard_map/ppermute | solution.py:414
  2.5 4.1 %collective-permute-start = (bf16[96,128]{1,0:T(8,128)(2,1)S(1)}, bf16[96,128]{1,0:T(8,128)(2,1)S(1)}, u32[]{:S(2)}, u32[]{:S(2)}) collective-permute-start(bf16[96,128]{1,0:T(8,128)(2,1)S(1)} %get-tuple-element.24.own), channel_id=1, source_target_pairs={{0,1},{2,3},{1,0},{3,2},{4,5},{6,7},{5,4},{7,6},{8,9},{10,11},{9,8... | collective-permute-start | bytes 73736 | tf_op jit(solution)/shard_map/ppermute | solution.py:415
  6.7 0.0 copy-start.1
  6.7 0.0 collective-permute-start.4
  6.7 1.9 %collective-permute-start.5 = (bf16[528,128]{1,0:T(8,128)(2,1)S(1)}, bf16[528,128]{1,0:T(8,128)(2,1)S(1)}, u32[]{:S(2)}, u32[]{:S(2)}) collective-permute-start(bf16[528,128]{1,0:T(8,128)(2,1)S(1)} %get-tuple-element.37), channel_id=1, source_target_pairs={{0,2},{1,3},{2,0},{3,1},{4,6},{5,7},{6,4},{7,5},{8,10},{9,11},{10,... | collective-permute-start | bytes 405512 | tf_op jit(solution)/shard_map/ppermute | solution.py:429
  8.6 0.0 collective-permute-done.from_first.col_first
  8.6 0.0 collective-permute-done.1.from_second.col_second
  8.6 0.0 copy-done
  8.6 0.2 mid.1
  8.8 0.1 collective-permute-start.2
  8.9 1.6 %collective-permute-start.3 = (bf16[48,640]{1,0:T(8,128)(2,1)S(1)}, bf16[48,640]{1,0:T(8,128)(2,1)S(1)}, u32[]{:S(2)}, u32[]{:S(2)}) collective-permute-start(bf16[48,640]{1,0:T(8,128)(2,1)S(1)} %get-tuple-element.29), channel_id=1, source_target_pairs={{4,8},{12,0},{8,4},{0,12},{5,9},{13,1},{9,5},{1,13},{6,10},{14,2},... | collective-permute-start | bytes 184328 | tf_op jit(solution)/shard_map/ppermute | solution.py:432
  10.5 0.0 copy-done.1
  10.5 2.6 %collective-permute-start.6 = (bf16[512,128]{1,0:T(8,128)(2,1)S(1)}, bf16[512,128]{1,0:T(8,128)(2,1)S(1)}, u32[]{:S(2)}, u32[]{:S(2)}) collective-permute-start(bf16[512,128]{1,0:T(8,128)(2,1)S(1)} %bitcast.2), channel_id=1, source_target_pairs={{0,3},{1,2},{2,1},{3,0},{4,7},{5,6},{6,5},{7,4},{8,11},{9,10},{10,... | collective-permute-start | bytes 393224 | tf_op jit(solution)/shard_map/ppermute | solution.py:429
  13.1 0.5 %own.1 = (f32[3,256,256]{2,1,0:T(8,128)S(1)}, f32[12,8,128]{2,1,0:T(8,128)S(1)}, f32[12,8,128]{2,1,0:T(8,128)S(1)}, bf16[256,256]{1,0:T(8,128)(2,1)S(1)}, bf16[2...) custom-call(s32[256,512]{1,0:T(8,128)S(1)} %copy-done, bf16[2,12,2,33]{3,2,1,0:T(2,128)(2,1)S(1)} %get-tuple-element.22.taps), custom_call_target="tpu_custom_call" | custom-call | flops 1000000 | bytes 1000000 | tf_op jit(solution)/shard_map/own/pallas_call | solution.py:435
  13.6 0.0 collective-permute-done.2.row_first
  13.6 0.0 collective-permute-done.3.row_second
  13.6 5.8 %socs.1 = (f32[4,176,256]{2,1,0:T(8,128)S(1)}, s32[16,128]{1,0:T(8,128)S(1)}) custom-call(f32[12]{0:T(128)} %weights.1, f32[3,256,256]{2,1,0:T(8,128)S(1)} %get-tuple-element.23.windows, bf16[48,640]{1,0:T(8,128)(2,1)S(1)} %collective-permute-done.2.row_first, bf16[48,640]{1,0:T(8,128)(2,1)S(1)} %collective-permute-done.3.row_second, ...), custom_call_target="tpu_custom_call" | custom-call | flops 750000000 | bytes 100000 | tf_op jit(solution)/shard_map/socs/pallas_call | solution.py:452
  19.5 0.5 %rows.1.blurred_rows = f32[256,640]{1,0:T(8,128)S(1)} custom-call(f32[4,176,256]{2,1,0:T(8,128)S(1)} %get-tuple-element.33.acc, bf16[256,256]{1,0:T(8,128)(2,1)S(1)} %get-tuple-element.34.g_row), custom_call_target="tpu_custom_call" | custom-call | flops 1000000 | bytes 100000 | tf_op jit(solution)/shard_map/rows/pallas_call | solution.py:470
  20.0 0.0 collective-permute-done.4.rest_1_
  20.0 0.0 collective-permute-done.5.rest_2_
  20.0 0.0 collective-permute-done.6.rest_3_
  20.0 2.3 %final.1 = f32[256,512]{1,0:T(8,128)} custom-call(s32[16,128]{1,0:T(8,128)S(1)} %get-tuple-element.32.images, f32[256,640]{1,0:T(8,128)S(1)} %rows.1.blurred_rows, bf16[256,256]{1,0:T(8,128)(2,1)S(1)} %get-tuple-element.35.g_far, bf16[256,256]{1,0:T(8,128)(2,1)S(1)} %get-tuple-element.36.g_col, bf16[512,128]{1,0:T(8,128)(2,1)S(1)} %bitcast.3, ...), custom_call_target="tpu_custom_call" | custom-call | tf_op jit(solution)/shard_map/final/pallas_call | solution.py:481
Async XLA Ops:
  0.0 8.6 %copy-start = (s32[256,512]{1,0:T(8,128)S(1)}, s32[256,512]{1,0:T(8,128)}, u32[]{:S(2)}) copy-start(s32[256,512]{1,0:T(8,128)} %mask.5) | copy-start | bytes 1572868
  2.0 6.6 %collective-permute-start.1 = (bf16[128,128]{1,0:T(8,128)(2,1)S(1)}, bf16[128,128]{1,0:T(8,128)(2,1)S(1)}, u32[]{:S(2)}, u32[]{:S(2)}) collective-permute-start(bf16[128,128]{1,0:T(8,128)(2,1)S(1)} %get-tuple-element.25), channel_id=1, source_target_pairs={{1,2},{2,1},{0,4},{3,7},{5,6},{6,5},{4,0},{7,3},{9,10},{10,9},{8,1... | collective-permute-start | bytes 98312 | tf_op jit(solution)/shard_map/ppermute | solution.py:414
  2.5 6.1 %collective-permute-start = (bf16[96,128]{1,0:T(8,128)(2,1)S(1)}, bf16[96,128]{1,0:T(8,128)(2,1)S(1)}, u32[]{:S(2)}, u32[]{:S(2)}) collective-permute-start(bf16[96,128]{1,0:T(8,128)(2,1)S(1)} %get-tuple-element.24.own), channel_id=1, source_target_pairs={{0,1},{2,3},{1,0},{3,2},{4,5},{6,7},{5,4},{7,6},{8,9},{10,11},{9,8... | collective-permute-start | bytes 73736 | tf_op jit(solution)/shard_map/ppermute | solution.py:415
  6.7 3.8 %copy-start.1 = (bf16[8,64,128]{2,1,0:T(8,128)(2,1)S(1)}, bf16[8,64,128]{2,1,0:T(8,128)(2,1)}, u32[]{:S(2)}) copy-start(bf16[8,64,128]{2,1,0:T(8,128)(2,1)} %param.12) | copy-start | bytes 393220
  6.7 13.3 %collective-permute-start.4 = (bf16[528,128]{1,0:T(8,128)(2,1)S(1)}, bf16[528,128]{1,0:T(8,128)(2,1)S(1)}, u32[]{:S(2)}, u32[]{:S(2)}) collective-permute-start(bf16[528,128]{1,0:T(8,128)(2,1)S(1)} %get-tuple-element.37), channel_id=1, source_target_pairs={{0,1},{1,0},{2,3},{3,2},{4,5},{5,4},{6,7},{7,6},{8,9},{9,8},{10,11... | collective-permute-start | bytes 405512 | tf_op jit(solution)/shard_map/ppermute | solution.py:429
  6.7 13.3 %collective-permute-start.5 = (bf16[528,128]{1,0:T(8,128)(2,1)S(1)}, bf16[528,128]{1,0:T(8,128)(2,1)S(1)}, u32[]{:S(2)}, u32[]{:S(2)}) collective-permute-start(bf16[528,128]{1,0:T(8,128)(2,1)S(1)} %get-tuple-element.37), channel_id=1, source_target_pairs={{0,2},{1,3},{2,0},{3,1},{4,6},{5,7},{6,4},{7,5},{8,10},{9,11},{10,... | collective-permute-start | bytes 405512 | tf_op jit(solution)/shard_map/ppermute | solution.py:429
  8.8 4.8 %collective-permute-start.2 = (bf16[48,640]{1,0:T(8,128)(2,1)S(1)}, bf16[48,640]{1,0:T(8,128)(2,1)S(1)}, u32[]{:S(2)}, u32[]{:S(2)}) collective-permute-start(bf16[48,640]{1,0:T(8,128)(2,1)S(1)} %get-tuple-element.28), channel_id=1, source_target_pairs={{0,4},{8,12},{4,0},{12,8},{1,5},{9,13},{5,1},{13,9},{2,6},{10,14},... | collective-permute-start | bytes 184328 | tf_op jit(solution)/shard_map/ppermute | solution.py:432
  8.9 4.7 %collective-permute-start.3 = (bf16[48,640]{1,0:T(8,128)(2,1)S(1)}, bf16[48,640]{1,0:T(8,128)(2,1)S(1)}, u32[]{:S(2)}, u32[]{:S(2)}) collective-permute-start(bf16[48,640]{1,0:T(8,128)(2,1)S(1)} %get-tuple-element.29), channel_id=1, source_target_pairs={{4,8},{12,0},{8,4},{0,12},{5,9},{13,1},{9,5},{1,13},{6,10},{14,2},... | collective-permute-start | bytes 184328 | tf_op jit(solution)/shard_map/ppermute | solution.py:432
  10.5 9.5 %collective-permute-start.6 = (bf16[512,128]{1,0:T(8,128)(2,1)S(1)}, bf16[512,128]{1,0:T(8,128)(2,1)S(1)}, u32[]{:S(2)}, u32[]{:S(2)}) collective-permute-start(bf16[512,128]{1,0:T(8,128)(2,1)S(1)} %bitcast.2), channel_id=1, source_target_pairs={{0,3},{1,2},{2,1},{3,0},{4,7},{5,6},{6,5},{7,4},{8,11},{9,10},{10,... | collective-permute-start | bytes 393224 | tf_op jit(solution)/shard_map/ppermute | solution.py:429

commit v14 on v13

--- a/solution.py
+++ b/solution.py
@@ -318,18 +318,16 @@
 
 
 def final_kernel(images, blurred_rows, g_far, g_col, *rest):
-    shards = rest[:-6]
-    out, cells, table, placed, blurred, sem = rest[-6:]
+    shards = rest[:-4]
+    out, cells, placed, blurred = rest[-4:]
     per = (cells.shape[0] - 1) // len(shards)
     rows, cols = out.shape
-    fetch = pltpu.make_async_copy(images, table, sem)
-    fetch.start()
+    table = images[...]
     for i, shard in enumerate(shards):
         rows_of = shard.shape[0] - per * 64
         cells[i * per : (i + 1) * per] = shard[rows_of:, :].reshape(per, 64, 128)
     cells[len(shards) * per] = jnp.zeros((64, 128), BF16)
 
-    fetch.wait()
     slot_rows, slot_cols = rows // 64, cols // 128
     for i in range(-1, slot_rows + 1):
         for j in range(-1, slot_cols + 1):
@@ -485,10 +483,8 @@
         out_specs=VMEM,
         scratch_shapes=[
             pltpu.VMEM((n_col * per + 1, 64, 128), BF16),
-            pltpu.SMEM((SLOTS, 128), jnp.int32),
             pltpu.VMEM((384, cols + 256), BF16),
             pltpu.VMEM((2, rows, WIDE), BF16),
-            pltpu.SemaphoreType.DMA,
         ],
         compiler_params=PARAMS,
         name="final",

time: 22.5 us -> 21.9 us (0.973)
  Pallas kernels: 10.6 us -> 10.1 us
    pallas_call x1, Pallas kernels: 2.33 us -> 1.78 us  [on_device(): pl.pallas_call(final_kernel, out_shape=shape((rows, cols), F32), in_specs...]
  transfers between devices with their start and end apart: 7 -> 7, of which waited for: 0 -> 0; matrix products, arithmetic and copies ran while one was open for 0% -> 0% of each run, Pallas kernels for 31% -> 32%
where the time goes in v14:
time: 21.9 us; the launch traced here: 21.8 us
  starting transfers between devices  10.9 us (50%)
  Pallas kernels  10.1 us (46%)
  between operations  0.79 us (4%)
    pallas_call x1, Pallas kernels, on_device(): pl.pallas_call(functools.partial(socs_kernel, entries, per, n_col * per),...  5.83 us
    ppermute x3, starting transfers between devices, on_device(): blocks[d] = lax.ppermute(part, 'col', [(i, i ^ d) for i in range(n_col)])  4.53 us
    ppermute x1, starting transfers between devices, on_device(): col_first = lax.ppermute(to_first, 'col', swaps(n_col)[0])  4.15 us
    pallas_call x1, Pallas kernels, on_device(): pl.pallas_call(final_kernel, out_shape=shape((rows, cols), F32), in_specs...  1.78 us
    ppermute x2, starting transfers between devices, on_device(): lax.ppermute(x, 'row', pairs)  1.68 us
    pallas_call x1, Pallas kernels, on_device(): pl.pallas_call(prep_kernel, out_shape=(shape((2 * HALF_STRIP, 128), BF16)...  1.29 us
    ppermute x1, starting transfers between devices, on_device(): col_second = lax.ppermute(to_second, ('row', 'col'), second)  0.52 us
    pallas_call x1, Pallas kernels, on_device(): pl.pallas_call(functools.partial(rows_kernel, n_row, n_col), out_shape=sh...  0.48 us
  transfers between devices with their start and end apart: 7, of which 0 were waited for; matrix products, arithmetic and copies ran while one was open for 0% of the time, Pallas kernels for 32%

profile of v14, /device:TPU:0, one launch (start us, length us, event | category | flops | bytes accessed | tf_op | source)
XLA Modules:
  0.0 21.8 jit_solution(7392163289014959483)
XLA Ops:
  0.0 0.0 copy-start
  0.7 1.3 %prep.1 = (bf16[96,128]{1,0:T(8,128)(2,1)S(1)}, bf16[128,128]{1,0:T(8,128)(2,1)S(1)}, bf16[528,128]{1,0:T(8,128)(2,1)S(1)}, bf16[2,12,2,33]{3,2,1,0:T(2,128)(2,1)S(1)}) custom-call(s32[256,512]{1,0:T(8,128)} %mask.5, s32[1,1,8]{2,1,0:T(1,128)} %ids.1, s32[1,1,8]{2,1,0:T(1,128)} %slots.1, s32[1,1]{1,0:T(1,128)S(6)} %copy.9.count, bf16[12,2,33]{2,1,0:T(2,128)(2,1)} %across.1, ...), custom_call_target="tpu_custom_call" | custom-call | tf_op jit(solution)/shard_map/prep/pallas_call | solution.py:380
  2.0 0.5 %collective-permute-start.1 = (bf16[128,128]{1,0:T(8,128)(2,1)S(1)}, bf16[128,128]{1,0:T(8,128)(2,1)S(1)}, u32[]{:S(2)}, u32[]{:S(2)}) collective-permute-start(bf16[128,128]{1,0:T(8,128)(2,1)S(1)} %get-tuple-element.25), channel_id=1, source_target_pairs={{1,2},{2,1},{0,4},{3,7},{5,6},{6,5},{4,0},{7,3},{9,10},{10,9},{8,1... | collective-permute-start | bytes 98312 | tf_op jit(solution)/shard_map/ppermute | solution.py:412
  2.5 4.1 %collective-permute-start = (bf16[96,128]{1,0:T(8,128)(2,1)S(1)}, bf16[96,128]{1,0:T(8,128)(2,1)S(1)}, u32[]{:S(2)}, u32[]{:S(2)}) collective-permute-start(bf16[96,128]{1,0:T(8,128)(2,1)S(1)} %get-tuple-element.24.own), channel_id=1, source_target_pairs={{0,1},{2,3},{1,0},{3,2},{4,5},{6,7},{5,4},{7,6},{8,9},{10,11},{9,8... | collective-permute-start | bytes 73736 | tf_op jit(solution)/shard_map/ppermute | solution.py:413
  6.7 0.0 copy-start.1
  6.7 0.0 collective-permute-start.4
  6.7 1.9 %collective-permute-start.5 = (bf16[528,128]{1,0:T(8,128)(2,1)S(1)}, bf16[528,128]{1,0:T(8,128)(2,1)S(1)}, u32[]{:S(2)}, u32[]{:S(2)}) collective-permute-start(bf16[528,128]{1,0:T(8,128)(2,1)S(1)} %get-tuple-element.37), channel_id=1, source_target_pairs={{0,2},{1,3},{2,0},{3,1},{4,6},{5,7},{6,4},{7,5},{8,10},{9,11},{10,... | collective-permute-start | bytes 405512 | tf_op jit(solution)/shard_map/ppermute | solution.py:427
  8.6 0.0 collective-permute-done.from_first.col_first
  8.6 0.0 collective-permute-done.1.from_second.col_second
  8.6 0.0 copy-done
  8.6 0.2 %mid.1 = (bf16[48,640]{1,0:T(8,128)(2,1)S(1)}, bf16[48,640]{1,0:T(8,128)(2,1)S(1)}) custom-call(s32[256,512]{1,0:T(8,128)S(1)} %copy-done, bf16[96,128]{1,0:T(8,128)(2,1)S(1)} %collective-permute-done.from_first.col_first, bf16[128,128]{1,0:T(8,128)(2,1)S(1)} %collective-permute-done.1.from_second.col_second, bf16[96,128]{1,0:T(8,128)(2,1)S(1)} %get-tuple-element.24.own), custom_call_target="tpu_custom_call" | custom-call | tf_op jit(solution)/shard_map/mid/pallas_call | solution.py:415
  8.8 0.1 collective-permute-start.2
  8.9 1.6 %collective-permute-start.3 = (bf16[48,640]{1,0:T(8,128)(2,1)S(1)}, bf16[48,640]{1,0:T(8,128)(2,1)S(1)}, u32[]{:S(2)}, u32[]{:S(2)}) collective-permute-start(bf16[48,640]{1,0:T(8,128)(2,1)S(1)} %get-tuple-element.29), channel_id=1, source_target_pairs={{4,8},{12,0},{8,4},{0,12},{5,9},{13,1},{9,5},{1,13},{6,10},{14,2},... | collective-permute-start | bytes 184328 | tf_op jit(solution)/shard_map/ppermute | solution.py:430
  10.5 0.0 copy-done.1
  10.5 2.6 %collective-permute-start.6 = (bf16[512,128]{1,0:T(8,128)(2,1)S(1)}, bf16[512,128]{1,0:T(8,128)(2,1)S(1)}, u32[]{:S(2)}, u32[]{:S(2)}) collective-permute-start(bf16[512,128]{1,0:T(8,128)(2,1)S(1)} %bitcast.2), channel_id=1, source_target_pairs={{0,3},{1,2},{2,1},{3,0},{4,7},{5,6},{6,5},{7,4},{8,11},{9,10},{10,... | collective-permute-start | bytes 393224 | tf_op jit(solution)/shard_map/ppermute | solution.py:427
  13.1 0.5 %own.1 = (f32[3,256,256]{2,1,0:T(8,128)S(1)}, f32[12,8,128]{2,1,0:T(8,128)S(1)}, f32[12,8,128]{2,1,0:T(8,128)S(1)}, bf16[256,256]{1,0:T(8,128)(2,1)S(1)}, bf16[2...) custom-call(s32[256,512]{1,0:T(8,128)S(1)} %copy-done, bf16[2,12,2,33]{3,2,1,0:T(2,128)(2,1)S(1)} %get-tuple-element.22.taps), custom_call_target="tpu_custom_call" | custom-call | flops 1000000 | bytes 1000000 | tf_op jit(solution)/shard_map/own/pallas_call | solution.py:433
  13.6 0.0 collective-permute-done.2.row_first
  13.6 0.0 collective-permute-done.3.row_second
  13.6 5.8 %socs.1 = (f32[4,176,256]{2,1,0:T(8,128)S(1)}, s32[16,128]{1,0:T(8,128)S(1)}) custom-call(f32[12]{0:T(128)} %weights.1, f32[3,256,256]{2,1,0:T(8,128)S(1)} %get-tuple-element.23.windows, bf16[48,640]{1,0:T(8,128)(2,1)S(1)} %collective-permute-done.2.row_first, bf16[48,640]{1,0:T(8,128)(2,1)S(1)} %collective-permute-done.3.row_second, ...), custom_call_target="tpu_custom_call" | custom-call | flops 750000000 | bytes 100000 | tf_op jit(solution)/shard_map/socs/pallas_call | solution.py:450
  19.5 0.5 %rows.1.blurred_rows = f32[256,640]{1,0:T(8,128)S(1)} custom-call(f32[4,176,256]{2,1,0:T(8,128)S(1)} %get-tuple-element.33.acc, bf16[256,256]{1,0:T(8,128)(2,1)S(1)} %get-tuple-element.34.g_row), custom_call_target="tpu_custom_call" | custom-call | flops 1000000 | bytes 100000 | tf_op jit(solution)/shard_map/rows/pallas_call | solution.py:468
  20.0 0.0 collective-permute-done.4.rest_1_
  20.0 0.0 collective-permute-done.5.rest_2_
  20.0 0.0 collective-permute-done.6.rest_3_
  20.0 1.8 %final.1 = f32[256,512]{1,0:T(8,128)} custom-call(s32[16,128]{1,0:T(8,128)S(1)} %get-tuple-element.32.images, f32[256,640]{1,0:T(8,128)S(1)} %rows.1.blurred_rows, bf16[256,256]{1,0:T(8,128)(2,1)S(1)} %get-tuple-element.35.g_far, bf16[256,256]{1,0:T(8,128)(2,1)S(1)} %get-tuple-element.36.g_col, bf16[512,128]{1,0:T(8,128)(2,1)S(1)} %bitcast.3, ...), custom_call_target="tpu_custom_call" | custom-call | tf_op jit(solution)/shard_map/final/pallas_call | solution.py:479
Async XLA Ops:
  0.0 8.6 %copy-start = (s32[256,512]{1,0:T(8,128)S(1)}, s32[256,512]{1,0:T(8,128)}, u32[]{:S(2)}) copy-start(s32[256,512]{1,0:T(8,128)} %mask.5) | copy-start | bytes 1572868
  2.0 6.6 %collective-permute-start.1 = (bf16[128,128]{1,0:T(8,128)(2,1)S(1)}, bf16[128,128]{1,0:T(8,128)(2,1)S(1)}, u32[]{:S(2)}, u32[]{:S(2)}) collective-permute-start(bf16[128,128]{1,0:T(8,128)(2,1)S(1)} %get-tuple-element.25), channel_id=1, source_target_pairs={{1,2},{2,1},{0,4},{3,7},{5,6},{6,5},{4,0},{7,3},{9,10},{10,9},{8,1... | collective-permute-start | bytes 98312 | tf_op jit(solution)/shard_map/ppermute | solution.py:412
  2.5 6.1 %collective-permute-start = (bf16[96,128]{1,0:T(8,128)(2,1)S(1)}, bf16[96,128]{1,0:T(8,128)(2,1)S(1)}, u32[]{:S(2)}, u32[]{:S(2)}) collective-permute-start(bf16[96,128]{1,0:T(8,128)(2,1)S(1)} %get-tuple-element.24.own), channel_id=1, source_target_pairs={{0,1},{2,3},{1,0},{3,2},{4,5},{6,7},{5,4},{7,6},{8,9},{10,11},{9,8... | collective-permute-start | bytes 73736 | tf_op jit(solution)/shard_map/ppermute | solution.py:413
  6.7 3.8 %copy-start.1 = (bf16[8,64,128]{2,1,0:T(8,128)(2,1)S(1)}, bf16[8,64,128]{2,1,0:T(8,128)(2,1)}, u32[]{:S(2)}) copy-start(bf16[8,64,128]{2,1,0:T(8,128)(2,1)} %param.12) | copy-start | bytes 393220
  6.7 13.3 %collective-permute-start.4 = (bf16[528,128]{1,0:T(8,128)(2,1)S(1)}, bf16[528,128]{1,0:T(8,128)(2,1)S(1)}, u32[]{:S(2)}, u32[]{:S(2)}) collective-permute-start(bf16[528,128]{1,0:T(8,128)(2,1)S(1)} %get-tuple-element.37), channel_id=1, source_target_pairs={{0,1},{1,0},{2,3},{3,2},{4,5},{5,4},{6,7},{7,6},{8,9},{9,8},{10,11... | collective-permute-start | bytes 405512 | tf_op jit(solution)/shard_map/ppermute | solution.py:427
  6.7 13.3 %collective-permute-start.5 = (bf16[528,128]{1,0:T(8,128)(2,1)S(1)}, bf16[528,128]{1,0:T(8,128)(2,1)S(1)}, u32[]{:S(2)}, u32[]{:S(2)}) collective-permute-start(bf16[528,128]{1,0:T(8,128)(2,1)S(1)} %get-tuple-element.37), channel_id=1, source_target_pairs={{0,2},{1,3},{2,0},{3,1},{4,6},{5,7},{6,4},{7,5},{8,10},{9,11},{10,... | collective-permute-start | bytes 405512 | tf_op jit(solution)/shard_map/ppermute | solution.py:427
  8.8 4.8 %collective-permute-start.2 = (bf16[48,640]{1,0:T(8,128)(2,1)S(1)}, bf16[48,640]{1,0:T(8,128)(2,1)S(1)}, u32[]{:S(2)}, u32[]{:S(2)}) collective-permute-start(bf16[48,640]{1,0:T(8,128)(2,1)S(1)} %get-tuple-element.28), channel_id=1, source_target_pairs={{0,4},{8,12},{4,0},{12,8},{1,5},{9,13},{5,1},{13,9},{2,6},{10,14},... | collective-permute-start | bytes 184328 | tf_op jit(solution)/shard_map/ppermute | solution.py:430
  8.9 4.7 %collective-permute-start.3 = (bf16[48,640]{1,0:T(8,128)(2,1)S(1)}, bf16[48,640]{1,0:T(8,128)(2,1)S(1)}, u32[]{:S(2)}, u32[]{:S(2)}) collective-permute-start(bf16[48,640]{1,0:T(8,128)(2,1)S(1)} %get-tuple-element.29), channel_id=1, source_target_pairs={{4,8},{12,0},{8,4},{0,12},{5,9},{13,1},{9,5},{1,13},{6,10},{14,2},... | collective-permute-start | bytes 184328 | tf_op jit(solution)/shard_map/ppermute | solution.py:430
  10.5 9.5 %collective-permute-start.6 = (bf16[512,128]{1,0:T(8,128)(2,1)S(1)}, bf16[512,128]{1,0:T(8,128)(2,1)S(1)}, u32[]{:S(2)}, u32[]{:S(2)}) collective-permute-start(bf16[512,128]{1,0:T(8,128)(2,1)S(1)} %bitcast.2), channel_id=1, source_target_pairs={{0,3},{1,2},{2,1},{3,0},{4,7},{5,6},{6,5},{7,4},{8,11},{9,10},{10,... | collective-permute-start | bytes 393224 | tf_op jit(solution)/shard_map/ppermute | solution.py:427

commit v15 on v14

--- a/solution.py
+++ b/solution.py
@@ -21,7 +21,7 @@
 RIGHT_AT = 56
 HALF_STRIP = STRIP + 16
 SPARE = 16
-GROUP = 2
+GROUP = 1
 WIDE = 640
 SLOTS = 16
 F32 = jnp.float32
@@ -214,9 +214,12 @@
         edge_rows += [part[MAIN - RIM :], lower_rows[:, lanes]]
     edge_rows.append(jnp.zeros((256 - NB * EDGE_IN, 256), F32))
     x_win[NB] = jnp.concatenate(edge_rows, axis=0).astype(BF16)
-    acc[...] = jnp.zeros(acc.shape, F32)
-    for ref in across + down:
-        ref[...] = jnp.zeros(ref.shape, BF16)
+    for s in range(2):
+        for q in range(2 * GROUP):
+            across[s][q, 0:96, 128:256] = jnp.zeros((96, 128), BF16)
+            across[s][q, 128:CB, 0:128] = jnp.zeros((CB - 128, 128), BF16)
+            down[s][q, 0:128, 128:256] = jnp.zeros((128, 128), BF16)
+            down[s][q, 160:256, 0:128] = jnp.zeros((96, 128), BF16)
 
     slot = lax.broadcasted_iota(jnp.int32, (SLOTS, 128), 0).astype(F32)
     lane = lax.broadcasted_iota(jnp.int32, (SLOTS, 128), 1)
@@ -272,7 +275,8 @@
     def pass_two(m, s):
         for q in range(2 * GROUP):
             second = dot_nn(first[s][q].reshape((NB + 1) * CB, 256), down[s][q])
-            acc[...] += (scale[GROUP * m + q // 2] * (second * second)).reshape(acc.shape)
+            part = (scale[GROUP * m + q // 2] * (second * second)).reshape(acc.shape)
+            acc[...] = part if m == 0 and q == 0 else acc[...] + part
 
     def stage(m, s):
         pass_one(s)

time: 21.9 us -> 22 us (level)
  no operation moved by 1% of the time
where the time goes in v15:
time: 22 us; the launch traced here: 21.8 us
  starting transfers between devices  10.9 us (50%)
  Pallas kernels  10.1 us (46%)
  between operations  0.79 us (4%)
    pallas_call x1, Pallas kernels, on_device(): pl.pallas_call(functools.partial(socs_kernel, entries, per, n_col * per),...  5.87 us
    ppermute x3, starting transfers between devices, on_device(): blocks[d] = lax.ppermute(part, 'col', [(i, i ^ d) for i in range(n_col)])  4.53 us
    ppermute x1, starting transfers between devices, on_device(): col_first = lax.ppermute(to_first, 'col', swaps(n_col)[0])  4.15 us
    pallas_call x1, Pallas kernels, on_device(): pl.pallas_call(final_kernel, out_shape=shape((rows, cols), F32), in_specs...  1.78 us
    ppermute x2, starting transfers between devices, on_device(): lax.ppermute(x, 'row', pairs)  1.68 us
    pallas_call x1, Pallas kernels, on_device(): pl.pallas_call(prep_kernel, out_shape=(shape((2 * HALF_STRIP, 128), BF16)...  1.29 us
    ppermute x1, starting transfers between devices, on_device(): col_second = lax.ppermute(to_second, ('row', 'col'), second)  0.52 us
    pallas_call x1, Pallas kernels, on_device(): pl.pallas_call(own_kernel, out_shape=(shape((NB, rows, 256), F32), shape(...  0.48 us
  transfers between devices with their start and end apart: 7, of which 0 were waited for; matrix products, arithmetic and copies ran while one was open for 0% of the time, Pallas kernels for 32%

profile of v15, /device:TPU:0, one launch (start us, length us, event | category | flops | bytes accessed | tf_op | source)
XLA Modules:
  0.0 21.8 jit_solution(17741705767091856661)
XLA Ops:
  0.0 0.0 copy-start
  0.7 1.3 %prep.1 = (bf16[96,128]{1,0:T(8,128)(2,1)S(1)}, bf16[128,128]{1,0:T(8,128)(2,1)S(1)}, bf16[528,128]{1,0:T(8,128)(2,1)S(1)}, bf16[2,12,2,33]{3,2,1,0:T(2,128)(2,1)S(1)}) custom-call(s32[256,512]{1,0:T(8,128)} %mask.5, s32[1,1,8]{2,1,0:T(1,128)} %ids.1, s32[1,1,8]{2,1,0:T(1,128)} %slots.1, s32[1,1]{1,0:T(1,128)S(6)} %copy.9.count, bf16[12,2,33]{2,1,0:T(2,128)(2,1)} %across.1, ...), custom_call_target="tpu_custom_call" | custom-call | tf_op jit(solution)/shard_map/prep/pallas_call | solution.py:384
  2.0 0.5 %collective-permute-start.1 = (bf16[128,128]{1,0:T(8,128)(2,1)S(1)}, bf16[128,128]{1,0:T(8,128)(2,1)S(1)}, u32[]{:S(2)}, u32[]{:S(2)}) collective-permute-start(bf16[128,128]{1,0:T(8,128)(2,1)S(1)} %get-tuple-element.25), channel_id=1, source_target_pairs={{1,2},{2,1},{0,4},{3,7},{5,6},{6,5},{4,0},{7,3},{9,10},{10,9},{8,1... | collective-permute-start | bytes 98312 | tf_op jit(solution)/shard_map/ppermute | solution.py:416
  2.5 4.1 %collective-permute-start = (bf16[96,128]{1,0:T(8,128)(2,1)S(1)}, bf16[96,128]{1,0:T(8,128)(2,1)S(1)}, u32[]{:S(2)}, u32[]{:S(2)}) collective-permute-start(bf16[96,128]{1,0:T(8,128)(2,1)S(1)} %get-tuple-element.24.own), channel_id=1, source_target_pairs={{0,1},{2,3},{1,0},{3,2},{4,5},{6,7},{5,4},{7,6},{8,9},{10,11},{9,8... | collective-permute-start | bytes 73736 | tf_op jit(solution)/shard_map/ppermute | solution.py:417
  6.7 0.0 copy-start.1
  6.7 0.0 collective-permute-start.4
  6.7 1.9 %collective-permute-start.5 = (bf16[528,128]{1,0:T(8,128)(2,1)S(1)}, bf16[528,128]{1,0:T(8,128)(2,1)S(1)}, u32[]{:S(2)}, u32[]{:S(2)}) collective-permute-start(bf16[528,128]{1,0:T(8,128)(2,1)S(1)} %get-tuple-element.37), channel_id=1, source_target_pairs={{0,2},{1,3},{2,0},{3,1},{4,6},{5,7},{6,4},{7,5},{8,10},{9,11},{10,... | collective-permute-start | bytes 405512 | tf_op jit(solution)/shard_map/ppermute | solution.py:431
  8.6 0.0 collective-permute-done.from_first.col_first
  8.6 0.0 collective-permute-done.1.from_second.col_second
  8.6 0.0 copy-done
  8.6 0.2 %mid.1 = (bf16[48,640]{1,0:T(8,128)(2,1)S(1)}, bf16[48,640]{1,0:T(8,128)(2,1)S(1)}) custom-call(s32[256,512]{1,0:T(8,128)S(1)} %copy-done, bf16[96,128]{1,0:T(8,128)(2,1)S(1)} %collective-permute-done.from_first.col_first, bf16[128,128]{1,0:T(8,128)(2,1)S(1)} %collective-permute-done.1.from_second.col_second, bf16[96,128]{1,0:T(8,128)(2,1)S(1)} %get-tuple-element.24.own), custom_call_target="tpu_custom_call" | custom-call | tf_op jit(solution)/shard_map/mid/pallas_call | solution.py:419
  8.8 0.1 collective-permute-start.2
  8.9 1.6 %collective-permute-start.3 = (bf16[48,640]{1,0:T(8,128)(2,1)S(1)}, bf16[48,640]{1,0:T(8,128)(2,1)S(1)}, u32[]{:S(2)}, u32[]{:S(2)}) collective-permute-start(bf16[48,640]{1,0:T(8,128)(2,1)S(1)} %get-tuple-element.29), channel_id=1, source_target_pairs={{4,8},{12,0},{8,4},{0,12},{5,9},{13,1},{9,5},{1,13},{6,10},{14,2},... | collective-permute-start | bytes 184328 | tf_op jit(solution)/shard_map/ppermute | solution.py:434
  10.5 0.0 copy-done.1
  10.5 2.6 %collective-permute-start.6 = (bf16[512,128]{1,0:T(8,128)(2,1)S(1)}, bf16[512,128]{1,0:T(8,128)(2,1)S(1)}, u32[]{:S(2)}, u32[]{:S(2)}) collective-permute-start(bf16[512,128]{1,0:T(8,128)(2,1)S(1)} %bitcast.2), channel_id=1, source_target_pairs={{0,3},{1,2},{2,1},{3,0},{4,7},{5,6},{6,5},{7,4},{8,11},{9,10},{10,... | collective-permute-start | bytes 393224 | tf_op jit(solution)/shard_map/ppermute | solution.py:431
  13.1 0.5 %own.1 = (f32[3,256,256]{2,1,0:T(8,128)S(1)}, f32[12,8,128]{2,1,0:T(8,128)S(1)}, f32[12,8,128]{2,1,0:T(8,128)S(1)}, bf16[256,256]{1,0:T(8,128)(2,1)S(1)}, bf16[2...) custom-call(s32[256,512]{1,0:T(8,128)S(1)} %copy-done, bf16[2,12,2,33]{3,2,1,0:T(2,128)(2,1)S(1)} %get-tuple-element.22.taps), custom_call_target="tpu_custom_call" | custom-call | flops 1000000 | bytes 1000000 | tf_op jit(solution)/shard_map/own/pallas_call | solution.py:437
  13.6 0.0 collective-permute-done.2.row_first
  13.6 0.0 collective-permute-done.3.row_second
  13.6 5.9 %socs.1 = (f32[4,176,256]{2,1,0:T(8,128)S(1)}, s32[16,128]{1,0:T(8,128)S(1)}) custom-call(f32[12]{0:T(128)} %weights.1, f32[3,256,256]{2,1,0:T(8,128)S(1)} %get-tuple-element.23.windows, bf16[48,640]{1,0:T(8,128)(2,1)S(1)} %collective-permute-done.2.row_first, bf16[48,640]{1,0:T(8,128)(2,1)S(1)} %collective-permute-done.3.row_second, ...), custom_call_target="tpu_custom_call" | custom-call | flops 750000000 | bytes 100000 | tf_op jit(solution)/shard_map/socs/pallas_call | solution.py:454
  19.5 0.5 %rows.1.blurred_rows = f32[256,640]{1,0:T(8,128)S(1)} custom-call(f32[4,176,256]{2,1,0:T(8,128)S(1)} %get-tuple-element.33.acc, bf16[256,256]{1,0:T(8,128)(2,1)S(1)} %get-tuple-element.34.g_row), custom_call_target="tpu_custom_call" | custom-call | flops 1000000 | bytes 100000 | tf_op jit(solution)/shard_map/rows/pallas_call | solution.py:472
  20.0 0.0 collective-permute-done.4.rest_1_
  20.0 0.0 collective-permute-done.5.rest_2_
  20.0 0.0 collective-permute-done.6.rest_3_
  20.0 1.8 %final.1 = f32[256,512]{1,0:T(8,128)} custom-call(s32[16,128]{1,0:T(8,128)S(1)} %get-tuple-element.32.images, f32[256,640]{1,0:T(8,128)S(1)} %rows.1.blurred_rows, bf16[256,256]{1,0:T(8,128)(2,1)S(1)} %get-tuple-element.35.g_far, bf16[256,256]{1,0:T(8,128)(2,1)S(1)} %get-tuple-element.36.g_col, bf16[512,128]{1,0:T(8,128)(2,1)S(1)} %bitcast.3, ...), custom_call_target="tpu_custom_call" | custom-call | tf_op jit(solution)/shard_map/final/pallas_call | solution.py:483
Async XLA Ops:
  0.0 8.6 %copy-start = (s32[256,512]{1,0:T(8,128)S(1)}, s32[256,512]{1,0:T(8,128)}, u32[]{:S(2)}) copy-start(s32[256,512]{1,0:T(8,128)} %mask.5) | copy-start | bytes 1572868
  2.0 6.6 %collective-permute-start.1 = (bf16[128,128]{1,0:T(8,128)(2,1)S(1)}, bf16[128,128]{1,0:T(8,128)(2,1)S(1)}, u32[]{:S(2)}, u32[]{:S(2)}) collective-permute-start(bf16[128,128]{1,0:T(8,128)(2,1)S(1)} %get-tuple-element.25), channel_id=1, source_target_pairs={{1,2},{2,1},{0,4},{3,7},{5,6},{6,5},{4,0},{7,3},{9,10},{10,9},{8,1... | collective-permute-start | bytes 98312 | tf_op jit(solution)/shard_map/ppermute | solution.py:416
  2.5 6.1 %collective-permute-start = (bf16[96,128]{1,0:T(8,128)(2,1)S(1)}, bf16[96,128]{1,0:T(8,128)(2,1)S(1)}, u32[]{:S(2)}, u32[]{:S(2)}) collective-permute-start(bf16[96,128]{1,0:T(8,128)(2,1)S(1)} %get-tuple-element.24.own), channel_id=1, source_target_pairs={{0,1},{2,3},{1,0},{3,2},{4,5},{6,7},{5,4},{7,6},{8,9},{10,11},{9,8... | collective-permute-start | bytes 73736 | tf_op jit(solution)/shard_map/ppermute | solution.py:417
  6.7 3.8 %copy-start.1 = (bf16[8,64,128]{2,1,0:T(8,128)(2,1)S(1)}, bf16[8,64,128]{2,1,0:T(8,128)(2,1)}, u32[]{:S(2)}) copy-start(bf16[8,64,128]{2,1,0:T(8,128)(2,1)} %param.12) | copy-start | bytes 393220
  6.7 13.3 %collective-permute-start.4 = (bf16[528,128]{1,0:T(8,128)(2,1)S(1)}, bf16[528,128]{1,0:T(8,128)(2,1)S(1)}, u32[]{:S(2)}, u32[]{:S(2)}) collective-permute-start(bf16[528,128]{1,0:T(8,128)(2,1)S(1)} %get-tuple-element.37), channel_id=1, source_target_pairs={{0,1},{1,0},{2,3},{3,2},{4,5},{5,4},{6,7},{7,6},{8,9},{9,8},{10,11... | collective-permute-start | bytes 405512 | tf_op jit(solution)/shard_map/ppermute | solution.py:431
  6.7 13.3 %collective-permute-start.5 = (bf16[528,128]{1,0:T(8,128)(2,1)S(1)}, bf16[528,128]{1,0:T(8,128)(2,1)S(1)}, u32[]{:S(2)}, u32[]{:S(2)}) collective-permute-start(bf16[528,128]{1,0:T(8,128)(2,1)S(1)} %get-tuple-element.37), channel_id=1, source_target_pairs={{0,2},{1,3},{2,0},{3,1},{4,6},{5,7},{6,4},{7,5},{8,10},{9,11},{10,... | collective-permute-start | bytes 405512 | tf_op jit(solution)/shard_map/ppermute | solution.py:431
  8.8 4.8 %collective-permute-start.2 = (bf16[48,640]{1,0:T(8,128)(2,1)S(1)}, bf16[48,640]{1,0:T(8,128)(2,1)S(1)}, u32[]{:S(2)}, u32[]{:S(2)}) collective-permute-start(bf16[48,640]{1,0:T(8,128)(2,1)S(1)} %get-tuple-element.28), channel_id=1, source_target_pairs={{0,4},{8,12},{4,0},{12,8},{1,5},{9,13},{5,1},{13,9},{2,6},{10,14},... | collective-permute-start | bytes 184328 | tf_op jit(solution)/shard_map/ppermute | solution.py:434
  8.9 4.7 %collective-permute-start.3 = (bf16[48,640]{1,0:T(8,128)(2,1)S(1)}, bf16[48,640]{1,0:T(8,128)(2,1)S(1)}, u32[]{:S(2)}, u32[]{:S(2)}) collective-permute-start(bf16[48,640]{1,0:T(8,128)(2,1)S(1)} %get-tuple-element.29), channel_id=1, source_target_pairs={{4,8},{12,0},{8,4},{0,12},{5,9},{13,1},{9,5},{1,13},{6,10},{14,2},... | collective-permute-start | bytes 184328 | tf_op jit(solution)/shard_map/ppermute | solution.py:434
  10.5 9.5 %collective-permute-start.6 = (bf16[512,128]{1,0:T(8,128)(2,1)S(1)}, bf16[512,128]{1,0:T(8,128)(2,1)S(1)}, u32[]{:S(2)}, u32[]{:S(2)}) collective-permute-start(bf16[512,128]{1,0:T(8,128)(2,1)S(1)} %bitcast.2), channel_id=1, source_target_pairs={{0,3},{1,2},{2,1},{3,0},{4,7},{5,6},{6,5},{7,4},{8,11},{9,10},{10,... | collective-permute-start | bytes 393224 | tf_op jit(solution)/shard_map/ppermute | solution.py:431

commit v16 on v15

--- a/solution.py
+++ b/solution.py
@@ -21,7 +21,7 @@
 RIGHT_AT = 56
 HALF_STRIP = STRIP + 16
 SPARE = 16
-GROUP = 1
+GROUP = 2
 WIDE = 640
 SLOTS = 16
 F32 = jnp.float32
@@ -425,6 +425,8 @@
         name="mid",
     )(mask_pixels, col_first, col_second, to_first)
     late, to_above, to_below = lax.optimization_barrier((library, to_above, to_below))
+    met = lax.ppermute(kernel_weights, "row", [(i, i ^ 1) for i in range(n_row)])
+    block, met = lax.optimization_barrier((block, met))
     blocks = {0: library}
     for d in sorted(range(1, n_col), key=lambda d: (d == n_col - 1, -(d & -d))):
         part = late if d == n_col - 1 else block
@@ -454,7 +456,7 @@
     acc, images = pl.pallas_call(
         functools.partial(socs_kernel, entries, per, n_col * per),
         out_shape=(shape((NB + 1, CB, 256), F32), shape((SLOTS, 128), jnp.int32)),
-        in_specs=[HBM] + [VMEM] * 8,
+        in_specs=[pl.BlockSpec(memory_space=pl.ANY)] + [VMEM] * 8,
         out_specs=(VMEM,) * 2,
         scratch_shapes=[
             pltpu.VMEM((NB + 1, 256, 256), BF16),
@@ -467,7 +469,7 @@
         compiler_params=PARAMS,
         cost_estimate=pl.CostEstimate(flops=75 * 10**7, bytes_accessed=10**5, transcendentals=0),
         name="socs",
-    )(in_hbm(kernel_weights), windows, row_first, row_second, col_first, col_second, to_first, ahead, back)
+    )(met, windows, row_first, row_second, col_first, col_second, to_first, ahead, back)
 
     blurred_rows = pl.pallas_call(
         functools.partial(rows_kernel, n_row, n_col),

time: 22 us -> 22.6 us (1.027)
  waiting for transfers between devices: 0.02 us -> 1.14 us
  Pallas kernels: 10.1 us -> 9.76 us
    ppermute x0 -> x1, waiting for transfers between devices: none -> 1.12 us  [on_device(): lax.ppermute(kernel_weights, 'row', [(i, i ^ 1) for i in range(n_row)])]
    pallas_call x1, Pallas kernels: 5.87 us -> 5.52 us  [on_device(): pl.pallas_call(functools.partial(socs_kernel, entries, per, n_col * per),...]
  transfers between devices with their start and end apart: 7 -> 8, of which waited for: 0 -> 1; matrix products, arithmetic and copies ran while one was open for 0% -> 0% of each run, Pallas kernels for 32% -> 30%
where the time goes in v16:
time: 22.6 us; the launch traced here: 22.4 us
  starting transfers between devices  10.7 us (47%)
  Pallas kernels  9.76 us (43%)
  waiting for transfers between devices  1.14 us (5%)
  between operations  0.81 us (4%)
    pallas_call x1, Pallas kernels, on_device(): pl.pallas_call(functools.partial(socs_kernel, entries, per, n_col * per),...  5.52 us
    ppermute x3, starting transfers between devices, on_device(): blocks[d] = lax.ppermute(part, 'col', [(i, i ^ d) for i in range(n_col)])  4.39 us
    ppermute x1, starting transfers between devices, on_device(): col_first = lax.ppermute(to_first, 'col', swaps(n_col)[0])  4.15 us
    pallas_call x1, Pallas kernels, on_device(): pl.pallas_call(final_kernel, out_shape=shape((rows, cols), F32), in_specs...  1.78 us
    ppermute x2, starting transfers between devices, on_device(): lax.ppermute(x, 'row', pairs)  1.68 us
    pallas_call x1, Pallas kernels, on_device(): pl.pallas_call(prep_kernel, out_shape=(shape((2 * HALF_STRIP, 128), BF16)...  1.29 us
    ppermute x1, waiting for transfers between devices, on_device(): lax.ppermute(kernel_weights, 'row', [(i, i ^ 1) for i in range(n_row)])  1.12 us
    ppermute x1, starting transfers between devices, on_device(): col_second = lax.ppermute(to_second, ('row', 'col'), second)  0.52 us
  transfers between devices with their start and end apart: 8, of which 1 were waited for; matrix products, arithmetic and copies ran while one was open for 0% of the time, Pallas kernels for 30%

profile of v16, /device:TPU:0, one launch (start us, length us, event | category | flops | bytes accessed | tf_op | source)
XLA Modules:
  0.0 22.4 jit_solution(4332641929954567687)
XLA Ops:
  0.7 1.3 %prep.1 = (bf16[96,128]{1,0:T(8,128)(2,1)S(1)}, bf16[128,128]{1,0:T(8,128)(2,1)S(1)}, bf16[528,128]{1,0:T(8,128)(2,1)S(1)}, bf16[2,12,2,33]{3,2,1,0:T(2,128)(2,1)S(1)}) custom-call(s32[256,512]{1,0:T(8,128)} %mask.5, s32[1,1,8]{2,1,0:T(1,128)} %ids.1, s32[1,1,8]{2,1,0:T(1,128)} %slots.1, s32[1,1]{1,0:T(1,128)S(6)} %copy.9.count, bf16[12,2,33]{2,1,0:T(2,128)(2,1)} %across.1, ...), custom_call_target="tpu_custom_call" | custom-call | tf_op jit(solution)/shard_map/prep/pallas_call | solution.py:384
  2.0 0.0 copy-start.2
  2.0 0.5 %collective-permute-start.2 = (bf16[128,128]{1,0:T(8,128)(2,1)S(1)}, bf16[128,128]{1,0:T(8,128)(2,1)S(1)}, u32[]{:S(2)}, u32[]{:S(2)}) collective-permute-start(bf16[128,128]{1,0:T(8,128)(2,1)S(1)} %get-tuple-element.29), channel_id=1, source_target_pairs={{1,2},{2,1},{0,4},{3,7},{5,6},{6,5},{4,0},{7,3},{9,10},{10,9},{8,1... | collective-permute-start | bytes 98312 | tf_op jit(solution)/shard_map/ppermute | solution.py:416
  2.5 4.1 %collective-permute-start.1 = (bf16[96,128]{1,0:T(8,128)(2,1)S(1)}, bf16[96,128]{1,0:T(8,128)(2,1)S(1)}, u32[]{:S(2)}, u32[]{:S(2)}) collective-permute-start(bf16[96,128]{1,0:T(8,128)(2,1)S(1)} %get-tuple-element.28.own), channel_id=1, source_target_pairs={{0,1},{2,3},{1,0},{3,2},{4,5},{6,7},{5,4},{7,6},{8,9},{10,11},{9,8... | collective-permute-start | bytes 73736 | tf_op jit(solution)/shard_map/ppermute | solution.py:417
  6.7 0.0 copy-done.2
  6.7 0.0 collective-permute-start
  6.7 1.1 %collective-permute-done.weights = f32[12]{0:T(128)S(1)} collective-permute-done((f32[12]{0:T(128)S(1)}, f32[12]{0:T(128)S(1)}, u32[]{:S(2)}, u32[]{:S(2)}) %collective-permute-start) | collective-permute-done | bytes 80 | tf_op jit(solution)/shard_map/ppermute | solution.py:428
  7.8 0.0 collective-permute-start.5
  7.8 1.9 %collective-permute-start.6 = (bf16[528,128]{1,0:T(8,128)(2,1)S(1)}, bf16[528,128]{1,0:T(8,128)(2,1)S(1)}, u32[]{:S(2)}, u32[]{:S(2)}) collective-permute-start(bf16[528,128]{1,0:T(8,128)(2,1)S(1)} %get-tuple-element.41), channel_id=1, source_target_pairs={{0,2},{1,3},{2,0},{3,1},{4,6},{5,7},{6,4},{7,5},{8,10},{9,11},{10,... | collective-permute-start | bytes 405512 | tf_op jit(solution)/shard_map/ppermute | solution.py:433
  9.7 0.0 collective-permute-done.1.from_first.col_first
  9.7 0.0 collective-permute-done.2.from_second.col_second
  9.7 0.2 mid.1
  10.0 0.1 collective-permute-start.3
  10.0 1.6 %collective-permute-start.4 = (bf16[48,640]{1,0:T(8,128)(2,1)S(1)}, bf16[48,640]{1,0:T(8,128)(2,1)S(1)}, u32[]{:S(2)}, u32[]{:S(2)}) collective-permute-start(bf16[48,640]{1,0:T(8,128)(2,1)S(1)} %get-tuple-element.33), channel_id=1, source_target_pairs={{4,8},{12,0},{8,4},{0,12},{5,9},{13,1},{9,5},{1,13},{6,10},{14,2},... | collective-permute-start | bytes 184328 | tf_op jit(solution)/shard_map/ppermute | solution.py:436
  11.7 2.5 %collective-permute-start.7 = (bf16[512,128]{1,0:T(8,128)(2,1)S(1)}, bf16[512,128]{1,0:T(8,128)(2,1)S(1)}, u32[]{:S(2)}, u32[]{:S(2)}) collective-permute-start(bf16[512,128]{1,0:T(8,128)(2,1)S(1)} %bitcast.2), channel_id=1, source_target_pairs={{0,3},{1,2},{2,1},{3,0},{4,7},{5,6},{6,5},{7,4},{8,11},{9,10},{10,... | collective-permute-start | bytes 393224 | tf_op jit(solution)/shard_map/ppermute | solution.py:433
  14.1 0.5 %own.1 = (f32[3,256,256]{2,1,0:T(8,128)S(1)}, f32[12,8,128]{2,1,0:T(8,128)S(1)}, f32[12,8,128]{2,1,0:T(8,128)S(1)}, bf16[256,256]{1,0:T(8,128)(2,1)S(1)}, bf16[2...) custom-call(s32[256,512]{1,0:T(8,128)S(1)} %copy-done, bf16[2,12,2,33]{3,2,1,0:T(2,128)(2,1)S(1)} %get-tuple-element.26.taps), custom_call_target="tpu_custom_call" | custom-call | flops 1000000 | bytes 1000000 | tf_op jit(solution)/shard_map/own/pallas_call | solution.py:439
  14.6 0.0 collective-permute-done.3.row_first
  14.6 0.0 collective-permute-done.4.row_second
  14.6 5.5 %socs.1 = (f32[4,176,256]{2,1,0:T(8,128)S(1)}, s32[16,128]{1,0:T(8,128)S(1)}) custom-call(f32[12]{0:T(128)S(1)} %collective-permute-done.weights, f32[3,256,256]{2,1,0:T(8,128)S(1)} %get-tuple-element.27.windows, bf16[48,640]{1,0:T(8,128)(2,1)S(1)} %collective-permute-done.3.row_first, bf16[48,640]{1,0:T(8,128)(2,1)S(1)} %collective-permute-done.4.row_second, ...), custom_call_target="tpu_custom_call" | custom-call | flops 750000000 | bytes 100000 | tf_op jit(solution)/shard_map/socs/pallas_call | solution.py:456
  20.2 0.5 %rows.1.blurred_rows = f32[256,640]{1,0:T(8,128)S(1)} custom-call(f32[4,176,256]{2,1,0:T(8,128)S(1)} %get-tuple-element.37.acc, bf16[256,256]{1,0:T(8,128)(2,1)S(1)} %get-tuple-element.38.g_row), custom_call_target="tpu_custom_call" | custom-call | flops 1000000 | bytes 100000 | tf_op jit(solution)/shard_map/rows/pallas_call | solution.py:474
  20.6 0.0 collective-permute-done.5.rest_1_
  20.6 0.0 collective-permute-done.6.rest_2_
  20.7 0.0 collective-permute-done.7.rest_3_
  20.7 1.8 %final.1 = f32[256,512]{1,0:T(8,128)} custom-call(s32[16,128]{1,0:T(8,128)S(1)} %get-tuple-element.36.images, f32[256,640]{1,0:T(8,128)S(1)} %rows.1.blurred_rows, bf16[256,256]{1,0:T(8,128)(2,1)S(1)} %get-tuple-element.39.g_far, bf16[256,256]{1,0:T(8,128)(2,1)S(1)} %get-tuple-element.40.g_col, bf16[512,128]{1,0:T(8,128)(2,1)S(1)} %bitcast.3, ...), custom_call_target="tpu_custom_call" | custom-call | tf_op jit(solution)/shard_map/final/pallas_call | solution.py:485
  (4 shorter events, 0.0 us)
Async XLA Ops:
  0.0 9.7 %copy-start = (s32[256,512]{1,0:T(8,128)S(1)}, s32[256,512]{1,0:T(8,128)}, u32[]{:S(2)}) copy-start(s32[256,512]{1,0:T(8,128)} %mask.5) | copy-start | bytes 1572868
  2.0 4.7 %copy-start.2 = (f32[12]{0:T(128)S(1)}, f32[12]{0:T(128)}, u32[]{:S(2)}) copy-start(f32[12]{0:T(128)} %param.11) | copy-start | bytes 148
  2.0 7.7 %collective-permute-start.2 = (bf16[128,128]{1,0:T(8,128)(2,1)S(1)}, bf16[128,128]{1,0:T(8,128)(2,1)S(1)}, u32[]{:S(2)}, u32[]{:S(2)}) collective-permute-start(bf16[128,128]{1,0:T(8,128)(2,1)S(1)} %get-tuple-element.29), channel_id=1, source_target_pairs={{1,2},{2,1},{0,4},{3,7},{5,6},{6,5},{4,0},{7,3},{9,10},{10,9},{8,1... | collective-permute-start | bytes 98312 | tf_op jit(solution)/shard_map/ppermute | solution.py:416
  2.5 7.2 %collective-permute-start.1 = (bf16[96,128]{1,0:T(8,128)(2,1)S(1)}, bf16[96,128]{1,0:T(8,128)(2,1)S(1)}, u32[]{:S(2)}, u32[]{:S(2)}) collective-permute-start(bf16[96,128]{1,0:T(8,128)(2,1)S(1)} %get-tuple-element.28.own), channel_id=1, source_target_pairs={{0,1},{2,3},{1,0},{3,2},{4,5},{6,7},{5,4},{7,6},{8,9},{10,11},{9,8... | collective-permute-start | bytes 73736 | tf_op jit(solution)/shard_map/ppermute | solution.py:417
  6.7 1.1 %collective-permute-start = (f32[12]{0:T(128)S(1)}, f32[12]{0:T(128)S(1)}, u32[]{:S(2)}, u32[]{:S(2)}) collective-permute-start(f32[12]{0:T(128)S(1)} %copy-done.2), channel_id=1, source_target_pairs={{0,4},{4,0},{8,12},{12,8},{1,5},{5,1},{9,13},{13,9},{2,6},{6,2},{1... | collective-permute-start | bytes 152 | tf_op jit(solution)/shard_map/ppermute | solution.py:428
  7.8 3.8 %copy-start.1 = (bf16[8,64,128]{2,1,0:T(8,128)(2,1)S(1)}, bf16[8,64,128]{2,1,0:T(8,128)(2,1)}, u32[]{:S(2)}) copy-start(bf16[8,64,128]{2,1,0:T(8,128)(2,1)} %param.12) | copy-start | bytes 393220
  7.8 12.8 %collective-permute-start.5 = (bf16[528,128]{1,0:T(8,128)(2,1)S(1)}, bf16[528,128]{1,0:T(8,128)(2,1)S(1)}, u32[]{:S(2)}, u32[]{:S(2)}) collective-permute-start(bf16[528,128]{1,0:T(8,128)(2,1)S(1)} %get-tuple-element.41), channel_id=1, source_target_pairs={{0,1},{1,0},{2,3},{3,2},{4,5},{5,4},{6,7},{7,6},{8,9},{9,8},{10,11... | collective-permute-start | bytes 405512 | tf_op jit(solution)/shard_map/ppermute | solution.py:433
  7.8 12.8 %collective-permute-start.6 = (bf16[528,128]{1,0:T(8,128)(2,1)S(1)}, bf16[528,128]{1,0:T(8,128)(2,1)S(1)}, u32[]{:S(2)}, u32[]{:S(2)}) collective-permute-start(bf16[528,128]{1,0:T(8,128)(2,1)S(1)} %get-tuple-element.41), channel_id=1, source_target_pairs={{0,2},{1,3},{2,0},{3,1},{4,6},{5,7},{6,4},{7,5},{8,10},{9,11},{10,... | collective-permute-start | bytes 405512 | tf_op jit(solution)/shard_map/ppermute | solution.py:433
  10.0 4.6 %collective-permute-start.3 = (bf16[48,640]{1,0:T(8,128)(2,1)S(1)}, bf16[48,640]{1,0:T(8,128)(2,1)S(1)}, u32[]{:S(2)}, u32[]{:S(2)}) collective-permute-start(bf16[48,640]{1,0:T(8,128)(2,1)S(1)} %get-tuple-element.32), channel_id=1, source_target_pairs={{0,4},{8,12},{4,0},{12,8},{1,5},{9,13},{5,1},{13,9},{2,6},{10,14},... | collective-permute-start | bytes 184328 | tf_op jit(solution)/shard_map/ppermute | solution.py:436
  10.0 4.6 %collective-permute-start.4 = (bf16[48,640]{1,0:T(8,128)(2,1)S(1)}, bf16[48,640]{1,0:T(8,128)(2,1)S(1)}, u32[]{:S(2)}, u32[]{:S(2)}) collective-permute-start(bf16[48,640]{1,0:T(8,128)(2,1)S(1)} %get-tuple-element.33), channel_id=1, source_target_pairs={{4,8},{12,0},{8,4},{0,12},{5,9},{13,1},{9,5},{1,13},{6,10},{14,2},... | collective-permute-start | bytes 184328 | tf_op jit(solution)/shard_map/ppermute | solution.py:436
  11.7 9.0 %collective-permute-start.7 = (bf16[512,128]{1,0:T(8,128)(2,1)S(1)}, bf16[512,128]{1,0:T(8,128)(2,1)S(1)}, u32[]{:S(2)}, u32[]{:S(2)}) collective-permute-start(bf16[512,128]{1,0:T(8,128)(2,1)S(1)} %bitcast.2), channel_id=1, source_target_pairs={{0,3},{1,2},{2,1},{3,0},{4,7},{5,6},{6,5},{7,4},{8,11},{9,10},{10,... | collective-permute-start | bytes 393224 | tf_op jit(solution)/shard_map/ppermute | solution.py:433

commit v17 on v15

--- a/solution.py
+++ b/solution.py
@@ -21,7 +21,7 @@
 RIGHT_AT = 56
 HALF_STRIP = STRIP + 16
 SPARE = 16
-GROUP = 1
+GROUP = 2
 WIDE = 640
 SLOTS = 16
 F32 = jnp.float32
@@ -426,8 +426,8 @@
     )(mask_pixels, col_first, col_second, to_first)
     late, to_above, to_below = lax.optimization_barrier((library, to_above, to_below))
     blocks = {0: library}
-    for d in sorted(range(1, n_col), key=lambda d: (d == n_col - 1, -(d & -d))):
-        part = late if d == n_col - 1 else block
+    for d in sorted(range(1, n_col), key=lambda d: d == 2):
+        part = late if d == 2 else block
         blocks[d] = lax.ppermute(part, "col", [(i, i ^ d) for i in range(n_col)])
     shards = [blocks[d] for d in range(n_col)]
     row_first, row_second = (

time: 22 us -> 23.6 us (1.073)
  waiting for transfers between devices: 0.02 us -> 2.58 us
  starting transfers between devices: 10.9 us -> 10 us
    ppermute x3, waiting for transfers between devices: 0.01 us -> 2.02 us  [on_device(): blocks[d] = lax.ppermute(part, 'col', [(i, i ^ d) for i in range(n_col)])]
    ppermute x3, starting transfers between devices: 4.53 us -> 3.7 us  [on_device(): blocks[d] = lax.ppermute(part, 'col', [(i, i ^ d) for i in range(n_col)])]
    ppermute x2, waiting for transfers between devices: 0.01 us -> 0.56 us  [on_device(): lax.ppermute(x, 'row', pairs)]
  transfers between devices with their start and end apart: 7 -> 7, of which waited for: 0 -> 2; matrix products, arithmetic and copies ran while one was open for 0% -> 0% of each run, Pallas kernels for 32% -> 30%
where the time goes in v17:
time: 23.6 us; the launch traced here: 23.4 us
  Pallas kernels  10 us (42%)
  starting transfers between devices  10 us (42%)
  waiting for transfers between devices  2.58 us (11%)
  between operations  0.78 us (3%)
    pallas_call x1, Pallas kernels, on_device(): pl.pallas_call(functools.partial(socs_kernel, entries, per, n_col * per),...  5.79 us
    ppermute x1, starting transfers between devices, on_device(): col_first = lax.ppermute(to_first, 'col', swaps(n_col)[0])  4.15 us
    ppermute x3, starting transfers between devices, on_device(): blocks[d] = lax.ppermute(part, 'col', [(i, i ^ d) for i in range(n_col)])  3.7 us
    ppermute x3, waiting for transfers between devices, on_device(): blocks[d] = lax.ppermute(part, 'col', [(i, i ^ d) for i in range(n_col)])  2.02 us
    pallas_call x1, Pallas kernels, on_device(): pl.pallas_call(final_kernel, out_shape=shape((rows, cols), F32), in_specs...  1.78 us
    ppermute x2, starting transfers between devices, on_device(): lax.ppermute(x, 'row', pairs)  1.68 us
    pallas_call x1, Pallas kernels, on_device(): pl.pallas_call(prep_kernel, out_shape=(shape((2 * HALF_STRIP, 128), BF16)...  1.29 us
    ppermute x2, waiting for transfers between devices, on_device(): lax.ppermute(x, 'row', pairs)  0.56 us
  transfers between devices with their start and end apart: 7, of which 2 were waited for; matrix products, arithmetic and copies ran while one was open for 0% of the time, Pallas kernels for 30%

profile of v17, /device:TPU:0, one launch (start us, length us, event | category | flops | bytes accessed | tf_op | source)
XLA Modules:
  0.0 23.4 jit_solution(6719554463715938652)
XLA Ops:
  0.0 0.0 copy-start
  0.7 1.3 %prep.1 = (bf16[96,128]{1,0:T(8,128)(2,1)S(1)}, bf16[128,128]{1,0:T(8,128)(2,1)S(1)}, bf16[528,128]{1,0:T(8,128)(2,1)S(1)}, bf16[2,12,2,33]{3,2,1,0:T(2,128)(2,1)S(1)}) custom-call(s32[256,512]{1,0:T(8,128)} %mask.5, s32[1,1,8]{2,1,0:T(1,128)} %ids.1, s32[1,1,8]{2,1,0:T(1,128)} %slots.1, s32[1,1]{1,0:T(1,128)S(6)} %copy.9.count, bf16[12,2,33]{2,1,0:T(2,128)(2,1)} %across.1, ...), custom_call_target="tpu_custom_call" | custom-call | tf_op jit(solution)/shard_map/prep/pallas_call | solution.py:384
  2.0 0.5 %collective-permute-start.1 = (bf16[128,128]{1,0:T(8,128)(2,1)S(1)}, bf16[128,128]{1,0:T(8,128)(2,1)S(1)}, u32[]{:S(2)}, u32[]{:S(2)}) collective-permute-start(bf16[128,128]{1,0:T(8,128)(2,1)S(1)} %get-tuple-element.25), channel_id=1, source_target_pairs={{1,2},{2,1},{0,4},{3,7},{5,6},{6,5},{4,0},{7,3},{9,10},{10,9},{8,1... | collective-permute-start | bytes 98312 | tf_op jit(solution)/shard_map/ppermute | solution.py:416
  2.5 4.1 %collective-permute-start = (bf16[96,128]{1,0:T(8,128)(2,1)S(1)}, bf16[96,128]{1,0:T(8,128)(2,1)S(1)}, u32[]{:S(2)}, u32[]{:S(2)}) collective-permute-start(bf16[96,128]{1,0:T(8,128)(2,1)S(1)} %get-tuple-element.24.own), channel_id=1, source_target_pairs={{0,1},{2,3},{1,0},{3,2},{4,5},{6,7},{5,4},{7,6},{8,9},{10,11},{9,8... | collective-permute-start | bytes 73736 | tf_op jit(solution)/shard_map/ppermute | solution.py:417
  6.7 0.0 copy-start.1
  6.7 0.0 collective-permute-start.4
  6.7 2.5 %collective-permute-start.6 = (bf16[528,128]{1,0:T(8,128)(2,1)S(1)}, bf16[528,128]{1,0:T(8,128)(2,1)S(1)}, u32[]{:S(2)}, u32[]{:S(2)}) collective-permute-start(bf16[528,128]{1,0:T(8,128)(2,1)S(1)} %get-tuple-element.37), channel_id=1, source_target_pairs={{0,3},{1,2},{2,1},{3,0},{4,7},{5,6},{6,5},{7,4},{8,11},{9,10},{10,... | collective-permute-start | bytes 405512 | tf_op jit(solution)/shard_map/ppermute | solution.py:431
  9.2 0.0 collective-permute-done.from_first.col_first
  9.2 0.0 collective-permute-done.1.from_second.col_second
  9.2 0.0 copy-done
  9.2 0.2 mid.1
  9.5 0.1 collective-permute-start.2
  9.6 1.6 %collective-permute-start.3 = (bf16[48,640]{1,0:T(8,128)(2,1)S(1)}, bf16[48,640]{1,0:T(8,128)(2,1)S(1)}, u32[]{:S(2)}, u32[]{:S(2)}) collective-permute-start(bf16[48,640]{1,0:T(8,128)(2,1)S(1)} %get-tuple-element.29), channel_id=1, source_target_pairs={{4,8},{12,0},{8,4},{0,12},{5,9},{13,1},{9,5},{1,13},{6,10},{14,2},... | collective-permute-start | bytes 184328 | tf_op jit(solution)/shard_map/ppermute | solution.py:434
  11.2 0.0 copy-done.1
  11.2 1.2 %collective-permute-start.5 = (bf16[512,128]{1,0:T(8,128)(2,1)S(1)}, bf16[512,128]{1,0:T(8,128)(2,1)S(1)}, u32[]{:S(2)}, u32[]{:S(2)}) collective-permute-start(bf16[512,128]{1,0:T(8,128)(2,1)S(1)} %bitcast.2), channel_id=1, source_target_pairs={{0,2},{1,3},{2,0},{3,1},{4,6},{5,7},{6,4},{7,5},{8,10},{9,11},{10,... | collective-permute-start | bytes 393224 | tf_op jit(solution)/shard_map/ppermute | solution.py:431
  12.3 0.5 %own.1 = (f32[3,256,256]{2,1,0:T(8,128)S(1)}, f32[12,8,128]{2,1,0:T(8,128)S(1)}, f32[12,8,128]{2,1,0:T(8,128)S(1)}, bf16[256,256]{1,0:T(8,128)(2,1)S(1)}, bf16[2...) custom-call(s32[256,512]{1,0:T(8,128)S(1)} %copy-done, bf16[2,12,2,33]{3,2,1,0:T(2,128)(2,1)S(1)} %get-tuple-element.22.taps), custom_call_target="tpu_custom_call" | custom-call | flops 1000000 | bytes 1000000 | tf_op jit(solution)/shard_map/own/pallas_call | solution.py:437
  12.8 0.0 collective-permute-done.2.row_first
  12.8 0.6 %collective-permute-done.3.row_second = bf16[48,640]{1,0:T(8,128)(2,1)S(1)} collective-permute-done((bf16[48,640]{1,0:T(8,128)(2,1)S(1)}, bf16[48,640]{1,0:T(8,128)(2,1)S(1)}, u32[]{:S(2)}, u32[]{:S(2)}) %collective-permute-start.3) | collective-permute-done | bytes 61472 | tf_op jit(solution)/shard_map/ppermute | solution.py:434
  13.4 5.8 %socs.1 = (f32[4,176,256]{2,1,0:T(8,128)S(1)}, s32[16,128]{1,0:T(8,128)S(1)}) custom-call(f32[12]{0:T(128)} %weights.1, f32[3,256,256]{2,1,0:T(8,128)S(1)} %get-tuple-element.23.windows, bf16[48,640]{1,0:T(8,128)(2,1)S(1)} %collective-permute-done.2.row_first, bf16[48,640]{1,0:T(8,128)(2,1)S(1)} %collective-permute-done.3.row_second, ...), custom_call_target="tpu_custom_call" | custom-call | flops 750000000 | bytes 100000 | tf_op jit(solution)/shard_map/socs/pallas_call | solution.py:454
  19.2 0.5 %rows.1.blurred_rows = f32[256,640]{1,0:T(8,128)S(1)} custom-call(f32[4,176,256]{2,1,0:T(8,128)S(1)} %get-tuple-element.33.acc, bf16[256,256]{1,0:T(8,128)(2,1)S(1)} %get-tuple-element.34.g_row), custom_call_target="tpu_custom_call" | custom-call | flops 1000000 | bytes 100000 | tf_op jit(solution)/shard_map/rows/pallas_call | solution.py:472
  19.6 0.0 collective-permute-done.4.rest_1_
  19.6 0.0 collective-permute-done.6.rest_3_
  19.7 2.0 %collective-permute-done.5.rest_2_ = bf16[512,128]{1,0:T(8,128)(2,1)S(1)} collective-permute-done((bf16[512,128]{1,0:T(8,128)(2,1)S(1)}, bf16[512,128]{1,0:T(8,128)(2,1)S(1)}, u32[]{:S(2)}, u32[]{:S(2)}) %collective-permute-start.5) | collective-permute-done | bytes 131104 | tf_op jit(solution)/shard_map/ppermute | solution.py:431
  21.7 1.8 %final.1 = f32[256,512]{1,0:T(8,128)} custom-call(s32[16,128]{1,0:T(8,128)S(1)} %get-tuple-element.32.images, f32[256,640]{1,0:T(8,128)S(1)} %rows.1.blurred_rows, bf16[256,256]{1,0:T(8,128)(2,1)S(1)} %get-tuple-element.35.g_far, bf16[256,256]{1,0:T(8,128)(2,1)S(1)} %get-tuple-element.36.g_col, bf16[512,128]{1,0:T(8,128)(2,1)S(1)} %bitcast.3, ...), custom_call_target="tpu_custom_call" | custom-call | tf_op jit(solution)/shard_map/final/pallas_call | solution.py:483
Async XLA Ops:
  0.0 9.2 %copy-start = (s32[256,512]{1,0:T(8,128)S(1)}, s32[256,512]{1,0:T(8,128)}, u32[]{:S(2)}) copy-start(s32[256,512]{1,0:T(8,128)} %mask.5) | copy-start | bytes 1572868
  2.0 7.2 %collective-permute-start.1 = (bf16[128,128]{1,0:T(8,128)(2,1)S(1)}, bf16[128,128]{1,0:T(8,128)(2,1)S(1)}, u32[]{:S(2)}, u32[]{:S(2)}) collective-permute-start(bf16[128,128]{1,0:T(8,128)(2,1)S(1)} %get-tuple-element.25), channel_id=1, source_target_pairs={{1,2},{2,1},{0,4},{3,7},{5,6},{6,5},{4,0},{7,3},{9,10},{10,9},{8,1... | collective-permute-start | bytes 98312 | tf_op jit(solution)/shard_map/ppermute | solution.py:416
  2.5 6.7 %collective-permute-start = (bf16[96,128]{1,0:T(8,128)(2,1)S(1)}, bf16[96,128]{1,0:T(8,128)(2,1)S(1)}, u32[]{:S(2)}, u32[]{:S(2)}) collective-permute-start(bf16[96,128]{1,0:T(8,128)(2,1)S(1)} %get-tuple-element.24.own), channel_id=1, source_target_pairs={{0,1},{2,3},{1,0},{3,2},{4,5},{6,7},{5,4},{7,6},{8,9},{10,11},{9,8... | collective-permute-start | bytes 73736 | tf_op jit(solution)/shard_map/ppermute | solution.py:417
  6.7 4.5 %copy-start.1 = (bf16[8,64,128]{2,1,0:T(8,128)(2,1)S(1)}, bf16[8,64,128]{2,1,0:T(8,128)(2,1)}, u32[]{:S(2)}) copy-start(bf16[8,64,128]{2,1,0:T(8,128)(2,1)} %param.12) | copy-start | bytes 393220
  6.7 13.0 %collective-permute-start.4 = (bf16[528,128]{1,0:T(8,128)(2,1)S(1)}, bf16[528,128]{1,0:T(8,128)(2,1)S(1)}, u32[]{:S(2)}, u32[]{:S(2)}) collective-permute-start(bf16[528,128]{1,0:T(8,128)(2,1)S(1)} %get-tuple-element.37), channel_id=1, source_target_pairs={{0,1},{1,0},{2,3},{3,2},{4,5},{5,4},{6,7},{7,6},{8,9},{9,8},{10,11... | collective-permute-start | bytes 405512 | tf_op jit(solution)/shard_map/ppermute | solution.py:431
  6.7 12.9 %collective-permute-start.6 = (bf16[528,128]{1,0:T(8,128)(2,1)S(1)}, bf16[528,128]{1,0:T(8,128)(2,1)S(1)}, u32[]{:S(2)}, u32[]{:S(2)}) collective-permute-start(bf16[528,128]{1,0:T(8,128)(2,1)S(1)} %get-tuple-element.37), channel_id=1, source_target_pairs={{0,3},{1,2},{2,1},{3,0},{4,7},{5,6},{6,5},{7,4},{8,11},{9,10},{10,... | collective-permute-start | bytes 405512 | tf_op jit(solution)/shard_map/ppermute | solution.py:431
  9.5 3.3 %collective-permute-start.2 = (bf16[48,640]{1,0:T(8,128)(2,1)S(1)}, bf16[48,640]{1,0:T(8,128)(2,1)S(1)}, u32[]{:S(2)}, u32[]{:S(2)}) collective-permute-start(bf16[48,640]{1,0:T(8,128)(2,1)S(1)} %get-tuple-element.28), channel_id=1, source_target_pairs={{0,4},{8,12},{4,0},{12,8},{1,5},{9,13},{5,1},{13,9},{2,6},{10,14},... | collective-permute-start | bytes 184328 | tf_op jit(solution)/shard_map/ppermute | solution.py:434
  9.6 3.8 %collective-permute-start.3 = (bf16[48,640]{1,0:T(8,128)(2,1)S(1)}, bf16[48,640]{1,0:T(8,128)(2,1)S(1)}, u32[]{:S(2)}, u32[]{:S(2)}) collective-permute-start(bf16[48,640]{1,0:T(8,128)(2,1)S(1)} %get-tuple-element.29), channel_id=1, source_target_pairs={{4,8},{12,0},{8,4},{0,12},{5,9},{13,1},{9,5},{1,13},{6,10},{14,2},... | collective-permute-start | bytes 184328 | tf_op jit(solution)/shard_map/ppermute | solution.py:434
  11.2 10.5 %collective-permute-start.5 = (bf16[512,128]{1,0:T(8,128)(2,1)S(1)}, bf16[512,128]{1,0:T(8,128)(2,1)S(1)}, u32[]{:S(2)}, u32[]{:S(2)}) collective-permute-start(bf16[512,128]{1,0:T(8,128)(2,1)S(1)} %bitcast.2), channel_id=1, source_target_pairs={{0,2},{1,3},{2,0},{3,1},{4,6},{5,7},{6,4},{7,5},{8,10},{9,11},{10,... | collective-permute-start | bytes 393224 | tf_op jit(solution)/shard_map/ppermute | solution.py:431

commit v18 on v16

--- a/solution.py
+++ b/solution.py
@@ -59,7 +59,7 @@
 
 
 def prep_kernel(
-    mask, ids, slots, count, across, down, library, to_first, to_second, block, taps, ends, a_ids, a_slots, sems
+    mask, ids, slots, count, across, down, library, weights, to_first, to_second, block, taps, line_weights, ends, a_ids, a_slots, sems
 ):
     rows, cols = mask.shape
     copies = [
@@ -70,6 +70,7 @@
         pltpu.make_async_copy(across, taps.at[0], sems.at[4]),
         pltpu.make_async_copy(down, taps.at[1], sems.at[5]),
         pltpu.make_async_copy(library, block.at[SPARE:], sems.at[6]),
+        pltpu.make_async_copy(weights, line_weights, sems.at[7]),
     ]
     for copy in copies:
         copy.start()
@@ -381,25 +382,26 @@
     in_hbm = lambda x: pltpu.with_memory_space_constraint(x, pltpu.HBM)
     mask_hbm = in_hbm(mask_pixels)
 
-    to_first, to_second, block, taps = pl.pallas_call(
+    to_first, to_second, block, taps, line_weights = pl.pallas_call(
         prep_kernel,
         out_shape=(
             shape((2 * HALF_STRIP, 128), BF16),
             shape((128, 128), BF16),
             shape((SPARE + per * 64, 128), BF16),
             shape((2,) + across_taps.shape, BF16),
+            shape(kernel_weights.shape, F32),
         ),
-        in_specs=[HBM] * 3 + [VMEM] + [HBM] * 3,
-        out_specs=(VMEM,) * 4,
+        in_specs=[HBM] * 3 + [VMEM] + [HBM] * 4,
+        out_specs=(VMEM,) * 5,
         scratch_shapes=[
             pltpu.VMEM((2, rows, 128), jnp.int32),
             pltpu.VMEM(cell_ids.shape, jnp.int32),
             pltpu.VMEM(cell_slots.shape, jnp.int32),
-            pltpu.SemaphoreType.DMA((7,)),
+            pltpu.SemaphoreType.DMA((8,)),
         ],
         compiler_params=PARAMS,
         name="prep",
-    )(mask_hbm, in_hbm(cell_ids), in_hbm(cell_slots), cell_count, in_hbm(across_taps), in_hbm(down_taps), in_hbm(library))
+    )(mask_hbm, in_hbm(cell_ids), in_hbm(cell_slots), cell_count, in_hbm(across_taps), in_hbm(down_taps), in_hbm(library), in_hbm(kernel_weights))
 
     def swaps(n):
         rounds = []
@@ -425,16 +427,17 @@
         name="mid",
     )(mask_pixels, col_first, col_second, to_first)
     late, to_above, to_below = lax.optimization_barrier((library, to_above, to_below))
-    met = lax.ppermute(kernel_weights, "row", [(i, i ^ 1) for i in range(n_row)])
-    block, met = lax.optimization_barrier((block, met))
     blocks = {0: library}
     for d in sorted(range(1, n_col), key=lambda d: (d == n_col - 1, -(d & -d))):
         part = late if d == n_col - 1 else block
         blocks[d] = lax.ppermute(part, "col", [(i, i ^ d) for i in range(n_col)])
     shards = [blocks[d] for d in range(n_col)]
-    row_first, row_second = (
-        lax.ppermute(x, "row", pairs) for x, pairs in zip((to_above, to_below), swaps(n_row))
-    )
+    ends = []
+    for f in range(lax.axis_size("frames")):
+        ends += [(f * n_row + a, f * n_row + b) for a, b in swaps(n_row)[1] if abs(a - b) == 1]
+        ends += [(f * n_row + a, (f ^ 1) * n_row + a) for a in (0, n_row - 1)]
+    row_first = lax.ppermute(to_above, "row", swaps(n_row)[0])
+    row_second = lax.ppermute(to_below, ("frames", "row"), ends)
 
     windows, ahead, back, g_row, g_far, g_col = pl.pallas_call(
         own_kernel,
@@ -456,7 +459,7 @@
     acc, images = pl.pallas_call(
         functools.partial(socs_kernel, entries, per, n_col * per),
         out_shape=(shape((NB + 1, CB, 256), F32), shape((SLOTS, 128), jnp.int32)),
-        in_specs=[pl.BlockSpec(memory_space=pl.ANY)] + [VMEM] * 8,
+        in_specs=[VMEM] * 9,
         out_specs=(VMEM,) * 2,
         scratch_shapes=[
             pltpu.VMEM((NB + 1, 256, 256), BF16),
@@ -469,7 +472,7 @@
         compiler_params=PARAMS,
         cost_estimate=pl.CostEstimate(flops=75 * 10**7, bytes_accessed=10**5, transcendentals=0),
         name="socs",
-    )(met, windows, row_first, row_second, col_first, col_second, to_first, ahead, back)
+    )(line_weights, windows, row_first, row_second, col_first, col_second, to_first, ahead, back)
 
     blurred_rows = pl.pallas_call(
         functools.partial(rows_kernel, n_row, n_col),

time: 22.6 us -> 21.6 us (0.956)
  waiting for transfers between devices: 1.14 us -> 0.02 us
    ppermute x3 -> x2, waiting for transfers between devices: 1.12 us -> 0.01 us  [the longest x1 0.01 us: on_device(): row_first = lax.ppermute(to_above, 'row', swaps(n_row)[0])]
    ppermute x3 -> x2, starting transfers between devices: 1.68 us -> 1.66 us  [the longest x1 1.58 us: on_device(): row_second = lax.ppermute(to_below, ('frames', 'row'), ends)]
  transfers between devices with their start and end apart: 8 -> 7, of which waited for: 1 -> 0; matrix products, arithmetic and copies ran while one was open for 0% -> 0% of each run, Pallas kernels for 30% -> 31%
where the time goes in v18:
time: 21.6 us; the launch traced here: 21.4 us
  starting transfers between devices  10.9 us (50%)
  Pallas kernels  9.77 us (45%)
  between operations  0.8 us (4%)
    pallas_call x1, Pallas kernels, on_device(): pl.pallas_call(functools.partial(socs_kernel, entries, per, n_col * per),...  5.52 us
    ppermute x3, starting transfers between devices, on_device(): blocks[d] = lax.ppermute(part, 'col', [(i, i ^ d) for i in range(n_col)])  4.53 us
    ppermute x1, starting transfers between devices, on_device(): col_first = lax.ppermute(to_first, 'col', swaps(n_col)[0])  4.15 us
    pallas_call x1, Pallas kernels, on_device(): pl.pallas_call(final_kernel, out_shape=shape((rows, cols), F32), in_specs...  1.78 us
    ppermute x1, starting transfers between devices, on_device(): row_second = lax.ppermute(to_below, ('frames', 'row'), ends)  1.58 us
    pallas_call x1, Pallas kernels, on_device(): pl.pallas_call(prep_kernel, out_shape=(shape((2 * HALF_STRIP, 128), BF16)...  1.3 us
    ppermute x1, starting transfers between devices, on_device(): col_second = lax.ppermute(to_second, ('row', 'col'), second)  0.52 us
    pallas_call x1, Pallas kernels, on_device(): pl.pallas_call(own_kernel, out_shape=(shape((NB, rows, 256), F32), shape(...  0.47 us
  transfers between devices with their start and end apart: 7, of which 0 were waited for; matrix products, arithmetic and copies ran while one was open for 0% of the time, Pallas kernels for 31%

profile of v18, /device:TPU:0, one launch (start us, length us, event | category | flops | bytes accessed | tf_op | source)
XLA Modules:
  0.0 21.4 jit_solution(8218452355570853642)
XLA Ops:
  0.0 0.0 copy-start
  0.7 1.3 %prep.1 = (bf16[96,128]{1,0:T(8,128)(2,1)S(1)}, bf16[128,128]{1,0:T(8,128)(2,1)S(1)}, bf16[528,128]{1,0:T(8,128)(2,1)S(1)}, bf16[2,12,2,33]{3,2,1,0:T(2,128)(2,1)S(1)}, f32[12]{0:T(128)S(1)}) custom-call(s32[256,512]{1,0:T(8,128)} %mask.5, s32[1,1,8]{2,1,0:T(1,128)} %ids.1, s32[1,1,8]{2,1,0:T(1,128)} %slots.1, s32[1,1]{1,0:T(1,128)S(6)} %copy.9.count, ...), custom_call_target="tpu_custom_call" | custom-call | tf_op jit(solution)/shard_map/prep/pallas_call | solution.py:385
  2.0 0.5 %collective-permute-start.1 = (bf16[128,128]{1,0:T(8,128)(2,1)S(1)}, bf16[128,128]{1,0:T(8,128)(2,1)S(1)}, u32[]{:S(2)}, u32[]{:S(2)}) collective-permute-start(bf16[128,128]{1,0:T(8,128)(2,1)S(1)} %get-tuple-element.27), channel_id=1, source_target_pairs={{1,2},{2,1},{0,4},{3,7},{5,6},{6,5},{4,0},{7,3},{9,10},{10,9},{8,1... | collective-permute-start | bytes 98312 | tf_op jit(solution)/shard_map/ppermute | solution.py:418
  2.5 4.1 %collective-permute-start = (bf16[96,128]{1,0:T(8,128)(2,1)S(1)}, bf16[96,128]{1,0:T(8,128)(2,1)S(1)}, u32[]{:S(2)}, u32[]{:S(2)}) collective-permute-start(bf16[96,128]{1,0:T(8,128)(2,1)S(1)} %get-tuple-element.26.own), channel_id=1, source_target_pairs={{0,1},{2,3},{1,0},{3,2},{4,5},{6,7},{5,4},{7,6},{8,9},{10,11},{9,8... | collective-permute-start | bytes 73736 | tf_op jit(solution)/shard_map/ppermute | solution.py:419
  6.7 0.0 copy-start.1
  6.7 0.0 collective-permute-start.4
  6.7 1.9 %collective-permute-start.5 = (bf16[528,128]{1,0:T(8,128)(2,1)S(1)}, bf16[528,128]{1,0:T(8,128)(2,1)S(1)}, u32[]{:S(2)}, u32[]{:S(2)}) collective-permute-start(bf16[528,128]{1,0:T(8,128)(2,1)S(1)} %get-tuple-element.39), channel_id=1, source_target_pairs={{0,2},{1,3},{2,0},{3,1},{4,6},{5,7},{6,4},{7,5},{8,10},{9,11},{10,... | collective-permute-start | bytes 405512 | tf_op jit(solution)/shard_map/ppermute | solution.py:433
  8.6 0.0 collective-permute-done.from_first.col_first
  8.6 0.0 collective-permute-done.1.from_second.col_second
  8.6 0.0 copy-done
  8.6 0.2 %mid.1 = (bf16[48,640]{1,0:T(8,128)(2,1)S(1)}, bf16[48,640]{1,0:T(8,128)(2,1)S(1)}) custom-call(s32[256,512]{1,0:T(8,128)S(1)} %copy-done, bf16[96,128]{1,0:T(8,128)(2,1)S(1)} %collective-permute-done.from_first.col_first, bf16[128,128]{1,0:T(8,128)(2,1)S(1)} %collective-permute-done.1.from_second.col_second, bf16[96,128]{1,0:T(8,128)(2,1)S(1)} %get-tuple-element.26.own), custom_call_target="tpu_custom_call" | custom-call | tf_op jit(solution)/shard_map/mid/pallas_call | solution.py:421
  8.8 0.1 collective-permute-start.2
  8.9 1.6 %collective-permute-start.3 = (bf16[48,640]{1,0:T(8,128)(2,1)S(1)}, bf16[48,640]{1,0:T(8,128)(2,1)S(1)}, u32[]{:S(2)}, u32[]{:S(2)}) collective-permute-start(bf16[48,640]{1,0:T(8,128)(2,1)S(1)} %get-tuple-element.31), channel_id=1, source_target_pairs={{4,8},{8,4},{0,16},{12,28},{20,24},{24,20},{16,0},{28,12},{5,9},{9... | collective-permute-start | bytes 184328 | tf_op jit(solution)/shard_map/ppermute | solution.py:440
  10.5 0.0 copy-done.1
  10.5 2.6 %collective-permute-start.6 = (bf16[512,128]{1,0:T(8,128)(2,1)S(1)}, bf16[512,128]{1,0:T(8,128)(2,1)S(1)}, u32[]{:S(2)}, u32[]{:S(2)}) collective-permute-start(bf16[512,128]{1,0:T(8,128)(2,1)S(1)} %bitcast.2), channel_id=1, source_target_pairs={{0,3},{1,2},{2,1},{3,0},{4,7},{5,6},{6,5},{7,4},{8,11},{9,10},{10,... | collective-permute-start | bytes 393224 | tf_op jit(solution)/shard_map/ppermute | solution.py:433
  13.1 0.5 %own.1 = (f32[3,256,256]{2,1,0:T(8,128)S(1)}, f32[12,8,128]{2,1,0:T(8,128)S(1)}, f32[12,8,128]{2,1,0:T(8,128)S(1)}, bf16[256,256]{1,0:T(8,128)(2,1)S(1)}, bf16[2...) custom-call(s32[256,512]{1,0:T(8,128)S(1)} %copy-done, bf16[2,12,2,33]{3,2,1,0:T(2,128)(2,1)S(1)} %get-tuple-element.24.taps), custom_call_target="tpu_custom_call" | custom-call | flops 1000000 | bytes 1000000 | tf_op jit(solution)/shard_map/own/pallas_call | solution.py:442
  13.6 0.0 collective-permute-done.2.row_first
  13.6 0.0 collective-permute-done.3.row_second
  13.6 5.5 %socs.1 = (f32[4,176,256]{2,1,0:T(8,128)S(1)}, s32[16,128]{1,0:T(8,128)S(1)}) custom-call(f32[12]{0:T(128)S(1)} %get-tuple-element.23.weights, f32[3,256,256]{2,1,0:T(8,128)S(1)} %get-tuple-element.25.windows, bf16[48,640]{1,0:T(8,128)(2,1)S(1)} %collective-permute-done.2.row_first, bf16[48,640]{1,0:T(8,128)(2,1)S(1)} %collective-permute-done.3.row_second, ...), custom_call_target="tpu_custom_call" | custom-call | flops 750000000 | bytes 100000 | tf_op jit(solution)/shard_map/socs/pallas_call | solution.py:459
  19.2 0.5 %rows.1.blurred_rows = f32[256,640]{1,0:T(8,128)S(1)} custom-call(f32[4,176,256]{2,1,0:T(8,128)S(1)} %get-tuple-element.35.acc, bf16[256,256]{1,0:T(8,128)(2,1)S(1)} %get-tuple-element.36.g_row), custom_call_target="tpu_custom_call" | custom-call | flops 1000000 | bytes 100000 | tf_op jit(solution)/shard_map/rows/pallas_call | solution.py:477
  19.6 0.0 collective-permute-done.4.rest_1_
  19.6 0.0 collective-permute-done.5.rest_2_
  19.7 0.0 collective-permute-done.6.rest_3_
  19.7 1.8 %final.1 = f32[256,512]{1,0:T(8,128)} custom-call(s32[16,128]{1,0:T(8,128)S(1)} %get-tuple-element.34.images, f32[256,640]{1,0:T(8,128)S(1)} %rows.1.blurred_rows, bf16[256,256]{1,0:T(8,128)(2,1)S(1)} %get-tuple-element.37.g_far, bf16[256,256]{1,0:T(8,128)(2,1)S(1)} %get-tuple-element.38.g_col, bf16[512,128]{1,0:T(8,128)(2,1)S(1)} %bitcast.3, ...), custom_call_target="tpu_custom_call" | custom-call | tf_op jit(solution)/shard_map/final/pallas_call | solution.py:488
Async XLA Ops:
  0.0 8.6 %copy-start = (s32[256,512]{1,0:T(8,128)S(1)}, s32[256,512]{1,0:T(8,128)}, u32[]{:S(2)}) copy-start(s32[256,512]{1,0:T(8,128)} %mask.5) | copy-start | bytes 1572868
  2.0 6.6 %collective-permute-start.1 = (bf16[128,128]{1,0:T(8,128)(2,1)S(1)}, bf16[128,128]{1,0:T(8,128)(2,1)S(1)}, u32[]{:S(2)}, u32[]{:S(2)}) collective-permute-start(bf16[128,128]{1,0:T(8,128)(2,1)S(1)} %get-tuple-element.27), channel_id=1, source_target_pairs={{1,2},{2,1},{0,4},{3,7},{5,6},{6,5},{4,0},{7,3},{9,10},{10,9},{8,1... | collective-permute-start | bytes 98312 | tf_op jit(solution)/shard_map/ppermute | solution.py:418
  2.5 6.1 %collective-permute-start = (bf16[96,128]{1,0:T(8,128)(2,1)S(1)}, bf16[96,128]{1,0:T(8,128)(2,1)S(1)}, u32[]{:S(2)}, u32[]{:S(2)}) collective-permute-start(bf16[96,128]{1,0:T(8,128)(2,1)S(1)} %get-tuple-element.26.own), channel_id=1, source_target_pairs={{0,1},{2,3},{1,0},{3,2},{4,5},{6,7},{5,4},{7,6},{8,9},{10,11},{9,8... | collective-permute-start | bytes 73736 | tf_op jit(solution)/shard_map/ppermute | solution.py:419
  6.7 3.8 %copy-start.1 = (bf16[8,64,128]{2,1,0:T(8,128)(2,1)S(1)}, bf16[8,64,128]{2,1,0:T(8,128)(2,1)}, u32[]{:S(2)}) copy-start(bf16[8,64,128]{2,1,0:T(8,128)(2,1)} %param.12) | copy-start | bytes 393220
  6.7 13.0 %collective-permute-start.4 = (bf16[528,128]{1,0:T(8,128)(2,1)S(1)}, bf16[528,128]{1,0:T(8,128)(2,1)S(1)}, u32[]{:S(2)}, u32[]{:S(2)}) collective-permute-start(bf16[528,128]{1,0:T(8,128)(2,1)S(1)} %get-tuple-element.39), channel_id=1, source_target_pairs={{0,1},{1,0},{2,3},{3,2},{4,5},{5,4},{6,7},{7,6},{8,9},{9,8},{10,11... | collective-permute-start | bytes 405512 | tf_op jit(solution)/shard_map/ppermute | solution.py:433
  6.7 12.9 %collective-permute-start.5 = (bf16[528,128]{1,0:T(8,128)(2,1)S(1)}, bf16[528,128]{1,0:T(8,128)(2,1)S(1)}, u32[]{:S(2)}, u32[]{:S(2)}) collective-permute-start(bf16[528,128]{1,0:T(8,128)(2,1)S(1)} %get-tuple-element.39), channel_id=1, source_target_pairs={{0,2},{1,3},{2,0},{3,1},{4,6},{5,7},{6,4},{7,5},{8,10},{9,11},{10,... | collective-permute-start | bytes 405512 | tf_op jit(solution)/shard_map/ppermute | solution.py:433
  8.8 4.8 %collective-permute-start.2 = (bf16[48,640]{1,0:T(8,128)(2,1)S(1)}, bf16[48,640]{1,0:T(8,128)(2,1)S(1)}, u32[]{:S(2)}, u32[]{:S(2)}) collective-permute-start(bf16[48,640]{1,0:T(8,128)(2,1)S(1)} %get-tuple-element.30), channel_id=1, source_target_pairs={{0,4},{8,12},{4,0},{12,8},{1,5},{9,13},{5,1},{13,9},{2,6},{10,14},... | collective-permute-start | bytes 184328 | tf_op jit(solution)/shard_map/ppermute | solution.py:439
  8.9 4.7 %collective-permute-start.3 = (bf16[48,640]{1,0:T(8,128)(2,1)S(1)}, bf16[48,640]{1,0:T(8,128)(2,1)S(1)}, u32[]{:S(2)}, u32[]{:S(2)}) collective-permute-start(bf16[48,640]{1,0:T(8,128)(2,1)S(1)} %get-tuple-element.31), channel_id=1, source_target_pairs={{4,8},{8,4},{0,16},{12,28},{20,24},{24,20},{16,0},{28,12},{5,9},{9... | collective-permute-start | bytes 184328 | tf_op jit(solution)/shard_map/ppermute | solution.py:440
  10.5 9.2 %collective-permute-start.6 = (bf16[512,128]{1,0:T(8,128)(2,1)S(1)}, bf16[512,128]{1,0:T(8,128)(2,1)S(1)}, u32[]{:S(2)}, u32[]{:S(2)}) collective-permute-start(bf16[512,128]{1,0:T(8,128)(2,1)S(1)} %bitcast.2), channel_id=1, source_target_pairs={{0,3},{1,2},{2,1},{3,0},{4,7},{5,6},{6,5},{7,4},{8,11},{9,10},{10,... | collective-permute-start | bytes 393224 | tf_op jit(solution)/shard_map/ppermute | solution.py:433

commit v19 on v18

--- a/solution.py
+++ b/solution.py
@@ -74,6 +74,11 @@
     ]
     for copy in copies:
         copy.start()
+    even = lax.rem(lax.axis_index("col"), 2) == 0
+    copies[0].wait()
+    first = dot_nt(eye(STRIP, 128, 0), ends[0].astype(F32).astype(BF16))
+    copies[1].wait()
+    last = dot_nt(eye(STRIP, 128, 128 - STRIP), ends[1].astype(F32).astype(BF16))
     for copy in copies[2:4]:
         copy.wait()
     line = lax.broadcasted_iota(jnp.int32, (16, 128), 0)
@@ -93,11 +98,6 @@
         strip[HALF_STRIP + STRIP : 2 * HALF_STRIP, :] = jnp.zeros((16, 128), BF16)
     block[0:SPARE, :] = jnp.zeros((SPARE, 128), BF16)
     to_second[2 * HALF_STRIP :, :] = jnp.zeros((128 - 2 * HALF_STRIP, 128), BF16)
-    even = lax.rem(lax.axis_index("col"), 2) == 0
-    copies[0].wait()
-    first = dot_nt(eye(STRIP, 128, 0), ends[0].astype(F32).astype(BF16))
-    copies[1].wait()
-    last = dot_nt(eye(STRIP, 128, 128 - STRIP), ends[1].astype(F32).astype(BF16))
     for strip, part in ((to_first, jnp.where(even, last, first)), (to_second, jnp.where(even, first, last))):
         strip[0:STRIP, :] = part[:, 0:128].astype(BF16)
         strip[HALF_STRIP : HALF_STRIP + STRIP, :] = part[:, 128:256].astype(BF16)
@@ -161,10 +161,37 @@
     g_col[:, 0:128], g_col[:, 128:256] = blur_matrix((256, 128), 0)
 
 
+def blur_rows(n_row, n_col, acc, g_row, out, flat):
+    rows = out.shape[0]
+    cols = CB * NB - 2 * BLUR_HALF
+    row, col = lax.axis_index("row"), lax.axis_index("col")
+    at_row = lax.broadcasted_iota(jnp.int32, (8, 384), 1) - BLUR_HALF
+    row_ok = ((row > 0) | (at_row >= 0)) & ((row < n_row - 1) | (at_row < rows))
+    row_ok = jnp.where(row_ok, 1.0, 0.0)
+    for b in range(NB):
+        edge = acc[NB, :, EDGE_IN * b : EDGE_IN * b + EDGE_OUT]
+        part = jnp.concatenate(
+            [acc[b, :, 0:MAIN], edge, jnp.zeros((CB, 384 - MAIN - EDGE_OUT), F32)], axis=1
+        )
+        part = part * row_ok[0:1]
+        if b == 0:
+            part = jnp.concatenate([jnp.where(col > 0, part[0:8], 0.0), part[8:]], axis=0)
+        if b == NB - 1:
+            part = jnp.concatenate([part[0 : CB - 8], jnp.where(col < n_col - 1, part[CB - 8 :], 0.0)], axis=0)
+        flat[b * CB : (b + 1) * CB, :] = part.astype(BF16)
+    flat[NB * CB :, :] = jnp.zeros((flat.shape[0] - NB * CB, 384), BF16)
+
+    for i in range(rows // 128):
+        part = dot_nt(g_row[...], flat[:, 128 * i : 128 * i + 256])
+        out[128 * i : 128 * i + 128, :] = part[0:128] + part[128:]
+
+
 def socs_kernel(
     entries,
     per,
     empty,
+    n_row,
+    n_col,
     weights,
     windows,
     row_first,
@@ -174,8 +201,11 @@
     own,
     ahead,
     back,
+    g_row,
+    out,
+    images,
     acc,
-    images,
+    flat,
     x_win,
     scale,
     sem,
@@ -295,31 +325,7 @@
     for m in range(1, groups):
         stage(m, m % 2)
     pass_two(groups - 1, (groups - 1) % 2)
-
-
-def rows_kernel(n_row, n_col, acc, g_row, out, flat):
-    rows = out.shape[0]
-    cols = CB * NB - 2 * BLUR_HALF
-    row, col = lax.axis_index("row"), lax.axis_index("col")
-    at_row = lax.broadcasted_iota(jnp.int32, (8, 384), 1) - BLUR_HALF
-    row_ok = ((row > 0) | (at_row >= 0)) & ((row < n_row - 1) | (at_row < rows))
-    row_ok = jnp.where(row_ok, 1.0, 0.0)
-    for b in range(NB):
-        edge = acc[NB, :, EDGE_IN * b : EDGE_IN * b + EDGE_OUT]
-        part = jnp.concatenate(
-            [acc[b, :, 0:MAIN], edge, jnp.zeros((CB, 384 - MAIN - EDGE_OUT), F32)], axis=1
-        )
-        part = part * row_ok[0:1]
-        if b == 0:
-            part = jnp.concatenate([jnp.where(col > 0, part[0:8], 0.0), part[8:]], axis=0)
-        if b == NB - 1:
-            part = jnp.concatenate([part[0 : CB - 8], jnp.where(col < n_col - 1, part[CB - 8 :], 0.0)], axis=0)
-        flat[b * CB : (b + 1) * CB, :] = part.astype(BF16)
-    flat[NB * CB :, :] = jnp.zeros((flat.shape[0] - NB * CB, 384), BF16)
-
-    for i in range(rows // 128):
-        part = dot_nt(g_row[...], flat[:, 128 * i : 128 * i + 256])
-        out[128 * i : 128 * i + 128, :] = part[0:128] + part[128:]
+    blur_rows(n_row, n_col, acc, g_row, out, flat)
 
 
 def final_kernel(images, blurred_rows, g_far, g_col, *rest):
@@ -456,12 +462,14 @@
         name="own",
     )(mask_pixels, taps)
 
-    acc, images = pl.pallas_call(
-        functools.partial(socs_kernel, entries, per, n_col * per),
-        out_shape=(shape((NB + 1, CB, 256), F32), shape((SLOTS, 128), jnp.int32)),
-        in_specs=[VMEM] * 9,
+    blurred_rows, images = pl.pallas_call(
+        functools.partial(socs_kernel, entries, per, n_col * per, n_row, n_col),
+        out_shape=(shape((rows, WIDE), F32), shape((SLOTS, 128), jnp.int32)),
+        in_specs=[VMEM] * 10,
         out_specs=(VMEM,) * 2,
         scratch_shapes=[
+            pltpu.VMEM((NB + 1, CB, 256), F32),
+            pltpu.VMEM((WIDE, 384), BF16),
             pltpu.VMEM((NB + 1, 256, 256), BF16),
             pltpu.SMEM(kernel_weights.shape, F32),
             pltpu.SemaphoreType.DMA,
@@ -472,18 +480,7 @@
         compiler_params=PARAMS,
         cost_estimate=pl.CostEstimate(flops=75 * 10**7, bytes_accessed=10**5, transcendentals=0),
         name="socs",
-    )(line_weights, windows, row_first, row_second, col_first, col_second, to_first, ahead, back)
-
-    blurred_rows = pl.pallas_call(
-        functools.partial(rows_kernel, n_row, n_col),
-        out_shape=shape((rows, WIDE), F32),
-        in_specs=[VMEM] * 2,
-        out_specs=VMEM,
-        scratch_shapes=[pltpu.VMEM((WIDE, 384), BF16)],
-        compiler_params=PARAMS,
-        cost_estimate=pl.CostEstimate(flops=10**6, bytes_accessed=10**5, transcendentals=0),
-        name="rows",
-    )(acc, g_row)
+    )(line_weights, windows, row_first, row_second, col_first, col_second, to_first, ahead, back, g_row)
 
     return pl.pallas_call(
         final_kernel,

time: 21.6 us -> 21.8 us (level)
  Pallas kernels: 9.77 us -> 10 us
    pallas_call x2 -> x1, Pallas kernels: 5.99 us -> 6.15 us  [on_device(): pl.pallas_call(functools.partial(socs_kernel, entries, per, n_col * per,...]
  transfers between devices with their start and end apart: 7 -> 7, of which waited for: 0 -> 0; matrix products, arithmetic and copies ran while one was open for 0% -> 0% of each run, Pallas kernels for 31% -> 32%
where the time goes in v19:
time: 21.8 us; the launch traced here: 21.7 us
  starting transfers between devices  10.9 us (50%)
  Pallas kernels  10 us (46%)
  between operations  0.79 us (4%)
    pallas_call x1, Pallas kernels, on_device(): pl.pallas_call(functools.partial(socs_kernel, entries, per, n_col * per,...  6.15 us
    ppermute x3, starting transfers between devices, on_device(): blocks[d] = lax.ppermute(part, 'col', [(i, i ^ d) for i in range(n_col)])  4.53 us
    ppermute x1, starting transfers between devices, on_device(): col_first = lax.ppermute(to_first, 'col', swaps(n_col)[0])  4.15 us
    pallas_call x1, Pallas kernels, on_device(): pl.pallas_call(final_kernel, out_shape=shape((rows, cols), F32), in_specs...  1.78 us
    ppermute x1, starting transfers between devices, on_device(): row_second = lax.ppermute(to_below, ('frames', 'row'), ends)  1.58 us
    pallas_call x1, Pallas kernels, on_device(): pl.pallas_call(prep_kernel, out_shape=(shape((2 * HALF_STRIP, 128), BF16)...  1.38 us
    ppermute x1, starting transfers between devices, on_device(): col_second = lax.ppermute(to_second, ('row', 'col'), second)  0.52 us
    pallas_call x1, Pallas kernels, on_device(): pl.pallas_call(own_kernel, out_shape=(shape((NB, rows, 256), F32), shape(...  0.47 us
  transfers between devices with their start and end apart: 7, of which 0 were waited for; matrix products, arithmetic and copies ran while one was open for 0% of the time, Pallas kernels for 32%

profile of v19, /device:TPU:0, one launch (start us, length us, event | category | flops | bytes accessed | tf_op | source)
XLA Modules:
  0.0 21.7 jit_solution(16067886083325801963)
XLA Ops:
  0.0 0.0 copy-start
  0.7 1.4 %prep.1 = (bf16[96,128]{1,0:T(8,128)(2,1)S(1)}, bf16[128,128]{1,0:T(8,128)(2,1)S(1)}, bf16[528,128]{1,0:T(8,128)(2,1)S(1)}, bf16[2,12,2,33]{3,2,1,0:T(2,128)(2,1)S(1)}, f32[12]{0:T(128)S(1)}) custom-call(s32[256,512]{1,0:T(8,128)} %mask.5, s32[1,1,8]{2,1,0:T(1,128)} %ids.1, s32[1,1,8]{2,1,0:T(1,128)} %slots.1, s32[1,1]{1,0:T(1,128)S(6)} %copy.9.count, ...), custom_call_target="tpu_custom_call" | custom-call | tf_op jit(solution)/shard_map/prep/pallas_call | solution.py:391
  2.1 0.5 %collective-permute-start.1 = (bf16[128,128]{1,0:T(8,128)(2,1)S(1)}, bf16[128,128]{1,0:T(8,128)(2,1)S(1)}, u32[]{:S(2)}, u32[]{:S(2)}) collective-permute-start(bf16[128,128]{1,0:T(8,128)(2,1)S(1)} %get-tuple-element.27), channel_id=1, source_target_pairs={{1,2},{2,1},{0,4},{3,7},{5,6},{6,5},{4,0},{7,3},{9,10},{10,9},{8,1... | collective-permute-start | bytes 98312 | tf_op jit(solution)/shard_map/ppermute | solution.py:424
  2.6 4.1 %collective-permute-start = (bf16[96,128]{1,0:T(8,128)(2,1)S(1)}, bf16[96,128]{1,0:T(8,128)(2,1)S(1)}, u32[]{:S(2)}, u32[]{:S(2)}) collective-permute-start(bf16[96,128]{1,0:T(8,128)(2,1)S(1)} %get-tuple-element.26.own), channel_id=1, source_target_pairs={{0,1},{2,3},{1,0},{3,2},{4,5},{6,7},{5,4},{7,6},{8,9},{10,11},{9,8... | collective-permute-start | bytes 73736 | tf_op jit(solution)/shard_map/ppermute | solution.py:425
  6.8 0.0 copy-start.1
  6.8 0.0 collective-permute-start.4
  6.8 1.9 %collective-permute-start.5 = (bf16[528,128]{1,0:T(8,128)(2,1)S(1)}, bf16[528,128]{1,0:T(8,128)(2,1)S(1)}, u32[]{:S(2)}, u32[]{:S(2)}) collective-permute-start(bf16[528,128]{1,0:T(8,128)(2,1)S(1)} %get-tuple-element.39), channel_id=1, source_target_pairs={{0,2},{1,3},{2,0},{3,1},{4,6},{5,7},{6,4},{7,5},{8,10},{9,11},{10,... | collective-permute-start | bytes 405512 | tf_op jit(solution)/shard_map/ppermute | solution.py:439
  8.7 0.0 collective-permute-done.from_first.col_first
  8.7 0.0 collective-permute-done.1.from_second.col_second
  8.7 0.0 copy-done
  8.7 0.2 %mid.1 = (bf16[48,640]{1,0:T(8,128)(2,1)S(1)}, bf16[48,640]{1,0:T(8,128)(2,1)S(1)}) custom-call(s32[256,512]{1,0:T(8,128)S(1)} %copy-done, bf16[96,128]{1,0:T(8,128)(2,1)S(1)} %collective-permute-done.from_first.col_first, bf16[128,128]{1,0:T(8,128)(2,1)S(1)} %collective-permute-done.1.from_second.col_second, bf16[96,128]{1,0:T(8,128)(2,1)S(1)} %get-tuple-element.26.own), custom_call_target="tpu_custom_call" | custom-call | tf_op jit(solution)/shard_map/mid/pallas_call | solution.py:427
  8.9 0.1 collective-permute-start.2
  9.0 1.6 %collective-permute-start.3 = (bf16[48,640]{1,0:T(8,128)(2,1)S(1)}, bf16[48,640]{1,0:T(8,128)(2,1)S(1)}, u32[]{:S(2)}, u32[]{:S(2)}) collective-permute-start(bf16[48,640]{1,0:T(8,128)(2,1)S(1)} %get-tuple-element.31), channel_id=1, source_target_pairs={{4,8},{8,4},{0,16},{12,28},{20,24},{24,20},{16,0},{28,12},{5,9},{9... | collective-permute-start | bytes 184328 | tf_op jit(solution)/shard_map/ppermute | solution.py:446
  10.6 0.0 copy-done.1
  10.6 2.6 %collective-permute-start.6 = (bf16[512,128]{1,0:T(8,128)(2,1)S(1)}, bf16[512,128]{1,0:T(8,128)(2,1)S(1)}, u32[]{:S(2)}, u32[]{:S(2)}) collective-permute-start(bf16[512,128]{1,0:T(8,128)(2,1)S(1)} %bitcast.2), channel_id=1, source_target_pairs={{0,3},{1,2},{2,1},{3,0},{4,7},{5,6},{6,5},{7,4},{8,11},{9,10},{10,... | collective-permute-start | bytes 393224 | tf_op jit(solution)/shard_map/ppermute | solution.py:439
  13.2 0.5 %own.1 = (f32[3,256,256]{2,1,0:T(8,128)S(1)}, f32[12,8,128]{2,1,0:T(8,128)S(1)}, f32[12,8,128]{2,1,0:T(8,128)S(1)}, bf16[256,256]{1,0:T(8,128)(2,1)S(1)}, bf16[2...) custom-call(s32[256,512]{1,0:T(8,128)S(1)} %copy-done, bf16[2,12,2,33]{3,2,1,0:T(2,128)(2,1)S(1)} %get-tuple-element.24.taps), custom_call_target="tpu_custom_call" | custom-call | flops 1000000 | bytes 1000000 | tf_op jit(solution)/shard_map/own/pallas_call | solution.py:448
  13.7 0.0 collective-permute-done.2.row_first
  13.7 0.0 collective-permute-done.3.row_second
  13.7 6.1 %socs.1 = (f32[256,640]{1,0:T(8,128)S(1)}, s32[16,128]{1,0:T(8,128)S(1)}) custom-call(f32[12]{0:T(128)S(1)} %get-tuple-element.23.weights, f32[3,256,256]{2,1,0:T(8,128)S(1)} %get-tuple-element.25.windows, bf16[48,640]{1,0:T(8,128)(2,1)S(1)} %collective-permute-done.2.row_first, bf16[48,640]{1,0:T(8,128)(2,1)S(1)} %collective-permute-done.3.row_second, ...), custom_call_target="tpu_custom_call" | custom-call | flops 750000000 | bytes 100000 | tf_op jit(solution)/shard_map/socs/pallas_call | solution.py:465
  19.9 0.0 collective-permute-done.4.rest_1_
  19.9 0.0 collective-permute-done.5.rest_2_
  19.9 0.0 collective-permute-done.6.rest_3_
  19.9 1.8 %final.1 = f32[256,512]{1,0:T(8,128)} custom-call(s32[16,128]{1,0:T(8,128)S(1)} %get-tuple-element.35.images, f32[256,640]{1,0:T(8,128)S(1)} %get-tuple-element.36.blurred_rows, bf16[256,256]{1,0:T(8,128)(2,1)S(1)} %get-tuple-element.37.g_far, bf16[256,256]{1,0:T(8,128)(2,1)S(1)} %get-tuple-element.38.g_col, bf16[512,128]{1,0:T(8,128)(2,1)S(1)} %bitcast.3, ...), custom_call_target="tpu_custom_call" | custom-call | tf_op jit(solution)/shard_map/final/pallas_call | solution.py:485
Async XLA Ops:
  0.0 8.7 %copy-start = (s32[256,512]{1,0:T(8,128)S(1)}, s32[256,512]{1,0:T(8,128)}, u32[]{:S(2)}) copy-start(s32[256,512]{1,0:T(8,128)} %mask.5) | copy-start | bytes 1572868
  2.1 6.6 %collective-permute-start.1 = (bf16[128,128]{1,0:T(8,128)(2,1)S(1)}, bf16[128,128]{1,0:T(8,128)(2,1)S(1)}, u32[]{:S(2)}, u32[]{:S(2)}) collective-permute-start(bf16[128,128]{1,0:T(8,128)(2,1)S(1)} %get-tuple-element.27), channel_id=1, source_target_pairs={{1,2},{2,1},{0,4},{3,7},{5,6},{6,5},{4,0},{7,3},{9,10},{10,9},{8,1... | collective-permute-start | bytes 98312 | tf_op jit(solution)/shard_map/ppermute | solution.py:424
  2.6 6.1 %collective-permute-start = (bf16[96,128]{1,0:T(8,128)(2,1)S(1)}, bf16[96,128]{1,0:T(8,128)(2,1)S(1)}, u32[]{:S(2)}, u32[]{:S(2)}) collective-permute-start(bf16[96,128]{1,0:T(8,128)(2,1)S(1)} %get-tuple-element.26.own), channel_id=1, source_target_pairs={{0,1},{2,3},{1,0},{3,2},{4,5},{6,7},{5,4},{7,6},{8,9},{10,11},{9,8... | collective-permute-start | bytes 73736 | tf_op jit(solution)/shard_map/ppermute | solution.py:425
  6.8 3.8 %copy-start.1 = (bf16[8,64,128]{2,1,0:T(8,128)(2,1)S(1)}, bf16[8,64,128]{2,1,0:T(8,128)(2,1)}, u32[]{:S(2)}) copy-start(bf16[8,64,128]{2,1,0:T(8,128)(2,1)} %param.12) | copy-start | bytes 393220
  6.8 13.1 %collective-permute-start.4 = (bf16[528,128]{1,0:T(8,128)(2,1)S(1)}, bf16[528,128]{1,0:T(8,128)(2,1)S(1)}, u32[]{:S(2)}, u32[]{:S(2)}) collective-permute-start(bf16[528,128]{1,0:T(8,128)(2,1)S(1)} %get-tuple-element.39), channel_id=1, source_target_pairs={{0,1},{1,0},{2,3},{3,2},{4,5},{5,4},{6,7},{7,6},{8,9},{9,8},{10,11... | collective-permute-start | bytes 405512 | tf_op jit(solution)/shard_map/ppermute | solution.py:439
  6.8 13.1 %collective-permute-start.5 = (bf16[528,128]{1,0:T(8,128)(2,1)S(1)}, bf16[528,128]{1,0:T(8,128)(2,1)S(1)}, u32[]{:S(2)}, u32[]{:S(2)}) collective-permute-start(bf16[528,128]{1,0:T(8,128)(2,1)S(1)} %get-tuple-element.39), channel_id=1, source_target_pairs={{0,2},{1,3},{2,0},{3,1},{4,6},{5,7},{6,4},{7,5},{8,10},{9,11},{10,... | collective-permute-start | bytes 405512 | tf_op jit(solution)/shard_map/ppermute | solution.py:439
  8.9 4.8 %collective-permute-start.2 = (bf16[48,640]{1,0:T(8,128)(2,1)S(1)}, bf16[48,640]{1,0:T(8,128)(2,1)S(1)}, u32[]{:S(2)}, u32[]{:S(2)}) collective-permute-start(bf16[48,640]{1,0:T(8,128)(2,1)S(1)} %get-tuple-element.30), channel_id=1, source_target_pairs={{0,4},{8,12},{4,0},{12,8},{1,5},{9,13},{5,1},{13,9},{2,6},{10,14},... | collective-permute-start | bytes 184328 | tf_op jit(solution)/shard_map/ppermute | solution.py:445
  9.0 4.7 %collective-permute-start.3 = (bf16[48,640]{1,0:T(8,128)(2,1)S(1)}, bf16[48,640]{1,0:T(8,128)(2,1)S(1)}, u32[]{:S(2)}, u32[]{:S(2)}) collective-permute-start(bf16[48,640]{1,0:T(8,128)(2,1)S(1)} %get-tuple-element.31), channel_id=1, source_target_pairs={{4,8},{8,4},{0,16},{12,28},{20,24},{24,20},{16,0},{28,12},{5,9},{9... | collective-permute-start | bytes 184328 | tf_op jit(solution)/shard_map/ppermute | solution.py:446
  10.6 9.3 %collective-permute-start.6 = (bf16[512,128]{1,0:T(8,128)(2,1)S(1)}, bf16[512,128]{1,0:T(8,128)(2,1)S(1)}, u32[]{:S(2)}, u32[]{:S(2)}) collective-permute-start(bf16[512,128]{1,0:T(8,128)(2,1)S(1)} %bitcast.2), channel_id=1, source_target_pairs={{0,3},{1,2},{2,1},{3,0},{4,7},{5,6},{6,5},{7,4},{8,11},{9,10},{10,... | collective-permute-start | bytes 393224 | tf_op jit(solution)/shard_map/ppermute | solution.py:439

commit v20 on v18

--- a/solution.py
+++ b/solution.py
@@ -274,10 +274,13 @@
                 first[s][q, j] = part[q * CB : (q + 1) * CB]
 
     def pass_two(m, s):
-        for q in range(2 * GROUP):
-            second = dot_nn(first[s][q].reshape((NB + 1) * CB, 256), down[s][q])
-            part = (scale[GROUP * m + q // 2] * (second * second)).reshape(acc.shape)
-            acc[...] = part if m == 0 and q == 0 else acc[...] + part
+        for g in range(GROUP):
+            total = None
+            for q in (2 * g, 2 * g + 1):
+                second = dot_nn(first[s][q].reshape((NB + 1) * CB, 256), down[s][q])
+                total = second * second if total is None else total + second * second
+            part = (scale[GROUP * m + g] * total).reshape(acc.shape)
+            acc[...] = part if m == 0 and g == 0 else acc[...] + part
 
     def stage(m, s):
         pass_one(s)
@@ -428,8 +431,8 @@
     )(mask_pixels, col_first, col_second, to_first)
     late, to_above, to_below = lax.optimization_barrier((library, to_above, to_below))
     blocks = {0: library}
-    for d in sorted(range(1, n_col), key=lambda d: (d == n_col - 1, -(d & -d))):
-        part = late if d == n_col - 1 else block
+    for d in sorted(range(1, n_col), key=lambda d: d == 1):
+        part = late if d == 1 else block
         blocks[d] = lax.ppermute(part, "col", [(i, i ^ d) for i in range(n_col)])
     shards = [blocks[d] for d in range(n_col)]
     ends = []

time: 21.6 us -> 22.6 us (1.046)
  waiting for transfers between devices: 0.02 us -> 1.79 us
  starting transfers between devices: 10.9 us -> 10.1 us
    ppermute x3, waiting for transfers between devices: 0.01 us -> 1.02 us  [on_device(): blocks[d] = lax.ppermute(part, 'col', [(i, i ^ d) for i in range(n_col)])]
    ppermute x1, waiting for transfers between devices: 0.01 us -> 0.76 us  [on_device(): row_second = lax.ppermute(to_below, ('frames', 'row'), ends)]
    ppermute x3, starting transfers between devices: 4.53 us -> 3.82 us  [on_device(): blocks[d] = lax.ppermute(part, 'col', [(i, i ^ d) for i in range(n_col)])]
  transfers between devices with their start and end apart: 7 -> 7, of which waited for: 0 -> 2; matrix products, arithmetic and copies ran while one was open for 0% -> 0% of each run, Pallas kernels for 31% -> 30%
where the time goes in v20:
time: 22.6 us; the launch traced here: 22.5 us
  starting transfers between devices  10.1 us (45%)
  Pallas kernels  9.73 us (43%)
  waiting for transfers between devices  1.79 us (8%)
  between operations  0.78 us (3%)
    pallas_call x1, Pallas kernels, on_device(): pl.pallas_call(functools.partial(socs_kernel, entries, per, n_col * per),...  5.49 us
    ppermute x1, starting transfers between devices, on_device(): col_first = lax.ppermute(to_first, 'col', swaps(n_col)[0])  4.15 us
    ppermute x3, starting transfers between devices, on_device(): blocks[d] = lax.ppermute(part, 'col', [(i, i ^ d) for i in range(n_col)])  3.82 us
    pallas_call x1, Pallas kernels, on_device(): pl.pallas_call(final_kernel, out_shape=shape((rows, cols), F32), in_specs...  1.78 us
    ppermute x1, starting transfers between devices, on_device(): row_second = lax.ppermute(to_below, ('frames', 'row'), ends)  1.58 us
    pallas_call x1, Pallas kernels, on_device(): pl.pallas_call(prep_kernel, out_shape=(shape((2 * HALF_STRIP, 128), BF16)...  1.3 us
    ppermute x3, waiting for transfers between devices, on_device(): blocks[d] = lax.ppermute(part, 'col', [(i, i ^ d) for i in range(n_col)])  1.02 us
    ppermute x1, waiting for transfers between devices, on_device(): row_second = lax.ppermute(to_below, ('frames', 'row'), ends)  0.76 us
  transfers between devices with their start and end apart: 7, of which 2 were waited for; matrix products, arithmetic and copies ran while one was open for 0% of the time, Pallas kernels for 30%

profile of v20, /device:TPU:0, one launch (start us, length us, event | category | flops | bytes accessed | tf_op | source)
XLA Modules:
  0.0 22.5 jit_solution(13253977823052321419)
XLA Ops:
  0.0 0.0 copy-start
  0.7 1.3 %prep.1 = (bf16[96,128]{1,0:T(8,128)(2,1)S(1)}, bf16[128,128]{1,0:T(8,128)(2,1)S(1)}, bf16[528,128]{1,0:T(8,128)(2,1)S(1)}, bf16[2,12,2,33]{3,2,1,0:T(2,128)(2,1)S(1)}, f32[12]{0:T(128)S(1)}) custom-call(s32[256,512]{1,0:T(8,128)} %mask.5, s32[1,1,8]{2,1,0:T(1,128)} %ids.1, s32[1,1,8]{2,1,0:T(1,128)} %slots.1, s32[1,1]{1,0:T(1,128)S(6)} %copy.9.count, ...), custom_call_target="tpu_custom_call" | custom-call | tf_op jit(solution)/shard_map/prep/pallas_call | solution.py:388
  2.0 0.5 %collective-permute-start.1 = (bf16[128,128]{1,0:T(8,128)(2,1)S(1)}, bf16[128,128]{1,0:T(8,128)(2,1)S(1)}, u32[]{:S(2)}, u32[]{:S(2)}) collective-permute-start(bf16[128,128]{1,0:T(8,128)(2,1)S(1)} %get-tuple-element.27), channel_id=1, source_target_pairs={{1,2},{2,1},{0,4},{3,7},{5,6},{6,5},{4,0},{7,3},{9,10},{10,9},{8,1... | collective-permute-start | bytes 98312 | tf_op jit(solution)/shard_map/ppermute | solution.py:421
  2.5 4.1 %collective-permute-start = (bf16[96,128]{1,0:T(8,128)(2,1)S(1)}, bf16[96,128]{1,0:T(8,128)(2,1)S(1)}, u32[]{:S(2)}, u32[]{:S(2)}) collective-permute-start(bf16[96,128]{1,0:T(8,128)(2,1)S(1)} %get-tuple-element.26.own), channel_id=1, source_target_pairs={{0,1},{2,3},{1,0},{3,2},{4,5},{6,7},{5,4},{7,6},{8,9},{10,11},{9,8... | collective-permute-start | bytes 73736 | tf_op jit(solution)/shard_map/ppermute | solution.py:422
  6.7 0.0 copy-start.1
  6.7 1.1 %collective-permute-start.5 = (bf16[528,128]{1,0:T(8,128)(2,1)S(1)}, bf16[528,128]{1,0:T(8,128)(2,1)S(1)}, u32[]{:S(2)}, u32[]{:S(2)}) collective-permute-start(bf16[528,128]{1,0:T(8,128)(2,1)S(1)} %get-tuple-element.40), channel_id=1, source_target_pairs={{0,2},{1,3},{2,0},{3,1},{4,6},{5,7},{6,4},{7,5},{8,10},{9,11},{10,... | collective-permute-start | bytes 405512 | tf_op jit(solution)/shard_map/ppermute | solution.py:436
  7.8 1.3 %collective-permute-start.6 = (bf16[528,128]{1,0:T(8,128)(2,1)S(1)}, bf16[528,128]{1,0:T(8,128)(2,1)S(1)}, u32[]{:S(2)}, u32[]{:S(2)}) collective-permute-start(bf16[528,128]{1,0:T(8,128)(2,1)S(1)} %get-tuple-element.40), channel_id=1, source_target_pairs={{0,3},{1,2},{2,1},{3,0},{4,7},{5,6},{6,5},{7,4},{8,11},{9,10},{10,... | collective-permute-start | bytes 405512 | tf_op jit(solution)/shard_map/ppermute | solution.py:436
  9.1 0.0 collective-permute-done.from_first.col_first
  9.1 0.0 collective-permute-done.1.from_second.col_second
  9.1 0.0 copy-done
  9.1 0.2 mid.1
  9.3 0.1 collective-permute-start.2
  9.4 1.6 %collective-permute-start.3 = (bf16[48,640]{1,0:T(8,128)(2,1)S(1)}, bf16[48,640]{1,0:T(8,128)(2,1)S(1)}, u32[]{:S(2)}, u32[]{:S(2)}) collective-permute-start(bf16[48,640]{1,0:T(8,128)(2,1)S(1)} %get-tuple-element.31), channel_id=1, source_target_pairs={{4,8},{8,4},{0,16},{12,28},{20,24},{24,20},{16,0},{28,12},{5,9},{9... | collective-permute-start | bytes 184328 | tf_op jit(solution)/shard_map/ppermute | solution.py:443
  11.0 0.0 copy-done.1
  11.0 1.5 %collective-permute-start.4 = (bf16[512,128]{1,0:T(8,128)(2,1)S(1)}, bf16[512,128]{1,0:T(8,128)(2,1)S(1)}, u32[]{:S(2)}, u32[]{:S(2)}) collective-permute-start(bf16[512,128]{1,0:T(8,128)(2,1)S(1)} %bitcast.2), channel_id=1, source_target_pairs={{0,1},{1,0},{2,3},{3,2},{4,5},{5,4},{6,7},{7,6},{8,9},{9,8},{10,11... | collective-permute-start | bytes 393224 | tf_op jit(solution)/shard_map/ppermute | solution.py:436
  12.4 0.5 %own.1 = (f32[3,256,256]{2,1,0:T(8,128)S(1)}, f32[12,8,128]{2,1,0:T(8,128)S(1)}, f32[12,8,128]{2,1,0:T(8,128)S(1)}, bf16[256,256]{1,0:T(8,128)(2,1)S(1)}, bf16[2...) custom-call(s32[256,512]{1,0:T(8,128)S(1)} %copy-done, bf16[2,12,2,33]{3,2,1,0:T(2,128)(2,1)S(1)} %get-tuple-element.24.taps), custom_call_target="tpu_custom_call" | custom-call | flops 1000000 | bytes 1000000 | tf_op jit(solution)/shard_map/own/pallas_call | solution.py:445
  12.9 0.0 collective-permute-done.2.row_first
  12.9 0.8 %collective-permute-done.3.row_second = bf16[48,640]{1,0:T(8,128)(2,1)S(1)} collective-permute-done((bf16[48,640]{1,0:T(8,128)(2,1)S(1)}, bf16[48,640]{1,0:T(8,128)(2,1)S(1)}, u32[]{:S(2)}, u32[]{:S(2)}) %collective-permute-start.3) | collective-permute-done | bytes 61472 | tf_op jit(solution)/shard_map/ppermute | solution.py:443
  13.7 5.5 %socs.1 = (f32[4,176,256]{2,1,0:T(8,128)S(1)}, s32[16,128]{1,0:T(8,128)S(1)}) custom-call(f32[12]{0:T(128)S(1)} %get-tuple-element.23.weights, f32[3,256,256]{2,1,0:T(8,128)S(1)} %get-tuple-element.25.windows, bf16[48,640]{1,0:T(8,128)(2,1)S(1)} %collective-permute-done.2.row_first, bf16[48,640]{1,0:T(8,128)(2,1)S(1)} %collective-permute-done.3.row_second, ...), custom_call_target="tpu_custom_call" | custom-call | flops 750000000 | bytes 100000 | tf_op jit(solution)/shard_map/socs/pallas_call | solution.py:462
  19.2 0.5 %rows.1.blurred_rows = f32[256,640]{1,0:T(8,128)S(1)} custom-call(f32[4,176,256]{2,1,0:T(8,128)S(1)} %get-tuple-element.35.acc, bf16[256,256]{1,0:T(8,128)(2,1)S(1)} %get-tuple-element.36.g_row), custom_call_target="tpu_custom_call" | custom-call | flops 1000000 | bytes 100000 | tf_op jit(solution)/shard_map/rows/pallas_call | solution.py:480
  19.6 0.0 collective-permute-done.5.rest_2_
  19.6 0.0 collective-permute-done.6.rest_3_
  19.7 1.0 %collective-permute-done.4.rest_1_ = bf16[512,128]{1,0:T(8,128)(2,1)S(1)} collective-permute-done((bf16[512,128]{1,0:T(8,128)(2,1)S(1)}, bf16[512,128]{1,0:T(8,128)(2,1)S(1)}, u32[]{:S(2)}, u32[]{:S(2)}) %collective-permute-start.4) | collective-permute-done | bytes 131104 | tf_op jit(solution)/shard_map/ppermute | solution.py:436
  20.7 1.8 %final.1 = f32[256,512]{1,0:T(8,128)} custom-call(s32[16,128]{1,0:T(8,128)S(1)} %get-tuple-element.34.images, f32[256,640]{1,0:T(8,128)S(1)} %rows.1.blurred_rows, bf16[256,256]{1,0:T(8,128)(2,1)S(1)} %get-tuple-element.37.g_far, bf16[256,256]{1,0:T(8,128)(2,1)S(1)} %get-tuple-element.38.g_col, bf16[512,128]{1,0:T(8,128)(2,1)S(1)} %bitcast.3, ...), custom_call_target="tpu_custom_call" | custom-call | tf_op jit(solution)/shard_map/final/pallas_call | solution.py:491
Async XLA Ops:
  0.0 9.1 %copy-start = (s32[256,512]{1,0:T(8,128)S(1)}, s32[256,512]{1,0:T(8,128)}, u32[]{:S(2)}) copy-start(s32[256,512]{1,0:T(8,128)} %mask.5) | copy-start | bytes 1572868
  2.0 7.0 %collective-permute-start.1 = (bf16[128,128]{1,0:T(8,128)(2,1)S(1)}, bf16[128,128]{1,0:T(8,128)(2,1)S(1)}, u32[]{:S(2)}, u32[]{:S(2)}) collective-permute-start(bf16[128,128]{1,0:T(8,128)(2,1)S(1)} %get-tuple-element.27), channel_id=1, source_target_pairs={{1,2},{2,1},{0,4},{3,7},{5,6},{6,5},{4,0},{7,3},{9,10},{10,9},{8,1... | collective-permute-start | bytes 98312 | tf_op jit(solution)/shard_map/ppermute | solution.py:421
  2.5 6.5 %collective-permute-start = (bf16[96,128]{1,0:T(8,128)(2,1)S(1)}, bf16[96,128]{1,0:T(8,128)(2,1)S(1)}, u32[]{:S(2)}, u32[]{:S(2)}) collective-permute-start(bf16[96,128]{1,0:T(8,128)(2,1)S(1)} %get-tuple-element.26.own), channel_id=1, source_target_pairs={{0,1},{2,3},{1,0},{3,2},{4,5},{6,7},{5,4},{7,6},{8,9},{10,11},{9,8... | collective-permute-start | bytes 73736 | tf_op jit(solution)/shard_map/ppermute | solution.py:422
  6.7 4.3 %copy-start.1 = (bf16[8,64,128]{2,1,0:T(8,128)(2,1)S(1)}, bf16[8,64,128]{2,1,0:T(8,128)(2,1)}, u32[]{:S(2)}) copy-start(bf16[8,64,128]{2,1,0:T(8,128)(2,1)} %param.12) | copy-start | bytes 393220
  6.7 13.0 %collective-permute-start.5 = (bf16[528,128]{1,0:T(8,128)(2,1)S(1)}, bf16[528,128]{1,0:T(8,128)(2,1)S(1)}, u32[]{:S(2)}, u32[]{:S(2)}) collective-permute-start(bf16[528,128]{1,0:T(8,128)(2,1)S(1)} %get-tuple-element.40), channel_id=1, source_target_pairs={{0,2},{1,3},{2,0},{3,1},{4,6},{5,7},{6,4},{7,5},{8,10},{9,11},{10,... | collective-permute-start | bytes 405512 | tf_op jit(solution)/shard_map/ppermute | solution.py:436
  7.8 11.9 %collective-permute-start.6 = (bf16[528,128]{1,0:T(8,128)(2,1)S(1)}, bf16[528,128]{1,0:T(8,128)(2,1)S(1)}, u32[]{:S(2)}, u32[]{:S(2)}) collective-permute-start(bf16[528,128]{1,0:T(8,128)(2,1)S(1)} %get-tuple-element.40), channel_id=1, source_target_pairs={{0,3},{1,2},{2,1},{3,0},{4,7},{5,6},{6,5},{7,4},{8,11},{9,10},{10,... | collective-permute-start | bytes 405512 | tf_op jit(solution)/shard_map/ppermute | solution.py:436
  9.3 3.6 %collective-permute-start.2 = (bf16[48,640]{1,0:T(8,128)(2,1)S(1)}, bf16[48,640]{1,0:T(8,128)(2,1)S(1)}, u32[]{:S(2)}, u32[]{:S(2)}) collective-permute-start(bf16[48,640]{1,0:T(8,128)(2,1)S(1)} %get-tuple-element.30), channel_id=1, source_target_pairs={{0,4},{8,12},{4,0},{12,8},{1,5},{9,13},{5,1},{13,9},{2,6},{10,14},... | collective-permute-start | bytes 184328 | tf_op jit(solution)/shard_map/ppermute | solution.py:442
  9.4 4.3 %collective-permute-start.3 = (bf16[48,640]{1,0:T(8,128)(2,1)S(1)}, bf16[48,640]{1,0:T(8,128)(2,1)S(1)}, u32[]{:S(2)}, u32[]{:S(2)}) collective-permute-start(bf16[48,640]{1,0:T(8,128)(2,1)S(1)} %get-tuple-element.31), channel_id=1, source_target_pairs={{4,8},{8,4},{0,16},{12,28},{20,24},{24,20},{16,0},{28,12},{5,9},{9... | collective-permute-start | bytes 184328 | tf_op jit(solution)/shard_map/ppermute | solution.py:443
  11.0 9.7 %collective-permute-start.4 = (bf16[512,128]{1,0:T(8,128)(2,1)S(1)}, bf16[512,128]{1,0:T(8,128)(2,1)S(1)}, u32[]{:S(2)}, u32[]{:S(2)}) collective-permute-start(bf16[512,128]{1,0:T(8,128)(2,1)S(1)} %bitcast.2), channel_id=1, source_target_pairs={{0,1},{1,0},{2,3},{3,2},{4,5},{5,4},{6,7},{7,6},{8,9},{9,8},{10,11... | collective-permute-start | bytes 393224 | tf_op jit(solution)/shard_map/ppermute | solution.py:436

commit v21 on v20

--- a/solution.py
+++ b/solution.py
@@ -105,7 +105,7 @@
         copy.wait()
 
 
-def mid_kernel(mask, from_first, from_second, own, to_first, to_second):
+def mid_kernel(mask, from_first, from_second, own, earlier, to_first, to_second):
     rows, cols = mask.shape
     left, right = sides("col", join(from_first), join(from_second))
     tables = jnp.concatenate(
@@ -421,27 +421,6 @@
     col_second = lax.ppermute(to_second, ("row", "col"), second)
     col_first = lax.ppermute(to_first, "col", swaps(n_col)[0])
 
-    to_above, to_below = pl.pallas_call(
-        mid_kernel,
-        out_shape=(shape((STRIP + 16, WIDE), BF16),) * 2,
-        in_specs=[VMEM] * 4,
-        out_specs=(VMEM,) * 2,
-        compiler_params=PARAMS,
-        name="mid",
-    )(mask_pixels, col_first, col_second, to_first)
-    late, to_above, to_below = lax.optimization_barrier((library, to_above, to_below))
-    blocks = {0: library}
-    for d in sorted(range(1, n_col), key=lambda d: d == 1):
-        part = late if d == 1 else block
-        blocks[d] = lax.ppermute(part, "col", [(i, i ^ d) for i in range(n_col)])
-    shards = [blocks[d] for d in range(n_col)]
-    ends = []
-    for f in range(lax.axis_size("frames")):
-        ends += [(f * n_row + a, f * n_row + b) for a, b in swaps(n_row)[1] if abs(a - b) == 1]
-        ends += [(f * n_row + a, (f ^ 1) * n_row + a) for a in (0, n_row - 1)]
-    row_first = lax.ppermute(to_above, "row", swaps(n_row)[0])
-    row_second = lax.ppermute(to_below, ("frames", "row"), ends)
-
     windows, ahead, back, g_row, g_far, g_col = pl.pallas_call(
         own_kernel,
         out_shape=(
@@ -458,6 +437,27 @@
         cost_estimate=pl.CostEstimate(flops=10**6, bytes_accessed=10**6, transcendentals=0),
         name="own",
     )(mask_pixels, taps)
+
+    to_above, to_below = pl.pallas_call(
+        mid_kernel,
+        out_shape=(shape((STRIP + 16, WIDE), BF16),) * 2,
+        in_specs=[VMEM] * 5,
+        out_specs=(VMEM,) * 2,
+        compiler_params=PARAMS,
+        name="mid",
+    )(mask_pixels, col_first, col_second, to_first, g_row)
+    late, to_above, to_below = lax.optimization_barrier((library, to_above, to_below))
+    blocks = {0: library}
+    for d in sorted(range(1, n_col), key=lambda d: (d == n_col - 1, -(d & -d))):
+        part = late if d == n_col - 1 else block
+        blocks[d] = lax.ppermute(part, "col", [(i, i ^ d) for i in range(n_col)])
+    shards = [blocks[d] for d in range(n_col)]
+    ends = []
+    for f in range(lax.axis_size("frames")):
+        ends += [(f * n_row + a, f * n_row + b) for a, b in swaps(n_row)[1] if abs(a - b) == 1]
+        ends += [(f * n_row + a, (f ^ 1) * n_row + a) for a in (0, n_row - 1)]
+    row_first = lax.ppermute(to_above, "row", swaps(n_row)[0])
+    row_second = lax.ppermute(to_below, ("frames", "row"), ends)
 
     acc, images = pl.pallas_call(
         functools.partial(socs_kernel, entries, per, n_col * per),

time: 22.6 us -> 21.6 us (0.956)
  waiting for transfers between devices: 1.79 us -> 0.24 us
  starting transfers between devices: 10.1 us -> 10.7 us
    ppermute x3, waiting for transfers between devices: 1.02 us -> 0.01 us  [on_device(): blocks[d] = lax.ppermute(part, 'col', [(i, i ^ d) for i in range(n_col)])]
    ppermute x3, starting transfers between devices: 3.82 us -> 4.39 us  [on_device(): blocks[d] = lax.ppermute(part, 'col', [(i, i ^ d) for i in range(n_col)])]
    ppermute x1, waiting for transfers between devices: 0.76 us -> 0.22 us  [on_device(): row_second = lax.ppermute(to_below, ('frames', 'row'), ends)]
  transfers between devices with their start and end apart: 7 -> 7, of which waited for: 2 -> 1; matrix products, arithmetic and copies ran while one was open for 0% -> 0% of each run, Pallas kernels for 30% -> 31%
where the time goes in v21:
time: 21.6 us; the launch traced here: 21.5 us
  starting transfers between devices  10.7 us (50%)
  Pallas kernels  9.73 us (45%)
  between operations  0.8 us (4%)
  waiting for transfers between devices  0.24 us (1%)
    pallas_call x1, Pallas kernels, on_device(): pl.pallas_call(functools.partial(socs_kernel, entries, per, n_col * per),...  5.48 us
    ppermute x3, starting transfers between devices, on_device(): blocks[d] = lax.ppermute(part, 'col', [(i, i ^ d) for i in range(n_col)])  4.39 us
    ppermute x1, starting transfers between devices, on_device(): col_first = lax.ppermute(to_first, 'col', swaps(n_col)[0])  4.15 us
    pallas_call x1, Pallas kernels, on_device(): pl.pallas_call(final_kernel, out_shape=shape((rows, cols), F32), in_specs...  1.78 us
    ppermute x1, starting transfers between devices, on_device(): row_second = lax.ppermute(to_below, ('frames', 'row'), ends)  1.58 us
    pallas_call x1, Pallas kernels, on_device(): pl.pallas_call(prep_kernel, out_shape=(shape((2 * HALF_STRIP, 128), BF16)...  1.3 us
    ppermute x1, starting transfers between devices, on_device(): col_second = lax.ppermute(to_second, ('row', 'col'), second)  0.52 us
    pallas_call x1, Pallas kernels, on_device(): pl.pallas_call(own_kernel, out_shape=(shape((NB, rows, 256), F32), shape(...  0.48 us
  transfers between devices with their start and end apart: 7, of which 1 were waited for; matrix products, arithmetic and copies ran while one was open for 0% of the time, Pallas kernels for 31%

profile of v21, /device:TPU:0, one launch (start us, length us, event | category | flops | bytes accessed | tf_op | source)
XLA Modules:
  0.0 21.5 jit_solution(10401130301797234441)
XLA Ops:
  0.0 0.0 copy-start
  0.7 1.3 %prep.1 = (bf16[96,128]{1,0:T(8,128)(2,1)S(1)}, bf16[128,128]{1,0:T(8,128)(2,1)S(1)}, bf16[528,128]{1,0:T(8,128)(2,1)S(1)}, bf16[2,12,2,33]{3,2,1,0:T(2,128)(2,1)S(1)}, f32[12]{0:T(128)S(1)}) custom-call(s32[256,512]{1,0:T(8,128)} %mask.5, s32[1,1,8]{2,1,0:T(1,128)} %ids.1, s32[1,1,8]{2,1,0:T(1,128)} %slots.1, s32[1,1]{1,0:T(1,128)S(6)} %copy.9.count, ...), custom_call_target="tpu_custom_call" | custom-call | tf_op jit(solution)/shard_map/prep/pallas_call | solution.py:388
  2.0 0.5 %collective-permute-start.1 = (bf16[128,128]{1,0:T(8,128)(2,1)S(1)}, bf16[128,128]{1,0:T(8,128)(2,1)S(1)}, u32[]{:S(2)}, u32[]{:S(2)}) collective-permute-start(bf16[128,128]{1,0:T(8,128)(2,1)S(1)} %get-tuple-element.27), channel_id=1, source_target_pairs={{1,2},{2,1},{0,4},{3,7},{5,6},{6,5},{4,0},{7,3},{9,10},{10,9},{8,1... | collective-permute-start | bytes 98312 | tf_op jit(solution)/shard_map/ppermute | solution.py:421
  2.5 4.1 %collective-permute-start = (bf16[96,128]{1,0:T(8,128)(2,1)S(1)}, bf16[96,128]{1,0:T(8,128)(2,1)S(1)}, u32[]{:S(2)}, u32[]{:S(2)}) collective-permute-start(bf16[96,128]{1,0:T(8,128)(2,1)S(1)} %get-tuple-element.26.own), channel_id=1, source_target_pairs={{0,1},{2,3},{1,0},{3,2},{4,5},{6,7},{5,4},{7,6},{8,9},{10,11},{9,8... | collective-permute-start | bytes 73736 | tf_op jit(solution)/shard_map/ppermute | solution.py:422
  6.7 0.0 collective-permute-start.4
  6.7 1.9 %collective-permute-start.5 = (bf16[528,128]{1,0:T(8,128)(2,1)S(1)}, bf16[528,128]{1,0:T(8,128)(2,1)S(1)}, u32[]{:S(2)}, u32[]{:S(2)}) collective-permute-start(bf16[528,128]{1,0:T(8,128)(2,1)S(1)} %get-tuple-element.39), channel_id=1, source_target_pairs={{0,2},{1,3},{2,0},{3,1},{4,6},{5,7},{6,4},{7,5},{8,10},{9,11},{10,... | collective-permute-start | bytes 405512 | tf_op jit(solution)/shard_map/ppermute | solution.py:453
  8.6 0.0 copy-done
  8.6 0.5 %own.1 = (f32[3,256,256]{2,1,0:T(8,128)S(1)}, f32[12,8,128]{2,1,0:T(8,128)S(1)}, f32[12,8,128]{2,1,0:T(8,128)S(1)}, bf16[256,256]{1,0:T(8,128)(2,1)S(1)}, bf16[2...) custom-call(s32[256,512]{1,0:T(8,128)S(1)} %copy-done, bf16[2,12,2,33]{3,2,1,0:T(2,128)(2,1)S(1)} %get-tuple-element.24.taps), custom_call_target="tpu_custom_call" | custom-call | flops 1000000 | bytes 1000000 | tf_op jit(solution)/shard_map/own/pallas_call | solution.py:424
  9.1 0.0 collective-permute-done.from_first.col_first
  9.1 0.0 collective-permute-done.1.from_second.col_second
  9.1 0.0 copy-start.1
  9.1 0.2 %mid.1 = (bf16[48,640]{1,0:T(8,128)(2,1)S(1)}, bf16[48,640]{1,0:T(8,128)(2,1)S(1)}) custom-call(s32[256,512]{1,0:T(8,128)S(1)} %copy-done, bf16[96,128]{1,0:T(8,128)(2,1)S(1)} %collective-permute-done.from_first.col_first, bf16[128,128]{1,0:T(8,128)(2,1)S(1)} %collective-permute-done.1.from_second.col_second, bf16[96,128]{1,0:T(8,128)(2,1)S(1)} %get-tuple-element.26.own, ...), custom_call_target="tpu_custom_call" | custom-call | tf_op jit(solution)/shard_map/mid/pallas_call | solution.py:441
  9.3 0.1 collective-permute-start.2
  9.4 1.6 %collective-permute-start.3 = (bf16[48,640]{1,0:T(8,128)(2,1)S(1)}, bf16[48,640]{1,0:T(8,128)(2,1)S(1)}, u32[]{:S(2)}, u32[]{:S(2)}) collective-permute-start(bf16[48,640]{1,0:T(8,128)(2,1)S(1)} %get-tuple-element.32), channel_id=1, source_target_pairs={{4,8},{8,4},{0,16},{12,28},{20,24},{24,20},{16,0},{28,12},{5,9},{9... | collective-permute-start | bytes 184328 | tf_op jit(solution)/shard_map/ppermute | solution.py:460
  11.0 0.0 copy-done.1
  11.0 2.5 %collective-permute-start.6 = (bf16[512,128]{1,0:T(8,128)(2,1)S(1)}, bf16[512,128]{1,0:T(8,128)(2,1)S(1)}, u32[]{:S(2)}, u32[]{:S(2)}) collective-permute-start(bf16[512,128]{1,0:T(8,128)(2,1)S(1)} %bitcast.2), channel_id=1, source_target_pairs={{0,3},{1,2},{2,1},{3,0},{4,7},{5,6},{6,5},{7,4},{8,11},{9,10},{10,... | collective-permute-start | bytes 393224 | tf_op jit(solution)/shard_map/ppermute | solution.py:453
  13.5 0.0 collective-permute-done.2.row_first
  13.5 0.2 %collective-permute-done.3.row_second = bf16[48,640]{1,0:T(8,128)(2,1)S(1)} collective-permute-done((bf16[48,640]{1,0:T(8,128)(2,1)S(1)}, bf16[48,640]{1,0:T(8,128)(2,1)S(1)}, u32[]{:S(2)}, u32[]{:S(2)}) %collective-permute-start.3) | collective-permute-done | bytes 61472 | tf_op jit(solution)/shard_map/ppermute | solution.py:460
  13.7 5.5 %socs.1 = (f32[4,176,256]{2,1,0:T(8,128)S(1)}, s32[16,128]{1,0:T(8,128)S(1)}) custom-call(f32[12]{0:T(128)S(1)} %get-tuple-element.23.weights, f32[3,256,256]{2,1,0:T(8,128)S(1)} %get-tuple-element.25.windows, bf16[48,640]{1,0:T(8,128)(2,1)S(1)} %collective-permute-done.2.row_first, bf16[48,640]{1,0:T(8,128)(2,1)S(1)} %collective-permute-done.3.row_second, ...), custom_call_target="tpu_custom_call" | custom-call | flops 750000000 | bytes 100000 | tf_op jit(solution)/shard_map/socs/pallas_call | solution.py:462
  19.2 0.5 %rows.1.blurred_rows = f32[256,640]{1,0:T(8,128)S(1)} custom-call(f32[4,176,256]{2,1,0:T(8,128)S(1)} %get-tuple-element.36.acc, bf16[256,256]{1,0:T(8,128)(2,1)S(1)} %get-tuple-element.28.earlier.g_row), custom_call_target="tpu_custom_call" | custom-call | flops 1000000 | bytes 100000 | tf_op jit(solution)/shard_map/rows/pallas_call | solution.py:480
  19.7 0.0 collective-permute-done.4.rest_1_
  19.7 0.0 collective-permute-done.5.rest_2_
  19.7 0.0 collective-permute-done.6.rest_3_
  19.7 1.8 %final.1 = f32[256,512]{1,0:T(8,128)} custom-call(s32[16,128]{1,0:T(8,128)S(1)} %get-tuple-element.35.images, f32[256,640]{1,0:T(8,128)S(1)} %rows.1.blurred_rows, bf16[256,256]{1,0:T(8,128)(2,1)S(1)} %get-tuple-element.37.g_far, bf16[256,256]{1,0:T(8,128)(2,1)S(1)} %get-tuple-element.38.g_col, bf16[512,128]{1,0:T(8,128)(2,1)S(1)} %bitcast.3, ...), custom_call_target="tpu_custom_call" | custom-call | tf_op jit(solution)/shard_map/final/pallas_call | solution.py:491
Async XLA Ops:
  0.0 8.6 %copy-start = (s32[256,512]{1,0:T(8,128)S(1)}, s32[256,512]{1,0:T(8,128)}, u32[]{:S(2)}) copy-start(s32[256,512]{1,0:T(8,128)} %mask.5) | copy-start | bytes 1572868
  2.0 7.1 %collective-permute-start.1 = (bf16[128,128]{1,0:T(8,128)(2,1)S(1)}, bf16[128,128]{1,0:T(8,128)(2,1)S(1)}, u32[]{:S(2)}, u32[]{:S(2)}) collective-permute-start(bf16[128,128]{1,0:T(8,128)(2,1)S(1)} %get-tuple-element.27), channel_id=1, source_target_pairs={{1,2},{2,1},{0,4},{3,7},{5,6},{6,5},{4,0},{7,3},{9,10},{10,9},{8,1... | collective-permute-start | bytes 98312 | tf_op jit(solution)/shard_map/ppermute | solution.py:421
  2.5 6.5 %collective-permute-start = (bf16[96,128]{1,0:T(8,128)(2,1)S(1)}, bf16[96,128]{1,0:T(8,128)(2,1)S(1)}, u32[]{:S(2)}, u32[]{:S(2)}) collective-permute-start(bf16[96,128]{1,0:T(8,128)(2,1)S(1)} %get-tuple-element.26.own), channel_id=1, source_target_pairs={{0,1},{2,3},{1,0},{3,2},{4,5},{6,7},{5,4},{7,6},{8,9},{10,11},{9,8... | collective-permute-start | bytes 73736 | tf_op jit(solution)/shard_map/ppermute | solution.py:422
  6.7 13.0 %collective-permute-start.4 = (bf16[528,128]{1,0:T(8,128)(2,1)S(1)}, bf16[528,128]{1,0:T(8,128)(2,1)S(1)}, u32[]{:S(2)}, u32[]{:S(2)}) collective-permute-start(bf16[528,128]{1,0:T(8,128)(2,1)S(1)} %get-tuple-element.39), channel_id=1, source_target_pairs={{0,1},{1,0},{2,3},{3,2},{4,5},{5,4},{6,7},{7,6},{8,9},{9,8},{10,11... | collective-permute-start | bytes 405512 | tf_op jit(solution)/shard_map/ppermute | solution.py:453
  6.7 13.0 %collective-permute-start.5 = (bf16[528,128]{1,0:T(8,128)(2,1)S(1)}, bf16[528,128]{1,0:T(8,128)(2,1)S(1)}, u32[]{:S(2)}, u32[]{:S(2)}) collective-permute-start(bf16[528,128]{1,0:T(8,128)(2,1)S(1)} %get-tuple-element.39), channel_id=1, source_target_pairs={{0,2},{1,3},{2,0},{3,1},{4,6},{5,7},{6,4},{7,5},{8,10},{9,11},{10,... | collective-permute-start | bytes 405512 | tf_op jit(solution)/shard_map/ppermute | solution.py:453
  9.1 1.9 %copy-start.1 = (bf16[8,64,128]{2,1,0:T(8,128)(2,1)S(1)}, bf16[8,64,128]{2,1,0:T(8,128)(2,1)}, u32[]{:S(2)}) copy-start(bf16[8,64,128]{2,1,0:T(8,128)(2,1)} %param.12) | copy-start | bytes 393220
  9.3 4.1 %collective-permute-start.2 = (bf16[48,640]{1,0:T(8,128)(2,1)S(1)}, bf16[48,640]{1,0:T(8,128)(2,1)S(1)}, u32[]{:S(2)}, u32[]{:S(2)}) collective-permute-start(bf16[48,640]{1,0:T(8,128)(2,1)S(1)} %get-tuple-element.31), channel_id=1, source_target_pairs={{0,4},{8,12},{4,0},{12,8},{1,5},{9,13},{5,1},{13,9},{2,6},{10,14},... | collective-permute-start | bytes 184328 | tf_op jit(solution)/shard_map/ppermute | solution.py:459
  9.4 4.3 %collective-permute-start.3 = (bf16[48,640]{1,0:T(8,128)(2,1)S(1)}, bf16[48,640]{1,0:T(8,128)(2,1)S(1)}, u32[]{:S(2)}, u32[]{:S(2)}) collective-permute-start(bf16[48,640]{1,0:T(8,128)(2,1)S(1)} %get-tuple-element.32), channel_id=1, source_target_pairs={{4,8},{8,4},{0,16},{12,28},{20,24},{24,20},{16,0},{28,12},{5,9},{9... | collective-permute-start | bytes 184328 | tf_op jit(solution)/shard_map/ppermute | solution.py:460
  11.0 8.7 %collective-permute-start.6 = (bf16[512,128]{1,0:T(8,128)(2,1)S(1)}, bf16[512,128]{1,0:T(8,128)(2,1)S(1)}, u32[]{:S(2)}, u32[]{:S(2)}) collective-permute-start(bf16[512,128]{1,0:T(8,128)(2,1)S(1)} %bitcast.2), channel_id=1, source_target_pairs={{0,3},{1,2},{2,1},{3,0},{4,7},{5,6},{6,5},{7,4},{8,11},{9,10},{10,... | collective-permute-start | bytes 393224 | tf_op jit(solution)/shard_map/ppermute | solution.py:453

commit v22 on v20

--- a/solution.py
+++ b/solution.py
@@ -431,8 +431,8 @@
     )(mask_pixels, col_first, col_second, to_first)
     late, to_above, to_below = lax.optimization_barrier((library, to_above, to_below))
     blocks = {0: library}
-    for d in sorted(range(1, n_col), key=lambda d: d == 1):
-        part = late if d == 1 else block
+    for d in sorted(range(1, n_col), key=lambda d: (d == n_col - 1, -(d & -d))):
+        part = late if d == n_col - 1 else block
         blocks[d] = lax.ppermute(part, "col", [(i, i ^ d) for i in range(n_col)])
     shards = [blocks[d] for d in range(n_col)]
     ends = []

time: 22.6 us -> 21.6 us (0.956)
  waiting for transfers between devices: 1.79 us -> 0.02 us
  starting transfers between devices: 10.1 us -> 10.9 us
    ppermute x3, waiting for transfers between devices: 1.02 us -> 0.01 us  [on_device(): blocks[d] = lax.ppermute(part, 'col', [(i, i ^ d) for i in range(n_col)])]
    ppermute x1, waiting for transfers between devices: 0.76 us -> 0.01 us  [on_device(): row_second = lax.ppermute(to_below, ('frames', 'row'), ends)]
    ppermute x3, starting transfers between devices: 3.82 us -> 4.53 us  [on_device(): blocks[d] = lax.ppermute(part, 'col', [(i, i ^ d) for i in range(n_col)])]
  transfers between devices with their start and end apart: 7 -> 7, of which waited for: 2 -> 0; matrix products, arithmetic and copies ran while one was open for 0% -> 0% of each run, Pallas kernels for 30% -> 31%
where the time goes in v22:
time: 21.6 us; the launch traced here: 21.4 us
  starting transfers between devices  10.9 us (50%)
  Pallas kernels  9.73 us (45%)
  between operations  0.8 us (4%)
    pallas_call x1, Pallas kernels, on_device(): pl.pallas_call(functools.partial(socs_kernel, entries, per, n_col * per),...  5.48 us
    ppermute x3, starting transfers between devices, on_device(): blocks[d] = lax.ppermute(part, 'col', [(i, i ^ d) for i in range(n_col)])  4.53 us
    ppermute x1, starting transfers between devices, on_device(): col_first = lax.ppermute(to_first, 'col', swaps(n_col)[0])  4.15 us
    pallas_call x1, Pallas kernels, on_device(): pl.pallas_call(final_kernel, out_shape=shape((rows, cols), F32), in_specs...  1.78 us
    ppermute x1, starting transfers between devices, on_device(): row_second = lax.ppermute(to_below, ('frames', 'row'), ends)  1.58 us
    pallas_call x1, Pallas kernels, on_device(): pl.pallas_call(prep_kernel, out_shape=(shape((2 * HALF_STRIP, 128), BF16)...  1.3 us
    ppermute x1, starting transfers between devices, on_device(): col_second = lax.ppermute(to_second, ('row', 'col'), second)  0.52 us
    pallas_call x1, Pallas kernels, on_device(): pl.pallas_call(own_kernel, out_shape=(shape((NB, rows, 256), F32), shape(...  0.47 us
  transfers between devices with their start and end apart: 7, of which 0 were waited for; matrix products, arithmetic and copies ran while one was open for 0% of the time, Pallas kernels for 31%

profile of v22, /device:TPU:0, one launch (start us, length us, event | category | flops | bytes accessed | tf_op | source)
XLA Modules:
  0.0 21.4 jit_solution(14789991312065944192)
XLA Ops:
  0.0 0.0 copy-start
  0.7 1.3 %prep.1 = (bf16[96,128]{1,0:T(8,128)(2,1)S(1)}, bf16[128,128]{1,0:T(8,128)(2,1)S(1)}, bf16[528,128]{1,0:T(8,128)(2,1)S(1)}, bf16[2,12,2,33]{3,2,1,0:T(2,128)(2,1)S(1)}, f32[12]{0:T(128)S(1)}) custom-call(s32[256,512]{1,0:T(8,128)} %mask.5, s32[1,1,8]{2,1,0:T(1,128)} %ids.1, s32[1,1,8]{2,1,0:T(1,128)} %slots.1, s32[1,1]{1,0:T(1,128)S(6)} %copy.9.count, ...), custom_call_target="tpu_custom_call" | custom-call | tf_op jit(solution)/shard_map/prep/pallas_call | solution.py:388
  2.0 0.5 %collective-permute-start.1 = (bf16[128,128]{1,0:T(8,128)(2,1)S(1)}, bf16[128,128]{1,0:T(8,128)(2,1)S(1)}, u32[]{:S(2)}, u32[]{:S(2)}) collective-permute-start(bf16[128,128]{1,0:T(8,128)(2,1)S(1)} %get-tuple-element.27), channel_id=1, source_target_pairs={{1,2},{2,1},{0,4},{3,7},{5,6},{6,5},{4,0},{7,3},{9,10},{10,9},{8,1... | collective-permute-start | bytes 98312 | tf_op jit(solution)/shard_map/ppermute | solution.py:421
  2.5 4.1 %collective-permute-start = (bf16[96,128]{1,0:T(8,128)(2,1)S(1)}, bf16[96,128]{1,0:T(8,128)(2,1)S(1)}, u32[]{:S(2)}, u32[]{:S(2)}) collective-permute-start(bf16[96,128]{1,0:T(8,128)(2,1)S(1)} %get-tuple-element.26.own), channel_id=1, source_target_pairs={{0,1},{2,3},{1,0},{3,2},{4,5},{6,7},{5,4},{7,6},{8,9},{10,11},{9,8... | collective-permute-start | bytes 73736 | tf_op jit(solution)/shard_map/ppermute | solution.py:422
  6.7 0.0 copy-start.1
  6.7 0.0 collective-permute-start.4
  6.7 1.9 %collective-permute-start.5 = (bf16[528,128]{1,0:T(8,128)(2,1)S(1)}, bf16[528,128]{1,0:T(8,128)(2,1)S(1)}, u32[]{:S(2)}, u32[]{:S(2)}) collective-permute-start(bf16[528,128]{1,0:T(8,128)(2,1)S(1)} %get-tuple-element.39), channel_id=1, source_target_pairs={{0,2},{1,3},{2,0},{3,1},{4,6},{5,7},{6,4},{7,5},{8,10},{9,11},{10,... | collective-permute-start | bytes 405512 | tf_op jit(solution)/shard_map/ppermute | solution.py:436
  8.6 0.0 collective-permute-done.from_first.col_first
  8.6 0.0 collective-permute-done.1.from_second.col_second
  8.6 0.0 copy-done
  8.6 0.2 %mid.1 = (bf16[48,640]{1,0:T(8,128)(2,1)S(1)}, bf16[48,640]{1,0:T(8,128)(2,1)S(1)}) custom-call(s32[256,512]{1,0:T(8,128)S(1)} %copy-done, bf16[96,128]{1,0:T(8,128)(2,1)S(1)} %collective-permute-done.from_first.col_first, bf16[128,128]{1,0:T(8,128)(2,1)S(1)} %collective-permute-done.1.from_second.col_second, bf16[96,128]{1,0:T(8,128)(2,1)S(1)} %get-tuple-element.26.own), custom_call_target="tpu_custom_call" | custom-call | tf_op jit(solution)/shard_map/mid/pallas_call | solution.py:424
  8.8 0.1 collective-permute-start.2
  8.9 1.6 %collective-permute-start.3 = (bf16[48,640]{1,0:T(8,128)(2,1)S(1)}, bf16[48,640]{1,0:T(8,128)(2,1)S(1)}, u32[]{:S(2)}, u32[]{:S(2)}) collective-permute-start(bf16[48,640]{1,0:T(8,128)(2,1)S(1)} %get-tuple-element.31), channel_id=1, source_target_pairs={{4,8},{8,4},{0,16},{12,28},{20,24},{24,20},{16,0},{28,12},{5,9},{9... | collective-permute-start | bytes 184328 | tf_op jit(solution)/shard_map/ppermute | solution.py:443
  10.5 0.0 copy-done.1
  10.5 2.6 %collective-permute-start.6 = (bf16[512,128]{1,0:T(8,128)(2,1)S(1)}, bf16[512,128]{1,0:T(8,128)(2,1)S(1)}, u32[]{:S(2)}, u32[]{:S(2)}) collective-permute-start(bf16[512,128]{1,0:T(8,128)(2,1)S(1)} %bitcast.2), channel_id=1, source_target_pairs={{0,3},{1,2},{2,1},{3,0},{4,7},{5,6},{6,5},{7,4},{8,11},{9,10},{10,... | collective-permute-start | bytes 393224 | tf_op jit(solution)/shard_map/ppermute | solution.py:436
  13.1 0.5 %own.1 = (f32[3,256,256]{2,1,0:T(8,128)S(1)}, f32[12,8,128]{2,1,0:T(8,128)S(1)}, f32[12,8,128]{2,1,0:T(8,128)S(1)}, bf16[256,256]{1,0:T(8,128)(2,1)S(1)}, bf16[2...) custom-call(s32[256,512]{1,0:T(8,128)S(1)} %copy-done, bf16[2,12,2,33]{3,2,1,0:T(2,128)(2,1)S(1)} %get-tuple-element.24.taps), custom_call_target="tpu_custom_call" | custom-call | flops 1000000 | bytes 1000000 | tf_op jit(solution)/shard_map/own/pallas_call | solution.py:445
  13.6 0.0 collective-permute-done.2.row_first
  13.6 0.0 collective-permute-done.3.row_second
  13.6 5.5 %socs.1 = (f32[4,176,256]{2,1,0:T(8,128)S(1)}, s32[16,128]{1,0:T(8,128)S(1)}) custom-call(f32[12]{0:T(128)S(1)} %get-tuple-element.23.weights, f32[3,256,256]{2,1,0:T(8,128)S(1)} %get-tuple-element.25.windows, bf16[48,640]{1,0:T(8,128)(2,1)S(1)} %collective-permute-done.2.row_first, bf16[48,640]{1,0:T(8,128)(2,1)S(1)} %collective-permute-done.3.row_second, ...), custom_call_target="tpu_custom_call" | custom-call | flops 750000000 | bytes 100000 | tf_op jit(solution)/shard_map/socs/pallas_call | solution.py:462
  19.1 0.5 %rows.1.blurred_rows = f32[256,640]{1,0:T(8,128)S(1)} custom-call(f32[4,176,256]{2,1,0:T(8,128)S(1)} %get-tuple-element.35.acc, bf16[256,256]{1,0:T(8,128)(2,1)S(1)} %get-tuple-element.36.g_row), custom_call_target="tpu_custom_call" | custom-call | flops 1000000 | bytes 100000 | tf_op jit(solution)/shard_map/rows/pallas_call | solution.py:480
  19.6 0.0 collective-permute-done.4.rest_1_
  19.6 0.0 collective-permute-done.5.rest_2_
  19.6 0.0 collective-permute-done.6.rest_3_
  19.6 1.8 %final.1 = f32[256,512]{1,0:T(8,128)} custom-call(s32[16,128]{1,0:T(8,128)S(1)} %get-tuple-element.34.images, f32[256,640]{1,0:T(8,128)S(1)} %rows.1.blurred_rows, bf16[256,256]{1,0:T(8,128)(2,1)S(1)} %get-tuple-element.37.g_far, bf16[256,256]{1,0:T(8,128)(2,1)S(1)} %get-tuple-element.38.g_col, bf16[512,128]{1,0:T(8,128)(2,1)S(1)} %bitcast.3, ...), custom_call_target="tpu_custom_call" | custom-call | tf_op jit(solution)/shard_map/final/pallas_call | solution.py:491
Async XLA Ops:
  0.0 8.6 %copy-start = (s32[256,512]{1,0:T(8,128)S(1)}, s32[256,512]{1,0:T(8,128)}, u32[]{:S(2)}) copy-start(s32[256,512]{1,0:T(8,128)} %mask.5) | copy-start | bytes 1572868
  2.0 6.6 %collective-permute-start.1 = (bf16[128,128]{1,0:T(8,128)(2,1)S(1)}, bf16[128,128]{1,0:T(8,128)(2,1)S(1)}, u32[]{:S(2)}, u32[]{:S(2)}) collective-permute-start(bf16[128,128]{1,0:T(8,128)(2,1)S(1)} %get-tuple-element.27), channel_id=1, source_target_pairs={{1,2},{2,1},{0,4},{3,7},{5,6},{6,5},{4,0},{7,3},{9,10},{10,9},{8,1... | collective-permute-start | bytes 98312 | tf_op jit(solution)/shard_map/ppermute | solution.py:421
  2.5 6.1 %collective-permute-start = (bf16[96,128]{1,0:T(8,128)(2,1)S(1)}, bf16[96,128]{1,0:T(8,128)(2,1)S(1)}, u32[]{:S(2)}, u32[]{:S(2)}) collective-permute-start(bf16[96,128]{1,0:T(8,128)(2,1)S(1)} %get-tuple-element.26.own), channel_id=1, source_target_pairs={{0,1},{2,3},{1,0},{3,2},{4,5},{6,7},{5,4},{7,6},{8,9},{10,11},{9,8... | collective-permute-start | bytes 73736 | tf_op jit(solution)/shard_map/ppermute | solution.py:422
  6.7 3.8 %copy-start.1 = (bf16[8,64,128]{2,1,0:T(8,128)(2,1)S(1)}, bf16[8,64,128]{2,1,0:T(8,128)(2,1)}, u32[]{:S(2)}) copy-start(bf16[8,64,128]{2,1,0:T(8,128)(2,1)} %param.12) | copy-start | bytes 393220
  6.7 12.9 %collective-permute-start.4 = (bf16[528,128]{1,0:T(8,128)(2,1)S(1)}, bf16[528,128]{1,0:T(8,128)(2,1)S(1)}, u32[]{:S(2)}, u32[]{:S(2)}) collective-permute-start(bf16[528,128]{1,0:T(8,128)(2,1)S(1)} %get-tuple-element.39), channel_id=1, source_target_pairs={{0,1},{1,0},{2,3},{3,2},{4,5},{5,4},{6,7},{7,6},{8,9},{9,8},{10,11... | collective-permute-start | bytes 405512 | tf_op jit(solution)/shard_map/ppermute | solution.py:436
  6.7 12.9 %collective-permute-start.5 = (bf16[528,128]{1,0:T(8,128)(2,1)S(1)}, bf16[528,128]{1,0:T(8,128)(2,1)S(1)}, u32[]{:S(2)}, u32[]{:S(2)}) collective-permute-start(bf16[528,128]{1,0:T(8,128)(2,1)S(1)} %get-tuple-element.39), channel_id=1, source_target_pairs={{0,2},{1,3},{2,0},{3,1},{4,6},{5,7},{6,4},{7,5},{8,10},{9,11},{10,... | collective-permute-start | bytes 405512 | tf_op jit(solution)/shard_map/ppermute | solution.py:436
  8.8 4.8 %collective-permute-start.2 = (bf16[48,640]{1,0:T(8,128)(2,1)S(1)}, bf16[48,640]{1,0:T(8,128)(2,1)S(1)}, u32[]{:S(2)}, u32[]{:S(2)}) collective-permute-start(bf16[48,640]{1,0:T(8,128)(2,1)S(1)} %get-tuple-element.30), channel_id=1, source_target_pairs={{0,4},{8,12},{4,0},{12,8},{1,5},{9,13},{5,1},{13,9},{2,6},{10,14},... | collective-permute-start | bytes 184328 | tf_op jit(solution)/shard_map/ppermute | solution.py:442
  8.9 4.7 %collective-permute-start.3 = (bf16[48,640]{1,0:T(8,128)(2,1)S(1)}, bf16[48,640]{1,0:T(8,128)(2,1)S(1)}, u32[]{:S(2)}, u32[]{:S(2)}) collective-permute-start(bf16[48,640]{1,0:T(8,128)(2,1)S(1)} %get-tuple-element.31), channel_id=1, source_target_pairs={{4,8},{8,4},{0,16},{12,28},{20,24},{24,20},{16,0},{28,12},{5,9},{9... | collective-permute-start | bytes 184328 | tf_op jit(solution)/shard_map/ppermute | solution.py:443
  10.5 9.1 %collective-permute-start.6 = (bf16[512,128]{1,0:T(8,128)(2,1)S(1)}, bf16[512,128]{1,0:T(8,128)(2,1)S(1)}, u32[]{:S(2)}, u32[]{:S(2)}) collective-permute-start(bf16[512,128]{1,0:T(8,128)(2,1)S(1)} %bitcast.2), channel_id=1, source_target_pairs={{0,3},{1,2},{2,1},{3,0},{4,7},{5,6},{6,5},{7,4},{8,11},{9,10},{10,... | collective-permute-start | bytes 393224 | tf_op jit(solution)/shard_map/ppermute | solution.py:436
